TPU v7x, 32 devices: a whole 2x2x4 slice. The times are simulated.
32 devices in a mesh: group: 2 (over x), expert: 16 (over z, y, core).
Axes of the slice: x: 2, y: 2, z: 4, core: 2. Of those that a mesh axis runs over, the one named last changes fastest.
Arguments:
- tokens: bfloat16 [2, 128, 2048], P('group', 'expert'), may hold values from -6 to 6
- norm_gain: float32 [2048], replicated, may hold values from 0.1 to 1.9
- routes: int32 [2, 2, 128, 8], P(None, 'group', 'expert'), may hold values from 0 to 15, all different within a row; in each aligned block of 8 rows (0 to 7, 8 to 15, ..., all dimensions but the last counted through in order) at most 8 rows name the same one
- route_scale: float32 [2, 2, 128, 8], P(None, 'group', 'expert'), may hold values from 0.1 to 1
- changed: int32 [2, 4], P('group'), may hold values from 0 to 15, as said below
- rollout_up: bfloat16 [16, 768, 2048], P('expert'), may hold values from -0.125 to 0.125
- rollout_down: bfloat16 [16, 768, 2048], P('expert'), may hold values from -0.21875 to 0.21875
- learner_up: bfloat16 [16, 768, 2048], P('expert', 'group'), may hold values from -0.125 to 0.125
- learner_down: bfloat16 [16, 768, 2048], P('expert', 'group'), may hold values from -0.21875 to 0.21875
Outputs:
- updated: bfloat16 [2, 128, 2048], P('group', 'expert')
Inputs may be any that keep to these rules, and one draw needn't show every extreme that they name: `routes`: at one step, no expert is named by more than 8 of the 8 rows of one device; some aligned block of 8 rows reaches 8. `changed`: each group's row lists 4 different experts.
All inputs are finite; a program needn't handle non-finite values.
Results may differ from a plain program's by a relative error of at most 0.0062.
Values may be sent and summed in bfloat16 or wider, within the bound.
No kernel may reach another device: no remote copies, remote signals or barrier semaphores. Data moves between devices by JAX's collectives and lax.ppermute only.
A program may use at most 64 MiB of HBM per device.

v0:
```python
import jax
import jax.numpy as jnp
from jax import lax
from jax.sharding import PartitionSpec as P


def normalize(state, norm_gain):
    scale = lax.rsqrt(jnp.mean(state * state, axis=-1, keepdims=True) + 1e-06)
    return (state * scale * norm_gain).astype(jnp.bfloat16)


def expert_apply(inputs, up_rows, down_rows):
    pre_act = lax.dot_general(
        inputs, up_rows, (((1,), (1,)), ((), ())), preferred_element_type=jnp.float32
    )
    hidden = jax.nn.silu(pre_act).astype(jnp.bfloat16)
    return jnp.dot(hidden, down_rows, preferred_element_type=jnp.float32)


def local(
    tokens,
    norm_gain,
    routes,
    route_scale,
    changed,
    rollout_up,
    rollout_down,
    learner_up,
    learner_down,
):
    experts = lax.axis_size("expert")
    owner_index = lax.axis_index("expert")
    row_count = tokens.shape[1]
    top_count = routes.shape[3]
    steps_total = routes.shape[0]
    capacity = min(row_count, max(2, 2 * row_count * top_count // experts))
    is_fresh = jnp.any(changed[0] == owner_index)
    stale_up = rollout_up[0]
    stale_down = rollout_down[0]
    fresh_up, fresh_down = (
        lax.all_gather(learner_up, "group", axis=1, tiled=True),
        lax.all_gather(learner_down, "group", axis=1, tiled=True),
    )
    newer_up = jnp.where(is_fresh, fresh_up[0], stale_up)
    newer_down = jnp.where(is_fresh, fresh_down[0], stale_down)
    state = tokens[0].astype(jnp.float32)
    buffer_ids = jnp.arange(experts * capacity, dtype=jnp.int32)
    expert_ids = jnp.arange(experts, dtype=jnp.int32)
    for step in range(steps_total):
        normed = normalize(state, norm_gain)
        chosen = routes[step, 0]
        weights = route_scale[step, 0]
        hits = (chosen.reshape(-1)[:, None] == expert_ids[None, :]).astype(jnp.int32)
        before = jnp.cumsum(hits, axis=0) - hits
        slot_pos = jnp.sum(before * hits, axis=1).reshape(chosen.shape)
        target = chosen * capacity + slot_pos
        placed = (target[:, :, None] == buffer_ids[None, None, :]).astype(jnp.float32)
        merge_weights = jnp.sum(placed * weights[:, :, None], axis=1)

        def run_experts(received, step=step):
            flat = received.reshape(-1, received.shape[-1])
            if step == 0:
                result = expert_apply(flat, stale_up, stale_down)
            else:
                result = expert_apply(flat, newer_up, newer_down)
            answer = result.astype(jnp.bfloat16).reshape(received.shape)
            return lax.all_to_all(answer, "expert", split_axis=0, concat_axis=0, tiled=True)

        send_matrix = jnp.sum(placed, axis=1).astype(jnp.bfloat16)
        outgoing = lax.dot_general(
            send_matrix, normed, (((0,), (0,)), ((), ())), preferred_element_type=jnp.float32
        )
        outgoing = outgoing.astype(jnp.bfloat16).reshape(experts, capacity, -1)
        returned = run_experts(
            lax.all_to_all(outgoing, "expert", split_axis=0, concat_axis=0, tiled=True)
        )
        flat_back = returned.reshape(experts * capacity, -1).astype(jnp.float32)
        state = state + jnp.dot(merge_weights, flat_back, precision=lax.Precision.HIGHEST)
    return state.astype(jnp.bfloat16)[None]


def solution(mesh):
    placed = (
        P("group", "expert", None),
        P(),
        P(None, "group", "expert", None),
        P(None, "group", "expert", None),
        P("group", None),
        P("expert", None, None),
        P("expert", None, None),
        P("expert", "group", None),
        P("expert", "group", None),
    )
    return jax.shard_map(
        local, mesh=mesh, in_specs=placed, out_specs=P("group", "expert", None), check_vma=False
    )
```

profile of v0, /device:TPU:0, one launch (start us, length us, event | category | flops | bytes accessed | tf_op | source)
XLA Modules:
  0.0 137.2 jit_solution(8322882326334663757)
XLA Ops:
  6.5 0.7 all-gather.3.cloned.1.call-update
  7.3 0.7 fusion.60
  8.2 0.2 select_reduce_fusion.3
  8.6 0.1 reduce_window_sum.18
  8.8 0.2 select_reduce_fusion.1
  9.0 0.9 fusion.45
  9.9 0.7 slice_bitcast_fusion
  10.6 0.7 bitcast_add_fusion
  11.4 1.9 %fusion.19 = bf16[16,8,2048]{2,1,0:T(8,128)(2,1)} fusion(bf16[1,8,2048]{2,1,0:T(8,128)(2,1)} %param.9, f32[2048]{0:T(1024)} %param.10, f32[8]{0:T(128)S(1)} %add_rsqrt_fusion.1, bf16[8,128]{1,0:T(8,128)(2,1)S(1)} %get-tuple-element.7), kind=kOutput, calls=%fused_computation.18 | convolution fusion | flops 4521984 | bytes 567328 | tf_op jit(solution)/shard_map/dot_general | solution.py:70
  13.4 7.4 %all-to-all-start = ((bf16[16,8,2048]{2,1,0:T(8,128)(2,1)}), bf16[16,8,2048]{2,1,0:T(8,128)(2,1)S(1)}, u32[]{:S(2)}, u32[]{:S(2)}) async-start(bf16[16,8,2048]{2,1,0:T(8,128)(2,1)} %fusion.19), calls=%async_computation | async-start | bytes 1048576 | tf_op jit(solution)/shard_map/all_to_all | solution.py:75
  20.8 0.7 all-gather.5.cloned.1.call-update
  21.5 13.7 %all-to-all-done = bf16[16,8,2048]{2,1,0:T(8,128)(2,1)S(1)} async-done(((bf16[16,8,2048]{2,1,0:T(8,128)(2,1)}), bf16[16,8,2048]{2,1,0:T(8,128)(2,1)S(1)}, u32[]{:S(2)}, u32[]{:S(2)}) %all-to-all-start) | async-done | bytes 524320 | tf_op jit(solution)/shard_map/all_to_all | solution.py:75
  35.2 5.8 %fusion.16 = bf16[16,8,2048]{2,1,0:T(8,128)(2,1)} fusion(bf16[1,768,2048]{2,1,0:T(8,128)(2,1)} %param.15, bf16[1,768,2048]{2,1,0:T(8,128)(2,1)} %param.14, bf16[16,8,2048]{2,1,0:T(8,128)(2,1)S(1)} %all-to-all-done), kind=kOutput, calls=%fused_computation.17 | convolution fusion | flops 806060032 | bytes 7340032 | tf_op jit(solution)/shard_map/dot_general | solution.py:17
  41.0 4.2 %all-to-all-start.1 = ((bf16[16,8,2048]{2,1,0:T(8,128)(2,1)}), bf16[16,8,2048]{2,1,0:T(8,128)(2,1)S(1)}, u32[]{:S(2)}, u32[]{:S(2)}) async-start(bf16[16,8,2048]{2,1,0:T(8,128)(2,1)} %fusion.16), calls=%async_computation.1 | async-start | bytes 1048576 | tf_op jit(solution)/shard_map/all_to_all | solution.py:67
  45.4 14.4 %all-to-all-done.1 = bf16[16,8,2048]{2,1,0:T(8,128)(2,1)S(1)} async-done(((bf16[16,8,2048]{2,1,0:T(8,128)(2,1)}), bf16[16,8,2048]{2,1,0:T(8,128)(2,1)S(1)}, u32[]{:S(2)}, u32[]{:S(2)}) %all-to-all-start.1) | async-done | bytes 524320 | tf_op jit(solution)/shard_map/all_to_all | solution.py:67
  59.7 0.4 multiply_reduce_fusion
  60.2 1.2 fusion.20
  61.4 4.1 %all-to-all-start.2 = ((bf16[16,8,2048]{2,1,0:T(8,128)(2,1)}), bf16[16,8,2048]{2,1,0:T(8,128)(2,1)S(1)}, u32[]{:S(2)}, u32[]{:S(2)}) async-start(bf16[16,8,2048]{2,1,0:T(8,128)(2,1)} %fusion.20), calls=%async_computation.2 | async-start | bytes 1048576 | tf_op jit(solution)/shard_map/all_to_all | solution.py:75
  65.5 0.6 compare_reduce_fusion
  66.1 13.8 %all-to-all-done.2 = bf16[16,8,2048]{2,1,0:T(8,128)(2,1)S(1)} async-done(((bf16[16,8,2048]{2,1,0:T(8,128)(2,1)}), bf16[16,8,2048]{2,1,0:T(8,128)(2,1)S(1)}, u32[]{:S(2)}, u32[]{:S(2)}) %all-to-all-start.2) | async-done | bytes 524320 | tf_op jit(solution)/shard_map/all_to_all | solution.py:75
  79.9 23.1 %all-gather.5.cloned.1.call-done = bf16[1,768,2048]{2,1,0:T(8,128)(2,1)} async-done(((bf16[1,384,2048]{2,1,0:T(8,128)(2,1)}), bf16[1,768,2048]{2,1,0:T(8,128)(2,1)}) %all-gather.5.cloned.1.call-update) | async-done | bytes 3145744 | tf_op jit(solution)/shard_map/all_gather | solution.py:42
  103.1 6.5 %fusion.15 = bf16[16,8,2048]{2,1,0:T(8,128)(2,1)S(1)} fusion(bf16[1,768,2048]{2,1,0:T(8,128)(2,1)} %all-gather.5.cloned.1.call-done, bf16[1,768,2048]{2,1,0:T(8,128)(2,1)} %param.15, pred[]{:T(512)} %compare_reduce_fusion, bf16[1,768,2048]{2,1,0:T(8,128)(2,1)} %all-gather.3.cloned.1.call-done, bf16[1,768,2048]{2,1,0:T(8,128)(2,1)} %param.14, ...), kind=kOutput, calls=%fused_computation.16 | convolution fusion | flops 809205760 | bytes 13631489 | tf_op jit(solution)/shard_map/dot_general | solution.py:17
  109.6 19.9 %all_to_all.20 = bf16[16,8,2048]{2,1,0:T(8,128)(2,1)S(1)} all-to-all(bf16[16,8,2048]{2,1,0:T(8,128)(2,1)S(1)} %fusion.15), channel_id=1, replica_groups=mesh['group'=2,'expert'=16] {'expert'}, dimensions={0} | all-to-all | bytes 1048576 | tf_op jit(solution)/shard_map/all_to_all | solution.py:67
  129.5 0.9 fusion.22
  (20 shorter events, 0.8 us)
Async XLA Ops:
  6.5 73.4 %all-gather.3.cloned.1.call-start = ((), (), s32[]{:S(2)}) async-start(), calls=%async_computation.4 | async-start | bytes 4718592 | tf_op jit(solution)/shard_map/all_gather | solution.py:41
  13.4 21.9 %all-to-all-start = ((bf16[16,8,2048]{2,1,0:T(8,128)(2,1)}), bf16[16,8,2048]{2,1,0:T(8,128)(2,1)S(1)}, u32[]{:S(2)}, u32[]{:S(2)}) async-start(bf16[16,8,2048]{2,1,0:T(8,128)(2,1)} %fusion.19), calls=%async_computation | async-start | bytes 1048576 | tf_op jit(solution)/shard_map/all_to_all | solution.py:75
  20.8 82.3 %all-gather.5.cloned.1.call-start = ((), (), s32[]{:S(2)}) async-start(), calls=%async_computation.5 | async-start | bytes 4718592 | tf_op jit(solution)/shard_map/all_gather | solution.py:42
  21.5 38.2 %copy-start = (bf16[1,8,2048]{2,1,0:T(8,128)(2,1)S(1)}, bf16[1,8,2048]{2,1,0:T(8,128)(2,1)}, u32[]{:S(2)}) copy-start(bf16[1,8,2048]{2,1,0:T(8,128)(2,1)} %param.9) | copy-start | bytes 98308
  21.5 38.6 %copy-start.1 = (f32[2048]{0:T(1024)S(1)}, f32[2048]{0:T(1024)}, u32[]{:S(2)}) copy-start(f32[2048]{0:T(1024)} %param.10) | copy-start | bytes 24580
  41.0 24.4 %copy-start.2 = (s32[1,4]{1,0:T(1,128)S(1)}, s32[1,4]{1,0:T(1,128)}, u32[]{:S(2)}) copy-start(s32[1,4]{1,0:T(1,128)} %param.13) | copy-start | bytes 52
  41.0 18.7 %all-to-all-start.1 = ((bf16[16,8,2048]{2,1,0:T(8,128)(2,1)}), bf16[16,8,2048]{2,1,0:T(8,128)(2,1)S(1)}, u32[]{:S(2)}, u32[]{:S(2)}) async-start(bf16[16,8,2048]{2,1,0:T(8,128)(2,1)} %fusion.16), calls=%async_computation.1 | async-start | bytes 1048576 | tf_op jit(solution)/shard_map/all_to_all | solution.py:67
  61.4 18.6 %all-to-all-start.2 = ((bf16[16,8,2048]{2,1,0:T(8,128)(2,1)}), bf16[16,8,2048]{2,1,0:T(8,128)(2,1)S(1)}, u32[]{:S(2)}, u32[]{:S(2)}) async-start(bf16[16,8,2048]{2,1,0:T(8,128)(2,1)} %fusion.20), calls=%async_computation.2 | async-start | bytes 1048576 | tf_op jit(solution)/shard_map/all_to_all | solution.py:75
Sparse Core Ops, SparseCore 0:
  8.9 47.6 all-gather.2
  58.1 44.9 all-gather.4
where the time goes:
time: 138 us; the launch traced here: 137 us
  waiting for transfers between devices  66.4 us (48%)
  blocking collectives  19.9 us (14%)
  matrix products  16.8 us (12%)
  starting transfers between devices  15.8 us (11%)
  between operations  13.5 us (10%)
  other arithmetic  3.16 us (2%)
  local copies, waits for them, and re-layouts  1.75 us (1%)
    all_to_all x2, waiting for transfers between devices, local(): lax.all_to_all(outgoing, 'expert', split_axis=0, concat_axis=0, tiled=True)  27.5 us
    all_gather x1, waiting for transfers between devices, local(): lax.all_gather(learner_down, 'group', axis=1, tiled=True)  23.1 us
    all_to_all x1, blocking collectives, run_experts(): lax.all_to_all(answer, 'expert', split_axis=0, concat_axis=0, tiled=True)  19.9 us
    all_to_all x1, waiting for transfers between devices, run_experts(): lax.all_to_all(answer, 'expert', split_axis=0, concat_axis=0, tiled=True)  14.4 us
    dot_general x2, matrix products, expert_apply(): return jnp.dot(hidden, down_rows, preferred_element_type=jnp.float32)  12.3 us
    all_to_all x2, starting transfers between devices, local(): lax.all_to_all(outgoing, 'expert', split_axis=0, concat_axis=0, tiled=True)  11.5 us
    all_to_all x1, starting transfers between devices, run_experts(): lax.all_to_all(answer, 'expert', split_axis=0, concat_axis=0, tiled=True)  4.22 us
    dot_general x2, matrix products, local(): lax.dot_general(send_matrix, normed, (((0,), (0,)), ((), ())), preferred_...  3.09 us
  transfers between devices with their start and end apart: 5, of which 4 were waited for; matrix products, arithmetic and copies ran while one was open for 10% of the time, Pallas kernels for 0%

commit v1 on v0

v1 whole, which is shorter than its diff:
```python
import jax
import jax.numpy as jnp
from jax import lax
from jax.sharding import PartitionSpec as P


def normalize(state, norm_gain):
    scale = lax.rsqrt(jnp.mean(state * state, axis=-1, keepdims=True) + 1e-06)
    return (state * scale * norm_gain).astype(jnp.bfloat16)


def expert_apply(inputs, up_rows, down_rows):
    pre_act = lax.dot_general(
        inputs, up_rows, (((1,), (1,)), ((), ())), preferred_element_type=jnp.float32
    )
    hidden = jax.nn.silu(pre_act).astype(jnp.bfloat16)
    return jnp.dot(hidden, down_rows, preferred_element_type=jnp.float32)


def split_parts(value):
    parts = []
    rest = value
    for _ in range(3):
        part = lax.reduce_precision(rest, 8, 7)
        parts.append(part.astype(jnp.bfloat16))
        rest = rest - part
    return parts


def dense_weights(chosen, weights, expert_ids):
    hit = chosen[:, :, None] == expert_ids[None, None, :]
    return jnp.sum(jnp.where(hit, weights[:, :, None], 0.0), axis=1)


def pack(normed, tables):
    columns = [part for table in tables for part in split_parts(table)]
    width = sum(column.shape[1] for column in columns)
    padding = -width % 128
    columns.append(jnp.zeros((normed.shape[0], padding), jnp.bfloat16))
    return jnp.concatenate([normed] + columns, axis=1)


def unpack(gathered, width, experts, owner, index):
    start = width + 3 * index * experts
    parts = gathered[:, start : start + 3 * experts].astype(jnp.float32)
    parts = parts.reshape(-1, 3, experts)
    total = parts[:, 0] + parts[:, 1] + parts[:, 2]
    mine = jnp.arange(experts, dtype=jnp.int32)[None, :] == owner
    return jnp.sum(jnp.where(mine, total, 0.0), axis=1, keepdims=True)


def local(
    tokens,
    norm_gain,
    routes,
    route_scale,
    changed,
    rollout_up,
    rollout_down,
    learner_up,
    learner_down,
):
    experts = lax.axis_size("expert")
    groups = lax.axis_size("group")
    owner = lax.axis_index("expert")
    group = lax.axis_index("group")
    row_count, width = tokens.shape[1], tokens.shape[2]
    steps_total = routes.shape[0]
    stale_up = rollout_up[0]
    stale_down = rollout_down[0]
    expert_ids = jnp.arange(experts, dtype=jnp.int32)
    fresh_expert = jnp.any(changed[0][:, None] == expert_ids[None, :], axis=0)
    rows_all = row_count * experts
    split = rows_all < learner_up.shape[1]
    if not split:
        is_fresh = jnp.any(changed[0] == owner)
        newer_up = jnp.where(
            is_fresh, lax.all_gather(learner_up, "group", axis=1, tiled=True)[0], stale_up
        )
        newer_down = jnp.where(
            is_fresh, lax.all_gather(learner_down, "group", axis=1, tiled=True)[0], stale_down
        )
    state = tokens[0].astype(jnp.float32)
    for step in range(steps_total):
        normed = normalize(state, norm_gain)
        weights = dense_weights(routes[step, 0], route_scale[step, 0], expert_ids)
        if step == 0 or not split:
            packed = pack(normed, [weights])
            gathered = lax.all_gather(packed, "expert", axis=0, tiled=True)
            scale = unpack(gathered, width, experts, owner, 0)
            if step == 0:
                result = expert_apply(gathered[:, :width], stale_up, stale_down)
            else:
                result = expert_apply(gathered[:, :width], newer_up, newer_down)
            share = (result * scale).astype(jnp.bfloat16)
            delta = lax.psum_scatter(share, "expert", scatter_dimension=0, tiled=True)
        else:
            fresh = jnp.where(fresh_expert[None, :], weights, 0.0)
            packed = pack(normed, [weights - fresh, fresh])
            gathered = lax.all_gather(packed, ("group", "expert"), axis=0, tiled=True)
            own = lax.dynamic_slice_in_dim(gathered, group * rows_all, rows_all, 0)
            stale_scale = unpack(own, width, experts, owner, 0)
            fresh_scale = unpack(gathered, width, experts, owner, 1)
            stale = expert_apply(own[:, :width], stale_up, stale_down) * stale_scale
            newer = expert_apply(gathered[:, :width], learner_up[0], learner_down[0]) * fresh_scale
            newer = newer.reshape(groups, rows_all, width)
            at_home = (jnp.arange(groups) == group)[:, None, None]
            share = jnp.where(at_home, newer + stale[None], newer).astype(jnp.bfloat16)
            share = share.reshape(groups * rows_all, width)
            delta = lax.psum_scatter(share, ("group", "expert"), scatter_dimension=0, tiled=True)
        state = state + delta.astype(jnp.float32)
    return state.astype(jnp.bfloat16)[None]


def solution(mesh):
    placed = (
        P("group", "expert", None),
        P(),
        P(None, "group", "expert", None),
        P(None, "group", "expert", None),
        P("group", None),
        P("expert", None, None),
        P("expert", None, None),
        P("expert", "group", None),
        P("expert", "group", None),
    )
    return jax.shard_map(
        local, mesh=mesh, in_specs=placed, out_specs=P("group", "expert", None), check_vma=False
    )
```

time: 138 us -> 322 us (2.33)
  waiting for transfers between devices: 66.4 us -> 240 us
  local copies, waits for them, and re-layouts: 1.75 us -> 17.7 us
  starting transfers between devices: 15.8 us -> 0.09 us
  other arithmetic: 3.16 us -> 10.2 us
  blocking collectives: 19.9 us -> 24.7 us
    unnamed x2 -> x5, waiting for transfers between devices: 1.41 us -> 187 us
    all_to_all x3 -> x0, waiting for transfers between devices: 41.9 us -> none  [the longest x2 27.5 us: local(): lax.all_to_all(outgoing, 'expert', split_axis=0, concat_axis=0, tiled=True)]
    all_gather x2 -> x1, waiting for transfers between devices: 23.2 us -> 53 us  [local(): gathered = lax.all_gather(packed, ('group', 'expert'), axis=0, tiled=True)]
    all_gather x0 -> x1, blocking collectives: none -> 24.7 us  [local(): gathered = lax.all_gather(packed, 'expert', axis=0, tiled=True)]
    all_to_all x1 -> x0, blocking collectives: 19.9 us -> none  [run_experts(): lax.all_to_all(answer, 'expert', split_axis=0, concat_axis=0, tiled=True)]
    all_to_all x3 -> x0, starting transfers between devices: 15.7 us -> none  [the longest x2 11.5 us: local(): lax.all_to_all(outgoing, 'expert', split_axis=0, concat_axis=0, tiled=True)]
    unnamed x6 -> x14, local copies, waits for them, and re-layouts: 0.02 us -> 6.35 us
    mul x0 -> x2, other arithmetic: none -> 4.5 us  [normalize(): return (state * scale * norm_gain).astype(jnp.bfloat16)]
  transfers between devices with their start and end apart: 5 -> 3, of which waited for: 4 -> 3; matrix products, arithmetic and copies ran while one was open for 10% -> 0% of each run, Pallas kernels for 0% -> 0%
where the time goes in v1:
time: 322 us; the launch traced here: 321 us
  waiting for transfers between devices  240 us (75%)
  blocking collectives  24.7 us (8%)
  local copies, waits for them, and re-layouts  17.7 us (5%)
  matrix products  15.5 us (5%)
  between operations  13.2 us (4%)
  other arithmetic  10.2 us (3%)
    unnamed x5, waiting for transfers between devices  187 us
    all_gather x1, waiting for transfers between devices, local(): gathered = lax.all_gather(packed, ('group', 'expert'), axis=0, tiled=True)  53 us
    all_gather x1, blocking collectives, local(): gathered = lax.all_gather(packed, 'expert', axis=0, tiled=True)  24.7 us
    dot_general x3, matrix products, expert_apply(): return jnp.dot(hidden, down_rows, preferred_element_type=jnp.float32)  15.5 us
  transfers between devices with their start and end apart: 3, of which 3 were waited for; matrix products, arithmetic and copies ran while one was open for 0% of the time, Pallas kernels for 0%

profile of v1, /device:TPU:0, one launch (start us, length us, event | category | flops | bytes accessed | tf_op | source)
XLA Modules:
  0.0 321.3 jit_solution(17176081933167557314)
XLA Ops:
  6.5 0.9 slice_bitcast_fusion.1
  7.4 0.8 slice_bitcast_fusion
  8.3 1.8 copy.28
  10.1 1.3 fusion.21
  11.5 2.2 fusion.22
  13.6 1.2 copy.29
  14.9 24.7 %all_gather.6 = bf16[128,2176]{1,0:T(8,128)(2,1)S(1)} all-gather(bf16[8,2176]{1,0:T(8,128)(2,1)S(1)} %concatenate.6), channel_id=1, replica_groups=mesh['group'=2,'expert'=16] {'expert'}, dimensions={0}, use_global_device_ids=true | all-gather | bytes 591872 | tf_op jit(solution)/shard_map/all_gather | solution.py:89
  39.6 0.8 copy-done.1
  40.6 5.0 %fusion.15 = bf16[128,2048]{1,0:T(8,128)(2,1)} fusion(bf16[1,768,2048]{2,1,0:T(8,128)(2,1)S(1)} %copy-done, f32[128]{0:T(128)S(1)} %fusion.62, bf16[1,768,2048]{2,1,0:T(8,128)(2,1)} %param.14, bf16[128,2176]{1,0:T(8,128)(2,1)} %copy-done.1), kind=kOutput, calls=%fused_computation.13 | convolution fusion | flops 806322176 | bytes 7340544 | tf_op jit(solution)/shard_map/dot_general | solution.py:17
  45.8 53.0 %reduce-scatter.7.cloned.1.call-done = bf16[8,2048]{1,0:T(8,128)(2,1)} async-done(((bf16[128,2048]{1,0:T(8,128)(2,1)}), bf16[8,2048]{1,0:T(8,128)(2,1)}) %reduce-scatter.7.cloned.1.call-update) | async-done | bytes 32784
  98.9 1.8 copy.38
  100.6 1.5 multiply_reduce_fusion
  102.1 2.3 multiply_multiply_fusion
  104.5 1.2 copy.32
  106.6 53.0 %all-gather.2.cloned.1.call-done = bf16[256,2176]{1,0:T(8,128)(2,1)} async-done(((bf16[8,2176]{1,0:T(8,128)(2,1)}), bf16[256,2176]{1,0:T(8,128)(2,1)}) %all-gather.2.cloned.1.call-update) | async-done | bytes 1114128 | tf_op jit(solution)/shard_map/all_gather | solution.py:100
  159.6 0.8 dynamic-slice.1
  160.5 0.9 slice.82
  161.7 5.2 %fusion.12 = f32[128,2048]{1,0:T(8,128)} fusion(bf16[1,768,2048]{2,1,0:T(8,128)(2,1)S(1)} %copy-done, f32[128]{0:T(128)S(1)} %fusion.59, bf16[1,768,2048]{2,1,0:T(8,128)(2,1)} %param.14, bf16[256,2176]{1,0:T(8,128)(2,1)} %all-gather.2.cloned.1.call-done, s32[]{:T(128)S(6)} %select_n.35), kind=kOutput, calls=%fused_computation.12 | convolution fusion | flops 806060032 | bytes 7864836 | tf_op jit(solution)/shard_map/dot_general | solution.py:17
  166.8 2.8 add.97
  169.7 5.3 %fusion.8 = bf16[256,2048]{1,0:T(8,128)(2,1)} fusion(f32[256,2048]{1,0:T(8,128)} %bitcast.81, bf16[1,384,2048]{2,1,0:T(8,128)(2,1)} %param.17, f32[256]{0:T(256)S(1)} %fusion.56, pred[256]{0:T(512)(128)(4,1)S(1)} %broadcast_bitcast_fusion, bf16[1,384,2048]{2,1,0:T(8,128)(2,1)} %param.16, bf16[256,2176]{1,0:T(8,128)(2,1)} %all-gather.2.cloned.1.call-done), kind=kOutput, calls=%fused_computation.10 | convolution fusion | flops 807895040 | bytes 7341312 | tf_op jit(solution)/shard_map/dot_general | solution.py:17
  174.9 133.8 %reduce-scatter.9.cloned.1.call-done = bf16[8,2048]{1,0:T(8,128)(2,1)} async-done(((bf16[256,2048]{1,0:T(8,128)(2,1)}), bf16[8,2048]{1,0:T(8,128)(2,1)}) %reduce-scatter.9.cloned.1.call-update) | async-done | bytes 32784
  308.8 1.8 copy.40
  310.6 2.4 fusion.24
  312.9 1.8 copy.36
  (36 shorter events, 1.8 us)
Async XLA Ops:
  6.5 34.1 %copy-start = (bf16[1,768,2048]{2,1,0:T(8,128)(2,1)S(1)}, bf16[1,768,2048]{2,1,0:T(8,128)(2,1)}, u32[]{:S(2)}) copy-start(bf16[1,768,2048]{2,1,0:T(8,128)(2,1)} %param.15) | copy-start | bytes 9437188
  6.5 92.3 %reduce-scatter.7.cloned.1.call-start = ((), (), s32[]{:S(2)}) async-start(), calls=%async_computation.3 | async-start | bytes 557056
  39.6 0.8 copy-start.1
  40.6 5.1 %copy-start.3 = (s32[1,4]{1,0:T(1,128)S(1)}, s32[1,4]{1,0:T(1,128)}, u32[]{:S(2)}) copy-start(s32[1,4]{1,0:T(1,128)} %param.13) | copy-start | bytes 52
  45.6 56.5 %copy-start.2 = (f32[2048]{0:T(1024)S(1)}, f32[2048]{0:T(1024)}, u32[]{:S(2)}) copy-start(f32[2048]{0:T(1024)} %param.10) | copy-start | bytes 24580
  45.7 113.9 %all-gather.2.cloned.1.call-start = ((), (), s32[]{:S(2)}) async-start(), calls=%async_computation.2 | async-start | bytes 1148928 | tf_op jit(solution)/shard_map/all_gather | solution.py:100
  106.4 202.4 %reduce-scatter.9.cloned.1.call-start = ((), (), s32[]{:S(2)}) async-start(), calls=%async_computation.4 | async-start | bytes 1081344
Sparse Core Ops, SparseCore 0:
  45.8 53.0 reduce-scatter.6
  106.5 52.9 all-gather.1
  175.1 133.6 reduce-scatter.8

commit v2 on v1

v2 whole, which is shorter than its diff:
```python
import jax
import jax.numpy as jnp
from jax import lax
from jax.sharding import PartitionSpec as P


def normalize(state, norm_gain):
    scale = lax.rsqrt(jnp.mean(state * state, axis=-1, keepdims=True) + 1e-06)
    return (state * scale * norm_gain).astype(jnp.bfloat16)


def expert_apply(inputs, up_rows, down_rows):
    pre_act = lax.dot_general(
        inputs, up_rows, (((1,), (1,)), ((), ())), preferred_element_type=jnp.float32
    )
    hidden = jax.nn.silu(pre_act).astype(jnp.bfloat16)
    return jnp.dot(hidden, down_rows, preferred_element_type=jnp.float32)


def split_parts(value):
    parts = []
    rest = value
    for _ in range(3):
        part = lax.reduce_precision(rest, 8, 7)
        parts.append(part.astype(jnp.bfloat16))
        rest = rest - part
    return parts


def dense_weights(chosen, weights, expert_ids):
    hit = chosen[:, :, None] == expert_ids[None, None, :]
    return jnp.sum(jnp.where(hit, weights[:, :, None], 0.0), axis=1)


def pack(normed, tables):
    columns = [part for table in tables for part in split_parts(table)]
    width = sum(column.shape[1] for column in columns)
    padding = -width % 128
    columns.append(jnp.zeros((normed.shape[0], padding), jnp.bfloat16))
    return jnp.concatenate([normed] + columns, axis=1)


def unpack(gathered, width, experts, owner, index):
    start = width + 3 * index * experts
    parts = gathered[:, start : start + 3 * experts].astype(jnp.float32)
    total = parts[:, :experts] + parts[:, experts : 2 * experts] + parts[:, 2 * experts :]
    mine = jnp.arange(experts, dtype=jnp.int32)[None, :] == owner
    return jnp.sum(jnp.where(mine, total, 0.0), axis=1, keepdims=True)


def swap(value, axis, distance):
    size = lax.axis_size(axis)
    return lax.ppermute(value, axis, [(i, i ^ distance) for i in range(size)])


def gather_rows(block):
    count = lax.axis_size("expert") // 2
    parts = [block] + [swap(block, "expert", 2 * j) for j in range(1, count)]
    half = jnp.concatenate(parts, axis=0)
    return half, swap(half, "expert", 1)


def return_rows(near, far):
    count = lax.axis_size("expert") // 2
    total = near + swap(far.astype(jnp.bfloat16), "expert", 1).astype(jnp.float32)
    total = total.reshape(count, -1, total.shape[-1])
    sent = total.astype(jnp.bfloat16)
    result = total[0]
    for j in range(1, count):
        result = result + swap(sent[j], "expert", 2 * j).astype(jnp.float32)
    return result


def exchange_plan(tokens, norm_gain, routes, route_scale, changed, stale, learner):
    experts = lax.axis_size("expert")
    groups = lax.axis_size("group")
    owner = lax.axis_index("expert")
    row_count, width = tokens.shape[1], tokens.shape[2]
    expert_ids = jnp.arange(experts, dtype=jnp.int32)
    fresh_expert = jnp.any(changed[0][:, None] == expert_ids[None, :], axis=0)
    state = tokens[0].astype(jnp.float32)
    for step in range(routes.shape[0]):
        normed = normalize(state, norm_gain)
        weights = dense_weights(routes[step, 0], route_scale[step, 0], expert_ids)
        if step == 0:
            shares = []
            for rows in gather_rows(pack(normed, [weights])):
                scale = unpack(rows, width, experts, owner, 0)
                shares.append(expert_apply(rows[:, :width], *stale) * scale)
            state = state + return_rows(*shares)
        else:
            fresh = jnp.where(fresh_expert[None, :], weights, 0.0)
            block = pack(normed, [weights - fresh, fresh])
            blocks = [block] + [swap(block, "group", d) for d in range(1, groups)]
            shares = []
            for rows in gather_rows(jnp.concatenate(blocks, axis=0)):
                new = expert_apply(rows[:, :width], *learner)
                new = new * unpack(rows, width, experts, owner, 1)
                new = new.reshape(-1, groups, row_count, width)
                own = rows.reshape(-1, groups, row_count, rows.shape[-1])[:, 0]
                own = own.reshape(-1, rows.shape[-1])
                old = expert_apply(own[:, :width], *stale)
                old = old * unpack(own, width, experts, owner, 0)
                old = old.reshape(-1, 1, row_count, width)
                both = jnp.concatenate([new[:, :1] + old, new[:, 1:]], axis=1)
                shares.append(both.reshape(-1, width))
            total = return_rows(*shares).reshape(groups, row_count, width)
            delta = total[0]
            for d in range(1, groups):
                sent = total[d].astype(jnp.bfloat16)
                delta = delta + swap(sent, "group", d).astype(jnp.float32)
            state = state + delta
    return state.astype(jnp.bfloat16)[None]


def gather_plan(tokens, norm_gain, routes, route_scale, changed, stale, learner):
    experts = lax.axis_size("expert")
    owner_index = lax.axis_index("expert")
    row_count = tokens.shape[1]
    top_count = routes.shape[3]
    capacity = min(row_count, max(2, 2 * row_count * top_count // experts))
    is_fresh = jnp.any(changed[0] == owner_index)
    fresh = [lax.all_gather(part, "group", axis=0, tiled=True) for part in learner]
    newer = [jnp.where(is_fresh, new, old) for new, old in zip(fresh, stale)]
    state = tokens[0].astype(jnp.float32)
    buffer_ids = jnp.arange(experts * capacity, dtype=jnp.int32)
    expert_ids = jnp.arange(experts, dtype=jnp.int32)
    for step in range(routes.shape[0]):
        normed = normalize(state, norm_gain)
        chosen = routes[step, 0]
        weights = route_scale[step, 0]
        hits = (chosen.reshape(-1)[:, None] == expert_ids[None, :]).astype(jnp.int32)
        before = jnp.cumsum(hits, axis=0) - hits
        slot_pos = jnp.sum(before * hits, axis=1).reshape(chosen.shape)
        target = chosen * capacity + slot_pos
        placed = (target[:, :, None] == buffer_ids[None, None, :]).astype(jnp.float32)
        merge_weights = jnp.sum(placed * weights[:, :, None], axis=1)
        send_matrix = jnp.sum(placed, axis=1).astype(jnp.bfloat16)
        outgoing = lax.dot_general(
            send_matrix, normed, (((0,), (0,)), ((), ())), preferred_element_type=jnp.float32
        )
        outgoing = outgoing.astype(jnp.bfloat16).reshape(experts, capacity, -1)
        received = lax.all_to_all(outgoing, "expert", split_axis=0, concat_axis=0, tiled=True)
        flat = received.reshape(-1, received.shape[-1])
        result = expert_apply(flat, *(stale if step == 0 else newer))
        answer = result.astype(jnp.bfloat16).reshape(received.shape)
        returned = lax.all_to_all(answer, "expert", split_axis=0, concat_axis=0, tiled=True)
        flat_back = returned.reshape(experts * capacity, -1).astype(jnp.float32)
        state = state + jnp.dot(merge_weights, flat_back, precision=lax.Precision.HIGHEST)
    return state.astype(jnp.bfloat16)[None]


def local(
    tokens,
    norm_gain,
    routes,
    route_scale,
    changed,
    rollout_up,
    rollout_down,
    learner_up,
    learner_down,
):
    experts = lax.axis_size("expert")
    groups = lax.axis_size("group")
    fewer = tokens.shape[1] * experts < learner_up.shape[1]
    paired = experts & (experts - 1) == 0 and groups & (groups - 1) == 0 and experts > 1
    plan = exchange_plan if fewer and paired else gather_plan
    stale = (rollout_up[0], rollout_down[0])
    learner = (learner_up[0], learner_down[0])
    return plan(tokens, norm_gain, routes, route_scale, changed, stale, learner)


def solution(mesh):
    placed = (
        P("group", "expert", None),
        P(),
        P(None, "group", "expert", None),
        P(None, "group", "expert", None),
        P("group", None),
        P("expert", None, None),
        P("expert", None, None),
        P("expert", "group", None),
        P("expert", "group", None),
    )
    return jax.shard_map(
        local, mesh=mesh, in_specs=placed, out_specs=P("group", "expert", None), check_vma=False
    )
```

time: 322 us -> 138 us (0.43)
  waiting for transfers between devices: 240 us -> 34.4 us
  starting transfers between devices: 0.09 us -> 52.5 us
  blocking collectives: 24.7 us -> 0 us
  between operations: 13.2 us -> 0.27 us
  matrix products: 15.5 us -> 28.1 us
  local copies, waits for them, and re-layouts: 17.7 us -> 10.6 us
    unnamed x5 -> x0, waiting for transfers between devices: 187 us -> none
    all_gather x1 -> x0, waiting for transfers between devices: 53 us -> none  [local(): gathered = lax.all_gather(packed, ('group', 'expert'), axis=0, tiled=True)]
    ppermute x0 -> x34, starting transfers between devices: none -> 52.5 us  [swap(): return lax.ppermute(value, axis, [(i, i ^ distance) for i in range(size)])]
    ppermute x0 -> x34, waiting for transfers between devices: none -> 34.4 us  [swap(): return lax.ppermute(value, axis, [(i, i ^ distance) for i in range(size)])]
    all_gather x1 -> x0, blocking collectives: 24.7 us -> none  [local(): gathered = lax.all_gather(packed, 'expert', axis=0, tiled=True)]
    dot_general x3 -> x6, matrix products: 15.5 us -> 28.1 us  [expert_apply(): return jnp.dot(hidden, down_rows, preferred_element_type=jnp.float32)]
    mul x2 -> x0, other arithmetic: 4.5 us -> none  [normalize(): return (state * scale * norm_gain).astype(jnp.bfloat16)]
  transfers between devices with their start and end apart: 3 -> 34, of which waited for: 3 -> 18; matrix products, arithmetic and copies ran while one was open for 0% -> 6% of each run, Pallas kernels for 0% -> 0%
where the time goes in v2:
time: 138 us; the launch traced here: 137 us
  starting transfers between devices  52.5 us (38%)
  waiting for transfers between devices  34.4 us (25%)
  matrix products  28.1 us (20%)
  other arithmetic  11.5 us (8%)
  local copies, waits for them, and re-layouts  10.6 us (8%)
    ppermute x34, starting transfers between devices, swap(): return lax.ppermute(value, axis, [(i, i ^ distance) for i in range(size)])  52.5 us
    ppermute x34, waiting for transfers between devices, swap(): return lax.ppermute(value, axis, [(i, i ^ distance) for i in range(size)])  34.4 us
    dot_general x6, matrix products, expert_apply(): return jnp.dot(hidden, down_rows, preferred_element_type=jnp.float32)  28.1 us
    unnamed x39, local copies, waits for them, and re-layouts  5.16 us
    slice x2, local copies, waits for them, and re-layouts, exchange_plan(): both = jnp.concatenate([new[:, :1] + old, new[:, 1:]], axis=1)  3.66 us
    concatenate x2, other arithmetic, exchange_plan(): both = jnp.concatenate([new[:, :1] + old, new[:, 1:]], axis=1)  3.17 us
    reduce_sum x3, other arithmetic, unpack(): return jnp.sum(jnp.where(mine, total, 0.0), axis=1, keepdims=True)  3.1 us
  transfers between devices with their start and end apart: 34, of which 18 were waited for; matrix products, arithmetic and copies ran while one was open for 6% of the time, Pallas kernels for 0%

profile of v2, /device:TPU:0, one launch (start us, length us, event | category | flops | bytes accessed | tf_op | source)
XLA Modules:
  0.0 137.4 jit_solution(18196109805435639246)
XLA Ops:
  3.5 6.0 %collective-permute-start.6 = (bf16[8,2176]{1,0:T(8,128)(2,1)S(1)}, bf16[8,2176]{1,0:T(8,128)(2,1)S(1)}, u32[]{:S(2)}, u32[]{:S(2)}) collective-permute-start(bf16[8,2176]{1,0:T(8,128)(2,1)S(1)} %concatenate.23), channel_id=1, source_target_pairs={{0,14},{1,15},{2,12},{3,13},{4,10},{5,11},{6,8},{7,9},{8,6},{9,7},... | collective-permute-start | bytes 104456 | tf_op jit(solution)/shard_map/ppermute | solution.py:53
  10.5 2.0 %collective-permute-start.3 = (bf16[8,2176]{1,0:T(8,128)(2,1)S(1)}, bf16[8,2176]{1,0:T(8,128)(2,1)}, u32[]{:S(2)}, u32[]{:S(2)}) collective-permute-start(bf16[8,2176]{1,0:T(8,128)(2,1)S(1)} %concatenate.23), channel_id=1, source_target_pairs={{0,8},{1,9},{2,10},{3,11},{4,12},{5,13},{6,14},{7,15},{8,0},{9,1},... | collective-permute-start | bytes 104456 | tf_op jit(solution)/shard_map/ppermute | solution.py:53
  14.2 2.4 %collective-permute-done = bf16[8,2176]{1,0:T(8,128)(2,1)} collective-permute-done((bf16[8,2176]{1,0:T(8,128)(2,1)S(1)}, bf16[8,2176]{1,0:T(8,128)(2,1)}, u32[]{:S(2)}, u32[]{:S(2)}) %collective-permute-start) | collective-permute-done | bytes 34848 | tf_op jit(solution)/shard_map/ppermute | solution.py:53
  20.5 2.6 %collective-permute-start.2 = (bf16[8,2176]{1,0:T(8,128)(2,1)S(1)}, bf16[8,2176]{1,0:T(8,128)(2,1)S(1)}, u32[]{:S(2)}, u32[]{:S(2)}) collective-permute-start(bf16[8,2176]{1,0:T(8,128)(2,1)S(1)} %concatenate.23), channel_id=1, source_target_pairs={{0,6},{1,7},{2,4},{3,5},{4,2},{5,3},{6,0},{7,1},{8,14},{9,15},{10,... | collective-permute-start | bytes 104456 | tf_op jit(solution)/shard_map/ppermute | solution.py:53
  23.2 2.2 %collective-permute-done.2 = bf16[8,2176]{1,0:T(8,128)(2,1)S(1)} collective-permute-done((bf16[8,2176]{1,0:T(8,128)(2,1)S(1)}, bf16[8,2176]{1,0:T(8,128)(2,1)S(1)}, u32[]{:S(2)}, u32[]{:S(2)}) %collective-permute-start.2) | collective-permute-done | bytes 34848 | tf_op jit(solution)/shard_map/ppermute | solution.py:53
  29.3 4.8 %fusion.43 = bf16[64,2048]{1,0:T(8,128)(2,1)} fusion(bf16[1,768,2048]{2,1,0:T(8,128)(2,1)S(1)} %copy-done, f32[64]{0:T(128)S(1)} %get-tuple-element.10, bf16[1,768,2048]{2,1,0:T(8,128)(2,1)} %param.14, bf16[64,2176]{1,0:T(8,128)(2,1)} %copy-done.6), kind=kOutput, calls=%fused_computation.27 | convolution fusion | flops 403161088 | bytes 6816000 | tf_op jit(solution)/shard_map/dot_general | solution.py:17
  36.6 4.9 %fusion.160 = (bf16[64,2048]{1,0:T(8,128)(2,1)S(1)}, f32[64,2048]{1,0:T(8,128)}) fusion(bf16[64,2048]{1,0:T(8,128)(2,1)} %copy-done.7, f32[64]{0:T(128)S(1)} %get-tuple-element.9, bf16[1,768,2048]{2,1,0:T(8,128)(2,1)S(1)} %copy-done, bf16[1,768,2048]{2,1,0:T(8,128)(2,1)} %param.14, bf16[64,2176]{1,0:T(8,128)(2,1)} %copy-done.4), kind=kOutput, calls=%fused_computation.175 | convolution fusion | flops 403423232 | bytes 7602432 | tf_op jit(solution)/shard_map/dot_general | solution.py:17
  43.6 3.2 %collective-permute-start.15 = (bf16[8,2048]{1,0:T(8,128)(2,1)S(1)}, bf16[8,2048]{1,0:T(8,128)(2,1)S(1)}, u32[]{:S(2)}, u32[]{:S(2)}) collective-permute-start(bf16[8,2048]{1,0:T(8,128)(2,1)S(1)} %get-tuple-element.23), channel_id=1, source_target_pairs={{0,14},{1,15},{2,12},{3,13},{4,10},{5,11},{6,8},{7,9},{8,6},{9,7},... | collective-permute-start | bytes 98312 | tf_op jit(solution)/shard_map/ppermute | solution.py:53
  48.6 2.8 %collective-permute-start.12 = (bf16[8,2048]{1,0:T(8,128)(2,1)S(1)}, bf16[8,2048]{1,0:T(8,128)(2,1)S(1)}, u32[]{:S(2)}, u32[]{:S(2)}) collective-permute-start(bf16[8,2048]{1,0:T(8,128)(2,1)S(1)} %get-tuple-element.26), channel_id=1, source_target_pairs={{0,8},{1,9},{2,10},{3,11},{4,12},{5,13},{6,14},{7,15},{8,0},{9,1},... | collective-permute-start | bytes 98312 | tf_op jit(solution)/shard_map/ppermute | solution.py:53
  53.7 2.5 %collective-permute-done.11 = bf16[8,2048]{1,0:T(8,128)(2,1)S(1)} collective-permute-done((bf16[8,2048]{1,0:T(8,128)(2,1)S(1)}, bf16[8,2048]{1,0:T(8,128)(2,1)S(1)}, u32[]{:S(2)}, u32[]{:S(2)}) %collective-permute-start.11) | collective-permute-done | bytes 32800 | tf_op jit(solution)/shard_map/ppermute | solution.py:53
  58.9 2.4 %collective-permute-done.16 = bf16[8,2176]{1,0:T(8,128)(2,1)S(1)} collective-permute-done((bf16[8,2176]{1,0:T(8,128)(2,1)S(1)}, bf16[8,2176]{1,0:T(8,128)(2,1)S(1)}, u32[]{:S(2)}, u32[]{:S(2)}) %collective-permute-start.16) | collective-permute-done | bytes 34848 | tf_op jit(solution)/shard_map/ppermute | solution.py:53
  61.3 3.6 %collective-permute-start.23 = (bf16[16,2176]{1,0:T(8,128)(2,1)S(1)}, bf16[16,2176]{1,0:T(8,128)(2,1)S(1)}, u32[]{:S(2)}, u32[]{:S(2)}) collective-permute-start(bf16[16,2176]{1,0:T(8,128)(2,1)S(1)} %pad_maximum_fusion.2), channel_id=1, source_target_pairs={{0,14},{1,15},{2,12},{3,13},{4,10},{5,11},{6,8},{7,9},{8,6},{9,7},... | collective-permute-start | bytes 208904 | tf_op jit(solution)/shard_map/ppermute | solution.py:53
  70.5 2.8 %collective-permute-done.17 = bf16[16,2176]{1,0:T(8,128)(2,1)S(1)} collective-permute-done((bf16[16,2176]{1,0:T(8,128)(2,1)S(1)}, bf16[16,2176]{1,0:T(8,128)(2,1)S(1)}, u32[]{:S(2)}, u32[]{:S(2)}) %collective-permute-start.17) | collective-permute-done | bytes 69664 | tf_op jit(solution)/shard_map/ppermute | solution.py:53
  74.2 3.4 %collective-permute-done.18 = bf16[16,2176]{1,0:T(8,128)(2,1)S(1)} collective-permute-done((bf16[16,2176]{1,0:T(8,128)(2,1)S(1)}, bf16[16,2176]{1,0:T(8,128)(2,1)S(1)}, u32[]{:S(2)}, u32[]{:S(2)}) %collective-permute-start.18) | collective-permute-done | bytes 69664 | tf_op jit(solution)/shard_map/ppermute | solution.py:53
  79.3 3.5 %collective-permute-done.19 = bf16[16,2176]{1,0:T(8,128)(2,1)S(1)} collective-permute-done((bf16[16,2176]{1,0:T(8,128)(2,1)S(1)}, bf16[16,2176]{1,0:T(8,128)(2,1)S(1)}, u32[]{:S(2)}, u32[]{:S(2)}) %collective-permute-start.19) | collective-permute-done | bytes 69664 | tf_op jit(solution)/shard_map/ppermute | solution.py:53
  87.3 4.3 %convolution_multiply_fusion.1 = f32[128,2048]{1,0:T(8,128)} fusion(bf16[1,384,2048]{2,1,0:T(8,128)(2,1)} %param.17, f32[128]{0:T(128)} %get-tuple-element.8, bf16[1,384,2048]{2,1,0:T(8,128)(2,1)} %param.16, bf16[128,2176]{1,0:T(8,128)(2,1)} %copy-done.1), kind=kOutput, calls=%fused_computation.17 | convolution fusion | flops 403161088 | bytes 4719104 | tf_op jit(solution)/shard_map/dot_general | solution.py:17
  93.5 4.2 %convolution_multiply_fusion = f32[128,2048]{1,0:T(8,128)} fusion(bf16[1,384,2048]{2,1,0:T(8,128)(2,1)} %param.17, f32[128]{0:T(128)} %get-tuple-element.7, bf16[1,384,2048]{2,1,0:T(8,128)(2,1)} %param.16, bf16[128,2176]{1,0:T(8,128)(2,1)} %copy-done.2), kind=kOutput, calls=%fused_computation.16 | convolution fusion | flops 403161088 | bytes 4719104 | tf_op jit(solution)/shard_map/dot_general | solution.py:17
  101.0 4.9 %fusion.40 = bf16[8,1,8,2048]{3,2,1,0:T(8,128)(2,1)} fusion(bf16[1,768,2048]{2,1,0:T(8,128)(2,1)S(1)} %copy-done, f32[8,2,8,2048]{3,2,1,0:T(8,128)} %bitcast.124, f32[64]{0:T(128)} %get-tuple-element.5, bf16[1,768,2048]{2,1,0:T(8,128)(2,1)} %param.14, bf16[64,2176]{1,0:T(8,128)(2,1)} %copy-done.3), kind=kOutput, calls=%fused_computation.26 | convolution fusion | flops 403292160 | bytes 7340544 | tf_op jit(solution)/shard_map/dot_general | solution.py:17
  107.9 4.9 %fusion.37 = f32[8,1,8,2048]{3,2,1,0:T(8,128)} fusion(bf16[1,768,2048]{2,1,0:T(8,128)(2,1)S(1)} %copy-done, f32[8,2,8,2048]{3,2,1,0:T(8,128)} %bitcast.122, f32[64]{0:T(128)S(1)} %copy-done.10, bf16[1,768,2048]{2,1,0:T(8,128)(2,1)} %param.14, bf16[64,2176]{1,0:T(8,128)(2,1)S(1)} %slice_bitcast_fusion.1), kind=kOutput, calls=%fused_computation.25 | convolution fusion | flops 403161088 | bytes 7602688 | tf_op jit(solution)/shard_map/dot_general | solution.py:17
  115.4 2.3 %collective-permute-start.26 = (bf16[16,2048]{1,0:T(8,128)(2,1)S(1)}, bf16[16,2048]{1,0:T(8,128)(2,1)S(1)}, u32[]{:S(2)}, u32[]{:S(2)}) collective-permute-start(bf16[16,2048]{1,0:T(8,128)(2,1)S(1)} %get-tuple-element.15), channel_id=1, source_target_pairs={{0,2},{1,3},{2,0},{3,1},{4,6},{5,7},{6,4},{7,5},{8,10},{9,11},{10,... | collective-permute-start | bytes 196616 | tf_op jit(solution)/shard_map/ppermute | solution.py:53
  117.7 3.2 %collective-permute-start.32 = (bf16[16,2048]{1,0:T(8,128)(2,1)S(1)}, bf16[16,2048]{1,0:T(8,128)(2,1)S(1)}, u32[]{:S(2)}, u32[]{:S(2)}) collective-permute-start(bf16[16,2048]{1,0:T(8,128)(2,1)S(1)} %get-tuple-element.16), channel_id=1, source_target_pairs={{0,14},{1,15},{2,12},{3,13},{4,10},{5,11},{6,8},{7,9},{8,6},{9,7},... | collective-permute-start | bytes 196616 | tf_op jit(solution)/shard_map/ppermute | solution.py:53
  121.9 3.5 %collective-permute-start.29 = (bf16[16,2048]{1,0:T(8,128)(2,1)S(1)}, bf16[16,2048]{1,0:T(8,128)(2,1)S(1)}, u32[]{:S(2)}, u32[]{:S(2)}) collective-permute-start(bf16[16,2048]{1,0:T(8,128)(2,1)S(1)} %get-tuple-element.19), channel_id=1, source_target_pairs={{0,8},{1,9},{2,10},{3,11},{4,12},{5,13},{6,14},{7,15},{8,0},{9,1},... | collective-permute-start | bytes 196616 | tf_op jit(solution)/shard_map/ppermute | solution.py:53
  127.4 3.8 %collective-permute-done.30 = bf16[16,2048]{1,0:T(8,128)(2,1)S(1)} collective-permute-done((bf16[16,2048]{1,0:T(8,128)(2,1)S(1)}, bf16[16,2048]{1,0:T(8,128)(2,1)S(1)}, u32[]{:S(2)}, u32[]{:S(2)}) %collective-permute-start.30) | collective-permute-done | bytes 65568 | tf_op jit(solution)/shard_map/ppermute | solution.py:53
  134.4 2.4 %collective-permute-done.33 = bf16[8,2048]{1,0:T(8,128)(2,1)S(1)} collective-permute-done((bf16[8,2048]{1,0:T(8,128)(2,1)S(1)}, bf16[8,2048]{1,0:T(8,128)(2,1)S(1)}, u32[]{:S(2)}, u32[]{:S(2)}) %collective-permute-start.33) | collective-permute-done | bytes 32800 | tf_op jit(solution)/shard_map/ppermute | solution.py:53
  (130 shorter events, 54.3 us)
Async XLA Ops:
  3.5 23.4 %collective-permute-start.6 = (bf16[8,2176]{1,0:T(8,128)(2,1)S(1)}, bf16[8,2176]{1,0:T(8,128)(2,1)S(1)}, u32[]{:S(2)}, u32[]{:S(2)}) collective-permute-start(bf16[8,2176]{1,0:T(8,128)(2,1)S(1)} %concatenate.23), channel_id=1, source_target_pairs={{0,14},{1,15},{2,12},{3,13},{4,10},{5,11},{6,8},{7,9},{8,6},{9,7},... | collective-permute-start | bytes 104456 | tf_op jit(solution)/shard_map/ppermute | solution.py:53
  9.5 17.4 %collective-permute-start.5 = (bf16[8,2176]{1,0:T(8,128)(2,1)S(1)}, bf16[8,2176]{1,0:T(8,128)(2,1)S(1)}, u32[]{:S(2)}, u32[]{:S(2)}) collective-permute-start(bf16[8,2176]{1,0:T(8,128)(2,1)S(1)} %concatenate.23), channel_id=1, source_target_pairs={{0,12},{1,13},{2,14},{3,15},{4,8},{5,9},{6,10},{7,11},{8,4},{9,5},... | collective-permute-start | bytes 104456 | tf_op jit(solution)/shard_map/ppermute | solution.py:53
  9.8 16.4 %collective-permute-start.4 = (bf16[8,2176]{1,0:T(8,128)(2,1)S(1)}, bf16[8,2176]{1,0:T(8,128)(2,1)}, u32[]{:S(2)}, u32[]{:S(2)}) collective-permute-start(bf16[8,2176]{1,0:T(8,128)(2,1)S(1)} %concatenate.23), channel_id=1, source_target_pairs={{0,10},{1,11},{2,8},{3,9},{4,14},{5,15},{6,12},{7,13},{8,2},{9,3},... | collective-permute-start | bytes 104456 | tf_op jit(solution)/shard_map/ppermute | solution.py:53
  10.5 14.9 %collective-permute-start.3 = (bf16[8,2176]{1,0:T(8,128)(2,1)S(1)}, bf16[8,2176]{1,0:T(8,128)(2,1)}, u32[]{:S(2)}, u32[]{:S(2)}) collective-permute-start(bf16[8,2176]{1,0:T(8,128)(2,1)S(1)} %concatenate.23), channel_id=1, source_target_pairs={{0,8},{1,9},{2,10},{3,11},{4,12},{5,13},{6,14},{7,15},{8,0},{9,1},... | collective-permute-start | bytes 104456 | tf_op jit(solution)/shard_map/ppermute | solution.py:53
  20.5 4.8 %collective-permute-start.2 = (bf16[8,2176]{1,0:T(8,128)(2,1)S(1)}, bf16[8,2176]{1,0:T(8,128)(2,1)S(1)}, u32[]{:S(2)}, u32[]{:S(2)}) collective-permute-start(bf16[8,2176]{1,0:T(8,128)(2,1)S(1)} %concatenate.23), channel_id=1, source_target_pairs={{0,6},{1,7},{2,4},{3,5},{4,2},{5,3},{6,0},{7,1},{8,14},{9,15},{10,... | collective-permute-start | bytes 104456 | tf_op jit(solution)/shard_map/ppermute | solution.py:53
  41.5 9.8 %collective-permute-start.9 = (bf16[8,2048]{1,0:T(8,128)(2,1)S(1)}, bf16[8,2048]{1,0:T(8,128)(2,1)S(1)}, u32[]{:S(2)}, u32[]{:S(2)}) collective-permute-start(bf16[8,2048]{1,0:T(8,128)(2,1)S(1)} %get-tuple-element.22), channel_id=1, source_target_pairs={{0,2},{1,3},{2,0},{3,1},{4,6},{5,7},{6,4},{7,5},{8,10},{9,11},{10,... | collective-permute-start | bytes 98312 | tf_op jit(solution)/shard_map/ppermute | solution.py:53
  43.6 8.7 %collective-permute-start.15 = (bf16[8,2048]{1,0:T(8,128)(2,1)S(1)}, bf16[8,2048]{1,0:T(8,128)(2,1)S(1)}, u32[]{:S(2)}, u32[]{:S(2)}) collective-permute-start(bf16[8,2048]{1,0:T(8,128)(2,1)S(1)} %get-tuple-element.23), channel_id=1, source_target_pairs={{0,14},{1,15},{2,12},{3,13},{4,10},{5,11},{6,8},{7,9},{8,6},{9,7},... | collective-permute-start | bytes 98312 | tf_op jit(solution)/shard_map/ppermute | solution.py:53
  46.9 6.1 %collective-permute-start.14 = (bf16[8,2048]{1,0:T(8,128)(2,1)S(1)}, bf16[8,2048]{1,0:T(8,128)(2,1)S(1)}, u32[]{:S(2)}, u32[]{:S(2)}) collective-permute-start(bf16[8,2048]{1,0:T(8,128)(2,1)S(1)} %get-tuple-element.24), channel_id=1, source_target_pairs={{0,12},{1,13},{2,14},{3,15},{4,8},{5,9},{6,10},{7,11},{8,4},{9,5},... | collective-permute-start | bytes 98312 | tf_op jit(solution)/shard_map/ppermute | solution.py:53
  47.0 5.9 %collective-permute-start.13 = (bf16[8,2048]{1,0:T(8,128)(2,1)S(1)}, bf16[8,2048]{1,0:T(8,128)(2,1)S(1)}, u32[]{:S(2)}, u32[]{:S(2)}) collective-permute-start(bf16[8,2048]{1,0:T(8,128)(2,1)S(1)} %get-tuple-element.25), channel_id=1, source_target_pairs={{0,10},{1,11},{2,8},{3,9},{4,14},{5,15},{6,12},{7,13},{8,2},{9,3},... | collective-permute-start | bytes 98312 | tf_op jit(solution)/shard_map/ppermute | solution.py:53
  48.6 5.1 %collective-permute-start.12 = (bf16[8,2048]{1,0:T(8,128)(2,1)S(1)}, bf16[8,2048]{1,0:T(8,128)(2,1)S(1)}, u32[]{:S(2)}, u32[]{:S(2)}) collective-permute-start(bf16[8,2048]{1,0:T(8,128)(2,1)S(1)} %get-tuple-element.26), channel_id=1, source_target_pairs={{0,8},{1,9},{2,10},{3,11},{4,12},{5,13},{6,14},{7,15},{8,0},{9,1},... | collective-permute-start | bytes 98312 | tf_op jit(solution)/shard_map/ppermute | solution.py:53
  51.4 4.8 %collective-permute-start.11 = (bf16[8,2048]{1,0:T(8,128)(2,1)S(1)}, bf16[8,2048]{1,0:T(8,128)(2,1)S(1)}, u32[]{:S(2)}, u32[]{:S(2)}) collective-permute-start(bf16[8,2048]{1,0:T(8,128)(2,1)S(1)} %get-tuple-element.27), channel_id=1, source_target_pairs={{0,6},{1,7},{2,4},{3,5},{4,2},{5,3},{6,0},{7,1},{8,14},{9,15},{10,... | collective-permute-start | bytes 98312 | tf_op jit(solution)/shard_map/ppermute | solution.py:53
  61.3 21.6 %collective-permute-start.23 = (bf16[16,2176]{1,0:T(8,128)(2,1)S(1)}, bf16[16,2176]{1,0:T(8,128)(2,1)S(1)}, u32[]{:S(2)}, u32[]{:S(2)}) collective-permute-start(bf16[16,2176]{1,0:T(8,128)(2,1)S(1)} %pad_maximum_fusion.2), channel_id=1, source_target_pairs={{0,14},{1,15},{2,12},{3,13},{4,10},{5,11},{6,8},{7,9},{8,6},{9,7},... | collective-permute-start | bytes 208904 | tf_op jit(solution)/shard_map/ppermute | solution.py:53
  64.9 17.9 %collective-permute-start.22 = (bf16[16,2176]{1,0:T(8,128)(2,1)S(1)}, bf16[16,2176]{1,0:T(8,128)(2,1)S(1)}, u32[]{:S(2)}, u32[]{:S(2)}) collective-permute-start(bf16[16,2176]{1,0:T(8,128)(2,1)S(1)} %pad_maximum_fusion.2), channel_id=1, source_target_pairs={{0,12},{1,13},{2,14},{3,15},{4,8},{5,9},{6,10},{7,11},{8,4},{9,5},... | collective-permute-start | bytes 208904 | tf_op jit(solution)/shard_map/ppermute | solution.py:53
  66.1 16.8 %collective-permute-start.21 = (bf16[16,2176]{1,0:T(8,128)(2,1)S(1)}, bf16[16,2176]{1,0:T(8,128)(2,1)S(1)}, u32[]{:S(2)}, u32[]{:S(2)}) collective-permute-start(bf16[16,2176]{1,0:T(8,128)(2,1)S(1)} %pad_maximum_fusion.2), channel_id=1, source_target_pairs={{0,10},{1,11},{2,8},{3,9},{4,14},{5,15},{6,12},{7,13},{8,2},{9,3},... | collective-permute-start | bytes 208904 | tf_op jit(solution)/shard_map/ppermute | solution.py:53
  67.1 15.7 %collective-permute-start.20 = (bf16[16,2176]{1,0:T(8,128)(2,1)S(1)}, bf16[16,2176]{1,0:T(8,128)(2,1)S(1)}, u32[]{:S(2)}, u32[]{:S(2)}) collective-permute-start(bf16[16,2176]{1,0:T(8,128)(2,1)S(1)} %pad_maximum_fusion.2), channel_id=1, source_target_pairs={{0,8},{1,9},{2,10},{3,11},{4,12},{5,13},{6,14},{7,15},{8,0},{9,1},... | collective-permute-start | bytes 208904 | tf_op jit(solution)/shard_map/ppermute | solution.py:53
  77.6 5.2 %collective-permute-start.19 = (bf16[16,2176]{1,0:T(8,128)(2,1)S(1)}, bf16[16,2176]{1,0:T(8,128)(2,1)S(1)}, u32[]{:S(2)}, u32[]{:S(2)}) collective-permute-start(bf16[16,2176]{1,0:T(8,128)(2,1)S(1)} %pad_maximum_fusion.2), channel_id=1, source_target_pairs={{0,6},{1,7},{2,4},{3,5},{4,2},{5,3},{6,0},{7,1},{8,14},{9,15},{10,... | collective-permute-start | bytes 208904 | tf_op jit(solution)/shard_map/ppermute | solution.py:53
  107.8 6.4 %collective-permute-start.25 = (bf16[128,2048]{1,0:T(8,128)(2,1)}, bf16[128,2048]{1,0:T(8,128)(2,1)}, u32[]{:S(2)}, u32[]{:S(2)}) collective-permute-start(bf16[128,2048]{1,0:T(8,128)(2,1)} %bitcast.22), channel_id=1, source_target_pairs={{0,1},{1,0},{2,3},{3,2},{4,5},{5,4},{6,7},{7,6},{8,9},{9,8},{10,11... | collective-permute-start | bytes 1572872 | tf_op jit(solution)/shard_map/ppermute | solution.py:53
  115.4 9.9 %collective-permute-start.26 = (bf16[16,2048]{1,0:T(8,128)(2,1)S(1)}, bf16[16,2048]{1,0:T(8,128)(2,1)S(1)}, u32[]{:S(2)}, u32[]{:S(2)}) collective-permute-start(bf16[16,2048]{1,0:T(8,128)(2,1)S(1)} %get-tuple-element.15), channel_id=1, source_target_pairs={{0,2},{1,3},{2,0},{3,1},{4,6},{5,7},{6,4},{7,5},{8,10},{9,11},{10,... | collective-permute-start | bytes 196616 | tf_op jit(solution)/shard_map/ppermute | solution.py:53
  117.7 8.5 %collective-permute-start.32 = (bf16[16,2048]{1,0:T(8,128)(2,1)S(1)}, bf16[16,2048]{1,0:T(8,128)(2,1)S(1)}, u32[]{:S(2)}, u32[]{:S(2)}) collective-permute-start(bf16[16,2048]{1,0:T(8,128)(2,1)S(1)} %get-tuple-element.16), channel_id=1, source_target_pairs={{0,14},{1,15},{2,12},{3,13},{4,10},{5,11},{6,8},{7,9},{8,6},{9,7},... | collective-permute-start | bytes 196616 | tf_op jit(solution)/shard_map/ppermute | solution.py:53
  120.9 6.5 %collective-permute-start.31 = (bf16[16,2048]{1,0:T(8,128)(2,1)S(1)}, bf16[16,2048]{1,0:T(8,128)(2,1)S(1)}, u32[]{:S(2)}, u32[]{:S(2)}) collective-permute-start(bf16[16,2048]{1,0:T(8,128)(2,1)S(1)} %get-tuple-element.17), channel_id=1, source_target_pairs={{0,12},{1,13},{2,14},{3,15},{4,8},{5,9},{6,10},{7,11},{8,4},{9,5},... | collective-permute-start | bytes 196616 | tf_op jit(solution)/shard_map/ppermute | solution.py:53
  121.0 10.1 %collective-permute-start.30 = (bf16[16,2048]{1,0:T(8,128)(2,1)S(1)}, bf16[16,2048]{1,0:T(8,128)(2,1)S(1)}, u32[]{:S(2)}, u32[]{:S(2)}) collective-permute-start(bf16[16,2048]{1,0:T(8,128)(2,1)S(1)} %get-tuple-element.18), channel_id=1, source_target_pairs={{0,10},{1,11},{2,8},{3,9},{4,14},{5,15},{6,12},{7,13},{8,2},{9,3},... | collective-permute-start | bytes 196616 | tf_op jit(solution)/shard_map/ppermute | solution.py:53
  121.9 10.3 %collective-permute-start.29 = (bf16[16,2048]{1,0:T(8,128)(2,1)S(1)}, bf16[16,2048]{1,0:T(8,128)(2,1)S(1)}, u32[]{:S(2)}, u32[]{:S(2)}) collective-permute-start(bf16[16,2048]{1,0:T(8,128)(2,1)S(1)} %get-tuple-element.19), channel_id=1, source_target_pairs={{0,8},{1,9},{2,10},{3,11},{4,12},{5,13},{6,14},{7,15},{8,0},{9,1},... | collective-permute-start | bytes 196616 | tf_op jit(solution)/shard_map/ppermute | solution.py:53
  125.4 7.0 %collective-permute-start.28 = (bf16[16,2048]{1,0:T(8,128)(2,1)S(1)}, bf16[16,2048]{1,0:T(8,128)(2,1)S(1)}, u32[]{:S(2)}, u32[]{:S(2)}) collective-permute-start(bf16[16,2048]{1,0:T(8,128)(2,1)S(1)} %get-tuple-element.20), channel_id=1, source_target_pairs={{0,6},{1,7},{2,4},{3,5},{4,2},{5,3},{6,0},{7,1},{8,14},{9,15},{10,... | collective-permute-start | bytes 196616 | tf_op jit(solution)/shard_map/ppermute | solution.py:53
  126.2 6.6 %collective-permute-start.27 = (bf16[16,2048]{1,0:T(8,128)(2,1)S(1)}, bf16[16,2048]{1,0:T(8,128)(2,1)S(1)}, u32[]{:S(2)}, u32[]{:S(2)}) collective-permute-start(bf16[16,2048]{1,0:T(8,128)(2,1)S(1)} %get-tuple-element.21), channel_id=1, source_target_pairs={{0,4},{1,5},{2,6},{3,7},{4,0},{5,1},{6,2},{7,3},{8,12},{9,13},{10,... | collective-permute-start | bytes 196616 | tf_op jit(solution)/shard_map/ppermute | solution.py:53
  (22 other events, 138.6 us)

commit v3 on v2

v3 whole, which is shorter than its diff:
```python
import functools
import jax
import jax.numpy as jnp
from jax import lax
from jax.experimental import pallas as pl
from jax.experimental.pallas import tpu as pltpu
from jax.sharding import PartitionSpec as P

LANES = 128
MIB = 1 << 20


def normalize(state, norm_gain):
    scale = lax.rsqrt(jnp.mean(state * state, axis=-1, keepdims=True) + 1e-06)
    return (state * scale * norm_gain).astype(jnp.bfloat16)


def expert_apply(inputs, up_rows, down_rows):
    pre_act = lax.dot_general(
        inputs, up_rows, (((1,), (1,)), ((), ())), preferred_element_type=jnp.float32
    )
    hidden = jax.nn.silu(pre_act).astype(jnp.bfloat16)
    return jnp.dot(hidden, down_rows, preferred_element_type=jnp.float32)


def table_width(experts):
    return -(-6 * experts // LANES) * LANES


def weight_table(experts, chosen, weights, changed):
    shape = (chosen.shape[0], table_width(experts))
    lane = lax.broadcasted_iota(jnp.int32, shape, 1)
    section, expert = lane // experts, lane % experts
    dense = jnp.zeros(shape, jnp.float32)
    for k in range(chosen.shape[1]):
        dense = jnp.where(chosen[:, k : k + 1] == expert, weights[:, k : k + 1], dense)
    fresh = section < 0
    for item in changed:
        fresh = fresh | (expert == item)
    high = dense.astype(jnp.bfloat16).astype(jnp.float32)
    rest = dense - high
    middle = rest.astype(jnp.bfloat16).astype(jnp.float32)
    low = rest - middle
    part = section % 3
    value = jnp.where(part == 0, high, jnp.where(part == 1, middle, low))
    value = jnp.where(fresh, jnp.where(section < 3, 0.0, value), jnp.where(section < 3, value, 0.0))
    return jnp.where(section < 6, value, 0.0).astype(jnp.bfloat16)


def row_weights(experts, table, fresh):
    owner = lax.axis_index("expert")
    lane = lax.broadcasted_iota(jnp.int32, table.shape, 1)
    section = lane // experts
    first = 3 if fresh else 0
    mine = (lane % experts == owner) & (section >= first) & (section < first + 3)
    return jnp.sum(jnp.where(mine, table.astype(jnp.float32), 0.0), axis=1, keepdims=True)


def first_kernel(experts, tokens, gain, routes, scales, out):
    width = tokens.shape[1]
    normed = normalize(tokens[...].astype(jnp.float32), gain[...])
    table = weight_table(experts, routes[...], scales[...], [])
    for j in range(out.shape[0]):
        out[j, :, :width] = normed
        out[j, :, width:] = table


def next_kernel(experts, changed_count, previous, returned, gain, routes, scales, changed, state_out, out):
    width = previous.shape[1]
    state = previous[...].astype(jnp.float32) + jnp.sum(returned[...].astype(jnp.float32), axis=0)
    state_out[...] = state
    normed = normalize(state, gain[...])
    items = [changed[0, i] for i in range(changed_count)]
    table = weight_table(experts, routes[...], scales[...], items)
    for j in range(out.shape[0]):
        out[j, :, :width] = normed
        out[j, :, width:] = table


def last_kernel(previous, returned, out):
    state = previous[...] + jnp.sum(returned[...].astype(jnp.float32), axis=0)
    out[...] = state.astype(jnp.bfloat16)


def mlp_kernel(experts, fresh_flags, near, far, *refs):
    count = len(fresh_flags)
    sources = refs[: 2 * count]
    near_out, far_out = refs[2 * count : 2 * count + 2]
    buffers = refs[2 * count + 2 : 4 * count + 2]
    sems = refs[4 * count + 2]
    copies = [
        pltpu.make_async_copy(source, buffer, sems.at[i])
        for i, (source, buffer) in enumerate(zip(sources, buffers))
    ]
    for copy in copies:
        copy.start()
    half, width = near_out.shape
    inputs = jnp.concatenate([near[:, :width], far[:, :width]], axis=0)
    table = jnp.concatenate([near[:, width:], far[:, width:]], axis=0)
    total = None
    for i, fresh in enumerate(fresh_flags):
        copies[2 * i].wait()
        pre_act = lax.dot_general(
            inputs,
            buffers[2 * i][...],
            (((1,), (1,)), ((), ())),
            preferred_element_type=jnp.float32,
        )
        hidden = (pre_act / (1.0 + jnp.exp(-pre_act))).astype(jnp.bfloat16)
        copies[2 * i + 1].wait()
        result = jnp.dot(hidden, buffers[2 * i + 1][...], preferred_element_type=jnp.float32)
        result = result * row_weights(experts, table, fresh)
        total = result if total is None else total + result
    near_out[...] = total[:half]
    far_out[...] = total[half:].astype(jnp.bfloat16)


def run_mlp(near, far, weights, fresh_flags):
    experts = lax.axis_size("expert")
    rows = near.shape[0]
    width = weights[0].shape[1]
    hidden = sum(part.shape[0] for part in weights)
    in_vmem = pl.BlockSpec(memory_space=pltpu.VMEM)
    return pl.pallas_call(
        functools.partial(mlp_kernel, experts, fresh_flags),
        out_shape=(
            jax.ShapeDtypeStruct((rows, width), jnp.float32),
            jax.ShapeDtypeStruct((rows, width), jnp.bfloat16),
        ),
        in_specs=[in_vmem] * 2 + [pl.BlockSpec(memory_space=pl.ANY)] * len(weights),
        out_specs=(in_vmem, in_vmem),
        scratch_shapes=[pltpu.VMEM(part.shape, part.dtype) for part in weights]
        + [pltpu.SemaphoreType.DMA((len(weights),))],
        compiler_params=pltpu.CompilerParams(vmem_limit_bytes=32 * MIB),
        cost_estimate=pl.CostEstimate(
            flops=4 * rows * hidden * width, bytes_accessed=2 * hidden * width, transcendentals=0
        ),
    )(near, far, *weights)


def chip_groups(experts):
    return [list(range(core, experts, 2)) for core in range(2)]


def spread(blocks):
    return lax.all_to_all(
        blocks, "expert", 0, 0, axis_index_groups=chip_groups(lax.axis_size("expert")), tiled=True
    )


def swap(value, axis):
    size = lax.axis_size(axis)
    return lax.ppermute(value, axis, [(i, i ^ 1) for i in range(size)])


def exchange_plan(tokens, norm_gain, routes, route_scale, changed, stale, learner):
    experts = lax.axis_size("expert")
    chips = experts // 2
    row_count, width = tokens.shape[1], tokens.shape[2]
    packed = width + table_width(experts)
    half = chips * row_count
    gain = norm_gain[None]
    blocks_shape = jax.ShapeDtypeStruct((chips, row_count, packed), jnp.bfloat16)
    state_shape = jax.ShapeDtypeStruct((row_count, width), jnp.float32)
    in_vmem = pl.BlockSpec(memory_space=pltpu.VMEM)
    state = tokens[0]
    for step in range(routes.shape[0]):
        if step == 0:
            blocks = pl.pallas_call(
                functools.partial(first_kernel, experts), out_shape=blocks_shape
            )(state, gain, routes[step, 0], route_scale[step, 0])
        else:
            state, blocks = pl.pallas_call(
                functools.partial(next_kernel, experts, changed.shape[1]),
                in_specs=[in_vmem] * 5 + [pl.BlockSpec(memory_space=pltpu.SMEM)],
                out_shape=(state_shape, blocks_shape),
            )(state, returned, gain, routes[step, 0], route_scale[step, 0], changed)
        near = spread(blocks).reshape(half, packed)
        if step == 0:
            near_share, far_share = run_mlp(near, swap(near, "expert"), stale, (False,))
            share = near_share + swap(far_share, "expert").astype(jnp.float32)
        else:
            other = swap(near, "group")
            near_share, far_share = run_mlp(
                near, swap(near, "expert"), stale + learner, (False, True)
            )
            near_away, far_away = run_mlp(other, swap(other, "expert"), learner, (True,))
            away = near_away + swap(far_away, "expert").astype(jnp.float32)
            share = near_share + swap(far_share, "expert").astype(jnp.float32)
            share = share + swap(away.astype(jnp.bfloat16), "group").astype(jnp.float32)
        returned = spread(share.astype(jnp.bfloat16).reshape(chips, row_count, width))
    return pl.pallas_call(
        last_kernel, out_shape=jax.ShapeDtypeStruct((row_count, width), jnp.bfloat16)
    )(state, returned)[None]


def gather_plan(tokens, norm_gain, routes, route_scale, changed, stale, learner):
    experts = lax.axis_size("expert")
    owner_index = lax.axis_index("expert")
    row_count = tokens.shape[1]
    top_count = routes.shape[3]
    capacity = min(row_count, max(2, 2 * row_count * top_count // experts))
    is_fresh = jnp.any(changed[0] == owner_index)
    fresh = [lax.all_gather(part, "group", axis=0, tiled=True) for part in learner]
    newer = [jnp.where(is_fresh, new, old) for new, old in zip(fresh, stale)]
    state = tokens[0].astype(jnp.float32)
    buffer_ids = jnp.arange(experts * capacity, dtype=jnp.int32)
    expert_ids = jnp.arange(experts, dtype=jnp.int32)
    for step in range(routes.shape[0]):
        normed = normalize(state, norm_gain)
        chosen = routes[step, 0]
        weights = route_scale[step, 0]
        hits = (chosen.reshape(-1)[:, None] == expert_ids[None, :]).astype(jnp.int32)
        before = jnp.cumsum(hits, axis=0) - hits
        slot_pos = jnp.sum(before * hits, axis=1).reshape(chosen.shape)
        target = chosen * capacity + slot_pos
        placed = (target[:, :, None] == buffer_ids[None, None, :]).astype(jnp.float32)
        merge_weights = jnp.sum(placed * weights[:, :, None], axis=1)
        send_matrix = jnp.sum(placed, axis=1).astype(jnp.bfloat16)
        outgoing = lax.dot_general(
            send_matrix, normed, (((0,), (0,)), ((), ())), preferred_element_type=jnp.float32
        )
        outgoing = outgoing.astype(jnp.bfloat16).reshape(experts, capacity, -1)
        received = lax.all_to_all(outgoing, "expert", split_axis=0, concat_axis=0, tiled=True)
        flat = received.reshape(-1, received.shape[-1])
        result = expert_apply(flat, *(stale if step == 0 else newer))
        answer = result.astype(jnp.bfloat16).reshape(received.shape)
        returned = lax.all_to_all(answer, "expert", split_axis=0, concat_axis=0, tiled=True)
        flat_back = returned.reshape(experts * capacity, -1).astype(jnp.float32)
        state = state + jnp.dot(merge_weights, flat_back, precision=lax.Precision.HIGHEST)
    return state.astype(jnp.bfloat16)[None]


def local(
    tokens,
    norm_gain,
    routes,
    route_scale,
    changed,
    rollout_up,
    rollout_down,
    learner_up,
    learner_down,
):
    experts = lax.axis_size("expert")
    groups = lax.axis_size("group")
    fewer = tokens.shape[1] * experts < learner_up.shape[1]
    paired = experts % 2 == 0 and groups == 2 and routes.shape[0] == 2
    plan = exchange_plan if fewer and paired else gather_plan
    stale = (rollout_up[0], rollout_down[0])
    learner = (learner_up[0], learner_down[0])
    return plan(tokens, norm_gain, routes, route_scale, changed, stale, learner)


def solution(mesh):
    placed = (
        P("group", "expert", None),
        P(),
        P(None, "group", "expert", None),
        P(None, "group", "expert", None),
        P("group", None),
        P("expert", None, None),
        P("expert", None, None),
        P("expert", "group", None),
        P("expert", "group", None),
    )
    return jax.shard_map(
        local, mesh=mesh, in_specs=placed, out_specs=P("group", "expert", None), check_vma=False
    )
```

time: 138 us -> 104 us (0.75)
  blocking collectives: 0 us -> 56.6 us
  starting transfers between devices: 52.5 us -> 4.4 us
  matrix products: 28.1 us -> 0 us
  waiting for transfers between devices: 34.4 us -> 15.9 us
  Pallas kernels: 0 us -> 13.6 us
  other arithmetic: 11.5 us -> 0.18 us
  local copies, waits for them, and re-layouts: 10.6 us -> 12.5 us
    all_to_all x0 -> x4, blocking collectives: none -> 56.6 us  [spread(): lax.all_to_all(blocks, 'expert', 0, 0, axis_index_groups=chip_groups(lax....]
    ppermute x34 -> x8, starting transfers between devices: 52.5 us -> 4.4 us  [swap(): return lax.ppermute(value, axis, [(i, i ^ 1) for i in range(size)])]
    dot_general x6 -> x0, matrix products: 28.1 us -> none  [expert_apply(): return jnp.dot(hidden, down_rows, preferred_element_type=jnp.float32)]
    ppermute x34 -> x8, waiting for transfers between devices: 34.4 us -> 15.9 us  [swap(): return lax.ppermute(value, axis, [(i, i ^ 1) for i in range(size)])]
    pallas_call x0 -> x6, Pallas kernels: none -> 13.6 us  [the longest x3 8.51 us: run_mlp(): pl.pallas_call(functools.partial(mlp_kernel, experts, fresh_flags), out_s...]
    reduce_sum x6 -> x0, other arithmetic: 5.25 us -> none  [the longest x3 3.1 us: unpack(): return jnp.sum(jnp.where(mine, total, 0.0), axis=1, keepdims=True)]
    unnamed x39 -> x16, local copies, waits for them, and re-layouts: 5.16 us -> 9.9 us
    slice x5 -> x0, local copies, waits for them, and re-layouts: 3.72 us -> none  [the longest x2 3.66 us: exchange_plan(): both = jnp.concatenate([new[:, :1] + old, new[:, 1:]], axis=1)]
  transfers between devices with their start and end apart: 34 -> 8, of which waited for: 18 -> 5; matrix products, arithmetic and copies ran while one was open for 6% -> 0% of each run, Pallas kernels for 0% -> 6%
where the time goes in v3:
time: 104 us; the launch traced here: 103 us
  blocking collectives  56.6 us (54%)
  waiting for transfers between devices  15.9 us (15%)
  Pallas kernels  13.6 us (13%)
  local copies, waits for them, and re-layouts  12.5 us (12%)
  starting transfers between devices  4.4 us (4%)
    all_to_all x4, blocking collectives, spread(): lax.all_to_all(blocks, 'expert', 0, 0, axis_index_groups=chip_groups(lax....  56.6 us
    ppermute x8, waiting for transfers between devices, swap(): return lax.ppermute(value, axis, [(i, i ^ 1) for i in range(size)])  15.9 us
    unnamed x16, local copies, waits for them, and re-layouts  9.9 us
    pallas_call x3, Pallas kernels, run_mlp(): pl.pallas_call(functools.partial(mlp_kernel, experts, fresh_flags), out_s...  8.51 us
    ppermute x8, starting transfers between devices, swap(): return lax.ppermute(value, axis, [(i, i ^ 1) for i in range(size)])  4.4 us
  transfers between devices with their start and end apart: 8, of which 5 were waited for; matrix products, arithmetic and copies ran while one was open for 0% of the time, Pallas kernels for 6%

profile of v3, /device:TPU:0, one launch (start us, length us, event | category | flops | bytes accessed | tf_op | source)
XLA Modules:
  0.0 103.3 jit_solution(933167120357178397)
XLA Ops:
  0.0 1.3 %slice_bitcast_fusion.1 = (s32[8,8]{1,0:T(8,128)}, s32[8,8]{1,0:T(8,128)}) fusion(s32[2,1,8,8]{3,2,1,0:T(8,128)} %param.11), kind=kLoop, calls=%fused_computation.6 | loop fusion | bytes 1024 | tf_op jit(solution)/shard_map/squeeze | solution.py:177
  1.3 1.3 %slice_bitcast_fusion = (f32[8,8]{1,0:T(8,128)}, f32[8,8]{1,0:T(8,128)}) fusion(f32[2,1,8,8]{3,2,1,0:T(8,128)} %param.12), kind=kLoop, calls=%fused_computation.5 | loop fusion | bytes 1024 | tf_op jit(solution)/shard_map/squeeze | solution.py:177
  2.6 1.6 %shard_map.91 = bf16[8,8,2176]{2,1,0:T(8,128)(2,1)} custom-call(bf16[8,2048]{1,0:T(8,128)(2,1)} %bitcast.34, f32[1,2048]{1,0:T(1,128)} %bitcast.36, s32[8,8]{1,0:T(8,128)} %get-tuple-element.24.routes, f32[8,8]{1,0:T(8,128)} %get-tuple-element.22.scales), custom_call_target="tpu_custom_call" | custom-call | tf_op jit(solution)/shard_map/pallas_call | solution.py:169
  4.2 17.3 %all_to_all.20 = bf16[8,8,2176]{2,1,0:T(8,128)(2,1)S(1)} all-to-all(bf16[8,8,2176]{2,1,0:T(8,128)(2,1)} %shard_map.91), channel_id=1, replica_groups={{0,2,4,6,8,10,12,14},{1,3,5,7,9,11,13,15},{16,18,20,22,24,26,28,30},{17..., dimensions={0} | all-to-all | bytes 557056 | tf_op jit(solution)/shard_map/all_to_all | solution.py:146
  21.5 1.6 %collective-permute-done.far = bf16[64,2176]{1,0:T(8,128)(2,1)S(1)} collective-permute-done((bf16[64,2176]{1,0:T(8,128)(2,1)S(1)}, bf16[64,2176]{1,0:T(8,128)(2,1)S(1)}, u32[]{:S(2)}, u32[]{:S(2)}) %collective-permute-start) | collective-permute-done | bytes 278560 | tf_op jit(solution)/shard_map/ppermute | solution.py:153
  23.1 1.9 %copy-done = bf16[1,768,2048]{2,1,0:T(8,128)(2,1)S(1)} copy-done((bf16[1,768,2048]{2,1,0:T(8,128)(2,1)S(1)}, bf16[1,768,2048]{2,1,0:T(8,128)(2,1)}, u32[]{:S(2)}) %copy-start) | copy-done | bytes 3145752
  25.0 1.9 %copy-done.2 = bf16[1,768,2048]{2,1,0:T(8,128)(2,1)S(1)} copy-done((bf16[1,768,2048]{2,1,0:T(8,128)(2,1)S(1)}, bf16[1,768,2048]{2,1,0:T(8,128)(2,1)}, u32[]{:S(2)}) %copy-start.2) | copy-done | bytes 3145752
  26.9 2.7 %shard_map.92 = (f32[64,2048]{1,0:T(8,128)S(1)}, bf16[64,2048]{1,0:T(8,128)(2,1)S(1)}) custom-call(bf16[64,2176]{1,0:T(8,128)(2,1)S(1)} %bitcast.33, bf16[64,2176]{1,0:T(8,128)(2,1)S(1)} %collective-permute-done.far, bf16[768,2048]{1,0:T(8,128)(2,1)S(1)} %bitcast.21, bf16[768,2048]{1,0:T(8,128)(2,1)S(1)} %bitcast.23), custom_call_target="tpu_custom_call" | custom-call | flops 805306368 | bytes 6291456 | tf_op jit(solution)/shard_map/pallas_call | solution.py:124
  29.8 1.4 %collective-permute-done.1 = bf16[64,2048]{1,0:T(8,128)(2,1)S(1)} collective-permute-done((bf16[64,2048]{1,0:T(8,128)(2,1)S(1)}, bf16[64,2048]{1,0:T(8,128)(2,1)S(1)}, u32[]{:S(2)}, u32[]{:S(2)}) %collective-permute-start.1) | collective-permute-done | bytes 262176 | tf_op jit(solution)/shard_map/ppermute | solution.py:153
  31.3 12.6 %all_to_all.21.returned = bf16[8,8,2048]{2,1,0:T(8,128)(2,1)} all-to-all(bf16[8,8,2048]{2,1,0:T(8,128)(2,1)S(1)} %fusion), channel_id=1, replica_groups={{0,2,4,6,8,10,12,14},{1,3,5,7,9,11,13,15},{16,18,20,22,24,26,28,30},{17..., dimensions={0} | all-to-all | bytes 524288 | tf_op jit(solution)/shard_map/all_to_all | solution.py:146
  43.8 1.8 %shard_map.93 = (f32[8,2048]{1,0:T(8,128)}, bf16[8,8,2176]{2,1,0:T(8,128)(2,1)}) custom-call(bf16[8,2048]{1,0:T(8,128)(2,1)} %bitcast.35, bf16[8,8,2048]{2,1,0:T(8,128)(2,1)} %all_to_all.21.returned, f32[1,2048]{1,0:T(1,128)} %bitcast.37, s32[8,8]{1,0:T(8,128)} %get-tuple-element.23.routes, f32[8,8]{1,0:T(8,128)} %get-tuple-element.21.scales, s32[1,4]{1,0:T(1,128)} %changed.1), custom_call_target="tpu_custom_call" | custom-call | tf_op jit(solution)/shard_map/pallas_call | solution.py:173
  45.7 13.8 %all_to_all.22 = bf16[8,8,2176]{2,1,0:T(8,128)(2,1)S(1)} all-to-all(bf16[8,8,2176]{2,1,0:T(8,128)(2,1)} %get-tuple-element.16), channel_id=1, replica_groups={{0,2,4,6,8,10,12,14},{1,3,5,7,9,11,13,15},{16,18,20,22,24,26,28,30},{17..., dimensions={0} | all-to-all | bytes 557056 | tf_op jit(solution)/shard_map/all_to_all | solution.py:146
  59.4 1.5 %collective-permute-start.4 = (bf16[64,2176]{1,0:T(8,128)(2,1)S(1)}, bf16[64,2176]{1,0:T(8,128)(2,1)S(1)}, u32[]{:S(2)}, u32[]{:S(2)}) collective-permute-start(bf16[64,2176]{1,0:T(8,128)(2,1)S(1)} %bitcast.29), channel_id=1, source_target_pairs={{0,16},{16,0},{1,17},{17,1},{2,18},{18,2},{3,19},{19,3},{4,20},{20... | collective-permute-start | bytes 835592 | tf_op jit(solution)/shard_map/ppermute | solution.py:153
  60.9 5.1 %collective-permute-done.4.near = bf16[64,2176]{1,0:T(8,128)(2,1)S(1)} collective-permute-done((bf16[64,2176]{1,0:T(8,128)(2,1)S(1)}, bf16[64,2176]{1,0:T(8,128)(2,1)S(1)}, u32[]{:S(2)}, u32[]{:S(2)}) %collective-permute-start.4) | collective-permute-done | bytes 278560 | tf_op jit(solution)/shard_map/ppermute | solution.py:153
  67.6 1.4 %copy-done.4 = bf16[1,384,2048]{2,1,0:T(8,128)(2,1)S(1)} copy-done((bf16[1,384,2048]{2,1,0:T(8,128)(2,1)S(1)}, bf16[1,384,2048]{2,1,0:T(8,128)(2,1)}, u32[]{:S(2)}) %copy-start.4) | copy-done | bytes 1572888
  69.0 1.4 %copy-done.6 = bf16[1,384,2048]{2,1,0:T(8,128)(2,1)S(1)} copy-done((bf16[1,384,2048]{2,1,0:T(8,128)(2,1)S(1)}, bf16[1,384,2048]{2,1,0:T(8,128)(2,1)}, u32[]{:S(2)}) %copy-start.6) | copy-done | bytes 1572888
  70.4 1.6 %shard_map.95 = (f32[64,2048]{1,0:T(8,128)S(1)}, bf16[64,2048]{1,0:T(8,128)(2,1)S(1)}) custom-call(bf16[64,2176]{1,0:T(8,128)(2,1)S(1)} %collective-permute-done.4.near, bf16[64,2176]{1,0:T(8,128)(2,1)S(1)} %collective-permute-done.5.far, bf16[384,2048]{1,0:T(8,128)(2,1)S(1)} %bitcast.25, bf16[384,2048]{1,0:T(8,128)(2,1)S(1)} %bitcast.27), custom_call_target="tpu_custom_call" | custom-call | flops 402653184 | bytes 3145728 | tf_op jit(solution)/shard_map/pallas_call | solution.py:124
  72.2 1.9 %copy-done.3 = bf16[1,768,2048]{2,1,0:T(8,128)(2,1)S(1)} copy-done((bf16[1,768,2048]{2,1,0:T(8,128)(2,1)S(1)}, bf16[1,768,2048]{2,1,0:T(8,128)(2,1)}, u32[]{:S(2)}) %copy-start.3) | copy-done | bytes 3145752
  74.1 1.4 %copy-done.7 = bf16[1,384,2048]{2,1,0:T(8,128)(2,1)S(1)} copy-done((bf16[1,384,2048]{2,1,0:T(8,128)(2,1)S(1)}, bf16[1,384,2048]{2,1,0:T(8,128)(2,1)}, u32[]{:S(2)}) %copy-start.7) | copy-done | bytes 1572888
  75.5 4.2 %shard_map.94 = (f32[64,2048]{1,0:T(8,128)S(1)}, bf16[64,2048]{1,0:T(8,128)(2,1)S(1)}) custom-call(bf16[64,2176]{1,0:T(8,128)(2,1)S(1)} %bitcast.31, bf16[64,2176]{1,0:T(8,128)(2,1)S(1)} %collective-permute-done.2.far, bf16[768,2048]{1,0:T(8,128)(2,1)S(1)} %bitcast.22, bf16[768,2048]{1,0:T(8,128)(2,1)S(1)} %bitcast.24, bf16[384,2048]{1,0:T(8,128)(2,1)S(1)} %bitcast.26, ...), custom_call_target="tpu_custom_call" | custom-call | flops 1207959552 | bytes 9437184 | tf_op jit(solution)/shard_map/pallas_call | solution.py:124
  80.2 1.6 %collective-permute-start.7 = (bf16[64,2048]{1,0:T(8,128)(2,1)S(1)}, bf16[64,2048]{1,0:T(8,128)(2,1)S(1)}, u32[]{:S(2)}, u32[]{:S(2)}) collective-permute-start(bf16[64,2048]{1,0:T(8,128)(2,1)S(1)} %add_convert_fusion.1), channel_id=1, source_target_pairs={{0,16},{16,0},{1,17},{17,1},{2,18},{18,2},{3,19},{19,3},{4,20},{20... | collective-permute-start | bytes 786440 | tf_op jit(solution)/shard_map/ppermute | solution.py:153
  81.8 6.9 %collective-permute-done.7 = bf16[64,2048]{1,0:T(8,128)(2,1)S(1)} collective-permute-done((bf16[64,2048]{1,0:T(8,128)(2,1)S(1)}, bf16[64,2048]{1,0:T(8,128)(2,1)S(1)}, u32[]{:S(2)}, u32[]{:S(2)}) %collective-permute-start.7) | collective-permute-done | bytes 262176 | tf_op jit(solution)/shard_map/ppermute | solution.py:153
  88.7 13.0 %all_to_all.23.returned = bf16[8,8,2048]{2,1,0:T(8,128)(2,1)} all-to-all(bf16[8,8,2048]{2,1,0:T(8,128)(2,1)S(1)} %fusion.1), channel_id=1, replica_groups={{0,2,4,6,8,10,12,14},{1,3,5,7,9,11,13,15},{16,18,20,22,24,26,28,30},{17..., dimensions={0} | all-to-all | bytes 524288 | tf_op jit(solution)/shard_map/all_to_all | solution.py:146
  101.6 1.6 %shard_map.96 = bf16[8,2048]{1,0:T(8,128)(2,1)} custom-call(f32[8,2048]{1,0:T(8,128)} %get-tuple-element.15.previous, bf16[8,8,2048]{2,1,0:T(8,128)(2,1)} %all_to_all.23.returned), custom_call_target="tpu_custom_call" | custom-call | tf_op jit(solution)/shard_map/pallas_call | solution.py:192
  (23 shorter events, 2.6 us)
Async XLA Ops:
  21.5 1.6 %collective-permute-start = (bf16[64,2176]{1,0:T(8,128)(2,1)S(1)}, bf16[64,2176]{1,0:T(8,128)(2,1)S(1)}, u32[]{:S(2)}, u32[]{:S(2)}) collective-permute-start(bf16[64,2176]{1,0:T(8,128)(2,1)S(1)} %bitcast.32), channel_id=1, source_target_pairs={{0,1},{1,0},{2,3},{3,2},{4,5},{5,4},{6,7},{7,6},{8,9},{9,8},{10,11... | collective-permute-start | bytes 835592 | tf_op jit(solution)/shard_map/ppermute | solution.py:153
  23.1 1.9 %copy-start = (bf16[1,768,2048]{2,1,0:T(8,128)(2,1)S(1)}, bf16[1,768,2048]{2,1,0:T(8,128)(2,1)}, u32[]{:S(2)}) copy-start(bf16[1,768,2048]{2,1,0:T(8,128)(2,1)} %param.14) | copy-start | bytes 9437188
  25.0 1.9 %copy-start.2 = (bf16[1,768,2048]{2,1,0:T(8,128)(2,1)S(1)}, bf16[1,768,2048]{2,1,0:T(8,128)(2,1)}, u32[]{:S(2)}) copy-start(bf16[1,768,2048]{2,1,0:T(8,128)(2,1)} %param.15) | copy-start | bytes 9437188
  29.6 42.6 %copy-start.1 = (bf16[1,768,2048]{2,1,0:T(8,128)(2,1)S(1)}, bf16[1,768,2048]{2,1,0:T(8,128)(2,1)}, u32[]{:S(2)}) copy-start(bf16[1,768,2048]{2,1,0:T(8,128)(2,1)} %param.14) | copy-start | bytes 9437188
  29.6 1.6 %collective-permute-start.1 = (bf16[64,2048]{1,0:T(8,128)(2,1)S(1)}, bf16[64,2048]{1,0:T(8,128)(2,1)S(1)}, u32[]{:S(2)}, u32[]{:S(2)}) collective-permute-start(bf16[64,2048]{1,0:T(8,128)(2,1)S(1)} %get-tuple-element.14), channel_id=1, source_target_pairs={{0,1},{1,0},{2,3},{3,2},{4,5},{5,4},{6,7},{7,6},{8,9},{9,8},{10,11... | collective-permute-start | bytes 786440 | tf_op jit(solution)/shard_map/ppermute | solution.py:153
  59.4 6.5 %collective-permute-start.4 = (bf16[64,2176]{1,0:T(8,128)(2,1)S(1)}, bf16[64,2176]{1,0:T(8,128)(2,1)S(1)}, u32[]{:S(2)}, u32[]{:S(2)}) collective-permute-start(bf16[64,2176]{1,0:T(8,128)(2,1)S(1)} %bitcast.29), channel_id=1, source_target_pairs={{0,16},{16,0},{1,17},{17,1},{2,18},{18,2},{3,19},{19,3},{4,20},{20... | collective-permute-start | bytes 835592 | tf_op jit(solution)/shard_map/ppermute | solution.py:153
  66.0 1.6 %collective-permute-start.5 = (bf16[64,2176]{1,0:T(8,128)(2,1)S(1)}, bf16[64,2176]{1,0:T(8,128)(2,1)S(1)}, u32[]{:S(2)}, u32[]{:S(2)}) collective-permute-start(bf16[64,2176]{1,0:T(8,128)(2,1)S(1)} %collective-permute-done.4.near), channel_id=1, source_target_pairs={{0,1},{1,0},{2,3},{3,2},{4,5},{5,4},{6,7},{7,6},{8,9},{9,8},{10,11... | collective-permute-start | bytes 835592 | tf_op jit(solution)/shard_map/ppermute | solution.py:153
  66.0 6.2 %collective-permute-start.2 = (bf16[64,2176]{1,0:T(8,128)(2,1)S(1)}, bf16[64,2176]{1,0:T(8,128)(2,1)S(1)}, u32[]{:S(2)}, u32[]{:S(2)}) collective-permute-start(bf16[64,2176]{1,0:T(8,128)(2,1)S(1)} %bitcast.30), channel_id=1, source_target_pairs={{0,1},{1,0},{2,3},{3,2},{4,5},{5,4},{6,7},{7,6},{8,9},{9,8},{10,11... | collective-permute-start | bytes 835592 | tf_op jit(solution)/shard_map/ppermute | solution.py:153
  67.6 1.4 %copy-start.4 = (bf16[1,384,2048]{2,1,0:T(8,128)(2,1)S(1)}, bf16[1,384,2048]{2,1,0:T(8,128)(2,1)}, u32[]{:S(2)}) copy-start(bf16[1,384,2048]{2,1,0:T(8,128)(2,1)} %param.16) | copy-start | bytes 4718596
  69.0 1.4 %copy-start.6 = (bf16[1,384,2048]{2,1,0:T(8,128)(2,1)S(1)}, bf16[1,384,2048]{2,1,0:T(8,128)(2,1)}, u32[]{:S(2)}) copy-start(bf16[1,384,2048]{2,1,0:T(8,128)(2,1)} %param.17) | copy-start | bytes 4718596
  70.4 1.8 %copy-start.5 = (bf16[1,384,2048]{2,1,0:T(8,128)(2,1)S(1)}, bf16[1,384,2048]{2,1,0:T(8,128)(2,1)}, u32[]{:S(2)}) copy-start(bf16[1,384,2048]{2,1,0:T(8,128)(2,1)} %param.16) | copy-start | bytes 4718596
  71.9 8.2 %collective-permute-start.6 = (bf16[64,2048]{1,0:T(8,128)(2,1)S(1)}, bf16[64,2048]{1,0:T(8,128)(2,1)S(1)}, u32[]{:S(2)}, u32[]{:S(2)}) collective-permute-start(bf16[64,2048]{1,0:T(8,128)(2,1)S(1)} %get-tuple-element.20), channel_id=1, source_target_pairs={{0,1},{1,0},{2,3},{3,2},{4,5},{5,4},{6,7},{7,6},{8,9},{9,8},{10,11... | collective-permute-start | bytes 786440 | tf_op jit(solution)/shard_map/ppermute | solution.py:153
  72.2 1.9 %copy-start.3 = (bf16[1,768,2048]{2,1,0:T(8,128)(2,1)S(1)}, bf16[1,768,2048]{2,1,0:T(8,128)(2,1)}, u32[]{:S(2)}) copy-start(bf16[1,768,2048]{2,1,0:T(8,128)(2,1)} %param.15) | copy-start | bytes 9437188
  74.1 1.4 %copy-start.7 = (bf16[1,384,2048]{2,1,0:T(8,128)(2,1)S(1)}, bf16[1,384,2048]{2,1,0:T(8,128)(2,1)}, u32[]{:S(2)}) copy-start(bf16[1,384,2048]{2,1,0:T(8,128)(2,1)} %param.17) | copy-start | bytes 4718596
  79.7 2.1 %collective-permute-start.3 = (bf16[64,2048]{1,0:T(8,128)(2,1)S(1)}, bf16[64,2048]{1,0:T(8,128)(2,1)S(1)}, u32[]{:S(2)}, u32[]{:S(2)}) collective-permute-start(bf16[64,2048]{1,0:T(8,128)(2,1)S(1)} %get-tuple-element.18), channel_id=1, source_target_pairs={{0,1},{1,0},{2,3},{3,2},{4,5},{5,4},{6,7},{7,6},{8,9},{9,8},{10,11... | collective-permute-start | bytes 786440 | tf_op jit(solution)/shard_map/ppermute | solution.py:153
  80.2 8.4 %collective-permute-start.7 = (bf16[64,2048]{1,0:T(8,128)(2,1)S(1)}, bf16[64,2048]{1,0:T(8,128)(2,1)S(1)}, u32[]{:S(2)}, u32[]{:S(2)}) collective-permute-start(bf16[64,2048]{1,0:T(8,128)(2,1)S(1)} %add_convert_fusion.1), channel_id=1, source_target_pairs={{0,16},{16,0},{1,17},{17,1},{2,18},{18,2},{3,19},{19,3},{4,20},{20... | collective-permute-start | bytes 786440 | tf_op jit(solution)/shard_map/ppermute | solution.py:153

commit v4 on v3

--- a/solution.py
+++ b/solution.py
@@ -59,19 +59,19 @@
 def first_kernel(experts, tokens, gain, routes, scales, out):
     width = tokens.shape[1]
     normed = normalize(tokens[...].astype(jnp.float32), gain[...])
-    table = weight_table(experts, routes[...], scales[...], [])
+    table = weight_table(experts, routes[0, 0], scales[0, 0], [])
     for j in range(out.shape[0]):
         out[j, :, :width] = normed
         out[j, :, width:] = table
 
 
-def next_kernel(experts, changed_count, previous, returned, gain, routes, scales, changed, state_out, out):
+def next_kernel(experts, step, previous, returned, gain, routes, scales, changed, state_out, out):
     width = previous.shape[1]
     state = previous[...].astype(jnp.float32) + jnp.sum(returned[...].astype(jnp.float32), axis=0)
     state_out[...] = state
     normed = normalize(state, gain[...])
-    items = [changed[0, i] for i in range(changed_count)]
-    table = weight_table(experts, routes[...], scales[...], items)
+    items = [changed[0, i] for i in range(changed.shape[1])]
+    table = weight_table(experts, routes[step, 0], scales[step, 0], items)
     for j in range(out.shape[0]):
         out[j, :, :width] = normed
         out[j, :, width:] = table
@@ -82,34 +82,43 @@
     out[...] = state.astype(jnp.bfloat16)
 
 
-def mlp_kernel(experts, fresh_flags, near, far, *refs):
+def mlp_kernel(experts, fresh_flags, chunks, near, far, *refs):
     count = len(fresh_flags)
     sources = refs[: 2 * count]
     near_out, far_out = refs[2 * count : 2 * count + 2]
     buffers = refs[2 * count + 2 : 4 * count + 2]
     sems = refs[4 * count + 2]
-    copies = [
-        pltpu.make_async_copy(source, buffer, sems.at[i])
-        for i, (source, buffer) in enumerate(zip(sources, buffers))
-    ]
-    for copy in copies:
-        copy.start()
+
+    def copy(i, c):
+        size = sources[i].shape[0] // chunks[i]
+        part = pl.ds(c * size, size)
+        return pltpu.make_async_copy(sources[i].at[part], buffers[i].at[part], sems.at[i, c])
+
+    for i in range(2 * count):
+        for c in range(chunks[i]):
+            copy(i, c).start()
     half, width = near_out.shape
     inputs = jnp.concatenate([near[:, :width], far[:, :width]], axis=0)
     table = jnp.concatenate([near[:, width:], far[:, width:]], axis=0)
     total = None
     for i, fresh in enumerate(fresh_flags):
-        copies[2 * i].wait()
-        pre_act = lax.dot_general(
-            inputs,
-            buffers[2 * i][...],
-            (((1,), (1,)), ((), ())),
-            preferred_element_type=jnp.float32,
-        )
-        hidden = (pre_act / (1.0 + jnp.exp(-pre_act))).astype(jnp.bfloat16)
-        copies[2 * i + 1].wait()
+        scale = row_weights(experts, table, fresh)
+        hidden = []
+        size = sources[2 * i].shape[0] // chunks[2 * i]
+        for c in range(chunks[2 * i]):
+            copy(2 * i, c).wait()
+            pre_act = lax.dot_general(
+                inputs,
+                buffers[2 * i][c * size : (c + 1) * size],
+                (((1,), (1,)), ((), ())),
+                preferred_element_type=jnp.float32,
+            )
+            hidden.append((pre_act / (1.0 + jnp.exp(-pre_act))).astype(jnp.bfloat16))
+        hidden = jnp.concatenate(hidden, axis=1)
+        for c in range(chunks[2 * i + 1]):
+            copy(2 * i + 1, c).wait()
         result = jnp.dot(hidden, buffers[2 * i + 1][...], preferred_element_type=jnp.float32)
-        result = result * row_weights(experts, table, fresh)
+        result = result * scale
         total = result if total is None else total + result
     near_out[...] = total[:half]
     far_out[...] = total[half:].astype(jnp.bfloat16)
@@ -117,12 +126,12 @@
 
 def run_mlp(near, far, weights, fresh_flags):
     experts = lax.axis_size("expert")
-    rows = near.shape[0]
-    width = weights[0].shape[1]
-    hidden = sum(part.shape[0] for part in weights)
+    rows, width = near.shape[0], weights[0].shape[1]
+    hidden = sum(part.shape[0] for part in weights) // 2
+    chunks = [max(1, part.shape[0] // 384) if i % 2 == 0 else 1 for i, part in enumerate(weights)]
     in_vmem = pl.BlockSpec(memory_space=pltpu.VMEM)
     return pl.pallas_call(
-        functools.partial(mlp_kernel, experts, fresh_flags),
+        functools.partial(mlp_kernel, experts, fresh_flags, chunks),
         out_shape=(
             jax.ShapeDtypeStruct((rows, width), jnp.float32),
             jax.ShapeDtypeStruct((rows, width), jnp.bfloat16),
@@ -130,10 +139,10 @@
         in_specs=[in_vmem] * 2 + [pl.BlockSpec(memory_space=pl.ANY)] * len(weights),
         out_specs=(in_vmem, in_vmem),
         scratch_shapes=[pltpu.VMEM(part.shape, part.dtype) for part in weights]
-        + [pltpu.SemaphoreType.DMA((len(weights),))],
-        compiler_params=pltpu.CompilerParams(vmem_limit_bytes=32 * MIB),
+        + [pltpu.SemaphoreType.DMA((len(weights), max(chunks)))],
+        compiler_params=pltpu.CompilerParams(vmem_limit_bytes=20 * MIB),
         cost_estimate=pl.CostEstimate(
-            flops=4 * rows * hidden * width, bytes_accessed=2 * hidden * width, transcendentals=0
+            flops=8 * rows * hidden * width, bytes_accessed=4 * hidden * width, transcendentals=0
         ),
     )(near, far, *weights)
 
@@ -163,34 +172,52 @@
     blocks_shape = jax.ShapeDtypeStruct((chips, row_count, packed), jnp.bfloat16)
     state_shape = jax.ShapeDtypeStruct((row_count, width), jnp.float32)
     in_vmem = pl.BlockSpec(memory_space=pltpu.VMEM)
+    in_smem = pl.BlockSpec(memory_space=pltpu.SMEM)
+    small = pltpu.CompilerParams(vmem_limit_bytes=4 * MIB)
+    weight_bytes = 2 * sum(part.size for part in stale + learner)
+    long = pl.CostEstimate(
+        flops=640 * weight_bytes, bytes_accessed=2 * weight_bytes, transcendentals=0
+    )
     state = tokens[0]
     for step in range(routes.shape[0]):
         if step == 0:
             blocks = pl.pallas_call(
-                functools.partial(first_kernel, experts), out_shape=blocks_shape
-            )(state, gain, routes[step, 0], route_scale[step, 0])
+                functools.partial(first_kernel, experts),
+                in_specs=[in_vmem] * 4,
+                out_specs=in_vmem,
+                out_shape=blocks_shape,
+                compiler_params=small,
+                cost_estimate=long,
+            )(state, gain, routes, route_scale)
         else:
             state, blocks = pl.pallas_call(
-                functools.partial(next_kernel, experts, changed.shape[1]),
-                in_specs=[in_vmem] * 5 + [pl.BlockSpec(memory_space=pltpu.SMEM)],
+                functools.partial(next_kernel, experts, step),
+                in_specs=[in_vmem] * 5 + [in_smem],
+                out_specs=(in_vmem, in_vmem),
                 out_shape=(state_shape, blocks_shape),
-            )(state, returned, gain, routes[step, 0], route_scale[step, 0], changed)
+                compiler_params=small,
+                cost_estimate=long,
+            )(state, returned, gain, routes, route_scale, changed)
         near = spread(blocks).reshape(half, packed)
+        far = swap(near, "expert")
         if step == 0:
-            near_share, far_share = run_mlp(near, swap(near, "expert"), stale, (False,))
+            near_share, far_share = run_mlp(near, far, stale, (False,))
             share = near_share + swap(far_share, "expert").astype(jnp.float32)
         else:
             other = swap(near, "group")
-            near_share, far_share = run_mlp(
-                near, swap(near, "expert"), stale + learner, (False, True)
-            )
+            near_share, far_share = run_mlp(near, far, stale + learner, (False, True))
+            other, far_share = lax.optimization_barrier((other, far_share))
             near_away, far_away = run_mlp(other, swap(other, "expert"), learner, (True,))
             away = near_away + swap(far_away, "expert").astype(jnp.float32)
             share = near_share + swap(far_share, "expert").astype(jnp.float32)
             share = share + swap(away.astype(jnp.bfloat16), "group").astype(jnp.float32)
         returned = spread(share.astype(jnp.bfloat16).reshape(chips, row_count, width))
     return pl.pallas_call(
-        last_kernel, out_shape=jax.ShapeDtypeStruct((row_count, width), jnp.bfloat16)
+        last_kernel,
+        in_specs=[in_vmem] * 2,
+        out_specs=in_vmem,
+        out_shape=jax.ShapeDtypeStruct((row_count, width), jnp.bfloat16),
+        compiler_params=small,
     )(state, returned)[None]
 
 

time: 104 us -> 87.1 us (0.84)
  local copies, waits for them, and re-layouts: 12.5 us -> 2.89 us
  Pallas kernels: 13.6 us -> 9.9 us
  blocking collectives: 56.6 us -> 53.9 us
    unnamed x16 -> x26, local copies, waits for them, and re-layouts: 9.9 us -> 2.89 us
    pallas_call x6, Pallas kernels: 13.6 us -> 9.9 us  [the longest x3 8.41 us: run_mlp(): pl.pallas_call(functools.partial(mlp_kernel, experts, fresh_flags, chunks...]
    all_to_all x4, blocking collectives: 56.6 us -> 53.9 us  [spread(): lax.all_to_all(blocks, 'expert', 0, 0, axis_index_groups=chip_groups(lax....]
    squeeze x2 -> x0, local copies, waits for them, and re-layouts: 2.59 us -> none  [the longest x1 1.3 us: exchange_plan(): routes[step, 0]]
  transfers between devices with their start and end apart: 8 -> 8, of which waited for: 5 -> 7; matrix products, arithmetic and copies ran while one was open for 0% -> 0% of each run, Pallas kernels for 6% -> 5%
where the time goes in v4:
time: 87.1 us; the launch traced here: 86.7 us
  blocking collectives  53.9 us (62%)
  waiting for transfers between devices  15.8 us (18%)
  Pallas kernels  9.9 us (11%)
  starting transfers between devices  3.8 us (4%)
  local copies, waits for them, and re-layouts  2.89 us (3%)
    all_to_all x4, blocking collectives, spread(): lax.all_to_all(blocks, 'expert', 0, 0, axis_index_groups=chip_groups(lax....  53.9 us
    ppermute x8, waiting for transfers between devices, swap(): return lax.ppermute(value, axis, [(i, i ^ 1) for i in range(size)])  15.8 us
    pallas_call x3, Pallas kernels, run_mlp(): pl.pallas_call(functools.partial(mlp_kernel, experts, fresh_flags, chunks...  8.41 us
    ppermute x8, starting transfers between devices, swap(): return lax.ppermute(value, axis, [(i, i ^ 1) for i in range(size)])  3.8 us
    unnamed x26, local copies, waits for them, and re-layouts  2.89 us
  transfers between devices with their start and end apart: 8, of which 7 were waited for; matrix products, arithmetic and copies ran while one was open for 0% of the time, Pallas kernels for 5%

profile of v4, /device:TPU:0, one launch (start us, length us, event | category | flops | bytes accessed | tf_op | source)
XLA Modules:
  0.0 86.7 jit_solution(13977927759799849975)
XLA Ops:
  0.0 0.8 copy-done.4
  0.8 0.7 copy-done.6
  1.5 0.7 copy-done.8
  2.2 0.7 copy-done.10
  3.0 17.4 %all_to_all.20 = bf16[8,8,2176]{2,1,0:T(8,128)(2,1)S(1)} all-to-all(bf16[8,8,2176]{2,1,0:T(8,128)(2,1)S(1)} %shard_map.91), channel_id=1, replica_groups={{0,2,4,6,8,10,12,14},{1,3,5,7,9,11,13,15},{16,18,20,22,24,26,28,30},{17..., dimensions={0} | all-to-all | bytes 557056 | tf_op jit(solution)/shard_map/all_to_all | solution.py:155
  20.4 1.6 %collective-permute-done.far = bf16[64,2176]{1,0:T(8,128)(2,1)S(1)} collective-permute-done((bf16[64,2176]{1,0:T(8,128)(2,1)S(1)}, bf16[64,2176]{1,0:T(8,128)(2,1)S(1)}, u32[]{:S(2)}, u32[]{:S(2)}) %collective-permute-start) | collective-permute-done | bytes 278560 | tf_op jit(solution)/shard_map/ppermute | solution.py:162
  22.0 2.6 %shard_map.92 = (f32[64,2048]{1,0:T(8,128)S(1)}, bf16[64,2048]{1,0:T(8,128)(2,1)S(1)}) custom-call(bf16[64,2176]{1,0:T(8,128)(2,1)S(1)} %bitcast.25, bf16[64,2176]{1,0:T(8,128)(2,1)S(1)} %collective-permute-done.far, bf16[768,2048]{1,0:T(8,128)(2,1)S(1)} %bitcast.13, bf16[768,2048]{1,0:T(8,128)(2,1)S(1)} %bitcast.15), custom_call_target="tpu_custom_call" | custom-call | flops 805306368 | bytes 6291456 | tf_op jit(solution)/shard_map/pallas_call | solution.py:133
  24.6 0.2 collective-permute-start.1
  24.8 1.4 %collective-permute-done.1 = bf16[64,2048]{1,0:T(8,128)(2,1)S(1)} collective-permute-done((bf16[64,2048]{1,0:T(8,128)(2,1)S(1)}, bf16[64,2048]{1,0:T(8,128)(2,1)S(1)}, u32[]{:S(2)}, u32[]{:S(2)}) %collective-permute-start.1) | collective-permute-done | bytes 262176 | tf_op jit(solution)/shard_map/ppermute | solution.py:162
  26.3 11.9 %all_to_all.21.returned = bf16[8,8,2048]{2,1,0:T(8,128)(2,1)S(1)} all-to-all(bf16[8,8,2048]{2,1,0:T(8,128)(2,1)S(1)} %fusion), channel_id=1, replica_groups={{0,2,4,6,8,10,12,14},{1,3,5,7,9,11,13,15},{16,18,20,22,24,26,28,30},{17..., dimensions={0} | all-to-all | bytes 524288 | tf_op jit(solution)/shard_map/all_to_all | solution.py:155
  38.2 0.7 shard_map.93
  39.0 13.5 %all_to_all.22 = bf16[8,8,2176]{2,1,0:T(8,128)(2,1)S(1)} all-to-all(bf16[8,8,2176]{2,1,0:T(8,128)(2,1)S(1)} %get-tuple-element.18), channel_id=1, replica_groups={{0,2,4,6,8,10,12,14},{1,3,5,7,9,11,13,15},{16,18,20,22,24,26,28,30},{17..., dimensions={0} | all-to-all | bytes 557056 | tf_op jit(solution)/shard_map/all_to_all | solution.py:155
  52.5 1.5 %collective-permute-start.3 = (bf16[64,2176]{1,0:T(8,128)(2,1)S(1)}, bf16[64,2176]{1,0:T(8,128)(2,1)S(1)}, u32[]{:S(2)}, u32[]{:S(2)}) collective-permute-start(bf16[64,2176]{1,0:T(8,128)(2,1)S(1)} %bitcast.22), channel_id=1, source_target_pairs={{0,16},{16,0},{1,17},{17,1},{2,18},{18,2},{3,19},{19,3},{4,20},{20... | collective-permute-start | bytes 835592 | tf_op jit(solution)/shard_map/ppermute | solution.py:162
  54.0 4.2 %shard_map.94 = (f32[64,2048]{1,0:T(8,128)S(1)}, bf16[64,2048]{1,0:T(8,128)(2,1)S(1)}) custom-call(bf16[64,2176]{1,0:T(8,128)(2,1)S(1)} %bitcast.23, bf16[64,2176]{1,0:T(8,128)(2,1)S(1)} %collective-permute-done.2.far, bf16[768,2048]{1,0:T(8,128)(2,1)S(1)} %bitcast.14, bf16[768,2048]{1,0:T(8,128)(2,1)S(1)} %bitcast.16, bf16[384,2048]{1,0:T(8,128)(2,1)S(1)} %bitcast.17, ...), custom_call_target="tpu_custom_call" | custom-call | flops 1207959552 | bytes 9437184 | tf_op jit(solution)/shard_map/pallas_call | solution.py:133
  58.2 3.3 %collective-permute-done.3.near = bf16[64,2176]{1,0:T(8,128)(2,1)S(1)} collective-permute-done((bf16[64,2176]{1,0:T(8,128)(2,1)S(1)}, bf16[64,2176]{1,0:T(8,128)(2,1)S(1)}, u32[]{:S(2)}, u32[]{:S(2)}) %collective-permute-start.3) | collective-permute-done | bytes 278560 | tf_op jit(solution)/shard_map/ppermute | solution.py:162
  61.5 1.6 %collective-permute-done.5.far = bf16[64,2176]{1,0:T(8,128)(2,1)S(1)} collective-permute-done((bf16[64,2176]{1,0:T(8,128)(2,1)S(1)}, bf16[64,2176]{1,0:T(8,128)(2,1)S(1)}, u32[]{:S(2)}, u32[]{:S(2)}) %collective-permute-start.5) | collective-permute-done | bytes 278560 | tf_op jit(solution)/shard_map/ppermute | solution.py:162
  63.1 1.6 %shard_map.95 = (f32[64,2048]{1,0:T(8,128)S(1)}, bf16[64,2048]{1,0:T(8,128)(2,1)S(1)}) custom-call(bf16[64,2176]{1,0:T(8,128)(2,1)S(1)} %collective-permute-done.3.near, bf16[64,2176]{1,0:T(8,128)(2,1)S(1)} %collective-permute-done.5.far, bf16[384,2048]{1,0:T(8,128)(2,1)S(1)} %bitcast.18, bf16[384,2048]{1,0:T(8,128)(2,1)S(1)} %bitcast.20), custom_call_target="tpu_custom_call" | custom-call | flops 402653184 | bytes 3145728 | tf_op jit(solution)/shard_map/pallas_call | solution.py:133
  64.7 0.2 collective-permute-start.6
  64.9 0.4 collective-permute-start.4
  65.3 1.0 %collective-permute-done.6 = bf16[64,2048]{1,0:T(8,128)(2,1)S(1)} collective-permute-done((bf16[64,2048]{1,0:T(8,128)(2,1)S(1)}, bf16[64,2048]{1,0:T(8,128)(2,1)S(1)}, u32[]{:S(2)}, u32[]{:S(2)}) %collective-permute-start.6) | collective-permute-done | bytes 262176 | tf_op jit(solution)/shard_map/ppermute | solution.py:162
  66.4 1.5 %collective-permute-start.7 = (bf16[64,2048]{1,0:T(8,128)(2,1)S(1)}, bf16[64,2048]{1,0:T(8,128)(2,1)S(1)}, u32[]{:S(2)}, u32[]{:S(2)}) collective-permute-start(bf16[64,2048]{1,0:T(8,128)(2,1)S(1)} %add_convert_fusion.1), channel_id=1, source_target_pairs={{0,16},{16,0},{1,17},{17,1},{2,18},{18,2},{3,19},{19,3},{4,20},{20... | collective-permute-start | bytes 786440 | tf_op jit(solution)/shard_map/ppermute | solution.py:162
  67.9 6.9 %collective-permute-done.7 = bf16[64,2048]{1,0:T(8,128)(2,1)S(1)} collective-permute-done((bf16[64,2048]{1,0:T(8,128)(2,1)S(1)}, bf16[64,2048]{1,0:T(8,128)(2,1)S(1)}, u32[]{:S(2)}, u32[]{:S(2)}) %collective-permute-start.7) | collective-permute-done | bytes 262176 | tf_op jit(solution)/shard_map/ppermute | solution.py:162
  74.9 11.1 %all_to_all.23.returned = bf16[8,8,2048]{2,1,0:T(8,128)(2,1)S(1)} all-to-all(bf16[8,8,2048]{2,1,0:T(8,128)(2,1)S(1)} %fusion.1), channel_id=1, replica_groups={{0,2,4,6,8,10,12,14},{1,3,5,7,9,11,13,15},{16,18,20,22,24,26,28,30},{17..., dimensions={0} | all-to-all | bytes 524288 | tf_op jit(solution)/shard_map/all_to_all | solution.py:155
  86.0 0.7 shard_map.96
  (31 shorter events, 0.4 us)
Async XLA Ops:
  0.0 0.8 copy-start.4
  0.8 0.7 copy-start.6
  1.5 0.7 copy-start.8
  2.2 0.7 copy-start.10
  2.9 19.1 %copy-start = (bf16[1,768,2048]{2,1,0:T(8,128)(2,1)S(1)}, bf16[1,768,2048]{2,1,0:T(8,128)(2,1)}, u32[]{:S(2)}) copy-start(bf16[1,768,2048]{2,1,0:T(8,128)(2,1)} %param.14) | copy-start | bytes 9437188
  2.9 19.1 %copy-start.1 = (bf16[1,768,2048]{2,1,0:T(8,128)(2,1)S(1)}, bf16[1,768,2048]{2,1,0:T(8,128)(2,1)}, u32[]{:S(2)}) copy-start(bf16[1,768,2048]{2,1,0:T(8,128)(2,1)} %param.15) | copy-start | bytes 9437188
  20.4 1.6 %collective-permute-start = (bf16[64,2176]{1,0:T(8,128)(2,1)S(1)}, bf16[64,2176]{1,0:T(8,128)(2,1)S(1)}, u32[]{:S(2)}, u32[]{:S(2)}) collective-permute-start(bf16[64,2176]{1,0:T(8,128)(2,1)S(1)} %bitcast.24), channel_id=1, source_target_pairs={{0,1},{1,0},{2,3},{3,2},{4,5},{5,4},{6,7},{7,6},{8,9},{9,8},{10,11... | collective-permute-start | bytes 835592 | tf_op jit(solution)/shard_map/ppermute | solution.py:162
  21.9 16.2 %copy-start.5 = (bf16[1,8,2048]{2,1,0:T(8,128)(2,1)S(1)}, bf16[1,8,2048]{2,1,0:T(8,128)(2,1)}, u32[]{:S(2)}) copy-start(bf16[1,8,2048]{2,1,0:T(8,128)(2,1)} %param.9) | copy-start | bytes 98308
  21.9 16.2 %copy-start.7 = (f32[2048]{0:T(1024)S(1)}, f32[2048]{0:T(1024)}, u32[]{:S(2)}) copy-start(f32[2048]{0:T(1024)} %param.10) | copy-start | bytes 24580
  22.0 16.2 %copy-start.9 = (s32[2,1,8,8]{3,2,1,0:T(8,128)S(1)}, s32[2,1,8,8]{3,2,1,0:T(8,128)}, u32[]{:S(2)}) copy-start(s32[2,1,8,8]{3,2,1,0:T(8,128)} %routes.3) | copy-start | bytes 1540
  22.0 16.2 %copy-start.11 = (f32[2,1,8,8]{3,2,1,0:T(8,128)S(1)}, f32[2,1,8,8]{3,2,1,0:T(8,128)}, u32[]{:S(2)}) copy-start(f32[2,1,8,8]{3,2,1,0:T(8,128)} %scales.3) | copy-start | bytes 1540
  22.0 16.2 %copy-start.12 = (s32[1,4]{1,0:T(1,128)S(1)}, s32[1,4]{1,0:T(1,128)}, u32[]{:S(2)}) copy-start(s32[1,4]{1,0:T(1,128)} %changed.1) | copy-start | bytes 52
  24.6 1.6 %collective-permute-start.1 = (bf16[64,2048]{1,0:T(8,128)(2,1)S(1)}, bf16[64,2048]{1,0:T(8,128)(2,1)S(1)}, u32[]{:S(2)}, u32[]{:S(2)}) collective-permute-start(bf16[64,2048]{1,0:T(8,128)(2,1)S(1)} %get-tuple-element.16), channel_id=1, source_target_pairs={{0,1},{1,0},{2,3},{3,2},{4,5},{5,4},{6,7},{7,6},{8,9},{9,8},{10,11... | collective-permute-start | bytes 786440 | tf_op jit(solution)/shard_map/ppermute | solution.py:162
  38.2 15.8 %copy-start.2 = (bf16[1,384,2048]{2,1,0:T(8,128)(2,1)S(1)}, bf16[1,384,2048]{2,1,0:T(8,128)(2,1)}, u32[]{:S(2)}) copy-start(bf16[1,384,2048]{2,1,0:T(8,128)(2,1)} %param.16) | copy-start | bytes 4718596
  38.2 15.8 %copy-start.3 = (bf16[1,384,2048]{2,1,0:T(8,128)(2,1)S(1)}, bf16[1,384,2048]{2,1,0:T(8,128)(2,1)}, u32[]{:S(2)}) copy-start(bf16[1,384,2048]{2,1,0:T(8,128)(2,1)} %param.17) | copy-start | bytes 4718596
  52.5 1.6 %collective-permute-start.2 = (bf16[64,2176]{1,0:T(8,128)(2,1)S(1)}, bf16[64,2176]{1,0:T(8,128)(2,1)S(1)}, u32[]{:S(2)}, u32[]{:S(2)}) collective-permute-start(bf16[64,2176]{1,0:T(8,128)(2,1)S(1)} %bitcast.21), channel_id=1, source_target_pairs={{0,1},{1,0},{2,3},{3,2},{4,5},{5,4},{6,7},{7,6},{8,9},{9,8},{10,11... | collective-permute-start | bytes 835592 | tf_op jit(solution)/shard_map/ppermute | solution.py:162
  52.5 9.1 %collective-permute-start.3 = (bf16[64,2176]{1,0:T(8,128)(2,1)S(1)}, bf16[64,2176]{1,0:T(8,128)(2,1)S(1)}, u32[]{:S(2)}, u32[]{:S(2)}) collective-permute-start(bf16[64,2176]{1,0:T(8,128)(2,1)S(1)} %bitcast.22), channel_id=1, source_target_pairs={{0,16},{16,0},{1,17},{17,1},{2,18},{18,2},{3,19},{19,3},{4,20},{20... | collective-permute-start | bytes 835592 | tf_op jit(solution)/shard_map/ppermute | solution.py:162
  61.5 1.6 %collective-permute-start.5 = (bf16[64,2176]{1,0:T(8,128)(2,1)S(1)}, bf16[64,2176]{1,0:T(8,128)(2,1)S(1)}, u32[]{:S(2)}, u32[]{:S(2)}) collective-permute-start(bf16[64,2176]{1,0:T(8,128)(2,1)S(1)} %collective-permute-done.3.near), channel_id=1, source_target_pairs={{0,1},{1,0},{2,3},{3,2},{4,5},{5,4},{6,7},{7,6},{8,9},{9,8},{10,11... | collective-permute-start | bytes 835592 | tf_op jit(solution)/shard_map/ppermute | solution.py:162
  64.7 1.6 %collective-permute-start.6 = (bf16[64,2048]{1,0:T(8,128)(2,1)S(1)}, bf16[64,2048]{1,0:T(8,128)(2,1)S(1)}, u32[]{:S(2)}, u32[]{:S(2)}) collective-permute-start(bf16[64,2048]{1,0:T(8,128)(2,1)S(1)} %get-tuple-element.24), channel_id=1, source_target_pairs={{0,1},{1,0},{2,3},{3,2},{4,5},{5,4},{6,7},{7,6},{8,9},{9,8},{10,11... | collective-permute-start | bytes 786440 | tf_op jit(solution)/shard_map/ppermute | solution.py:162
  64.9 3.0 %collective-permute-start.4 = (bf16[64,2048]{1,0:T(8,128)(2,1)S(1)}, bf16[64,2048]{1,0:T(8,128)(2,1)S(1)}, u32[]{:S(2)}, u32[]{:S(2)}) collective-permute-start(bf16[64,2048]{1,0:T(8,128)(2,1)S(1)} %get-tuple-element.21), channel_id=1, source_target_pairs={{0,1},{1,0},{2,3},{3,2},{4,5},{5,4},{6,7},{7,6},{8,9},{9,8},{10,11... | collective-permute-start | bytes 786440 | tf_op jit(solution)/shard_map/ppermute | solution.py:162
  66.4 8.4 %collective-permute-start.7 = (bf16[64,2048]{1,0:T(8,128)(2,1)S(1)}, bf16[64,2048]{1,0:T(8,128)(2,1)S(1)}, u32[]{:S(2)}, u32[]{:S(2)}) collective-permute-start(bf16[64,2048]{1,0:T(8,128)(2,1)S(1)} %add_convert_fusion.1), channel_id=1, source_target_pairs={{0,16},{16,0},{1,17},{17,1},{2,18},{18,2},{3,19},{19,3},{4,20},{20... | collective-permute-start | bytes 786440 | tf_op jit(solution)/shard_map/ppermute | solution.py:162

commit v5 on v4

--- a/solution.py
+++ b/solution.py
@@ -56,9 +56,14 @@
     return jnp.sum(jnp.where(mine, table.astype(jnp.float32), 0.0), axis=1, keepdims=True)
 
 
-def first_kernel(experts, tokens, gain, routes, scales, out):
-    width = tokens.shape[1]
-    normed = normalize(tokens[...].astype(jnp.float32), gain[...])
+def first_kernel(tokens, out):
+    state = tokens[...].astype(jnp.float32)
+    out[...] = state * lax.rsqrt(jnp.mean(state * state, axis=-1, keepdims=True) + 1e-06)
+
+
+def pack_kernel(experts, scaled, gain, routes, scales, out):
+    width = scaled.shape[1]
+    normed = (scaled[...] * gain[...]).astype(jnp.bfloat16)
     table = weight_table(experts, routes[0, 0], scales[0, 0], [])
     for j in range(out.shape[0]):
         out[j, :, :width] = normed
@@ -82,43 +87,20 @@
     out[...] = state.astype(jnp.bfloat16)
 
 
-def mlp_kernel(experts, fresh_flags, chunks, near, far, *refs):
-    count = len(fresh_flags)
-    sources = refs[: 2 * count]
-    near_out, far_out = refs[2 * count : 2 * count + 2]
-    buffers = refs[2 * count + 2 : 4 * count + 2]
-    sems = refs[4 * count + 2]
-
-    def copy(i, c):
-        size = sources[i].shape[0] // chunks[i]
-        part = pl.ds(c * size, size)
-        return pltpu.make_async_copy(sources[i].at[part], buffers[i].at[part], sems.at[i, c])
-
-    for i in range(2 * count):
-        for c in range(chunks[i]):
-            copy(i, c).start()
+def mlp_kernel(experts, fresh_flags, near, far, *refs):
+    near_out, far_out = refs[-2:]
     half, width = near_out.shape
     inputs = jnp.concatenate([near[:, :width], far[:, :width]], axis=0)
     table = jnp.concatenate([near[:, width:], far[:, width:]], axis=0)
     total = None
     for i, fresh in enumerate(fresh_flags):
-        scale = row_weights(experts, table, fresh)
-        hidden = []
-        size = sources[2 * i].shape[0] // chunks[2 * i]
-        for c in range(chunks[2 * i]):
-            copy(2 * i, c).wait()
-            pre_act = lax.dot_general(
-                inputs,
-                buffers[2 * i][c * size : (c + 1) * size],
-                (((1,), (1,)), ((), ())),
-                preferred_element_type=jnp.float32,
-            )
-            hidden.append((pre_act / (1.0 + jnp.exp(-pre_act))).astype(jnp.bfloat16))
-        hidden = jnp.concatenate(hidden, axis=1)
-        for c in range(chunks[2 * i + 1]):
-            copy(2 * i + 1, c).wait()
-        result = jnp.dot(hidden, buffers[2 * i + 1][...], preferred_element_type=jnp.float32)
-        result = result * scale
+        up, down = refs[2 * i : 2 * i + 2]
+        pre_act = lax.dot_general(
+            inputs, up[...], (((1,), (1,)), ((), ())), preferred_element_type=jnp.float32
+        )
+        hidden = (pre_act / (1.0 + jnp.exp(-pre_act))).astype(jnp.bfloat16)
+        result = jnp.dot(hidden, down[...], preferred_element_type=jnp.float32)
+        result = result * row_weights(experts, table, fresh)
         total = result if total is None else total + result
     near_out[...] = total[:half]
     far_out[...] = total[half:].astype(jnp.bfloat16)
@@ -128,18 +110,15 @@
     experts = lax.axis_size("expert")
     rows, width = near.shape[0], weights[0].shape[1]
     hidden = sum(part.shape[0] for part in weights) // 2
-    chunks = [max(1, part.shape[0] // 384) if i % 2 == 0 else 1 for i, part in enumerate(weights)]
     in_vmem = pl.BlockSpec(memory_space=pltpu.VMEM)
     return pl.pallas_call(
-        functools.partial(mlp_kernel, experts, fresh_flags, chunks),
+        functools.partial(mlp_kernel, experts, fresh_flags),
         out_shape=(
             jax.ShapeDtypeStruct((rows, width), jnp.float32),
             jax.ShapeDtypeStruct((rows, width), jnp.bfloat16),
         ),
-        in_specs=[in_vmem] * 2 + [pl.BlockSpec(memory_space=pl.ANY)] * len(weights),
+        in_specs=[in_vmem] * (2 + len(weights)),
         out_specs=(in_vmem, in_vmem),
-        scratch_shapes=[pltpu.VMEM(part.shape, part.dtype) for part in weights]
-        + [pltpu.SemaphoreType.DMA((len(weights), max(chunks)))],
         compiler_params=pltpu.CompilerParams(vmem_limit_bytes=20 * MIB),
         cost_estimate=pl.CostEstimate(
             flops=8 * rows * hidden * width, bytes_accessed=4 * hidden * width, transcendentals=0
@@ -181,14 +160,21 @@
     state = tokens[0]
     for step in range(routes.shape[0]):
         if step == 0:
+            scaled = pl.pallas_call(
+                first_kernel,
+                in_specs=[in_vmem],
+                out_specs=in_vmem,
+                out_shape=state_shape,
+                compiler_params=small,
+                cost_estimate=long,
+            )(state)
             blocks = pl.pallas_call(
-                functools.partial(first_kernel, experts),
+                functools.partial(pack_kernel, experts),
                 in_specs=[in_vmem] * 4,
                 out_specs=in_vmem,
                 out_shape=blocks_shape,
                 compiler_params=small,
-                cost_estimate=long,
-            )(state, gain, routes, route_scale)
+            )(scaled, gain, routes, route_scale)
         else:
             state, blocks = pl.pallas_call(
                 functools.partial(next_kernel, experts, step),

time: 87.1 us -> 84.6 us (0.971)
  Pallas kernels: 9.9 us -> 7.88 us
  local copies, waits for them, and re-layouts: 2.89 us -> 1.39 us
  waiting for transfers between devices: 15.8 us -> 17 us
    pallas_call x4 -> x5, Pallas kernels: 8.53 us -> 6.51 us  [the longest x3 6.3 us: run_mlp(): pl.pallas_call(functools.partial(mlp_kernel, experts, fresh_flags), out_s...]
    unnamed x26 -> x20, local copies, waits for them, and re-layouts: 2.89 us -> 1.39 us
    ppermute x8, waiting for transfers between devices: 15.8 us -> 17 us  [swap(): return lax.ppermute(value, axis, [(i, i ^ 1) for i in range(size)])]
  transfers between devices with their start and end apart: 8 -> 8, of which waited for: 7 -> 7; matrix products, arithmetic and copies ran while one was open for 0% -> 0% of each run, Pallas kernels for 5% -> 3%
where the time goes in v5:
time: 84.6 us; the launch traced here: 84.3 us
  blocking collectives  53.9 us (64%)
  waiting for transfers between devices  17 us (20%)
  Pallas kernels  7.88 us (9%)
  starting transfers between devices  3.84 us (5%)
  local copies, waits for them, and re-layouts  1.39 us (2%)
    all_to_all x4, blocking collectives, spread(): lax.all_to_all(blocks, 'expert', 0, 0, axis_index_groups=chip_groups(lax....  53.9 us
    ppermute x8, waiting for transfers between devices, swap(): return lax.ppermute(value, axis, [(i, i ^ 1) for i in range(size)])  17 us
    pallas_call x3, Pallas kernels, run_mlp(): pl.pallas_call(functools.partial(mlp_kernel, experts, fresh_flags), out_s...  6.3 us
    ppermute x8, starting transfers between devices, swap(): return lax.ppermute(value, axis, [(i, i ^ 1) for i in range(size)])  3.84 us
  transfers between devices with their start and end apart: 8, of which 7 were waited for; matrix products, arithmetic and copies ran while one was open for 0% of the time, Pallas kernels for 3%

profile of v5, /device:TPU:0, one launch (start us, length us, event | category | flops | bytes accessed | tf_op | source)
XLA Modules:
  0.0 84.3 jit_solution(4374400529565165432)
XLA Ops:
  0.0 0.8 copy-done.7
  0.8 0.1 shard_map.91.scaled
  0.9 0.6 copy-done.4
  1.5 0.1 shard_map.92
  1.6 17.4 %all_to_all.20 = bf16[8,8,2176]{2,1,0:T(8,128)(2,1)S(1)} all-to-all(bf16[8,8,2176]{2,1,0:T(8,128)(2,1)S(1)} %shard_map.92), channel_id=1, replica_groups={{0,2,4,6,8,10,12,14},{1,3,5,7,9,11,13,15},{16,18,20,22,24,26,28,30},{17..., dimensions={0} | all-to-all | bytes 557056 | tf_op jit(solution)/shard_map/all_to_all | solution.py:134
  19.0 1.6 %collective-permute-done.far = bf16[64,2176]{1,0:T(8,128)(2,1)S(1)} collective-permute-done((bf16[64,2176]{1,0:T(8,128)(2,1)S(1)}, bf16[64,2176]{1,0:T(8,128)(2,1)S(1)}, u32[]{:S(2)}, u32[]{:S(2)}) %collective-permute-start) | collective-permute-done | bytes 278560 | tf_op jit(solution)/shard_map/ppermute | solution.py:141
  20.6 2.1 %shard_map.93 = (f32[64,2048]{1,0:T(8,128)S(1)}, bf16[64,2048]{1,0:T(8,128)(2,1)S(1)}) custom-call(bf16[64,2176]{1,0:T(8,128)(2,1)S(1)} %bitcast.25, bf16[64,2176]{1,0:T(8,128)(2,1)S(1)} %collective-permute-done.far, bf16[768,2048]{1,0:T(8,128)(2,1)S(1)} %bitcast.13, bf16[768,2048]{1,0:T(8,128)(2,1)S(1)} %bitcast.15), custom_call_target="tpu_custom_call" | custom-call | flops 805306368 | bytes 6291456 | tf_op jit(solution)/shard_map/pallas_call | solution.py:114
  22.7 0.2 collective-permute-start.1
  22.9 1.4 %collective-permute-done.1 = bf16[64,2048]{1,0:T(8,128)(2,1)S(1)} collective-permute-done((bf16[64,2048]{1,0:T(8,128)(2,1)S(1)}, bf16[64,2048]{1,0:T(8,128)(2,1)S(1)}, u32[]{:S(2)}, u32[]{:S(2)}) %collective-permute-start.1) | collective-permute-done | bytes 262176 | tf_op jit(solution)/shard_map/ppermute | solution.py:141
  24.4 11.9 %all_to_all.21.returned = bf16[8,8,2048]{2,1,0:T(8,128)(2,1)S(1)} all-to-all(bf16[8,8,2048]{2,1,0:T(8,128)(2,1)S(1)} %fusion), channel_id=1, replica_groups={{0,2,4,6,8,10,12,14},{1,3,5,7,9,11,13,15},{16,18,20,22,24,26,28,30},{17..., dimensions={0} | all-to-all | bytes 524288 | tf_op jit(solution)/shard_map/all_to_all | solution.py:134
  36.3 0.7 shard_map.94
  37.0 13.5 %all_to_all.22 = bf16[8,8,2176]{2,1,0:T(8,128)(2,1)S(1)} all-to-all(bf16[8,8,2176]{2,1,0:T(8,128)(2,1)S(1)} %get-tuple-element.18), channel_id=1, replica_groups={{0,2,4,6,8,10,12,14},{1,3,5,7,9,11,13,15},{16,18,20,22,24,26,28,30},{17..., dimensions={0} | all-to-all | bytes 557056 | tf_op jit(solution)/shard_map/all_to_all | solution.py:134
  50.5 1.5 %collective-permute-start.3 = (bf16[64,2176]{1,0:T(8,128)(2,1)S(1)}, bf16[64,2176]{1,0:T(8,128)(2,1)S(1)}, u32[]{:S(2)}, u32[]{:S(2)}) collective-permute-start(bf16[64,2176]{1,0:T(8,128)(2,1)S(1)} %bitcast.22), channel_id=1, source_target_pairs={{0,16},{16,0},{1,17},{17,1},{2,18},{18,2},{3,19},{19,3},{4,20},{20... | collective-permute-start | bytes 835592 | tf_op jit(solution)/shard_map/ppermute | solution.py:141
  52.1 2.9 %shard_map.95 = (f32[64,2048]{1,0:T(8,128)S(1)}, bf16[64,2048]{1,0:T(8,128)(2,1)S(1)}) custom-call(bf16[64,2176]{1,0:T(8,128)(2,1)S(1)} %bitcast.23, bf16[64,2176]{1,0:T(8,128)(2,1)S(1)} %collective-permute-done.2.far, bf16[768,2048]{1,0:T(8,128)(2,1)S(1)} %bitcast.14, bf16[768,2048]{1,0:T(8,128)(2,1)S(1)} %bitcast.16, bf16[384,2048]{1,0:T(8,128)(2,1)S(1)} %bitcast.17, ...), custom_call_target="tpu_custom_call" | custom-call | flops 1207959552 | bytes 9437184 | tf_op jit(solution)/shard_map/pallas_call | solution.py:114
  55.0 4.6 %collective-permute-done.3.near = bf16[64,2176]{1,0:T(8,128)(2,1)S(1)} collective-permute-done((bf16[64,2176]{1,0:T(8,128)(2,1)S(1)}, bf16[64,2176]{1,0:T(8,128)(2,1)S(1)}, u32[]{:S(2)}, u32[]{:S(2)}) %collective-permute-start.3) | collective-permute-done | bytes 278560 | tf_op jit(solution)/shard_map/ppermute | solution.py:141
  59.6 1.6 %collective-permute-done.5.far = bf16[64,2176]{1,0:T(8,128)(2,1)S(1)} collective-permute-done((bf16[64,2176]{1,0:T(8,128)(2,1)S(1)}, bf16[64,2176]{1,0:T(8,128)(2,1)S(1)}, u32[]{:S(2)}, u32[]{:S(2)}) %collective-permute-start.5) | collective-permute-done | bytes 278560 | tf_op jit(solution)/shard_map/ppermute | solution.py:141
  61.1 1.2 %shard_map.96 = (f32[64,2048]{1,0:T(8,128)S(1)}, bf16[64,2048]{1,0:T(8,128)(2,1)S(1)}) custom-call(bf16[64,2176]{1,0:T(8,128)(2,1)S(1)} %collective-permute-done.3.near, bf16[64,2176]{1,0:T(8,128)(2,1)S(1)} %collective-permute-done.5.far, bf16[384,2048]{1,0:T(8,128)(2,1)S(1)} %bitcast.18, bf16[384,2048]{1,0:T(8,128)(2,1)S(1)} %bitcast.20), custom_call_target="tpu_custom_call" | custom-call | flops 402653184 | bytes 3145728 | tf_op jit(solution)/shard_map/pallas_call | solution.py:114
  62.4 0.2 collective-permute-start.6
  62.6 0.4 collective-permute-start.4
  63.0 1.0 %collective-permute-done.6 = bf16[64,2048]{1,0:T(8,128)(2,1)S(1)} collective-permute-done((bf16[64,2048]{1,0:T(8,128)(2,1)S(1)}, bf16[64,2048]{1,0:T(8,128)(2,1)S(1)}, u32[]{:S(2)}, u32[]{:S(2)}) %collective-permute-start.6) | collective-permute-done | bytes 262176 | tf_op jit(solution)/shard_map/ppermute | solution.py:141
  64.0 1.6 %collective-permute-start.7 = (bf16[64,2048]{1,0:T(8,128)(2,1)S(1)}, bf16[64,2048]{1,0:T(8,128)(2,1)S(1)}, u32[]{:S(2)}, u32[]{:S(2)}) collective-permute-start(bf16[64,2048]{1,0:T(8,128)(2,1)S(1)} %add_convert_fusion.1), channel_id=1, source_target_pairs={{0,16},{16,0},{1,17},{17,1},{2,18},{18,2},{3,19},{19,3},{4,20},{20... | collective-permute-start | bytes 786440 | tf_op jit(solution)/shard_map/ppermute | solution.py:141
  65.6 6.8 %collective-permute-done.7 = bf16[64,2048]{1,0:T(8,128)(2,1)S(1)} collective-permute-done((bf16[64,2048]{1,0:T(8,128)(2,1)S(1)}, bf16[64,2048]{1,0:T(8,128)(2,1)S(1)}, u32[]{:S(2)}, u32[]{:S(2)}) %collective-permute-start.7) | collective-permute-done | bytes 262176 | tf_op jit(solution)/shard_map/ppermute | solution.py:141
  72.5 11.1 %all_to_all.23.returned = bf16[8,8,2048]{2,1,0:T(8,128)(2,1)S(1)} all-to-all(bf16[8,8,2048]{2,1,0:T(8,128)(2,1)S(1)} %fusion.1), channel_id=1, replica_groups={{0,2,4,6,8,10,12,14},{1,3,5,7,9,11,13,15},{16,18,20,22,24,26,28,30},{17..., dimensions={0} | all-to-all | bytes 524288 | tf_op jit(solution)/shard_map/all_to_all | solution.py:134
  83.7 0.7 shard_map.97
  (26 shorter events, 0.3 us)
Async XLA Ops:
  0.0 0.8 copy-start.7
  0.8 0.7 copy-start.4
  0.8 0.7 copy-start.5
  0.8 0.7 copy-start.6
  0.8 19.8 %copy-start = (bf16[1,768,2048]{2,1,0:T(8,128)(2,1)S(1)}, bf16[1,768,2048]{2,1,0:T(8,128)(2,1)}, u32[]{:S(2)}) copy-start(bf16[1,768,2048]{2,1,0:T(8,128)(2,1)} %param.14) | copy-start | bytes 9437188
  0.8 19.8 %copy-start.1 = (bf16[1,768,2048]{2,1,0:T(8,128)(2,1)S(1)}, bf16[1,768,2048]{2,1,0:T(8,128)(2,1)}, u32[]{:S(2)}) copy-start(bf16[1,768,2048]{2,1,0:T(8,128)(2,1)} %param.15) | copy-start | bytes 9437188
  19.0 1.6 %collective-permute-start = (bf16[64,2176]{1,0:T(8,128)(2,1)S(1)}, bf16[64,2176]{1,0:T(8,128)(2,1)S(1)}, u32[]{:S(2)}, u32[]{:S(2)}) collective-permute-start(bf16[64,2176]{1,0:T(8,128)(2,1)S(1)} %bitcast.24), channel_id=1, source_target_pairs={{0,1},{1,0},{2,3},{3,2},{4,5},{5,4},{6,7},{7,6},{8,9},{9,8},{10,11... | collective-permute-start | bytes 835592 | tf_op jit(solution)/shard_map/ppermute | solution.py:141
  20.6 15.7 %copy-start.8 = (bf16[1,8,2048]{2,1,0:T(8,128)(2,1)S(1)}, bf16[1,8,2048]{2,1,0:T(8,128)(2,1)}, u32[]{:S(2)}) copy-start(bf16[1,8,2048]{2,1,0:T(8,128)(2,1)} %param.9) | copy-start | bytes 98308
  20.6 15.7 %copy-start.9 = (s32[1,4]{1,0:T(1,128)S(1)}, s32[1,4]{1,0:T(1,128)}, u32[]{:S(2)}) copy-start(s32[1,4]{1,0:T(1,128)} %changed.1) | copy-start | bytes 52
  22.7 1.6 %collective-permute-start.1 = (bf16[64,2048]{1,0:T(8,128)(2,1)S(1)}, bf16[64,2048]{1,0:T(8,128)(2,1)S(1)}, u32[]{:S(2)}, u32[]{:S(2)}) collective-permute-start(bf16[64,2048]{1,0:T(8,128)(2,1)S(1)} %get-tuple-element.16), channel_id=1, source_target_pairs={{0,1},{1,0},{2,3},{3,2},{4,5},{5,4},{6,7},{7,6},{8,9},{9,8},{10,11... | collective-permute-start | bytes 786440 | tf_op jit(solution)/shard_map/ppermute | solution.py:141
  36.3 15.8 %copy-start.2 = (bf16[1,384,2048]{2,1,0:T(8,128)(2,1)S(1)}, bf16[1,384,2048]{2,1,0:T(8,128)(2,1)}, u32[]{:S(2)}) copy-start(bf16[1,384,2048]{2,1,0:T(8,128)(2,1)} %param.16) | copy-start | bytes 4718596
  36.3 15.8 %copy-start.3 = (bf16[1,384,2048]{2,1,0:T(8,128)(2,1)S(1)}, bf16[1,384,2048]{2,1,0:T(8,128)(2,1)}, u32[]{:S(2)}) copy-start(bf16[1,384,2048]{2,1,0:T(8,128)(2,1)} %param.17) | copy-start | bytes 4718596
  50.5 1.6 %collective-permute-start.2 = (bf16[64,2176]{1,0:T(8,128)(2,1)S(1)}, bf16[64,2176]{1,0:T(8,128)(2,1)S(1)}, u32[]{:S(2)}, u32[]{:S(2)}) collective-permute-start(bf16[64,2176]{1,0:T(8,128)(2,1)S(1)} %bitcast.21), channel_id=1, source_target_pairs={{0,1},{1,0},{2,3},{3,2},{4,5},{5,4},{6,7},{7,6},{8,9},{9,8},{10,11... | collective-permute-start | bytes 835592 | tf_op jit(solution)/shard_map/ppermute | solution.py:141
  50.5 9.1 %collective-permute-start.3 = (bf16[64,2176]{1,0:T(8,128)(2,1)S(1)}, bf16[64,2176]{1,0:T(8,128)(2,1)S(1)}, u32[]{:S(2)}, u32[]{:S(2)}) collective-permute-start(bf16[64,2176]{1,0:T(8,128)(2,1)S(1)} %bitcast.22), channel_id=1, source_target_pairs={{0,16},{16,0},{1,17},{17,1},{2,18},{18,2},{3,19},{19,3},{4,20},{20... | collective-permute-start | bytes 835592 | tf_op jit(solution)/shard_map/ppermute | solution.py:141
  59.6 1.6 %collective-permute-start.5 = (bf16[64,2176]{1,0:T(8,128)(2,1)S(1)}, bf16[64,2176]{1,0:T(8,128)(2,1)S(1)}, u32[]{:S(2)}, u32[]{:S(2)}) collective-permute-start(bf16[64,2176]{1,0:T(8,128)(2,1)S(1)} %collective-permute-done.3.near), channel_id=1, source_target_pairs={{0,1},{1,0},{2,3},{3,2},{4,5},{5,4},{6,7},{7,6},{8,9},{9,8},{10,11... | collective-permute-start | bytes 835592 | tf_op jit(solution)/shard_map/ppermute | solution.py:141
  62.4 1.6 %collective-permute-start.6 = (bf16[64,2048]{1,0:T(8,128)(2,1)S(1)}, bf16[64,2048]{1,0:T(8,128)(2,1)S(1)}, u32[]{:S(2)}, u32[]{:S(2)}) collective-permute-start(bf16[64,2048]{1,0:T(8,128)(2,1)S(1)} %get-tuple-element.24), channel_id=1, source_target_pairs={{0,1},{1,0},{2,3},{3,2},{4,5},{5,4},{6,7},{7,6},{8,9},{9,8},{10,11... | collective-permute-start | bytes 786440 | tf_op jit(solution)/shard_map/ppermute | solution.py:141
  62.6 3.0 %collective-permute-start.4 = (bf16[64,2048]{1,0:T(8,128)(2,1)S(1)}, bf16[64,2048]{1,0:T(8,128)(2,1)S(1)}, u32[]{:S(2)}, u32[]{:S(2)}) collective-permute-start(bf16[64,2048]{1,0:T(8,128)(2,1)S(1)} %get-tuple-element.21), channel_id=1, source_target_pairs={{0,1},{1,0},{2,3},{3,2},{4,5},{5,4},{6,7},{7,6},{8,9},{9,8},{10,11... | collective-permute-start | bytes 786440 | tf_op jit(solution)/shard_map/ppermute | solution.py:141
  64.0 8.4 %collective-permute-start.7 = (bf16[64,2048]{1,0:T(8,128)(2,1)S(1)}, bf16[64,2048]{1,0:T(8,128)(2,1)S(1)}, u32[]{:S(2)}, u32[]{:S(2)}) collective-permute-start(bf16[64,2048]{1,0:T(8,128)(2,1)S(1)} %add_convert_fusion.1), channel_id=1, source_target_pairs={{0,16},{16,0},{1,17},{17,1},{2,18},{18,2},{3,19},{19,3},{4,20},{20... | collective-permute-start | bytes 786440 | tf_op jit(solution)/shard_map/ppermute | solution.py:141

commit v6 on v5

--- a/solution.py
+++ b/solution.py
@@ -65,9 +65,8 @@
     width = scaled.shape[1]
     normed = (scaled[...] * gain[...]).astype(jnp.bfloat16)
     table = weight_table(experts, routes[0, 0], scales[0, 0], [])
-    for j in range(out.shape[0]):
-        out[j, :, :width] = normed
-        out[j, :, width:] = table
+    out[:, :width] = normed
+    out[:, width:] = table
 
 
 def next_kernel(experts, step, previous, returned, gain, routes, scales, changed, state_out, out):
@@ -77,9 +76,8 @@
     normed = normalize(state, gain[...])
     items = [changed[0, i] for i in range(changed.shape[1])]
     table = weight_table(experts, routes[step, 0], scales[step, 0], items)
-    for j in range(out.shape[0]):
-        out[j, :, :width] = normed
-        out[j, :, width:] = table
+    out[:, :width] = normed
+    out[:, width:] = table
 
 
 def last_kernel(previous, returned, out):
@@ -136,6 +134,12 @@
     )
 
 
+def gather(block):
+    return lax.all_gather(
+        block, "expert", axis_index_groups=chip_groups(lax.axis_size("expert")), tiled=True
+    )
+
+
 def swap(value, axis):
     size = lax.axis_size(axis)
     return lax.ppermute(value, axis, [(i, i ^ 1) for i in range(size)])
@@ -146,9 +150,8 @@
     chips = experts // 2
     row_count, width = tokens.shape[1], tokens.shape[2]
     packed = width + table_width(experts)
-    half = chips * row_count
     gain = norm_gain[None]
-    blocks_shape = jax.ShapeDtypeStruct((chips, row_count, packed), jnp.bfloat16)
+    block_shape = jax.ShapeDtypeStruct((row_count, packed), jnp.bfloat16)
     state_shape = jax.ShapeDtypeStruct((row_count, width), jnp.float32)
     in_vmem = pl.BlockSpec(memory_space=pltpu.VMEM)
     in_smem = pl.BlockSpec(memory_space=pltpu.SMEM)
@@ -168,23 +171,23 @@
                 compiler_params=small,
                 cost_estimate=long,
             )(state)
-            blocks = pl.pallas_call(
+            block = pl.pallas_call(
                 functools.partial(pack_kernel, experts),
                 in_specs=[in_vmem] * 4,
                 out_specs=in_vmem,
-                out_shape=blocks_shape,
+                out_shape=block_shape,
                 compiler_params=small,
             )(scaled, gain, routes, route_scale)
         else:
-            state, blocks = pl.pallas_call(
+            state, block = pl.pallas_call(
                 functools.partial(next_kernel, experts, step),
                 in_specs=[in_vmem] * 5 + [in_smem],
                 out_specs=(in_vmem, in_vmem),
-                out_shape=(state_shape, blocks_shape),
+                out_shape=(state_shape, block_shape),
                 compiler_params=small,
                 cost_estimate=long,
             )(state, returned, gain, routes, route_scale, changed)
-        near = spread(blocks).reshape(half, packed)
+        near = gather(block)
         far = swap(near, "expert")
         if step == 0:
             near_share, far_share = run_mlp(near, far, stale, (False,))

time: 84.6 us -> 121 us (1.43)
  blocking collectives: 53.9 us -> 90.1 us
    all_gather x0 -> x2, blocking collectives: none -> 63.8 us  [gather(): lax.all_gather(block, 'expert', axis_index_groups=chip_groups(lax.axis_si...]
    all_to_all x4 -> x2, blocking collectives: 53.9 us -> 26.2 us  [spread(): lax.all_to_all(blocks, 'expert', 0, 0, axis_index_groups=chip_groups(lax....]
  transfers between devices with their start and end apart: 8 -> 8, of which waited for: 7 -> 7; matrix products, arithmetic and copies ran while one was open for 0% -> 0% of each run, Pallas kernels for 3% -> 2%
where the time goes in v6:
time: 121 us; the launch traced here: 120 us
  blocking collectives  90.1 us (74%)
  waiting for transfers between devices  17 us (14%)
  Pallas kernels  7.85 us (6%)
  starting transfers between devices  3.84 us (3%)
  local copies, waits for them, and re-layouts  1.39 us (1%)
    all_gather x2, blocking collectives, gather(): lax.all_gather(block, 'expert', axis_index_groups=chip_groups(lax.axis_si...  63.8 us
    all_to_all x2, blocking collectives, spread(): lax.all_to_all(blocks, 'expert', 0, 0, axis_index_groups=chip_groups(lax....  26.2 us
    ppermute x8, waiting for transfers between devices, swap(): return lax.ppermute(value, axis, [(i, i ^ 1) for i in range(size)])  17 us
    pallas_call x3, Pallas kernels, run_mlp(): pl.pallas_call(functools.partial(mlp_kernel, experts, fresh_flags), out_s...  6.3 us
    ppermute x8, starting transfers between devices, swap(): return lax.ppermute(value, axis, [(i, i ^ 1) for i in range(size)])  3.84 us
  transfers between devices with their start and end apart: 8, of which 7 were waited for; matrix products, arithmetic and copies ran while one was open for 0% of the time, Pallas kernels for 2%

profile of v6, /device:TPU:0, one launch (start us, length us, event | category | flops | bytes accessed | tf_op | source)
XLA Modules:
  0.0 120.4 jit_solution(5075257999440822623)
XLA Ops:
  0.0 0.8 copy-done.7
  0.8 0.1 shard_map.91.scaled
  0.9 0.6 copy-done.4
  1.5 0.1 shard_map.92
  1.6 32.7 %all_gather.6.near = bf16[64,2176]{1,0:T(8,128)(2,1)S(1)} all-gather(bf16[8,2176]{1,0:T(8,128)(2,1)S(1)} %shard_map.92), channel_id=1, replica_groups={{0,2,4,6,8,10,12,14},{1,3,5,7,9,11,13,15},{16,18,20,22,24,26,28,30},{17..., dimensions={0}, use_global_device_ids=true | all-gather | bytes 313344 | tf_op jit(solution)/shard_map/all_gather | solution.py:138
  34.3 1.6 %collective-permute-done.far = bf16[64,2176]{1,0:T(8,128)(2,1)S(1)} collective-permute-done((bf16[64,2176]{1,0:T(8,128)(2,1)S(1)}, bf16[64,2176]{1,0:T(8,128)(2,1)S(1)}, u32[]{:S(2)}, u32[]{:S(2)}) %collective-permute-start) | collective-permute-done | bytes 278560 | tf_op jit(solution)/shard_map/ppermute | solution.py:145
  35.9 2.1 %shard_map.93 = (f32[64,2048]{1,0:T(8,128)S(1)}, bf16[64,2048]{1,0:T(8,128)(2,1)S(1)}) custom-call(bf16[64,2176]{1,0:T(8,128)(2,1)S(1)} %all_gather.6.near, bf16[64,2176]{1,0:T(8,128)(2,1)S(1)} %collective-permute-done.far, bf16[768,2048]{1,0:T(8,128)(2,1)S(1)} %bitcast.11, bf16[768,2048]{1,0:T(8,128)(2,1)S(1)} %bitcast.13), custom_call_target="tpu_custom_call" | custom-call | flops 805306368 | bytes 6291456 | tf_op jit(solution)/shard_map/pallas_call | solution.py:112
  38.0 0.2 collective-permute-start.1
  38.2 1.4 %collective-permute-done.1 = bf16[64,2048]{1,0:T(8,128)(2,1)S(1)} collective-permute-done((bf16[64,2048]{1,0:T(8,128)(2,1)S(1)}, bf16[64,2048]{1,0:T(8,128)(2,1)S(1)}, u32[]{:S(2)}, u32[]{:S(2)}) %collective-permute-start.1) | collective-permute-done | bytes 262176 | tf_op jit(solution)/shard_map/ppermute | solution.py:145
  39.7 14.6 %all_to_all.10.returned = bf16[8,8,2048]{2,1,0:T(8,128)(2,1)S(1)} all-to-all(bf16[8,8,2048]{2,1,0:T(8,128)(2,1)S(1)} %fusion), channel_id=1, replica_groups={{0,2,4,6,8,10,12,14},{1,3,5,7,9,11,13,15},{16,18,20,22,24,26,28,30},{17..., dimensions={0} | all-to-all | bytes 524288 | tf_op jit(solution)/shard_map/all_to_all | solution.py:132
  54.2 0.7 shard_map.94
  54.9 31.2 %all_gather.7.near = bf16[64,2176]{1,0:T(8,128)(2,1)S(1)} all-gather(bf16[8,2176]{1,0:T(8,128)(2,1)S(1)} %get-tuple-element.18), channel_id=1, replica_groups={{0,2,4,6,8,10,12,14},{1,3,5,7,9,11,13,15},{16,18,20,22,24,26,28,30},{17..., dimensions={0}, use_global_device_ids=true | all-gather | bytes 313344 | tf_op jit(solution)/shard_map/all_gather | solution.py:138
  86.1 1.5 %collective-permute-start.3 = (bf16[64,2176]{1,0:T(8,128)(2,1)S(1)}, bf16[64,2176]{1,0:T(8,128)(2,1)S(1)}, u32[]{:S(2)}, u32[]{:S(2)}) collective-permute-start(bf16[64,2176]{1,0:T(8,128)(2,1)S(1)} %all_gather.7.near), channel_id=1, source_target_pairs={{0,16},{16,0},{1,17},{17,1},{2,18},{18,2},{3,19},{19,3},{4,20},{20... | collective-permute-start | bytes 835592 | tf_op jit(solution)/shard_map/ppermute | solution.py:145
  87.7 2.9 %shard_map.95 = (f32[64,2048]{1,0:T(8,128)S(1)}, bf16[64,2048]{1,0:T(8,128)(2,1)S(1)}) custom-call(bf16[64,2176]{1,0:T(8,128)(2,1)S(1)} %all_gather.7.near, bf16[64,2176]{1,0:T(8,128)(2,1)S(1)} %collective-permute-done.2.far, bf16[768,2048]{1,0:T(8,128)(2,1)S(1)} %bitcast.12, bf16[768,2048]{1,0:T(8,128)(2,1)S(1)} %bitcast.14, ...), custom_call_target="tpu_custom_call" | custom-call | flops 1207959552 | bytes 9437184 | tf_op jit(solution)/shard_map/pallas_call | solution.py:112
  90.6 4.6 %collective-permute-done.3.near = bf16[64,2176]{1,0:T(8,128)(2,1)S(1)} collective-permute-done((bf16[64,2176]{1,0:T(8,128)(2,1)S(1)}, bf16[64,2176]{1,0:T(8,128)(2,1)S(1)}, u32[]{:S(2)}, u32[]{:S(2)}) %collective-permute-start.3) | collective-permute-done | bytes 278560 | tf_op jit(solution)/shard_map/ppermute | solution.py:145
  95.2 1.6 %collective-permute-done.5.far = bf16[64,2176]{1,0:T(8,128)(2,1)S(1)} collective-permute-done((bf16[64,2176]{1,0:T(8,128)(2,1)S(1)}, bf16[64,2176]{1,0:T(8,128)(2,1)S(1)}, u32[]{:S(2)}, u32[]{:S(2)}) %collective-permute-start.5) | collective-permute-done | bytes 278560 | tf_op jit(solution)/shard_map/ppermute | solution.py:145
  96.7 1.2 %shard_map.96 = (f32[64,2048]{1,0:T(8,128)S(1)}, bf16[64,2048]{1,0:T(8,128)(2,1)S(1)}) custom-call(bf16[64,2176]{1,0:T(8,128)(2,1)S(1)} %collective-permute-done.3.near, bf16[64,2176]{1,0:T(8,128)(2,1)S(1)} %collective-permute-done.5.far, bf16[384,2048]{1,0:T(8,128)(2,1)S(1)} %bitcast.16, bf16[384,2048]{1,0:T(8,128)(2,1)S(1)} %bitcast.18), custom_call_target="tpu_custom_call" | custom-call | flops 402653184 | bytes 3145728 | tf_op jit(solution)/shard_map/pallas_call | solution.py:112
  98.0 0.2 collective-permute-start.6
  98.2 0.4 collective-permute-start.4
  98.6 1.0 collective-permute-done.6
  99.6 1.6 %collective-permute-start.7 = (bf16[64,2048]{1,0:T(8,128)(2,1)S(1)}, bf16[64,2048]{1,0:T(8,128)(2,1)S(1)}, u32[]{:S(2)}, u32[]{:S(2)}) collective-permute-start(bf16[64,2048]{1,0:T(8,128)(2,1)S(1)} %add_convert_fusion.1), channel_id=1, source_target_pairs={{0,16},{16,0},{1,17},{17,1},{2,18},{18,2},{3,19},{19,3},{4,20},{20... | collective-permute-start | bytes 786440 | tf_op jit(solution)/shard_map/ppermute | solution.py:145
  101.2 6.8 %collective-permute-done.7 = bf16[64,2048]{1,0:T(8,128)(2,1)S(1)} collective-permute-done((bf16[64,2048]{1,0:T(8,128)(2,1)S(1)}, bf16[64,2048]{1,0:T(8,128)(2,1)S(1)}, u32[]{:S(2)}, u32[]{:S(2)}) %collective-permute-start.7) | collective-permute-done | bytes 262176 | tf_op jit(solution)/shard_map/ppermute | solution.py:145
  108.1 11.7 %all_to_all.11.returned = bf16[8,8,2048]{2,1,0:T(8,128)(2,1)S(1)} all-to-all(bf16[8,8,2048]{2,1,0:T(8,128)(2,1)S(1)} %fusion.1), channel_id=1, replica_groups={{0,2,4,6,8,10,12,14},{1,3,5,7,9,11,13,15},{16,18,20,22,24,26,28,30},{17..., dimensions={0} | all-to-all | bytes 524288 | tf_op jit(solution)/shard_map/all_to_all | solution.py:132
  119.8 0.7 shard_map.97
  (26 shorter events, 0.3 us)
Async XLA Ops:
  0.0 0.8 copy-start.7
  0.8 0.7 copy-start.4
  0.8 0.7 copy-start.5
  0.8 0.7 copy-start.6
  0.8 35.1 %copy-start = (bf16[1,768,2048]{2,1,0:T(8,128)(2,1)S(1)}, bf16[1,768,2048]{2,1,0:T(8,128)(2,1)}, u32[]{:S(2)}) copy-start(bf16[1,768,2048]{2,1,0:T(8,128)(2,1)} %param.14) | copy-start | bytes 9437188
  0.8 35.1 %copy-start.1 = (bf16[1,768,2048]{2,1,0:T(8,128)(2,1)S(1)}, bf16[1,768,2048]{2,1,0:T(8,128)(2,1)}, u32[]{:S(2)}) copy-start(bf16[1,768,2048]{2,1,0:T(8,128)(2,1)} %param.15) | copy-start | bytes 9437188
  34.3 1.6 %collective-permute-start = (bf16[64,2176]{1,0:T(8,128)(2,1)S(1)}, bf16[64,2176]{1,0:T(8,128)(2,1)S(1)}, u32[]{:S(2)}, u32[]{:S(2)}) collective-permute-start(bf16[64,2176]{1,0:T(8,128)(2,1)S(1)} %all_gather.6.near), channel_id=1, source_target_pairs={{0,1},{1,0},{2,3},{3,2},{4,5},{5,4},{6,7},{7,6},{8,9},{9,8},{10,11... | collective-permute-start | bytes 835592 | tf_op jit(solution)/shard_map/ppermute | solution.py:145
  35.9 18.4 %copy-start.8 = (bf16[1,8,2048]{2,1,0:T(8,128)(2,1)S(1)}, bf16[1,8,2048]{2,1,0:T(8,128)(2,1)}, u32[]{:S(2)}) copy-start(bf16[1,8,2048]{2,1,0:T(8,128)(2,1)} %param.9) | copy-start | bytes 98308
  35.9 18.4 %copy-start.9 = (s32[1,4]{1,0:T(1,128)S(1)}, s32[1,4]{1,0:T(1,128)}, u32[]{:S(2)}) copy-start(s32[1,4]{1,0:T(1,128)} %changed.1) | copy-start | bytes 52
  38.0 1.6 %collective-permute-start.1 = (bf16[64,2048]{1,0:T(8,128)(2,1)S(1)}, bf16[64,2048]{1,0:T(8,128)(2,1)S(1)}, u32[]{:S(2)}, u32[]{:S(2)}) collective-permute-start(bf16[64,2048]{1,0:T(8,128)(2,1)S(1)} %get-tuple-element.16), channel_id=1, source_target_pairs={{0,1},{1,0},{2,3},{3,2},{4,5},{5,4},{6,7},{7,6},{8,9},{9,8},{10,11... | collective-permute-start | bytes 786440 | tf_op jit(solution)/shard_map/ppermute | solution.py:145
  54.2 33.4 %copy-start.2 = (bf16[1,384,2048]{2,1,0:T(8,128)(2,1)S(1)}, bf16[1,384,2048]{2,1,0:T(8,128)(2,1)}, u32[]{:S(2)}) copy-start(bf16[1,384,2048]{2,1,0:T(8,128)(2,1)} %param.16) | copy-start | bytes 4718596
  54.2 33.4 %copy-start.3 = (bf16[1,384,2048]{2,1,0:T(8,128)(2,1)S(1)}, bf16[1,384,2048]{2,1,0:T(8,128)(2,1)}, u32[]{:S(2)}) copy-start(bf16[1,384,2048]{2,1,0:T(8,128)(2,1)} %param.17) | copy-start | bytes 4718596
  86.1 1.6 %collective-permute-start.2 = (bf16[64,2176]{1,0:T(8,128)(2,1)S(1)}, bf16[64,2176]{1,0:T(8,128)(2,1)S(1)}, u32[]{:S(2)}, u32[]{:S(2)}) collective-permute-start(bf16[64,2176]{1,0:T(8,128)(2,1)S(1)} %all_gather.7.near), channel_id=1, source_target_pairs={{0,1},{1,0},{2,3},{3,2},{4,5},{5,4},{6,7},{7,6},{8,9},{9,8},{10,11... | collective-permute-start | bytes 835592 | tf_op jit(solution)/shard_map/ppermute | solution.py:145
  86.1 9.1 %collective-permute-start.3 = (bf16[64,2176]{1,0:T(8,128)(2,1)S(1)}, bf16[64,2176]{1,0:T(8,128)(2,1)S(1)}, u32[]{:S(2)}, u32[]{:S(2)}) collective-permute-start(bf16[64,2176]{1,0:T(8,128)(2,1)S(1)} %all_gather.7.near), channel_id=1, source_target_pairs={{0,16},{16,0},{1,17},{17,1},{2,18},{18,2},{3,19},{19,3},{4,20},{20... | collective-permute-start | bytes 835592 | tf_op jit(solution)/shard_map/ppermute | solution.py:145
  95.2 1.6 %collective-permute-start.5 = (bf16[64,2176]{1,0:T(8,128)(2,1)S(1)}, bf16[64,2176]{1,0:T(8,128)(2,1)S(1)}, u32[]{:S(2)}, u32[]{:S(2)}) collective-permute-start(bf16[64,2176]{1,0:T(8,128)(2,1)S(1)} %collective-permute-done.3.near), channel_id=1, source_target_pairs={{0,1},{1,0},{2,3},{3,2},{4,5},{5,4},{6,7},{7,6},{8,9},{9,8},{10,11... | collective-permute-start | bytes 835592 | tf_op jit(solution)/shard_map/ppermute | solution.py:145
  98.0 1.6 %collective-permute-start.6 = (bf16[64,2048]{1,0:T(8,128)(2,1)S(1)}, bf16[64,2048]{1,0:T(8,128)(2,1)S(1)}, u32[]{:S(2)}, u32[]{:S(2)}) collective-permute-start(bf16[64,2048]{1,0:T(8,128)(2,1)S(1)} %get-tuple-element.24), channel_id=1, source_target_pairs={{0,1},{1,0},{2,3},{3,2},{4,5},{5,4},{6,7},{7,6},{8,9},{9,8},{10,11... | collective-permute-start | bytes 786440 | tf_op jit(solution)/shard_map/ppermute | solution.py:145
  98.2 3.0 %collective-permute-start.4 = (bf16[64,2048]{1,0:T(8,128)(2,1)S(1)}, bf16[64,2048]{1,0:T(8,128)(2,1)S(1)}, u32[]{:S(2)}, u32[]{:S(2)}) collective-permute-start(bf16[64,2048]{1,0:T(8,128)(2,1)S(1)} %get-tuple-element.21), channel_id=1, source_target_pairs={{0,1},{1,0},{2,3},{3,2},{4,5},{5,4},{6,7},{7,6},{8,9},{9,8},{10,11... | collective-permute-start | bytes 786440 | tf_op jit(solution)/shard_map/ppermute | solution.py:145
  99.6 8.4 %collective-permute-start.7 = (bf16[64,2048]{1,0:T(8,128)(2,1)S(1)}, bf16[64,2048]{1,0:T(8,128)(2,1)S(1)}, u32[]{:S(2)}, u32[]{:S(2)}) collective-permute-start(bf16[64,2048]{1,0:T(8,128)(2,1)S(1)} %add_convert_fusion.1), channel_id=1, source_target_pairs={{0,16},{16,0},{1,17},{17,1},{2,18},{18,2},{3,19},{19,3},{4,20},{20... | collective-permute-start | bytes 786440 | tf_op jit(solution)/shard_map/ppermute | solution.py:145

commit v7 on v5

--- a/solution.py
+++ b/solution.py
@@ -47,8 +47,7 @@
     return jnp.where(section < 6, value, 0.0).astype(jnp.bfloat16)
 
 
-def row_weights(experts, table, fresh):
-    owner = lax.axis_index("expert")
+def row_weights(experts, table, owner, fresh):
     lane = lax.broadcasted_iota(jnp.int32, table.shape, 1)
     section = lane // experts
     first = 3 if fresh else 0
@@ -87,43 +86,41 @@
     out[...] = state.astype(jnp.bfloat16)
 
 
-def mlp_kernel(experts, fresh_flags, near, far, *refs):
-    near_out, far_out = refs[-2:]
-    half, width = near_out.shape
-    inputs = jnp.concatenate([near[:, :width], far[:, :width]], axis=0)
-    table = jnp.concatenate([near[:, width:], far[:, width:]], axis=0)
+def mlp_kernel(experts, fresh_flags, rows, *refs):
+    out = refs[-1]
+    width = out.shape[1]
+    inputs, table = rows[:, :width], rows[:, width:]
+    own = lax.axis_index("expert")
     total = None
     for i, fresh in enumerate(fresh_flags):
-        up, down = refs[2 * i : 2 * i + 2]
-        pre_act = lax.dot_general(
-            inputs, up[...], (((1,), (1,)), ((), ())), preferred_element_type=jnp.float32
-        )
-        hidden = (pre_act / (1.0 + jnp.exp(-pre_act))).astype(jnp.bfloat16)
-        result = jnp.dot(hidden, down[...], preferred_element_type=jnp.float32)
-        result = result * row_weights(experts, table, fresh)
-        total = result if total is None else total + result
-    near_out[...] = total[:half]
-    far_out[...] = total[half:].astype(jnp.bfloat16)
-
-
-def run_mlp(near, far, weights, fresh_flags):
-    experts = lax.axis_size("expert")
-    rows, width = near.shape[0], weights[0].shape[1]
+        for core in range(2):
+            up, down = refs[4 * i + 2 * core : 4 * i + 2 * core + 2]
+            owner = own if core == 0 else own + 1 - 2 * lax.rem(own, 2)
+            pre_act = lax.dot_general(
+                inputs, up[...], (((1,), (1,)), ((), ())), preferred_element_type=jnp.float32
+            )
+            hidden = (pre_act / (1.0 + jnp.exp(-pre_act))).astype(jnp.bfloat16)
+            result = jnp.dot(hidden, down[...], preferred_element_type=jnp.float32)
+            result = result * row_weights(experts, table, owner, fresh)
+            total = result if total is None else total + result
+    out[...] = total.astype(out.dtype)
+
+
+def run_mlp(rows, weights, fresh_flags, out_type):
+    experts = lax.axis_size("expert")
+    count, width = rows.shape[0], weights[0].shape[1]
     hidden = sum(part.shape[0] for part in weights) // 2
     in_vmem = pl.BlockSpec(memory_space=pltpu.VMEM)
     return pl.pallas_call(
         functools.partial(mlp_kernel, experts, fresh_flags),
-        out_shape=(
-            jax.ShapeDtypeStruct((rows, width), jnp.float32),
-            jax.ShapeDtypeStruct((rows, width), jnp.bfloat16),
+        out_shape=jax.ShapeDtypeStruct((count, width), out_type),
+        in_specs=[in_vmem] * (1 + len(weights)),
+        out_specs=in_vmem,
+        compiler_params=pltpu.CompilerParams(vmem_limit_bytes=16 * MIB),
+        cost_estimate=pl.CostEstimate(
+            flops=8 * count * hidden * width, bytes_accessed=4 * hidden * width, transcendentals=0
         ),
-        in_specs=[in_vmem] * (2 + len(weights)),
-        out_specs=(in_vmem, in_vmem),
-        compiler_params=pltpu.CompilerParams(vmem_limit_bytes=20 * MIB),
-        cost_estimate=pl.CostEstimate(
-            flops=8 * rows * hidden * width, bytes_accessed=4 * hidden * width, transcendentals=0
-        ),
-    )(near, far, *weights)
+    )(rows, *weights)
 
 
 def chip_groups(experts):
@@ -157,6 +154,8 @@
     long = pl.CostEstimate(
         flops=640 * weight_bytes, bytes_accessed=2 * weight_bytes, transcendentals=0
     )
+    stale = stale + tuple(swap(part, "expert") for part in stale)
+    learner = learner + tuple(swap(part, "expert") for part in learner)
     state = tokens[0]
     for step in range(routes.shape[0]):
         if step == 0:
@@ -184,20 +183,16 @@
                 compiler_params=small,
                 cost_estimate=long,
             )(state, returned, gain, routes, route_scale, changed)
-        near = spread(blocks).reshape(half, packed)
-        far = swap(near, "expert")
+        rows = spread(blocks).reshape(half, packed)
         if step == 0:
-            near_share, far_share = run_mlp(near, far, stale, (False,))
-            share = near_share + swap(far_share, "expert").astype(jnp.float32)
+            share = run_mlp(rows, stale, (False,), jnp.bfloat16)
         else:
-            other = swap(near, "group")
-            near_share, far_share = run_mlp(near, far, stale + learner, (False, True))
-            other, far_share = lax.optimization_barrier((other, far_share))
-            near_away, far_away = run_mlp(other, swap(other, "expert"), learner, (True,))
-            away = near_away + swap(far_away, "expert").astype(jnp.float32)
-            share = near_share + swap(far_share, "expert").astype(jnp.float32)
-            share = share + swap(away.astype(jnp.bfloat16), "group").astype(jnp.float32)
-        returned = spread(share.astype(jnp.bfloat16).reshape(chips, row_count, width))
+            other = swap(rows, "group")
+            share = run_mlp(rows, stale + learner, (False, True), jnp.float32)
+            other, share = lax.optimization_barrier((other, share))
+            away = run_mlp(other, learner, (True,), jnp.bfloat16)
+            share = (share + swap(away, "group").astype(jnp.float32)).astype(jnp.bfloat16)
+        returned = spread(share.reshape(chips, row_count, width))
     return pl.pallas_call(
         last_kernel,
         in_specs=[in_vmem] * 2,

time: 84.6 us -> 87.8 us (1.038)
  blocking collectives: 53.9 us -> 36.8 us
  Pallas kernels: 7.88 us -> 21.4 us
  starting transfers between devices: 3.84 us -> 10.4 us
  local copies, waits for them, and re-layouts: 1.39 us -> 3.97 us
  waiting for transfers between devices: 17 us -> 14.7 us
    all_to_all x4 -> x3, blocking collectives: 53.9 us -> 36.8 us  [spread(): lax.all_to_all(blocks, 'expert', 0, 0, axis_index_groups=chip_groups(lax....]
    pallas_call x3, Pallas kernels: 6.3 us -> 19.8 us  [run_mlp(): pl.pallas_call(functools.partial(mlp_kernel, experts, fresh_flags), out_s...]
    ppermute x8 -> x6, waiting for transfers between devices: 17 us -> 5.85 us  [swap(): return lax.ppermute(value, axis, [(i, i ^ 1) for i in range(size)])]
    all_to_all x0 -> x1, waiting for transfers between devices: none -> 8.88 us  [spread(): lax.all_to_all(blocks, 'expert', 0, 0, axis_index_groups=chip_groups(lax....]
    all_to_all x0 -> x1, starting transfers between devices: none -> 7.28 us  [spread(): lax.all_to_all(blocks, 'expert', 0, 0, axis_index_groups=chip_groups(lax....]
    unnamed x20 -> x22, local copies, waits for them, and re-layouts: 1.39 us -> 3.97 us
    ppermute x8 -> x6, starting transfers between devices: 3.84 us -> 3.1 us  [swap(): return lax.ppermute(value, axis, [(i, i ^ 1) for i in range(size)])]
  transfers between devices with their start and end apart: 8 -> 7, of which waited for: 7 -> 2; matrix products, arithmetic and copies ran while one was open for 0% -> 0% of each run, Pallas kernels for 3% -> 19%
where the time goes in v7:
time: 87.8 us; the launch traced here: 87.4 us
  blocking collectives  36.8 us (42%)
  Pallas kernels  21.4 us (24%)
  waiting for transfers between devices  14.7 us (17%)
  starting transfers between devices  10.4 us (12%)
  local copies, waits for them, and re-layouts  3.97 us (5%)
    all_to_all x3, blocking collectives, spread(): lax.all_to_all(blocks, 'expert', 0, 0, axis_index_groups=chip_groups(lax....  36.8 us
    pallas_call x3, Pallas kernels, run_mlp(): pl.pallas_call(functools.partial(mlp_kernel, experts, fresh_flags), out_s...  19.8 us
    all_to_all x1, waiting for transfers between devices, spread(): lax.all_to_all(blocks, 'expert', 0, 0, axis_index_groups=chip_groups(lax....  8.88 us
    all_to_all x1, starting transfers between devices, spread(): lax.all_to_all(blocks, 'expert', 0, 0, axis_index_groups=chip_groups(lax....  7.28 us
    ppermute x6, waiting for transfers between devices, swap(): return lax.ppermute(value, axis, [(i, i ^ 1) for i in range(size)])  5.85 us
    unnamed x22, local copies, waits for them, and re-layouts  3.97 us
    ppermute x6, starting transfers between devices, swap(): return lax.ppermute(value, axis, [(i, i ^ 1) for i in range(size)])  3.1 us
  transfers between devices with their start and end apart: 7, of which 2 were waited for; matrix products, arithmetic and copies ran while one was open for 0% of the time, Pallas kernels for 19%

profile of v7, /device:TPU:0, one launch (start us, length us, event | category | flops | bytes accessed | tf_op | source)
XLA Modules:
  0.0 87.4 jit_solution(13400037230520851666)
XLA Ops:
  0.0 0.5 collective-permute-start
  0.5 0.1 collective-permute-start.1
  0.5 0.8 copy-done.8
  1.3 0.1 shard_map.91.scaled
  1.4 0.6 copy-done.5
  2.0 0.0 copy-done.6
  2.0 0.0 copy-done.7
  2.0 0.1 shard_map.92
  2.1 0.7 copy-done.4
  2.8 7.3 %all-to-all-start = ((bf16[8,8,2176]{2,1,0:T(8,128)(2,1)}), bf16[8,8,2176]{2,1,0:T(8,128)(2,1)S(1)}, u32[]{:S(2)}, u32[]{:S(2)}) async-start(bf16[8,8,2176]{2,1,0:T(8,128)(2,1)} %copy-done.4), calls=%async_computation | async-start | bytes 557056 | tf_op jit(solution)/shard_map/all_to_all | solution.py:131
  10.1 0.5 collective-permute-start.4
  10.6 8.9 %all-to-all-done = bf16[8,8,2176]{2,1,0:T(8,128)(2,1)S(1)} async-done(((bf16[8,8,2176]{2,1,0:T(8,128)(2,1)}), bf16[8,8,2176]{2,1,0:T(8,128)(2,1)S(1)}, u32[]{:S(2)}, u32[]{:S(2)}) %all-to-all-start) | async-done | bytes 278560 | tf_op jit(solution)/shard_map/all_to_all | solution.py:131
  19.5 1.9 %copy-done.1 = bf16[1,768,2048]{2,1,0:T(8,128)(2,1)S(1)} copy-done((bf16[1,768,2048]{2,1,0:T(8,128)(2,1)S(1)}, bf16[1,768,2048]{2,1,0:T(8,128)(2,1)}, u32[]{:S(2)}) %copy-start.1) | copy-done | bytes 3145752
  21.4 6.5 %shard_map.93 = bf16[64,2048]{1,0:T(8,128)(2,1)S(1)} custom-call(bf16[64,2176]{1,0:T(8,128)(2,1)S(1)} %bitcast.24, bf16[768,2048]{1,0:T(8,128)(2,1)S(1)} %bitcast.13, bf16[768,2048]{1,0:T(8,128)(2,1)S(1)} %bitcast.16, bf16[768,2048]{1,0:T(8,128)(2,1)} %collective-permute-done.refs_2_, bf16[768,2048]{1,0:T(8,128)(2,1)} %collective-permute-done.1.refs_3_), custom_call_target="tpu_custom_call" | custom-call | flops 1610612736 | bytes 12582912 | tf_op jit(solution)/shard_map/pallas_call | solution.py:114
  27.8 12.0 %all_to_all.20.returned = bf16[8,8,2048]{2,1,0:T(8,128)(2,1)S(1)} all-to-all(bf16[8,8,2048]{2,1,0:T(8,128)(2,1)S(1)} %bitcast.27), channel_id=1, replica_groups={{0,2,4,6,8,10,12,14},{1,3,5,7,9,11,13,15},{16,18,20,22,24,26,28,30},{17..., dimensions={0} | all-to-all | bytes 524288 | tf_op jit(solution)/shard_map/all_to_all | solution.py:131
  39.8 0.7 shard_map.94
  40.6 13.1 %all_to_all.21 = bf16[8,8,2176]{2,1,0:T(8,128)(2,1)S(1)} all-to-all(bf16[8,8,2176]{2,1,0:T(8,128)(2,1)S(1)} %get-tuple-element.10), channel_id=1, replica_groups={{0,2,4,6,8,10,12,14},{1,3,5,7,9,11,13,15},{16,18,20,22,24,26,28,30},{17..., dimensions={0} | all-to-all | bytes 557056 | tf_op jit(solution)/shard_map/all_to_all | solution.py:131
  53.7 1.5 %collective-permute-start.2 = (bf16[64,2176]{1,0:T(8,128)(2,1)S(1)}, bf16[64,2176]{1,0:T(8,128)(2,1)S(1)}, u32[]{:S(2)}, u32[]{:S(2)}) collective-permute-start(bf16[64,2176]{1,0:T(8,128)(2,1)S(1)} %bitcast.25), channel_id=1, source_target_pairs={{0,16},{16,0},{1,17},{17,1},{2,18},{18,2},{3,19},{19,3},{4,20},{20... | collective-permute-start | bytes 835592 | tf_op jit(solution)/shard_map/ppermute | solution.py:138
  55.2 9.5 %shard_map.95 = f32[64,2048]{1,0:T(8,128)S(1)} custom-call(bf16[64,2176]{1,0:T(8,128)(2,1)S(1)} %bitcast.26, bf16[768,2048]{1,0:T(8,128)(2,1)S(1)} %bitcast.14, bf16[768,2048]{1,0:T(8,128)(2,1)S(1)} %bitcast.17, bf16[768,2048]{1,0:T(8,128)(2,1)} %collective-permute-done.refs_2_, bf16[768,2048]{1,0:T(8,128)(2,1)} %collective-permute-done.1.refs_3_, ...), custom_call_target="tpu_custom_call" | custom-call | flops 2415919104 | bytes 18874368 | tf_op jit(solution)/shard_map/pallas_call | solution.py:114
  64.6 3.9 %shard_map.96 = bf16[64,2048]{1,0:T(8,128)(2,1)S(1)} custom-call(bf16[64,2176]{1,0:T(8,128)(2,1)S(1)} %collective-permute-done.2.rows, bf16[384,2048]{1,0:T(8,128)(2,1)S(1)} %bitcast.20, bf16[384,2048]{1,0:T(8,128)(2,1)S(1)} %bitcast.23, bf16[384,2048]{1,0:T(8,128)(2,1)} %collective-permute-done.3.refs_6_.refs_2_, ...), custom_call_target="tpu_custom_call" | custom-call | flops 805306368 | bytes 6291456 | tf_op jit(solution)/shard_map/pallas_call | solution.py:114
  68.5 0.6 collective-permute-start.5
  69.1 5.8 %collective-permute-done.5 = bf16[64,2048]{1,0:T(8,128)(2,1)S(1)} collective-permute-done((bf16[64,2048]{1,0:T(8,128)(2,1)S(1)}, bf16[64,2048]{1,0:T(8,128)(2,1)S(1)}, u32[]{:S(2)}, u32[]{:S(2)}) %collective-permute-start.5) | collective-permute-done | bytes 262176 | tf_op jit(solution)/shard_map/ppermute | solution.py:138
  75.0 11.7 %all_to_all.22.returned = bf16[8,8,2048]{2,1,0:T(8,128)(2,1)S(1)} all-to-all(bf16[8,8,2048]{2,1,0:T(8,128)(2,1)S(1)} %fusion), channel_id=1, replica_groups={{0,2,4,6,8,10,12,14},{1,3,5,7,9,11,13,15},{16,18,20,22,24,26,28,30},{17..., dimensions={0} | all-to-all | bytes 524288 | tf_op jit(solution)/shard_map/all_to_all | solution.py:131
  86.7 0.7 shard_map.97
  (23 shorter events, 0.1 us)
Async XLA Ops:
  0.0 19.5 %collective-permute-start = (bf16[768,2048]{1,0:T(8,128)(2,1)}, bf16[768,2048]{1,0:T(8,128)(2,1)}, u32[]{:S(2)}, u32[]{:S(2)}) collective-permute-start(bf16[768,2048]{1,0:T(8,128)(2,1)} %bitcast.12), channel_id=1, source_target_pairs={{0,1},{1,0},{2,3},{3,2},{4,5},{5,4},{6,7},{7,6},{8,9},{9,8},{10,11... | collective-permute-start | bytes 9437192 | tf_op jit(solution)/shard_map/ppermute | solution.py:138
  0.5 19.0 %collective-permute-start.1 = (bf16[768,2048]{1,0:T(8,128)(2,1)}, bf16[768,2048]{1,0:T(8,128)(2,1)}, u32[]{:S(2)}, u32[]{:S(2)}) collective-permute-start(bf16[768,2048]{1,0:T(8,128)(2,1)} %bitcast.15), channel_id=1, source_target_pairs={{0,1},{1,0},{2,3},{3,2},{4,5},{5,4},{6,7},{7,6},{8,9},{9,8},{10,11... | collective-permute-start | bytes 9437192 | tf_op jit(solution)/shard_map/ppermute | solution.py:138
  0.5 0.8 copy-start.8
  1.3 0.7 copy-start.5
  1.3 0.7 copy-start.6
  1.3 0.7 copy-start.7
  1.3 18.2 %copy-start = (bf16[1,768,2048]{2,1,0:T(8,128)(2,1)S(1)}, bf16[1,768,2048]{2,1,0:T(8,128)(2,1)}, u32[]{:S(2)}) copy-start(bf16[1,768,2048]{2,1,0:T(8,128)(2,1)} %param.14) | copy-start | bytes 9437188
  2.1 0.7 copy-start.4
  2.8 16.7 %all-to-all-start = ((bf16[8,8,2176]{2,1,0:T(8,128)(2,1)}), bf16[8,8,2176]{2,1,0:T(8,128)(2,1)S(1)}, u32[]{:S(2)}, u32[]{:S(2)}) async-start(bf16[8,8,2176]{2,1,0:T(8,128)(2,1)} %copy-done.4), calls=%async_computation | async-start | bytes 557056 | tf_op jit(solution)/shard_map/all_to_all | solution.py:131
  10.1 45.1 %collective-permute-start.3 = (bf16[384,2048]{1,0:T(8,128)(2,1)}, bf16[384,2048]{1,0:T(8,128)(2,1)}, u32[]{:S(2)}, u32[]{:S(2)}) collective-permute-start(bf16[384,2048]{1,0:T(8,128)(2,1)} %bitcast.18), channel_id=1, source_target_pairs={{0,1},{1,0},{2,3},{3,2},{4,5},{5,4},{6,7},{7,6},{8,9},{9,8},{10,11... | collective-permute-start | bytes 4718600 | tf_op jit(solution)/shard_map/ppermute | solution.py:138
  10.1 45.1 %collective-permute-start.4 = (bf16[384,2048]{1,0:T(8,128)(2,1)}, bf16[384,2048]{1,0:T(8,128)(2,1)}, u32[]{:S(2)}, u32[]{:S(2)}) collective-permute-start(bf16[384,2048]{1,0:T(8,128)(2,1)} %bitcast.21), channel_id=1, source_target_pairs={{0,1},{1,0},{2,3},{3,2},{4,5},{5,4},{6,7},{7,6},{8,9},{9,8},{10,11... | collective-permute-start | bytes 4718600 | tf_op jit(solution)/shard_map/ppermute | solution.py:138
  19.5 1.9 %copy-start.1 = (bf16[1,768,2048]{2,1,0:T(8,128)(2,1)S(1)}, bf16[1,768,2048]{2,1,0:T(8,128)(2,1)}, u32[]{:S(2)}) copy-start(bf16[1,768,2048]{2,1,0:T(8,128)(2,1)} %param.15) | copy-start | bytes 9437188
  21.4 18.4 %copy-start.9 = (bf16[1,8,2048]{2,1,0:T(8,128)(2,1)S(1)}, bf16[1,8,2048]{2,1,0:T(8,128)(2,1)}, u32[]{:S(2)}) copy-start(bf16[1,8,2048]{2,1,0:T(8,128)(2,1)} %param.9) | copy-start | bytes 98308
  21.4 18.4 %copy-start.10 = (s32[1,4]{1,0:T(1,128)S(1)}, s32[1,4]{1,0:T(1,128)}, u32[]{:S(2)}) copy-start(s32[1,4]{1,0:T(1,128)} %changed.1) | copy-start | bytes 52
  39.8 15.3 %copy-start.2 = (bf16[1,384,2048]{2,1,0:T(8,128)(2,1)S(1)}, bf16[1,384,2048]{2,1,0:T(8,128)(2,1)}, u32[]{:S(2)}) copy-start(bf16[1,384,2048]{2,1,0:T(8,128)(2,1)} %param.16) | copy-start | bytes 4718596
  39.8 15.3 %copy-start.3 = (bf16[1,384,2048]{2,1,0:T(8,128)(2,1)S(1)}, bf16[1,384,2048]{2,1,0:T(8,128)(2,1)}, u32[]{:S(2)}) copy-start(bf16[1,384,2048]{2,1,0:T(8,128)(2,1)} %param.17) | copy-start | bytes 4718596
  53.7 11.0 %collective-permute-start.2 = (bf16[64,2176]{1,0:T(8,128)(2,1)S(1)}, bf16[64,2176]{1,0:T(8,128)(2,1)S(1)}, u32[]{:S(2)}, u32[]{:S(2)}) collective-permute-start(bf16[64,2176]{1,0:T(8,128)(2,1)S(1)} %bitcast.25), channel_id=1, source_target_pairs={{0,16},{16,0},{1,17},{17,1},{2,18},{18,2},{3,19},{19,3},{4,20},{20... | collective-permute-start | bytes 835592 | tf_op jit(solution)/shard_map/ppermute | solution.py:138
  68.5 6.4 %collective-permute-start.5 = (bf16[64,2048]{1,0:T(8,128)(2,1)S(1)}, bf16[64,2048]{1,0:T(8,128)(2,1)S(1)}, u32[]{:S(2)}, u32[]{:S(2)}) collective-permute-start(bf16[64,2048]{1,0:T(8,128)(2,1)S(1)} %shard_map.96), channel_id=1, source_target_pairs={{0,16},{16,0},{1,17},{17,1},{2,18},{18,2},{3,19},{19,3},{4,20},{20... | collective-permute-start | bytes 786440 | tf_op jit(solution)/shard_map/ppermute | solution.py:138

commit v8 on v7

--- a/solution.py
+++ b/solution.py
@@ -7,6 +7,7 @@
 from jax.sharding import PartitionSpec as P
 
 LANES = 128
+MATMUL_ROWS = 128
 MIB = 1 << 20
 
 
@@ -86,41 +87,44 @@
     out[...] = state.astype(jnp.bfloat16)
 
 
-def mlp_kernel(experts, fresh_flags, rows, *refs):
-    out = refs[-1]
-    width = out.shape[1]
-    inputs, table = rows[:, :width], rows[:, width:]
+def mlp_kernel(experts, fresh, row_sets, *refs):
+    sources, refs = refs[:row_sets], refs[row_sets:]
+    weights, outs = refs[:4], refs[4:]
+    count, width = outs[0].shape
+    rows = jnp.concatenate([source[...] for source in sources], axis=0)
+    filled = jnp.concatenate([rows] * max(1, MATMUL_ROWS // rows.shape[0]), axis=0)
+    inputs, table = filled[:, :width], rows[:, width:]
     own = lax.axis_index("expert")
     total = None
-    for i, fresh in enumerate(fresh_flags):
-        for core in range(2):
-            up, down = refs[4 * i + 2 * core : 4 * i + 2 * core + 2]
-            owner = own if core == 0 else own + 1 - 2 * lax.rem(own, 2)
-            pre_act = lax.dot_general(
-                inputs, up[...], (((1,), (1,)), ((), ())), preferred_element_type=jnp.float32
-            )
-            hidden = (pre_act / (1.0 + jnp.exp(-pre_act))).astype(jnp.bfloat16)
-            result = jnp.dot(hidden, down[...], preferred_element_type=jnp.float32)
-            result = result * row_weights(experts, table, owner, fresh)
-            total = result if total is None else total + result
-    out[...] = total.astype(out.dtype)
-
-
-def run_mlp(rows, weights, fresh_flags, out_type):
-    experts = lax.axis_size("expert")
-    count, width = rows.shape[0], weights[0].shape[1]
+    for core in range(2):
+        up, down = weights[2 * core : 2 * core + 2]
+        owner = own if core == 0 else own + 1 - 2 * lax.rem(own, 2)
+        pre_act = lax.dot_general(
+            inputs, up[...], (((1,), (1,)), ((), ())), preferred_element_type=jnp.float32
+        )
+        hidden = (pre_act / (1.0 + jnp.exp(-pre_act))).astype(jnp.bfloat16)
+        result = jnp.dot(hidden, down[...], preferred_element_type=jnp.float32)
+        result = result[: rows.shape[0]] * row_weights(experts, table, owner, fresh)
+        total = result if total is None else total + result
+    for i, out in enumerate(outs):
+        out[...] = total[i * count : (i + 1) * count].astype(out.dtype)
+
+
+def run_mlp(row_sets, weights, fresh, out_types):
+    experts = lax.axis_size("expert")
+    count, width = row_sets[0].shape[0], weights[0].shape[1]
     hidden = sum(part.shape[0] for part in weights) // 2
     in_vmem = pl.BlockSpec(memory_space=pltpu.VMEM)
     return pl.pallas_call(
-        functools.partial(mlp_kernel, experts, fresh_flags),
-        out_shape=jax.ShapeDtypeStruct((count, width), out_type),
-        in_specs=[in_vmem] * (1 + len(weights)),
-        out_specs=in_vmem,
+        functools.partial(mlp_kernel, experts, fresh, len(row_sets)),
+        out_shape=[jax.ShapeDtypeStruct((count, width), out_type) for out_type in out_types],
+        in_specs=[in_vmem] * (len(row_sets) + len(weights)),
+        out_specs=[in_vmem] * len(out_types),
         compiler_params=pltpu.CompilerParams(vmem_limit_bytes=16 * MIB),
         cost_estimate=pl.CostEstimate(
             flops=8 * count * hidden * width, bytes_accessed=4 * hidden * width, transcendentals=0
         ),
-    )(rows, *weights)
+    )(*row_sets, *weights)
 
 
 def chip_groups(experts):
@@ -152,7 +156,7 @@
     small = pltpu.CompilerParams(vmem_limit_bytes=4 * MIB)
     weight_bytes = 2 * sum(part.size for part in stale + learner)
     long = pl.CostEstimate(
-        flops=640 * weight_bytes, bytes_accessed=2 * weight_bytes, transcendentals=0
+        flops=1280 * weight_bytes, bytes_accessed=2 * weight_bytes, transcendentals=0
     )
     stale = stale + tuple(swap(part, "expert") for part in stale)
     learner = learner + tuple(swap(part, "expert") for part in learner)
@@ -185,13 +189,14 @@
             )(state, returned, gain, routes, route_scale, changed)
         rows = spread(blocks).reshape(half, packed)
         if step == 0:
-            share = run_mlp(rows, stale, (False,), jnp.bfloat16)
+            (share,) = run_mlp([rows], stale, False, [jnp.bfloat16])
         else:
             other = swap(rows, "group")
-            share = run_mlp(rows, stale + learner, (False, True), jnp.float32)
-            other, share = lax.optimization_barrier((other, share))
-            away = run_mlp(other, learner, (True,), jnp.bfloat16)
-            share = (share + swap(away, "group").astype(jnp.float32)).astype(jnp.bfloat16)
+            (old,) = run_mlp([rows], stale, False, [jnp.float32])
+            other, old = lax.optimization_barrier((other, old))
+            new, away = run_mlp([rows, other], learner, True, [jnp.float32, jnp.bfloat16])
+            share = old + new + swap(away, "group").astype(jnp.float32)
+            share = share.astype(jnp.bfloat16)
         returned = spread(share.reshape(chips, row_count, width))
     return pl.pallas_call(
         last_kernel,

time: 87.8 us -> 80 us (0.911)
  Pallas kernels: 21.4 us -> 13.2 us
  blocking collectives: 36.8 us -> 43.1 us
  starting transfers between devices: 10.4 us -> 7.53 us
  local copies, waits for them, and re-layouts: 3.97 us -> 1.41 us
    pallas_call x3, Pallas kernels: 19.8 us -> 11.6 us  [run_mlp(): pl.pallas_call(functools.partial(mlp_kernel, experts, fresh, len(row_sets...]
    all_to_all x3, blocking collectives: 36.8 us -> 43.1 us  [spread(): lax.all_to_all(blocks, 'expert', 0, 0, axis_index_groups=chip_groups(lax....]
    all_to_all x1, starting transfers between devices: 7.28 us -> 3.41 us  [spread(): lax.all_to_all(blocks, 'expert', 0, 0, axis_index_groups=chip_groups(lax....]
    unnamed x22 -> x30, local copies, waits for them, and re-layouts: 3.97 us -> 1.41 us
    all_to_all x1, waiting for transfers between devices: 8.88 us -> 7.76 us  [spread(): lax.all_to_all(blocks, 'expert', 0, 0, axis_index_groups=chip_groups(lax....]
    ppermute x6, starting transfers between devices: 3.1 us -> 4.12 us  [swap(): return lax.ppermute(value, axis, [(i, i ^ 1) for i in range(size)])]
  transfers between devices with their start and end apart: 7 -> 7, of which waited for: 2 -> 3; matrix products, arithmetic and copies ran while one was open for 0% -> 0% of each run, Pallas kernels for 19% -> 5%
where the time goes in v8:
time: 80 us; the launch traced here: 79.6 us
  blocking collectives  43.1 us (54%)
  waiting for transfers between devices  14.2 us (18%)
  Pallas kernels  13.2 us (16%)
  starting transfers between devices  7.53 us (9%)
  local copies, waits for them, and re-layouts  1.41 us (2%)
    all_to_all x3, blocking collectives, spread(): lax.all_to_all(blocks, 'expert', 0, 0, axis_index_groups=chip_groups(lax....  43.1 us
    pallas_call x3, Pallas kernels, run_mlp(): pl.pallas_call(functools.partial(mlp_kernel, experts, fresh, len(row_sets...  11.6 us
    all_to_all x1, waiting for transfers between devices, spread(): lax.all_to_all(blocks, 'expert', 0, 0, axis_index_groups=chip_groups(lax....  7.76 us
    ppermute x6, waiting for transfers between devices, swap(): return lax.ppermute(value, axis, [(i, i ^ 1) for i in range(size)])  6.48 us
    ppermute x6, starting transfers between devices, swap(): return lax.ppermute(value, axis, [(i, i ^ 1) for i in range(size)])  4.12 us
    all_to_all x1, starting transfers between devices, spread(): lax.all_to_all(blocks, 'expert', 0, 0, axis_index_groups=chip_groups(lax....  3.41 us
  transfers between devices with their start and end apart: 7, of which 3 were waited for; matrix products, arithmetic and copies ran while one was open for 0% of the time, Pallas kernels for 5%

profile of v8, /device:TPU:0, one launch (start us, length us, event | category | flops | bytes accessed | tf_op | source)
XLA Modules:
  0.0 79.6 jit_solution(6824895351528413855)
XLA Ops:
  0.0 0.5 collective-permute-start
  0.5 0.1 collective-permute-start.1
  0.5 0.8 copy-done.12
  1.3 0.1 shard_map.91.scaled
  1.4 0.6 copy-done.9
  2.0 0.0 copy-done.10
  2.0 0.1 shard_map.92
  2.1 17.6 %all_to_all.20 = bf16[8,8,2176]{2,1,0:T(8,128)(2,1)S(1)} all-to-all(bf16[8,8,2176]{2,1,0:T(8,128)(2,1)S(1)} %shard_map.92), channel_id=1, replica_groups={{0,2,4,6,8,10,12,14},{1,3,5,7,9,11,13,15},{16,18,20,22,24,26,28,30},{17..., dimensions={0} | all-to-all | bytes 557056 | tf_op jit(solution)/shard_map/all_to_all | solution.py:135
  19.7 4.2 %shard_map.93 = bf16[64,2048]{1,0:T(8,128)(2,1)} custom-call(bf16[64,2176]{1,0:T(8,128)(2,1)S(1)} %bitcast.25, bf16[768,2048]{1,0:T(8,128)(2,1)S(1)} %bitcast.13, bf16[768,2048]{1,0:T(8,128)(2,1)S(1)} %bitcast.16, bf16[768,2048]{1,0:T(8,128)(2,1)S(1)} %collective-permute-done.refs_3_, bf16[768,2048]{1,0:T(8,128)(2,1)S(1)} %collective-permute-done.1.refs_4_), custom_call_target="tpu_custom_call" | custom-call | flops 1610612736 | bytes 12582912 | tf_op jit(solution)/shard_map/pallas_call | solution.py:118
  23.9 3.4 %all-to-all-start.1 = ((bf16[8,8,2048]{2,1,0:T(8,128)(2,1)}), bf16[8,8,2048]{2,1,0:T(8,128)(2,1)S(1)}, u32[]{:S(2)}, u32[]{:S(2)}) async-start(bf16[8,8,2048]{2,1,0:T(8,128)(2,1)} %bitcast.5), calls=%async_computation.1 | async-start | bytes 524288 | tf_op jit(solution)/shard_map/all_to_all | solution.py:135
  27.3 0.1 collective-permute-start.3
  27.4 0.5 collective-permute-start.4
  27.9 7.8 %all-to-all-done.1.returned = bf16[8,8,2048]{2,1,0:T(8,128)(2,1)S(1)} async-done(((bf16[8,8,2048]{2,1,0:T(8,128)(2,1)}), bf16[8,8,2048]{2,1,0:T(8,128)(2,1)S(1)}, u32[]{:S(2)}, u32[]{:S(2)}) %all-to-all-start.1) | async-done | bytes 262176 | tf_op jit(solution)/shard_map/all_to_all | solution.py:135
  35.7 0.7 shard_map.94
  36.4 13.1 %all_to_all.21 = bf16[8,8,2176]{2,1,0:T(8,128)(2,1)S(1)} all-to-all(bf16[8,8,2176]{2,1,0:T(8,128)(2,1)S(1)} %get-tuple-element.12), channel_id=1, replica_groups={{0,2,4,6,8,10,12,14},{1,3,5,7,9,11,13,15},{16,18,20,22,24,26,28,30},{17..., dimensions={0} | all-to-all | bytes 557056 | tf_op jit(solution)/shard_map/all_to_all | solution.py:135
  49.5 1.5 %collective-permute-start.2 = (bf16[64,2176]{1,0:T(8,128)(2,1)S(1)}, bf16[64,2176]{1,0:T(8,128)(2,1)S(1)}, u32[]{:S(2)}, u32[]{:S(2)}) collective-permute-start(bf16[64,2176]{1,0:T(8,128)(2,1)S(1)} %bitcast.18), channel_id=1, source_target_pairs={{0,16},{16,0},{1,17},{17,1},{2,18},{18,2},{3,19},{19,3},{4,20},{20... | collective-permute-start | bytes 835592 | tf_op jit(solution)/shard_map/ppermute | solution.py:142
  51.0 3.5 %shard_map.95 = f32[64,2048]{1,0:T(8,128)S(1)} custom-call(bf16[64,2176]{1,0:T(8,128)(2,1)S(1)} %bitcast.19, bf16[768,2048]{1,0:T(8,128)(2,1)S(1)} %bitcast.14, bf16[768,2048]{1,0:T(8,128)(2,1)S(1)} %bitcast.17, bf16[768,2048]{1,0:T(8,128)(2,1)S(1)} %copy-done.4, bf16[768,2048]{1,0:T(8,128)(2,1)S(1)} %copy-done.6), custom_call_target="tpu_custom_call" | custom-call | flops 1610612736 | bytes 12582912 | tf_op jit(solution)/shard_map/pallas_call | solution.py:118
  54.4 1.6 %collective-permute-done.2.refs_1_ = bf16[64,2176]{1,0:T(8,128)(2,1)S(1)} collective-permute-done((bf16[64,2176]{1,0:T(8,128)(2,1)S(1)}, bf16[64,2176]{1,0:T(8,128)(2,1)S(1)}, u32[]{:S(2)}, u32[]{:S(2)}) %collective-permute-start.2) | collective-permute-done | bytes 278560 | tf_op jit(solution)/shard_map/ppermute | solution.py:142
  56.0 4.0 %shard_map.96 = (f32[64,2048]{1,0:T(8,128)S(1)}, bf16[64,2048]{1,0:T(8,128)(2,1)S(1)}) custom-call(bf16[64,2176]{1,0:T(8,128)(2,1)S(1)} %bitcast.20, bf16[64,2176]{1,0:T(8,128)(2,1)S(1)} %collective-permute-done.2.refs_1_, bf16[384,2048]{1,0:T(8,128)(2,1)S(1)} %bitcast.22, bf16[384,2048]{1,0:T(8,128)(2,1)S(1)} %bitcast.24, ...), custom_call_target="tpu_custom_call" | custom-call | flops 805306368 | bytes 6291456 | tf_op jit(solution)/shard_map/pallas_call | solution.py:118
  60.0 1.6 %collective-permute-start.5 = (bf16[64,2048]{1,0:T(8,128)(2,1)S(1)}, bf16[64,2048]{1,0:T(8,128)(2,1)S(1)}, u32[]{:S(2)}, u32[]{:S(2)}) collective-permute-start(bf16[64,2048]{1,0:T(8,128)(2,1)S(1)} %get-tuple-element.16), channel_id=1, source_target_pairs={{0,16},{16,0},{1,17},{17,1},{2,18},{18,2},{3,19},{19,3},{4,20},{20... | collective-permute-start | bytes 786440 | tf_op jit(solution)/shard_map/ppermute | solution.py:142
  61.6 4.9 %collective-permute-done.5 = bf16[64,2048]{1,0:T(8,128)(2,1)S(1)} collective-permute-done((bf16[64,2048]{1,0:T(8,128)(2,1)S(1)}, bf16[64,2048]{1,0:T(8,128)(2,1)S(1)}, u32[]{:S(2)}, u32[]{:S(2)}) %collective-permute-start.5) | collective-permute-done | bytes 262176 | tf_op jit(solution)/shard_map/ppermute | solution.py:142
  66.5 0.1 fusion
  66.5 12.4 %all_to_all.22.returned = bf16[8,8,2048]{2,1,0:T(8,128)(2,1)S(1)} all-to-all(bf16[8,8,2048]{2,1,0:T(8,128)(2,1)S(1)} %fusion), channel_id=1, replica_groups={{0,2,4,6,8,10,12,14},{1,3,5,7,9,11,13,15},{16,18,20,22,24,26,28,30},{17..., dimensions={0} | all-to-all | bytes 524288 | tf_op jit(solution)/shard_map/all_to_all | solution.py:135
  79.0 0.7 shard_map.97
  (31 shorter events, 0.1 us)
Async XLA Ops:
  0.0 19.7 %collective-permute-start = (bf16[768,2048]{1,0:T(8,128)(2,1)}, bf16[768,2048]{1,0:T(8,128)(2,1)S(1)}, u32[]{:S(2)}, u32[]{:S(2)}) collective-permute-start(bf16[768,2048]{1,0:T(8,128)(2,1)} %bitcast.12), channel_id=1, source_target_pairs={{0,1},{1,0},{2,3},{3,2},{4,5},{5,4},{6,7},{7,6},{8,9},{9,8},{10,11... | collective-permute-start | bytes 9437192 | tf_op jit(solution)/shard_map/ppermute | solution.py:142
  0.5 19.2 %collective-permute-start.1 = (bf16[768,2048]{1,0:T(8,128)(2,1)}, bf16[768,2048]{1,0:T(8,128)(2,1)S(1)}, u32[]{:S(2)}, u32[]{:S(2)}) collective-permute-start(bf16[768,2048]{1,0:T(8,128)(2,1)} %bitcast.15), channel_id=1, source_target_pairs={{0,1},{1,0},{2,3},{3,2},{4,5},{5,4},{6,7},{7,6},{8,9},{9,8},{10,11... | collective-permute-start | bytes 9437192 | tf_op jit(solution)/shard_map/ppermute | solution.py:142
  0.5 0.8 copy-start.12
  1.3 0.7 copy-start.9
  1.3 0.7 copy-start.10
  1.3 0.7 copy-start.11
  1.3 18.4 %copy-start = (bf16[1,768,2048]{2,1,0:T(8,128)(2,1)S(1)}, bf16[1,768,2048]{2,1,0:T(8,128)(2,1)}, u32[]{:S(2)}) copy-start(bf16[1,768,2048]{2,1,0:T(8,128)(2,1)} %param.14) | copy-start | bytes 9437188
  1.3 18.4 %copy-start.1 = (bf16[1,768,2048]{2,1,0:T(8,128)(2,1)S(1)}, bf16[1,768,2048]{2,1,0:T(8,128)(2,1)}, u32[]{:S(2)}) copy-start(bf16[1,768,2048]{2,1,0:T(8,128)(2,1)} %param.15) | copy-start | bytes 9437188
  19.7 4.2 %copy-start.3 = (bf16[768,2048]{1,0:T(8,128)(2,1)}, bf16[768,2048]{1,0:T(8,128)(2,1)S(1)}, u32[]{:S(2)}) copy-start(bf16[768,2048]{1,0:T(8,128)(2,1)S(1)} %collective-permute-done.refs_3_) | copy-start | bytes 9437188
  19.7 4.2 %copy-start.5 = (bf16[768,2048]{1,0:T(8,128)(2,1)}, bf16[768,2048]{1,0:T(8,128)(2,1)S(1)}, u32[]{:S(2)}) copy-start(bf16[768,2048]{1,0:T(8,128)(2,1)S(1)} %collective-permute-done.1.refs_4_) | copy-start | bytes 9437188
  19.7 15.9 %copy-start.13 = (bf16[1,8,2048]{2,1,0:T(8,128)(2,1)S(1)}, bf16[1,8,2048]{2,1,0:T(8,128)(2,1)}, u32[]{:S(2)}) copy-start(bf16[1,8,2048]{2,1,0:T(8,128)(2,1)} %param.9) | copy-start | bytes 98308
  19.7 15.9 %copy-start.14 = (s32[1,4]{1,0:T(1,128)S(1)}, s32[1,4]{1,0:T(1,128)}, u32[]{:S(2)}) copy-start(s32[1,4]{1,0:T(1,128)} %changed.1) | copy-start | bytes 52
  23.9 11.8 %all-to-all-start.1 = ((bf16[8,8,2048]{2,1,0:T(8,128)(2,1)}), bf16[8,8,2048]{2,1,0:T(8,128)(2,1)S(1)}, u32[]{:S(2)}, u32[]{:S(2)}) async-start(bf16[8,8,2048]{2,1,0:T(8,128)(2,1)} %bitcast.5), calls=%async_computation.1 | async-start | bytes 524288 | tf_op jit(solution)/shard_map/all_to_all | solution.py:135
  27.3 28.7 %collective-permute-start.3 = (bf16[384,2048]{1,0:T(8,128)(2,1)}, bf16[384,2048]{1,0:T(8,128)(2,1)}, u32[]{:S(2)}, u32[]{:S(2)}) collective-permute-start(bf16[384,2048]{1,0:T(8,128)(2,1)} %bitcast.21), channel_id=1, source_target_pairs={{0,1},{1,0},{2,3},{3,2},{4,5},{5,4},{6,7},{7,6},{8,9},{9,8},{10,11... | collective-permute-start | bytes 4718600 | tf_op jit(solution)/shard_map/ppermute | solution.py:142
  27.4 28.6 %collective-permute-start.4 = (bf16[384,2048]{1,0:T(8,128)(2,1)}, bf16[384,2048]{1,0:T(8,128)(2,1)}, u32[]{:S(2)}, u32[]{:S(2)}) collective-permute-start(bf16[384,2048]{1,0:T(8,128)(2,1)} %bitcast.23), channel_id=1, source_target_pairs={{0,1},{1,0},{2,3},{3,2},{4,5},{5,4},{6,7},{7,6},{8,9},{9,8},{10,11... | collective-permute-start | bytes 4718600 | tf_op jit(solution)/shard_map/ppermute | solution.py:142
  35.7 15.3 %copy-start.2 = (bf16[1,768,2048]{2,1,0:T(8,128)(2,1)S(1)}, bf16[1,768,2048]{2,1,0:T(8,128)(2,1)}, u32[]{:S(2)}) copy-start(bf16[1,768,2048]{2,1,0:T(8,128)(2,1)} %param.15) | copy-start | bytes 9437188
  35.7 15.3 %copy-start.4 = (bf16[768,2048]{1,0:T(8,128)(2,1)S(1)}, bf16[768,2048]{1,0:T(8,128)(2,1)}, u32[]{:S(2)}) copy-start(bf16[768,2048]{1,0:T(8,128)(2,1)} %copy-done.3) | copy-start | bytes 9437188
  35.7 15.3 %copy-start.6 = (bf16[768,2048]{1,0:T(8,128)(2,1)S(1)}, bf16[768,2048]{1,0:T(8,128)(2,1)}, u32[]{:S(2)}) copy-start(bf16[768,2048]{1,0:T(8,128)(2,1)} %copy-done.5) | copy-start | bytes 9437188
  49.5 6.6 %copy-start.7 = (bf16[1,384,2048]{2,1,0:T(8,128)(2,1)S(1)}, bf16[1,384,2048]{2,1,0:T(8,128)(2,1)}, u32[]{:S(2)}) copy-start(bf16[1,384,2048]{2,1,0:T(8,128)(2,1)} %param.16) | copy-start | bytes 4718596
  49.5 6.6 %copy-start.8 = (bf16[1,384,2048]{2,1,0:T(8,128)(2,1)S(1)}, bf16[1,384,2048]{2,1,0:T(8,128)(2,1)}, u32[]{:S(2)}) copy-start(bf16[1,384,2048]{2,1,0:T(8,128)(2,1)} %param.17) | copy-start | bytes 4718596
  49.5 6.5 %collective-permute-start.2 = (bf16[64,2176]{1,0:T(8,128)(2,1)S(1)}, bf16[64,2176]{1,0:T(8,128)(2,1)S(1)}, u32[]{:S(2)}, u32[]{:S(2)}) collective-permute-start(bf16[64,2176]{1,0:T(8,128)(2,1)S(1)} %bitcast.18), channel_id=1, source_target_pairs={{0,16},{16,0},{1,17},{17,1},{2,18},{18,2},{3,19},{19,3},{4,20},{20... | collective-permute-start | bytes 835592 | tf_op jit(solution)/shard_map/ppermute | solution.py:142
  60.0 6.4 %collective-permute-start.5 = (bf16[64,2048]{1,0:T(8,128)(2,1)S(1)}, bf16[64,2048]{1,0:T(8,128)(2,1)S(1)}, u32[]{:S(2)}, u32[]{:S(2)}) collective-permute-start(bf16[64,2048]{1,0:T(8,128)(2,1)S(1)} %get-tuple-element.16), channel_id=1, source_target_pairs={{0,16},{16,0},{1,17},{17,1},{2,18},{18,2},{3,19},{19,3},{4,20},{20... | collective-permute-start | bytes 786440 | tf_op jit(solution)/shard_map/ppermute | solution.py:142

commit v9 on v8

--- a/solution.py
+++ b/solution.py
@@ -63,35 +63,46 @@
 
 def pack_kernel(experts, scaled, gain, routes, scales, out):
     width = scaled.shape[1]
-    normed = (scaled[...] * gain[...]).astype(jnp.bfloat16)
-    table = weight_table(experts, routes[0, 0], scales[0, 0], [])
-    for j in range(out.shape[0]):
-        out[j, :, :width] = normed
-        out[j, :, width:] = table
-
-
-def next_kernel(experts, step, previous, returned, gain, routes, scales, changed, state_out, out):
+    out[:, :width] = (scaled[...] * gain[...]).astype(jnp.bfloat16)
+    out[:, width:] = weight_table(experts, routes[0, 0], scales[0, 0], [])
+
+
+def next_kernel(experts, step, previous, kept, received, gain, routes, scales, changed, state_out, out):
     width = previous.shape[1]
-    state = previous[...].astype(jnp.float32) + jnp.sum(returned[...].astype(jnp.float32), axis=0)
+    state = previous[...].astype(jnp.float32) + (kept[...] + received[...].astype(jnp.float32))
     state_out[...] = state
-    normed = normalize(state, gain[...])
-    items = [changed[0, i] for i in range(changed.shape[1])]
-    table = weight_table(experts, routes[step, 0], scales[step, 0], items)
-    for j in range(out.shape[0]):
-        out[j, :, :width] = normed
-        out[j, :, width:] = table
-
-
-def last_kernel(previous, returned, out):
-    state = previous[...] + jnp.sum(returned[...].astype(jnp.float32), axis=0)
+    items = [changed[:, i : i + 1] for i in range(changed.shape[1])]
+    out[:, :width] = normalize(state, gain[...])
+    out[:, width:] = weight_table(experts, routes[step, 0], scales[step, 0], items)
+
+
+def last_kernel(previous, kept, received, out):
+    state = previous[...] + (kept[...] + received[...].astype(jnp.float32))
     out[...] = state.astype(jnp.bfloat16)
 
 
-def mlp_kernel(experts, fresh, row_sets, *refs):
-    sources, refs = refs[:row_sets], refs[row_sets:]
-    weights, outs = refs[:4], refs[4:]
-    count, width = outs[0].shape
+def join_kernel(first, second, out):
+    out[0] = first[...]
+    out[1] = second[...]
+
+
+def halve_kernel(kept, *refs):
+    received, (kept_out, sent_out) = refs[:-2], refs[-2:]
+    total = kept[...]
+    for part in received:
+        total = total + part[...].astype(jnp.float32)
+    count = kept_out.shape[0]
+    kept_out[...] = total[:count]
+    sent_out[...] = total[count:].astype(jnp.bfloat16)
+
+
+def mlp_kernel(experts, fresh, set_sizes, before, *refs):
+    refs = list(refs)
+    sources = [refs.pop(0) for _ in range(sum(set_sizes))]
+    weights = [refs.pop(0) for _ in range(4)]
+    earlier = refs.pop(0) if before else None
     rows = jnp.concatenate([source[...] for source in sources], axis=0)
+    width = refs[0].shape[1]
     filled = jnp.concatenate([rows] * max(1, MATMUL_ROWS // rows.shape[0]), axis=0)
     inputs, table = filled[:, :width], rows[:, width:]
     own = lax.axis_index("expert")
@@ -106,105 +117,140 @@
         result = jnp.dot(hidden, down[...], preferred_element_type=jnp.float32)
         result = result[: rows.shape[0]] * row_weights(experts, table, owner, fresh)
         total = result if total is None else total + result
-    for i, out in enumerate(outs):
-        out[...] = total[i * count : (i + 1) * count].astype(out.dtype)
-
-
-def run_mlp(row_sets, weights, fresh, out_types):
-    experts = lax.axis_size("expert")
-    count, width = row_sets[0].shape[0], weights[0].shape[1]
-    hidden = sum(part.shape[0] for part in weights) // 2
+    start = 0
+    for out in refs:
+        count = out.shape[0]
+        part = total[start : start + count]
+        if before and start < earlier.shape[0]:
+            part = part + earlier[start : start + count]
+        out[...] = part.astype(out.dtype)
+        start = start + count
+
+
+def on_vmem(kernel, inputs, outputs, limit=2 * MIB, cost=None):
     in_vmem = pl.BlockSpec(memory_space=pltpu.VMEM)
     return pl.pallas_call(
-        functools.partial(mlp_kernel, experts, fresh, len(row_sets)),
-        out_shape=[jax.ShapeDtypeStruct((count, width), out_type) for out_type in out_types],
-        in_specs=[in_vmem] * (len(row_sets) + len(weights)),
-        out_specs=[in_vmem] * len(out_types),
-        compiler_params=pltpu.CompilerParams(vmem_limit_bytes=16 * MIB),
-        cost_estimate=pl.CostEstimate(
-            flops=8 * count * hidden * width, bytes_accessed=4 * hidden * width, transcendentals=0
-        ),
-    )(*row_sets, *weights)
-
-
-def chip_groups(experts):
-    return [list(range(core, experts, 2)) for core in range(2)]
-
-
-def spread(blocks):
-    return lax.all_to_all(
-        blocks, "expert", 0, 0, axis_index_groups=chip_groups(lax.axis_size("expert")), tiled=True
-    )
-
-
-def swap(value, axis):
+        kernel,
+        out_shape=[jax.ShapeDtypeStruct(shape, kind) for shape, kind in outputs],
+        in_specs=[in_vmem] * len(inputs),
+        out_specs=[in_vmem] * len(outputs),
+        compiler_params=pltpu.CompilerParams(vmem_limit_bytes=limit),
+        cost_estimate=cost,
+    )(*inputs)
+
+
+def run_mlp(row_sets, weights, fresh, outputs, before=()):
+    width = weights[0].shape[1]
+    count = sum(part.shape[0] for rows in row_sets for part in rows)
+    hidden = sum(part.shape[0] for part in weights) // 2
+    kernel = functools.partial(
+        mlp_kernel,
+        lax.axis_size("expert"),
+        fresh,
+        [len(rows) for rows in row_sets],
+        len(before) > 0,
+    )
+    cost = pl.CostEstimate(
+        flops=8 * count * hidden * width, bytes_accessed=4 * hidden * width, transcendentals=0
+    )
+    inputs = [part for rows in row_sets for part in rows] + list(weights) + list(before)
+    outputs = [((rows, width), kind) for rows, kind in outputs]
+    return on_vmem(kernel, inputs, outputs, 8 * MIB, cost)
+
+
+def swap(value, axis, distance):
     size = lax.axis_size(axis)
-    return lax.ppermute(value, axis, [(i, i ^ 1) for i in range(size)])
+    return lax.ppermute(value, axis, [(i, i ^ distance) for i in range(size)])
+
+
+def swap_core(value):
+    return swap(value, "expert", 1)
+
+
+def swap_group(value):
+    return swap(value, "group", 1)
+
+
+def chip_distances():
+    distances = [2]
+    while 2 * distances[-1] < lax.axis_size("expert"):
+        distances.append(2 * distances[-1])
+    return distances
+
+
+def gather(block):
+    for distance in reversed(chip_distances()[1:]):
+        rows, width = block.shape
+        joined = ((2, rows, width), block.dtype)
+        (block,) = on_vmem(join_kernel, (block, swap(block, "expert", distance)), [joined])
+        block = block.reshape(2 * rows, width)
+    return block
+
+
+def halve(kept, *received):
+    rows, width = kept.shape
+    half = (rows // 2, width)
+    return on_vmem(
+        halve_kernel, (kept,) + received, [(half, jnp.float32), (half, jnp.bfloat16)], 4 * MIB
+    )
+
+
+def give_back(kept, *received):
+    for distance in chip_distances()[1:]:
+        kept, sent = halve(kept, *received)
+        received = (swap(sent, "expert", distance),)
+    return kept, received[0]
 
 
 def exchange_plan(tokens, norm_gain, routes, route_scale, changed, stale, learner):
     experts = lax.axis_size("expert")
-    chips = experts // 2
     row_count, width = tokens.shape[1], tokens.shape[2]
-    packed = width + table_width(experts)
-    half = chips * row_count
+    line = experts // 4 * row_count
+    near = chip_distances()[0]
     gain = norm_gain[None]
-    blocks_shape = jax.ShapeDtypeStruct((chips, row_count, packed), jnp.bfloat16)
-    state_shape = jax.ShapeDtypeStruct((row_count, width), jnp.float32)
-    in_vmem = pl.BlockSpec(memory_space=pltpu.VMEM)
-    in_smem = pl.BlockSpec(memory_space=pltpu.SMEM)
-    small = pltpu.CompilerParams(vmem_limit_bytes=4 * MIB)
+    block_shape = ((row_count, width + table_width(experts)), jnp.bfloat16)
+    state_shape = ((row_count, width), jnp.float32)
     weight_bytes = 2 * sum(part.size for part in stale + learner)
     long = pl.CostEstimate(
         flops=1280 * weight_bytes, bytes_accessed=2 * weight_bytes, transcendentals=0
     )
-    stale = stale + tuple(swap(part, "expert") for part in stale)
-    learner = learner + tuple(swap(part, "expert") for part in learner)
+    stale = stale + tuple(swap_core(part) for part in stale)
+    learner = learner + tuple(swap_core(part) for part in learner)
     state = tokens[0]
     for step in range(routes.shape[0]):
         if step == 0:
-            scaled = pl.pallas_call(
-                first_kernel,
-                in_specs=[in_vmem],
-                out_specs=in_vmem,
-                out_shape=state_shape,
-                compiler_params=small,
-                cost_estimate=long,
-            )(state)
-            blocks = pl.pallas_call(
+            (scaled,) = on_vmem(first_kernel, (state,), [state_shape], cost=long)
+            (block,) = on_vmem(
                 functools.partial(pack_kernel, experts),
-                in_specs=[in_vmem] * 4,
-                out_specs=in_vmem,
-                out_shape=blocks_shape,
-                compiler_params=small,
-            )(scaled, gain, routes, route_scale)
+                (scaled, gain, routes, route_scale),
+                [block_shape],
+            )
         else:
-            state, blocks = pl.pallas_call(
+            state, block = on_vmem(
                 functools.partial(next_kernel, experts, step),
-                in_specs=[in_vmem] * 5 + [in_smem],
-                out_specs=(in_vmem, in_vmem),
-                out_shape=(state_shape, blocks_shape),
-                compiler_params=small,
-                cost_estimate=long,
-            )(state, returned, gain, routes, route_scale, changed)
-        rows = spread(blocks).reshape(half, packed)
+                (state, kept, received, gain, routes, route_scale, changed),
+                [state_shape, block_shape],
+            )
+        rows = gather(block)
+        across = swap(rows, "expert", near)
+        mine = [(line, jnp.float32), (line, jnp.bfloat16)]
         if step == 0:
-            (share,) = run_mlp([rows], stale, False, [jnp.bfloat16])
+            kept, sent = run_mlp([(rows, across)], stale, False, mine)
+            kept, received = give_back(kept, swap(sent, "expert", near))
         else:
-            other = swap(rows, "group")
-            (old,) = run_mlp([rows], stale, False, [jnp.float32])
-            other, old = lax.optimization_barrier((other, old))
-            new, away = run_mlp([rows, other], learner, True, [jnp.float32, jnp.bfloat16])
-            share = old + new + swap(away, "group").astype(jnp.float32)
-            share = share.astype(jnp.bfloat16)
-        returned = spread(share.reshape(chips, row_count, width))
-    return pl.pallas_call(
-        last_kernel,
-        in_specs=[in_vmem] * 2,
-        out_specs=in_vmem,
-        out_shape=jax.ShapeDtypeStruct((row_count, width), jnp.bfloat16),
-        compiler_params=small,
-    )(state, returned)[None]
+            other, other_across = swap_group(rows), swap_group(across)
+            (old,) = run_mlp([(rows, across)], stale, False, [(2 * line, jnp.float32)])
+            other_across, old = lax.optimization_barrier((other_across, old))
+            kept, sent, away_kept, away_sent = run_mlp(
+                [(rows, across), (other, other_across)], learner, True, mine + mine, (old,)
+            )
+            away = away_kept + swap(away_sent, "expert", near).astype(jnp.float32)
+            away = swap_group(away.astype(jnp.bfloat16))
+            kept, received = give_back(kept, swap(sent, "expert", near), away)
+    (updated,) = on_vmem(
+        last_kernel, (state, kept, received), [((row_count, width), jnp.bfloat16)]
+    )
+    return updated[None]
 
 
 def gather_plan(tokens, norm_gain, routes, route_scale, changed, stale, learner):
@@ -258,7 +304,7 @@
     experts = lax.axis_size("expert")
     groups = lax.axis_size("group")
     fewer = tokens.shape[1] * experts < learner_up.shape[1]
-    paired = experts % 2 == 0 and groups == 2 and routes.shape[0] == 2
+    paired = experts & (experts - 1) == 0 and experts >= 8 and groups == 2
     plan = exchange_plan if fewer and paired else gather_plan
     stale = (rollout_up[0], rollout_down[0])
     learner = (learner_up[0], learner_down[0])

time: 80 us -> 80.2 us (level)
  blocking collectives: 43.1 us -> 0 us
  starting transfers between devices: 7.53 us -> 33.7 us
  waiting for transfers between devices: 14.2 us -> 34.6 us
  Pallas kernels: 13.2 us -> 10.1 us
    all_to_all x3 -> x0, blocking collectives: 43.1 us -> none  [spread(): lax.all_to_all(blocks, 'expert', 0, 0, axis_index_groups=chip_groups(lax....]
    ppermute x6 -> x20, starting transfers between devices: 4.12 us -> 33.7 us  [swap(): return lax.ppermute(value, axis, [(i, i ^ distance) for i in range(size)])]
    ppermute x6 -> x20, waiting for transfers between devices: 6.48 us -> 34.6 us  [swap(): return lax.ppermute(value, axis, [(i, i ^ distance) for i in range(size)])]
    all_to_all x1 -> x0, waiting for transfers between devices: 7.76 us -> none  [spread(): lax.all_to_all(blocks, 'expert', 0, 0, axis_index_groups=chip_groups(lax....]
    all_to_all x1 -> x0, starting transfers between devices: 3.41 us -> none  [spread(): lax.all_to_all(blocks, 'expert', 0, 0, axis_index_groups=chip_groups(lax....]
    pallas_call x7 -> x15, Pallas kernels: 13.2 us -> 10.1 us  [on_vmem(): pl.pallas_call(kernel, out_shape=[jax.ShapeDtypeStruct(shape, kind) for s...]
  transfers between devices with their start and end apart: 7 -> 20, of which waited for: 3 -> 14; matrix products, arithmetic and copies ran while one was open for 0% -> 0% of each run, Pallas kernels for 5% -> 9%
where the time goes in v9:
time: 80.2 us; the launch traced here: 80 us
  waiting for transfers between devices  34.6 us (43%)
  starting transfers between devices  33.7 us (42%)
  Pallas kernels  10.1 us (13%)
  local copies, waits for them, and re-layouts  1.4 us (2%)
    ppermute x20, waiting for transfers between devices, swap(): return lax.ppermute(value, axis, [(i, i ^ distance) for i in range(size)])  34.6 us
    ppermute x20, starting transfers between devices, swap(): return lax.ppermute(value, axis, [(i, i ^ distance) for i in range(size)])  33.7 us
    pallas_call x15, Pallas kernels, on_vmem(): pl.pallas_call(kernel, out_shape=[jax.ShapeDtypeStruct(shape, kind) for s...  10.1 us
  transfers between devices with their start and end apart: 20, of which 14 were waited for; matrix products, arithmetic and copies ran while one was open for 0% of the time, Pallas kernels for 9%

profile of v9, /device:TPU:0, one launch (start us, length us, event | category | flops | bytes accessed | tf_op | source)
XLA Modules:
  0.0 80.0 jit_solution(7223893924019998959)
XLA Ops:
  2.6 4.1 %collective-permute-start = (bf16[8,2176]{1,0:T(8,128)(2,1)S(1)}, bf16[8,2176]{1,0:T(8,128)(2,1)S(1)}, u32[]{:S(2)}, u32[]{:S(2)}) collective-permute-start(bf16[8,2176]{1,0:T(8,128)(2,1)S(1)} %shard_map.92.first), channel_id=1, source_target_pairs={{0,8},{1,9},{2,10},{3,11},{4,12},{5,13},{6,14},{7,15},{8,0},{9,1},... | collective-permute-start | bytes 104456 | tf_op jit(solution)/shard_map/ppermute | solution.py:163
  6.7 1.9 %collective-permute-done.second = bf16[8,2176]{1,0:T(8,128)(2,1)S(1)} collective-permute-done((bf16[8,2176]{1,0:T(8,128)(2,1)S(1)}, bf16[8,2176]{1,0:T(8,128)(2,1)S(1)}, u32[]{:S(2)}, u32[]{:S(2)}) %collective-permute-start) | collective-permute-done | bytes 34848 | tf_op jit(solution)/shard_map/ppermute | solution.py:163
  10.5 2.4 %collective-permute-done.1.second = bf16[16,2176]{1,0:T(8,128)(2,1)S(1)} collective-permute-done((bf16[16,2176]{1,0:T(8,128)(2,1)S(1)}, bf16[16,2176]{1,0:T(8,128)(2,1)S(1)}, u32[]{:S(2)}, u32[]{:S(2)}) %collective-permute-start.1) | collective-permute-done | bytes 69664 | tf_op jit(solution)/shard_map/ppermute | solution.py:163
  13.0 2.3 %collective-permute-start.2 = (bf16[32,2176]{1,0:T(8,128)(2,1)S(1)}, bf16[32,2176]{1,0:T(8,128)(2,1)S(1)}, u32[]{:S(2)}, u32[]{:S(2)}) collective-permute-start(bf16[32,2176]{1,0:T(8,128)(2,1)S(1)} %bitcast.25), channel_id=1, source_target_pairs={{0,2},{1,3},{2,0},{3,1},{4,6},{5,7},{6,4},{7,5},{8,10},{9,11},{10,... | collective-permute-start | bytes 417800 | tf_op jit(solution)/shard_map/ppermute | solution.py:163
  15.3 3.0 %collective-permute-done.2.refs_1_ = bf16[32,2176]{1,0:T(8,128)(2,1)S(1)} collective-permute-done((bf16[32,2176]{1,0:T(8,128)(2,1)S(1)}, bf16[32,2176]{1,0:T(8,128)(2,1)S(1)}, u32[]{:S(2)}, u32[]{:S(2)}) %collective-permute-start.2) | collective-permute-done | bytes 139296 | tf_op jit(solution)/shard_map/ppermute | solution.py:163
  18.3 3.5 %shard_map.95 = (f32[32,2048]{1,0:T(8,128)S(1)}, bf16[32,2048]{1,0:T(8,128)(2,1)S(1)}) custom-call(bf16[32,2176]{1,0:T(8,128)(2,1)S(1)} %bitcast.26, bf16[32,2176]{1,0:T(8,128)(2,1)S(1)} %collective-permute-done.2.refs_1_, bf16[768,2048]{1,0:T(8,128)(2,1)S(1)} %bitcast.12, bf16[768,2048]{1,0:T(8,128)(2,1)S(1)} %bitcast.15, ...), custom_call_target="tpu_custom_call" | custom-call | flops 1610612736 | bytes 12582912 | tf_op jit(solution)/shard_map/pallas_call | solution.py:132
  21.8 2.1 %collective-permute-start.5 = (bf16[32,2048]{1,0:T(8,128)(2,1)S(1)}, bf16[32,2048]{1,0:T(8,128)(2,1)S(1)}, u32[]{:S(2)}, u32[]{:S(2)}) collective-permute-start(bf16[32,2048]{1,0:T(8,128)(2,1)S(1)} %get-tuple-element.24), channel_id=1, source_target_pairs={{0,2},{1,3},{2,0},{3,1},{4,6},{5,7},{6,4},{7,5},{8,10},{9,11},{10,... | collective-permute-start | bytes 393224 | tf_op jit(solution)/shard_map/ppermute | solution.py:163
  23.9 2.9 %collective-permute-done.5.refs_0_ = bf16[32,2048]{1,0:T(8,128)(2,1)S(1)} collective-permute-done((bf16[32,2048]{1,0:T(8,128)(2,1)S(1)}, bf16[32,2048]{1,0:T(8,128)(2,1)S(1)}, u32[]{:S(2)}, u32[]{:S(2)}) %collective-permute-start.5) | collective-permute-done | bytes 131104 | tf_op jit(solution)/shard_map/ppermute | solution.py:163
  28.6 2.6 %collective-permute-done.6.refs_0_ = bf16[16,2048]{1,0:T(8,128)(2,1)S(1)} collective-permute-done((bf16[16,2048]{1,0:T(8,128)(2,1)S(1)}, bf16[16,2048]{1,0:T(8,128)(2,1)S(1)}, u32[]{:S(2)}, u32[]{:S(2)}) %collective-permute-start.6) | collective-permute-done | bytes 65568 | tf_op jit(solution)/shard_map/ppermute | solution.py:163
  31.2 2.8 %collective-permute-start.7 = (bf16[8,2048]{1,0:T(8,128)(2,1)S(1)}, bf16[8,2048]{1,0:T(8,128)(2,1)S(1)}, u32[]{:S(2)}, u32[]{:S(2)}) collective-permute-start(bf16[8,2048]{1,0:T(8,128)(2,1)S(1)} %get-tuple-element.28), channel_id=1, source_target_pairs={{0,8},{1,9},{2,10},{3,11},{4,12},{5,13},{6,14},{7,15},{8,0},{9,1},... | collective-permute-start | bytes 98312 | tf_op jit(solution)/shard_map/ppermute | solution.py:163
  34.0 2.1 %collective-permute-done.7.received = bf16[8,2048]{1,0:T(8,128)(2,1)S(1)} collective-permute-done((bf16[8,2048]{1,0:T(8,128)(2,1)S(1)}, bf16[8,2048]{1,0:T(8,128)(2,1)S(1)}, u32[]{:S(2)}, u32[]{:S(2)}) %collective-permute-start.7) | collective-permute-done | bytes 32800 | tf_op jit(solution)/shard_map/ppermute | solution.py:163
  36.2 2.8 %collective-permute-start.8 = (bf16[8,2176]{1,0:T(8,128)(2,1)S(1)}, bf16[8,2176]{1,0:T(8,128)(2,1)S(1)}, u32[]{:S(2)}, u32[]{:S(2)}) collective-permute-start(bf16[8,2176]{1,0:T(8,128)(2,1)S(1)} %get-tuple-element.30.first), channel_id=1, source_target_pairs={{0,8},{1,9},{2,10},{3,11},{4,12},{5,13},{6,14},{7,15},{8,0},{9,1},... | collective-permute-start | bytes 104456 | tf_op jit(solution)/shard_map/ppermute | solution.py:163
  39.0 2.1 %collective-permute-done.8.second = bf16[8,2176]{1,0:T(8,128)(2,1)S(1)} collective-permute-done((bf16[8,2176]{1,0:T(8,128)(2,1)S(1)}, bf16[8,2176]{1,0:T(8,128)(2,1)S(1)}, u32[]{:S(2)}, u32[]{:S(2)}) %collective-permute-start.8) | collective-permute-done | bytes 34848 | tf_op jit(solution)/shard_map/ppermute | solution.py:163
  42.8 2.6 %collective-permute-done.9.second = bf16[16,2176]{1,0:T(8,128)(2,1)S(1)} collective-permute-done((bf16[16,2176]{1,0:T(8,128)(2,1)S(1)}, bf16[16,2176]{1,0:T(8,128)(2,1)S(1)}, u32[]{:S(2)}, u32[]{:S(2)}) %collective-permute-start.9) | collective-permute-done | bytes 69664 | tf_op jit(solution)/shard_map/ppermute | solution.py:163
  45.5 2.2 %collective-permute-start.10 = (bf16[32,2176]{1,0:T(8,128)(2,1)S(1)}, bf16[32,2176]{1,0:T(8,128)(2,1)S(1)}, u32[]{:S(2)}, u32[]{:S(2)}) collective-permute-start(bf16[32,2176]{1,0:T(8,128)(2,1)S(1)} %bitcast.21), channel_id=1, source_target_pairs={{0,2},{1,3},{2,0},{3,1},{4,6},{5,7},{6,4},{7,5},{8,10},{9,11},{10,... | collective-permute-start | bytes 417800 | tf_op jit(solution)/shard_map/ppermute | solution.py:163
  50.7 2.8 %collective-permute-start.12 = (bf16[32,2176]{1,0:T(8,128)(2,1)S(1)}, bf16[32,2176]{1,0:T(8,128)(2,1)S(1)}, u32[]{:S(2)}, u32[]{:S(2)}) collective-permute-start(bf16[32,2176]{1,0:T(8,128)(2,1)S(1)} %collective-permute-done.10.refs_1_), channel_id=1, source_target_pairs={{0,16},{16,0},{1,17},{17,1},{2,18},{18,2},{3,19},{19,3},{4,20},{20... | collective-permute-start | bytes 417800 | tf_op jit(solution)/shard_map/ppermute | solution.py:163
  53.5 3.5 %shard_map.101.refs_8_ = f32[64,2048]{1,0:T(8,128)S(1)} custom-call(bf16[32,2176]{1,0:T(8,128)(2,1)S(1)} %bitcast.23, bf16[32,2176]{1,0:T(8,128)(2,1)S(1)} %collective-permute-done.10.refs_1_, bf16[768,2048]{1,0:T(8,128)(2,1)S(1)} %bitcast.13, bf16[768,2048]{1,0:T(8,128)(2,1)S(1)} %bitcast.16, bf16[768,2048]{1,0:T(8,128)(2,1)S(1)} %collective-permute-done.3.refs_4_, ...), custom_call_target="tpu_custom_call" | custom-call | flops 1610612736 | bytes 12582912 | tf_op jit(solution)/shard_map/pallas_call | solution.py:132
  57.9 2.1 %shard_map.102 = (f32[32,2048]{1,0:T(8,128)S(1)}, bf16[32,2048]{1,0:T(8,128)(2,1)S(1)}, f32[32,2048]{1,0:T(8,128)S(1)}, bf16[32,2048]{1,0:T(8,128)(2,1)S(1)}) custom-call(bf16[32,2176]{1,0:T(8,128)(2,1)S(1)} %bitcast.24, bf16[32,2176]{1,0:T(8,128)(2,1)S(1)} %collective-permute-done.10.refs_1_, bf16[32,2176]{1,0:T(8,128)(2,1)S(1)} %collective-permute-done.11.refs_2_, ...), custom_call_target="tpu_custom_call" | custom-call | flops 1610612736 | bytes 6291456 | tf_op jit(solution)/shard_map/pallas_call | solution.py:132
  62.1 2.9 %collective-permute-done.16 = bf16[32,2048]{1,0:T(8,128)(2,1)S(1)} collective-permute-done((bf16[32,2048]{1,0:T(8,128)(2,1)S(1)}, bf16[32,2048]{1,0:T(8,128)(2,1)S(1)}, u32[]{:S(2)}, u32[]{:S(2)}) %collective-permute-start.16) | collective-permute-done | bytes 131104 | tf_op jit(solution)/shard_map/ppermute | solution.py:163
  65.1 2.0 %collective-permute-start.17 = (bf16[32,2048]{1,0:T(8,128)(2,1)S(1)}, bf16[32,2048]{1,0:T(8,128)(2,1)S(1)}, u32[]{:S(2)}, u32[]{:S(2)}) collective-permute-start(bf16[32,2048]{1,0:T(8,128)(2,1)S(1)} %add_convert_fusion), channel_id=1, source_target_pairs={{0,16},{16,0},{1,17},{17,1},{2,18},{18,2},{3,19},{19,3},{4,20},{20... | collective-permute-start | bytes 393224 | tf_op jit(solution)/shard_map/ppermute | solution.py:163
  67.1 3.0 %collective-permute-done.17.refs_1_ = bf16[32,2048]{1,0:T(8,128)(2,1)S(1)} collective-permute-done((bf16[32,2048]{1,0:T(8,128)(2,1)S(1)}, bf16[32,2048]{1,0:T(8,128)(2,1)S(1)}, u32[]{:S(2)}, u32[]{:S(2)}) %collective-permute-start.17) | collective-permute-done | bytes 131104 | tf_op jit(solution)/shard_map/ppermute | solution.py:163
  70.9 3.6 %collective-permute-done.18.refs_0_ = bf16[16,2048]{1,0:T(8,128)(2,1)S(1)} collective-permute-done((bf16[16,2048]{1,0:T(8,128)(2,1)S(1)}, bf16[16,2048]{1,0:T(8,128)(2,1)S(1)}, u32[]{:S(2)}, u32[]{:S(2)}) %collective-permute-start.18) | collective-permute-done | bytes 65568 | tf_op jit(solution)/shard_map/ppermute | solution.py:163
  74.5 2.0 %collective-permute-start.19 = (bf16[8,2048]{1,0:T(8,128)(2,1)S(1)}, bf16[8,2048]{1,0:T(8,128)(2,1)S(1)}, u32[]{:S(2)}, u32[]{:S(2)}) collective-permute-start(bf16[8,2048]{1,0:T(8,128)(2,1)S(1)} %get-tuple-element.40), channel_id=1, source_target_pairs={{0,8},{1,9},{2,10},{3,11},{4,12},{5,13},{6,14},{7,15},{8,0},{9,1},... | collective-permute-start | bytes 98312 | tf_op jit(solution)/shard_map/ppermute | solution.py:163
  76.5 2.9 %collective-permute-done.19.received = bf16[8,2048]{1,0:T(8,128)(2,1)S(1)} collective-permute-done((bf16[8,2048]{1,0:T(8,128)(2,1)S(1)}, bf16[8,2048]{1,0:T(8,128)(2,1)S(1)}, u32[]{:S(2)}, u32[]{:S(2)}) %collective-permute-start.19) | collective-permute-done | bytes 32800 | tf_op jit(solution)/shard_map/ppermute | solution.py:163
  (52 shorter events, 15.7 us)
Async XLA Ops:
  0.0 18.3 %collective-permute-start.3 = (bf16[768,2048]{1,0:T(8,128)(2,1)}, bf16[768,2048]{1,0:T(8,128)(2,1)S(1)}, u32[]{:S(2)}, u32[]{:S(2)}) collective-permute-start(bf16[768,2048]{1,0:T(8,128)(2,1)} %bitcast.11), channel_id=1, source_target_pairs={{0,1},{1,0},{2,3},{3,2},{4,5},{5,4},{6,7},{7,6},{8,9},{9,8},{10,11... | collective-permute-start | bytes 9437192 | tf_op jit(solution)/shard_map/ppermute | solution.py:163
  0.5 17.9 %collective-permute-start.4 = (bf16[768,2048]{1,0:T(8,128)(2,1)}, bf16[768,2048]{1,0:T(8,128)(2,1)S(1)}, u32[]{:S(2)}, u32[]{:S(2)}) collective-permute-start(bf16[768,2048]{1,0:T(8,128)(2,1)} %bitcast.14), channel_id=1, source_target_pairs={{0,1},{1,0},{2,3},{3,2},{4,5},{5,4},{6,7},{7,6},{8,9},{9,8},{10,11... | collective-permute-start | bytes 9437192 | tf_op jit(solution)/shard_map/ppermute | solution.py:163
  0.5 57.4 %collective-permute-start.13 = (bf16[384,2048]{1,0:T(8,128)(2,1)}, bf16[384,2048]{1,0:T(8,128)(2,1)S(1)}, u32[]{:S(2)}, u32[]{:S(2)}) collective-permute-start(bf16[384,2048]{1,0:T(8,128)(2,1)} %bitcast.17), channel_id=1, source_target_pairs={{0,1},{1,0},{2,3},{3,2},{4,5},{5,4},{6,7},{7,6},{8,9},{9,8},{10,11... | collective-permute-start | bytes 4718600 | tf_op jit(solution)/shard_map/ppermute | solution.py:163
  1.0 56.9 %collective-permute-start.14 = (bf16[384,2048]{1,0:T(8,128)(2,1)}, bf16[384,2048]{1,0:T(8,128)(2,1)S(1)}, u32[]{:S(2)}, u32[]{:S(2)}) collective-permute-start(bf16[384,2048]{1,0:T(8,128)(2,1)} %bitcast.19), channel_id=1, source_target_pairs={{0,1},{1,0},{2,3},{3,2},{4,5},{5,4},{6,7},{7,6},{8,9},{9,8},{10,11... | collective-permute-start | bytes 4718600 | tf_op jit(solution)/shard_map/ppermute | solution.py:163
  1.8 16.5 %copy-start = (bf16[1,768,2048]{2,1,0:T(8,128)(2,1)S(1)}, bf16[1,768,2048]{2,1,0:T(8,128)(2,1)}, u32[]{:S(2)}) copy-start(bf16[1,768,2048]{2,1,0:T(8,128)(2,1)} %param.14) | copy-start | bytes 9437188
  1.8 16.5 %copy-start.1 = (bf16[1,768,2048]{2,1,0:T(8,128)(2,1)S(1)}, bf16[1,768,2048]{2,1,0:T(8,128)(2,1)}, u32[]{:S(2)}) copy-start(bf16[1,768,2048]{2,1,0:T(8,128)(2,1)} %param.15) | copy-start | bytes 9437188
  2.6 6.0 %collective-permute-start = (bf16[8,2176]{1,0:T(8,128)(2,1)S(1)}, bf16[8,2176]{1,0:T(8,128)(2,1)S(1)}, u32[]{:S(2)}, u32[]{:S(2)}) collective-permute-start(bf16[8,2176]{1,0:T(8,128)(2,1)S(1)} %shard_map.92.first), channel_id=1, source_target_pairs={{0,8},{1,9},{2,10},{3,11},{4,12},{5,13},{6,14},{7,15},{8,0},{9,1},... | collective-permute-start | bytes 104456 | tf_op jit(solution)/shard_map/ppermute | solution.py:163
  8.6 4.3 %collective-permute-start.1 = (bf16[16,2176]{1,0:T(8,128)(2,1)S(1)}, bf16[16,2176]{1,0:T(8,128)(2,1)S(1)}, u32[]{:S(2)}, u32[]{:S(2)}) collective-permute-start(bf16[16,2176]{1,0:T(8,128)(2,1)S(1)} %bitcast.27), channel_id=1, source_target_pairs={{0,4},{1,5},{2,6},{3,7},{4,0},{5,1},{6,2},{7,3},{8,12},{9,13},{10,... | collective-permute-start | bytes 208904 | tf_op jit(solution)/shard_map/ppermute | solution.py:163
  13.0 23.1 %copy-start.5 = (bf16[1,8,2048]{2,1,0:T(8,128)(2,1)S(1)}, bf16[1,8,2048]{2,1,0:T(8,128)(2,1)}, u32[]{:S(2)}) copy-start(bf16[1,8,2048]{2,1,0:T(8,128)(2,1)} %param.9) | copy-start | bytes 98308
  13.0 23.1 %copy-start.9 = (s32[1,4]{1,0:T(1,128)S(1)}, s32[1,4]{1,0:T(1,128)}, u32[]{:S(2)}) copy-start(s32[1,4]{1,0:T(1,128)} %changed.1) | copy-start | bytes 52
  13.0 5.3 %collective-permute-start.2 = (bf16[32,2176]{1,0:T(8,128)(2,1)S(1)}, bf16[32,2176]{1,0:T(8,128)(2,1)S(1)}, u32[]{:S(2)}, u32[]{:S(2)}) collective-permute-start(bf16[32,2176]{1,0:T(8,128)(2,1)S(1)} %bitcast.25), channel_id=1, source_target_pairs={{0,2},{1,3},{2,0},{3,1},{4,6},{5,7},{6,4},{7,5},{8,10},{9,11},{10,... | collective-permute-start | bytes 417800 | tf_op jit(solution)/shard_map/ppermute | solution.py:163
  21.8 5.0 %collective-permute-start.5 = (bf16[32,2048]{1,0:T(8,128)(2,1)S(1)}, bf16[32,2048]{1,0:T(8,128)(2,1)S(1)}, u32[]{:S(2)}, u32[]{:S(2)}) collective-permute-start(bf16[32,2048]{1,0:T(8,128)(2,1)S(1)} %get-tuple-element.24), channel_id=1, source_target_pairs={{0,2},{1,3},{2,0},{3,1},{4,6},{5,7},{6,4},{7,5},{8,10},{9,11},{10,... | collective-permute-start | bytes 393224 | tf_op jit(solution)/shard_map/ppermute | solution.py:163
  26.9 4.3 %collective-permute-start.6 = (bf16[16,2048]{1,0:T(8,128)(2,1)S(1)}, bf16[16,2048]{1,0:T(8,128)(2,1)S(1)}, u32[]{:S(2)}, u32[]{:S(2)}) collective-permute-start(bf16[16,2048]{1,0:T(8,128)(2,1)S(1)} %get-tuple-element.26), channel_id=1, source_target_pairs={{0,4},{1,5},{2,6},{3,7},{4,0},{5,1},{6,2},{7,3},{8,12},{9,13},{10,... | collective-permute-start | bytes 196616 | tf_op jit(solution)/shard_map/ppermute | solution.py:163
  31.2 4.9 %collective-permute-start.7 = (bf16[8,2048]{1,0:T(8,128)(2,1)S(1)}, bf16[8,2048]{1,0:T(8,128)(2,1)S(1)}, u32[]{:S(2)}, u32[]{:S(2)}) collective-permute-start(bf16[8,2048]{1,0:T(8,128)(2,1)S(1)} %get-tuple-element.28), channel_id=1, source_target_pairs={{0,8},{1,9},{2,10},{3,11},{4,12},{5,13},{6,14},{7,15},{8,0},{9,1},... | collective-permute-start | bytes 98312 | tf_op jit(solution)/shard_map/ppermute | solution.py:163
  36.2 4.9 %collective-permute-start.8 = (bf16[8,2176]{1,0:T(8,128)(2,1)S(1)}, bf16[8,2176]{1,0:T(8,128)(2,1)S(1)}, u32[]{:S(2)}, u32[]{:S(2)}) collective-permute-start(bf16[8,2176]{1,0:T(8,128)(2,1)S(1)} %get-tuple-element.30.first), channel_id=1, source_target_pairs={{0,8},{1,9},{2,10},{3,11},{4,12},{5,13},{6,14},{7,15},{8,0},{9,1},... | collective-permute-start | bytes 104456 | tf_op jit(solution)/shard_map/ppermute | solution.py:163
  41.1 4.3 %collective-permute-start.9 = (bf16[16,2176]{1,0:T(8,128)(2,1)S(1)}, bf16[16,2176]{1,0:T(8,128)(2,1)S(1)}, u32[]{:S(2)}, u32[]{:S(2)}) collective-permute-start(bf16[16,2176]{1,0:T(8,128)(2,1)S(1)} %bitcast.29), channel_id=1, source_target_pairs={{0,4},{1,5},{2,6},{3,7},{4,0},{5,1},{6,2},{7,3},{8,12},{9,13},{10,... | collective-permute-start | bytes 208904 | tf_op jit(solution)/shard_map/ppermute | solution.py:163
  45.5 5.2 %collective-permute-start.10 = (bf16[32,2176]{1,0:T(8,128)(2,1)S(1)}, bf16[32,2176]{1,0:T(8,128)(2,1)S(1)}, u32[]{:S(2)}, u32[]{:S(2)}) collective-permute-start(bf16[32,2176]{1,0:T(8,128)(2,1)S(1)} %bitcast.21), channel_id=1, source_target_pairs={{0,2},{1,3},{2,0},{3,1},{4,6},{5,7},{6,4},{7,5},{8,10},{9,11},{10,... | collective-permute-start | bytes 417800 | tf_op jit(solution)/shard_map/ppermute | solution.py:163
  47.7 10.2 %collective-permute-start.11 = (bf16[32,2176]{1,0:T(8,128)(2,1)S(1)}, bf16[32,2176]{1,0:T(8,128)(2,1)S(1)}, u32[]{:S(2)}, u32[]{:S(2)}) collective-permute-start(bf16[32,2176]{1,0:T(8,128)(2,1)S(1)} %bitcast.22), channel_id=1, source_target_pairs={{0,16},{16,0},{1,17},{17,1},{2,18},{18,2},{3,19},{19,3},{4,20},{20... | collective-permute-start | bytes 417800 | tf_op jit(solution)/shard_map/ppermute | solution.py:163
  50.7 7.1 %collective-permute-start.12 = (bf16[32,2176]{1,0:T(8,128)(2,1)S(1)}, bf16[32,2176]{1,0:T(8,128)(2,1)S(1)}, u32[]{:S(2)}, u32[]{:S(2)}) collective-permute-start(bf16[32,2176]{1,0:T(8,128)(2,1)S(1)} %collective-permute-done.10.refs_1_), channel_id=1, source_target_pairs={{0,16},{16,0},{1,17},{17,1},{2,18},{18,2},{3,19},{19,3},{4,20},{20... | collective-permute-start | bytes 417800 | tf_op jit(solution)/shard_map/ppermute | solution.py:163
  60.0 5.0 %collective-permute-start.16 = (bf16[32,2048]{1,0:T(8,128)(2,1)S(1)}, bf16[32,2048]{1,0:T(8,128)(2,1)S(1)}, u32[]{:S(2)}, u32[]{:S(2)}) collective-permute-start(bf16[32,2048]{1,0:T(8,128)(2,1)S(1)} %get-tuple-element.36), channel_id=1, source_target_pairs={{0,2},{1,3},{2,0},{3,1},{4,6},{5,7},{6,4},{7,5},{8,10},{9,11},{10,... | collective-permute-start | bytes 393224 | tf_op jit(solution)/shard_map/ppermute | solution.py:163
  61.6 5.5 %collective-permute-start.15 = (bf16[32,2048]{1,0:T(8,128)(2,1)S(1)}, bf16[32,2048]{1,0:T(8,128)(2,1)S(1)}, u32[]{:S(2)}, u32[]{:S(2)}) collective-permute-start(bf16[32,2048]{1,0:T(8,128)(2,1)S(1)} %get-tuple-element.34), channel_id=1, source_target_pairs={{0,2},{1,3},{2,0},{3,1},{4,6},{5,7},{6,4},{7,5},{8,10},{9,11},{10,... | collective-permute-start | bytes 393224 | tf_op jit(solution)/shard_map/ppermute | solution.py:163
  65.1 5.0 %collective-permute-start.17 = (bf16[32,2048]{1,0:T(8,128)(2,1)S(1)}, bf16[32,2048]{1,0:T(8,128)(2,1)S(1)}, u32[]{:S(2)}, u32[]{:S(2)}) collective-permute-start(bf16[32,2048]{1,0:T(8,128)(2,1)S(1)} %add_convert_fusion), channel_id=1, source_target_pairs={{0,16},{16,0},{1,17},{17,1},{2,18},{18,2},{3,19},{19,3},{4,20},{20... | collective-permute-start | bytes 393224 | tf_op jit(solution)/shard_map/ppermute | solution.py:163
  70.2 4.3 %collective-permute-start.18 = (bf16[16,2048]{1,0:T(8,128)(2,1)S(1)}, bf16[16,2048]{1,0:T(8,128)(2,1)S(1)}, u32[]{:S(2)}, u32[]{:S(2)}) collective-permute-start(bf16[16,2048]{1,0:T(8,128)(2,1)S(1)} %get-tuple-element.38), channel_id=1, source_target_pairs={{0,4},{1,5},{2,6},{3,7},{4,0},{5,1},{6,2},{7,3},{8,12},{9,13},{10,... | collective-permute-start | bytes 196616 | tf_op jit(solution)/shard_map/ppermute | solution.py:163
  74.5 4.9 %collective-permute-start.19 = (bf16[8,2048]{1,0:T(8,128)(2,1)S(1)}, bf16[8,2048]{1,0:T(8,128)(2,1)S(1)}, u32[]{:S(2)}, u32[]{:S(2)}) collective-permute-start(bf16[8,2048]{1,0:T(8,128)(2,1)S(1)} %get-tuple-element.40), channel_id=1, source_target_pairs={{0,8},{1,9},{2,10},{3,11},{4,12},{5,13},{6,14},{7,15},{8,0},{9,1},... | collective-permute-start | bytes 98312 | tf_op jit(solution)/shard_map/ppermute | solution.py:163
  (6 other events, 27.7 us)

commit v10 on v9

--- a/solution.py
+++ b/solution.py
@@ -158,17 +158,20 @@
     return on_vmem(kernel, inputs, outputs, 8 * MIB, cost)
 
 
-def swap(value, axis, distance):
-    size = lax.axis_size(axis)
-    return lax.ppermute(value, axis, [(i, i ^ distance) for i in range(size)])
-
-
 def swap_core(value):
-    return swap(value, "expert", 1)
+    size = lax.axis_size("expert")
+    return lax.ppermute(value, "expert", [(i, i ^ 1) for i in range(size)])
+
+
+def swap_chip(value, distance):
+    size = lax.axis_size("expert")
+    return lax.ppermute(value, "expert", [(i, i ^ distance ^ 1) for i in range(size)])
 
 
 def swap_group(value):
-    return swap(value, "group", 1)
+    size = lax.axis_size("expert")
+    pairs = [(i, i ^ size ^ 1) for i in range(2 * size)]
+    return lax.ppermute(value, ("group", "expert"), pairs)
 
 
 def chip_distances():
@@ -182,7 +185,7 @@
     for distance in reversed(chip_distances()[1:]):
         rows, width = block.shape
         joined = ((2, rows, width), block.dtype)
-        (block,) = on_vmem(join_kernel, (block, swap(block, "expert", distance)), [joined])
+        (block,) = on_vmem(join_kernel, (block, swap_chip(block, distance)), [joined])
         block = block.reshape(2 * rows, width)
     return block
 
@@ -198,7 +201,7 @@
 def give_back(kept, *received):
     for distance in chip_distances()[1:]:
         kept, sent = halve(kept, *received)
-        received = (swap(sent, "expert", distance),)
+        received = (swap_chip(sent, distance),)
     return kept, received[0]
 
 
@@ -232,11 +235,11 @@
                 [state_shape, block_shape],
             )
         rows = gather(block)
-        across = swap(rows, "expert", near)
+        across = swap_chip(rows, near)
         mine = [(line, jnp.float32), (line, jnp.bfloat16)]
         if step == 0:
             kept, sent = run_mlp([(rows, across)], stale, False, mine)
-            kept, received = give_back(kept, swap(sent, "expert", near))
+            kept, received = give_back(kept, swap_chip(sent, near))
         else:
             other, other_across = swap_group(rows), swap_group(across)
             (old,) = run_mlp([(rows, across)], stale, False, [(2 * line, jnp.float32)])
@@ -244,9 +247,9 @@
             kept, sent, away_kept, away_sent = run_mlp(
                 [(rows, across), (other, other_across)], learner, True, mine + mine, (old,)
             )
-            away = away_kept + swap(away_sent, "expert", near).astype(jnp.float32)
+            away = away_kept + swap_chip(away_sent, near).astype(jnp.float32)
             away = swap_group(away.astype(jnp.bfloat16))
-            kept, received = give_back(kept, swap(sent, "expert", near), away)
+            kept, received = give_back(kept, swap_chip(sent, near), away)
     (updated,) = on_vmem(
         last_kernel, (state, kept, received), [((row_count, width), jnp.bfloat16)]
     )

time: 80.2 us -> 79.4 us (0.990)
  waiting for transfers between devices: 34.6 us -> 33.3 us
    ppermute x20, waiting for transfers between devices: 34.6 us -> 33.3 us  [the longest x13 30.1 us: swap_chip(): lax.ppermute(value, 'expert', [(i, i ^ distance ^ 1) for i in range(size)])]
  transfers between devices with their start and end apart: 20 -> 20, of which waited for: 14 -> 15; matrix products, arithmetic and copies ran while one was open for 0% -> 0% of each run, Pallas kernels for 9% -> 9%
where the time goes in v10:
time: 79.4 us; the launch traced here: 79.2 us
  starting transfers between devices  34.2 us (43%)
  waiting for transfers between devices  33.3 us (42%)
  Pallas kernels  10.1 us (13%)
  local copies, waits for them, and re-layouts  1.4 us (2%)
    ppermute x13, waiting for transfers between devices, swap_chip(): lax.ppermute(value, 'expert', [(i, i ^ distance ^ 1) for i in range(size)])  30.1 us
    ppermute x13, starting transfers between devices, swap_chip(): lax.ppermute(value, 'expert', [(i, i ^ distance ^ 1) for i in range(size)])  27.9 us
    pallas_call x15, Pallas kernels, on_vmem(): pl.pallas_call(kernel, out_shape=[jax.ShapeDtypeStruct(shape, kind) for s...  10.1 us
    ppermute x3, starting transfers between devices, swap_group(): return lax.ppermute(value, ('group', 'expert'), pairs)  5.28 us
    ppermute x3, waiting for transfers between devices, swap_group(): return lax.ppermute(value, ('group', 'expert'), pairs)  3.25 us
  transfers between devices with their start and end apart: 20, of which 15 were waited for; matrix products, arithmetic and copies ran while one was open for 0% of the time, Pallas kernels for 9%

profile of v10, /device:TPU:0, one launch (start us, length us, event | category | flops | bytes accessed | tf_op | source)
XLA Modules:
  0.0 79.2 jit_solution(7618775684819281528)
XLA Ops:
  2.6 3.7 %collective-permute-start = (bf16[8,2176]{1,0:T(8,128)(2,1)S(1)}, bf16[8,2176]{1,0:T(8,128)(2,1)S(1)}, u32[]{:S(2)}, u32[]{:S(2)}) collective-permute-start(bf16[8,2176]{1,0:T(8,128)(2,1)S(1)} %shard_map.92.first), channel_id=1, source_target_pairs={{0,9},{1,8},{2,11},{3,10},{4,13},{5,12},{6,15},{7,14},{8,1},{9,0},... | collective-permute-start | bytes 104456 | tf_op jit(solution)/shard_map/ppermute | solution.py:168
  6.3 1.6 %collective-permute-done.second = bf16[8,2176]{1,0:T(8,128)(2,1)S(1)} collective-permute-done((bf16[8,2176]{1,0:T(8,128)(2,1)S(1)}, bf16[8,2176]{1,0:T(8,128)(2,1)S(1)}, u32[]{:S(2)}, u32[]{:S(2)}) %collective-permute-start) | collective-permute-done | bytes 34848 | tf_op jit(solution)/shard_map/ppermute | solution.py:168
  8.0 1.8 %collective-permute-start.1 = (bf16[16,2176]{1,0:T(8,128)(2,1)S(1)}, bf16[16,2176]{1,0:T(8,128)(2,1)S(1)}, u32[]{:S(2)}, u32[]{:S(2)}) collective-permute-start(bf16[16,2176]{1,0:T(8,128)(2,1)S(1)} %bitcast.27), channel_id=1, source_target_pairs={{0,5},{1,4},{2,7},{3,6},{4,1},{5,0},{6,3},{7,2},{8,13},{9,12},{10,... | collective-permute-start | bytes 208904 | tf_op jit(solution)/shard_map/ppermute | solution.py:168
  9.8 2.4 %collective-permute-done.1.second = bf16[16,2176]{1,0:T(8,128)(2,1)S(1)} collective-permute-done((bf16[16,2176]{1,0:T(8,128)(2,1)S(1)}, bf16[16,2176]{1,0:T(8,128)(2,1)S(1)}, u32[]{:S(2)}, u32[]{:S(2)}) %collective-permute-start.1) | collective-permute-done | bytes 69664 | tf_op jit(solution)/shard_map/ppermute | solution.py:168
  12.2 1.8 %collective-permute-start.2 = (bf16[32,2176]{1,0:T(8,128)(2,1)S(1)}, bf16[32,2176]{1,0:T(8,128)(2,1)S(1)}, u32[]{:S(2)}, u32[]{:S(2)}) collective-permute-start(bf16[32,2176]{1,0:T(8,128)(2,1)S(1)} %bitcast.25), channel_id=1, source_target_pairs={{0,3},{1,2},{2,1},{3,0},{4,7},{5,6},{6,5},{7,4},{8,11},{9,10},{10,... | collective-permute-start | bytes 417800 | tf_op jit(solution)/shard_map/ppermute | solution.py:168
  14.0 3.8 %collective-permute-done.2.refs_1_ = bf16[32,2176]{1,0:T(8,128)(2,1)S(1)} collective-permute-done((bf16[32,2176]{1,0:T(8,128)(2,1)S(1)}, bf16[32,2176]{1,0:T(8,128)(2,1)S(1)}, u32[]{:S(2)}, u32[]{:S(2)}) %collective-permute-start.2) | collective-permute-done | bytes 139296 | tf_op jit(solution)/shard_map/ppermute | solution.py:168
  17.8 3.5 %shard_map.95 = (f32[32,2048]{1,0:T(8,128)S(1)}, bf16[32,2048]{1,0:T(8,128)(2,1)S(1)}) custom-call(bf16[32,2176]{1,0:T(8,128)(2,1)S(1)} %bitcast.26, bf16[32,2176]{1,0:T(8,128)(2,1)S(1)} %collective-permute-done.2.refs_1_, bf16[768,2048]{1,0:T(8,128)(2,1)S(1)} %bitcast.12, bf16[768,2048]{1,0:T(8,128)(2,1)S(1)} %bitcast.15, ...), custom_call_target="tpu_custom_call" | custom-call | flops 1610612736 | bytes 12582912 | tf_op jit(solution)/shard_map/pallas_call | solution.py:132
  21.3 2.0 %collective-permute-start.5 = (bf16[32,2048]{1,0:T(8,128)(2,1)S(1)}, bf16[32,2048]{1,0:T(8,128)(2,1)S(1)}, u32[]{:S(2)}, u32[]{:S(2)}) collective-permute-start(bf16[32,2048]{1,0:T(8,128)(2,1)S(1)} %get-tuple-element.24), channel_id=1, source_target_pairs={{0,3},{1,2},{2,1},{3,0},{4,7},{5,6},{6,5},{7,4},{8,11},{9,10},{10,... | collective-permute-start | bytes 393224 | tf_op jit(solution)/shard_map/ppermute | solution.py:168
  23.3 3.6 %collective-permute-done.5.refs_0_ = bf16[32,2048]{1,0:T(8,128)(2,1)S(1)} collective-permute-done((bf16[32,2048]{1,0:T(8,128)(2,1)S(1)}, bf16[32,2048]{1,0:T(8,128)(2,1)S(1)}, u32[]{:S(2)}, u32[]{:S(2)}) %collective-permute-start.5) | collective-permute-done | bytes 131104 | tf_op jit(solution)/shard_map/ppermute | solution.py:168
  26.9 2.2 %collective-permute-start.6 = (bf16[16,2048]{1,0:T(8,128)(2,1)S(1)}, bf16[16,2048]{1,0:T(8,128)(2,1)S(1)}, u32[]{:S(2)}, u32[]{:S(2)}) collective-permute-start(bf16[16,2048]{1,0:T(8,128)(2,1)S(1)} %get-tuple-element.26), channel_id=1, source_target_pairs={{0,5},{1,4},{2,7},{3,6},{4,1},{5,0},{6,3},{7,2},{8,13},{9,12},{10,... | collective-permute-start | bytes 196616 | tf_op jit(solution)/shard_map/ppermute | solution.py:168
  29.1 2.2 %collective-permute-done.6.refs_0_ = bf16[16,2048]{1,0:T(8,128)(2,1)S(1)} collective-permute-done((bf16[16,2048]{1,0:T(8,128)(2,1)S(1)}, bf16[16,2048]{1,0:T(8,128)(2,1)S(1)}, u32[]{:S(2)}, u32[]{:S(2)}) %collective-permute-start.6) | collective-permute-done | bytes 65568 | tf_op jit(solution)/shard_map/ppermute | solution.py:168
  31.3 3.2 %collective-permute-start.7 = (bf16[8,2048]{1,0:T(8,128)(2,1)S(1)}, bf16[8,2048]{1,0:T(8,128)(2,1)S(1)}, u32[]{:S(2)}, u32[]{:S(2)}) collective-permute-start(bf16[8,2048]{1,0:T(8,128)(2,1)S(1)} %get-tuple-element.28), channel_id=1, source_target_pairs={{0,9},{1,8},{2,11},{3,10},{4,13},{5,12},{6,15},{7,14},{8,1},{9,0},... | collective-permute-start | bytes 98312 | tf_op jit(solution)/shard_map/ppermute | solution.py:168
  36.3 2.7 %collective-permute-start.8 = (bf16[8,2176]{1,0:T(8,128)(2,1)S(1)}, bf16[8,2176]{1,0:T(8,128)(2,1)S(1)}, u32[]{:S(2)}, u32[]{:S(2)}) collective-permute-start(bf16[8,2176]{1,0:T(8,128)(2,1)S(1)} %get-tuple-element.30.first), channel_id=1, source_target_pairs={{0,9},{1,8},{2,11},{3,10},{4,13},{5,12},{6,15},{7,14},{8,1},{9,0},... | collective-permute-start | bytes 104456 | tf_op jit(solution)/shard_map/ppermute | solution.py:168
  39.0 1.6 %collective-permute-done.8.second = bf16[8,2176]{1,0:T(8,128)(2,1)S(1)} collective-permute-done((bf16[8,2176]{1,0:T(8,128)(2,1)S(1)}, bf16[8,2176]{1,0:T(8,128)(2,1)S(1)}, u32[]{:S(2)}, u32[]{:S(2)}) %collective-permute-start.8) | collective-permute-done | bytes 34848 | tf_op jit(solution)/shard_map/ppermute | solution.py:168
  40.6 2.3 %collective-permute-start.9 = (bf16[16,2176]{1,0:T(8,128)(2,1)S(1)}, bf16[16,2176]{1,0:T(8,128)(2,1)S(1)}, u32[]{:S(2)}, u32[]{:S(2)}) collective-permute-start(bf16[16,2176]{1,0:T(8,128)(2,1)S(1)} %bitcast.29), channel_id=1, source_target_pairs={{0,5},{1,4},{2,7},{3,6},{4,1},{5,0},{6,3},{7,2},{8,13},{9,12},{10,... | collective-permute-start | bytes 208904 | tf_op jit(solution)/shard_map/ppermute | solution.py:168
  42.9 2.4 %collective-permute-done.9.second = bf16[16,2176]{1,0:T(8,128)(2,1)S(1)} collective-permute-done((bf16[16,2176]{1,0:T(8,128)(2,1)S(1)}, bf16[16,2176]{1,0:T(8,128)(2,1)S(1)}, u32[]{:S(2)}, u32[]{:S(2)}) %collective-permute-start.9) | collective-permute-done | bytes 69664 | tf_op jit(solution)/shard_map/ppermute | solution.py:168
  48.2 2.9 %collective-permute-done.10.refs_1_ = bf16[32,2176]{1,0:T(8,128)(2,1)S(1)} collective-permute-done((bf16[32,2176]{1,0:T(8,128)(2,1)S(1)}, bf16[32,2176]{1,0:T(8,128)(2,1)S(1)}, u32[]{:S(2)}, u32[]{:S(2)}) %collective-permute-start.10) | collective-permute-done | bytes 139296 | tf_op jit(solution)/shard_map/ppermute | solution.py:168
  52.6 3.5 %shard_map.101.refs_8_ = f32[64,2048]{1,0:T(8,128)S(1)} custom-call(bf16[32,2176]{1,0:T(8,128)(2,1)S(1)} %bitcast.23, bf16[32,2176]{1,0:T(8,128)(2,1)S(1)} %collective-permute-done.10.refs_1_, bf16[768,2048]{1,0:T(8,128)(2,1)S(1)} %bitcast.13, bf16[768,2048]{1,0:T(8,128)(2,1)S(1)} %bitcast.16, bf16[768,2048]{1,0:T(8,128)(2,1)S(1)} %collective-permute-done.3.refs_4_, ...), custom_call_target="tpu_custom_call" | custom-call | flops 1610612736 | bytes 12582912 | tf_op jit(solution)/shard_map/pallas_call | solution.py:132
  56.5 2.1 %shard_map.102 = (f32[32,2048]{1,0:T(8,128)S(1)}, bf16[32,2048]{1,0:T(8,128)(2,1)S(1)}, f32[32,2048]{1,0:T(8,128)S(1)}, bf16[32,2048]{1,0:T(8,128)(2,1)S(1)}) custom-call(bf16[32,2176]{1,0:T(8,128)(2,1)S(1)} %bitcast.24, bf16[32,2176]{1,0:T(8,128)(2,1)S(1)} %collective-permute-done.10.refs_1_, bf16[32,2176]{1,0:T(8,128)(2,1)S(1)} %collective-permute-done.11.refs_2_, ...), custom_call_target="tpu_custom_call" | custom-call | flops 1610612736 | bytes 6291456 | tf_op jit(solution)/shard_map/pallas_call | solution.py:132
  60.5 3.6 %collective-permute-done.16 = bf16[32,2048]{1,0:T(8,128)(2,1)S(1)} collective-permute-done((bf16[32,2048]{1,0:T(8,128)(2,1)S(1)}, bf16[32,2048]{1,0:T(8,128)(2,1)S(1)}, u32[]{:S(2)}, u32[]{:S(2)}) %collective-permute-start.16) | collective-permute-done | bytes 131104 | tf_op jit(solution)/shard_map/ppermute | solution.py:168
  64.1 2.2 %collective-permute-start.17 = (bf16[32,2048]{1,0:T(8,128)(2,1)S(1)}, bf16[32,2048]{1,0:T(8,128)(2,1)S(1)}, u32[]{:S(2)}, u32[]{:S(2)}) collective-permute-start(bf16[32,2048]{1,0:T(8,128)(2,1)S(1)} %add_convert_fusion), channel_id=1, source_target_pairs={{0,17},{1,16},{2,19},{3,18},{4,21},{5,20},{6,23},{7,22},{8,25},{9,... | collective-permute-start | bytes 393224 | tf_op jit(solution)/shard_map/ppermute | solution.py:174
  66.9 2.8 %collective-permute-done.17.refs_1_ = bf16[32,2048]{1,0:T(8,128)(2,1)S(1)} collective-permute-done((bf16[32,2048]{1,0:T(8,128)(2,1)S(1)}, bf16[32,2048]{1,0:T(8,128)(2,1)S(1)}, u32[]{:S(2)}, u32[]{:S(2)}) %collective-permute-start.17) | collective-permute-done | bytes 131104 | tf_op jit(solution)/shard_map/ppermute | solution.py:174
  71.3 2.2 %collective-permute-done.18.refs_0_ = bf16[16,2048]{1,0:T(8,128)(2,1)S(1)} collective-permute-done((bf16[16,2048]{1,0:T(8,128)(2,1)S(1)}, bf16[16,2048]{1,0:T(8,128)(2,1)S(1)}, u32[]{:S(2)}, u32[]{:S(2)}) %collective-permute-start.18) | collective-permute-done | bytes 65568 | tf_op jit(solution)/shard_map/ppermute | solution.py:168
  73.5 3.5 %collective-permute-start.19 = (bf16[8,2048]{1,0:T(8,128)(2,1)S(1)}, bf16[8,2048]{1,0:T(8,128)(2,1)S(1)}, u32[]{:S(2)}, u32[]{:S(2)}) collective-permute-start(bf16[8,2048]{1,0:T(8,128)(2,1)S(1)} %get-tuple-element.40), channel_id=1, source_target_pairs={{0,9},{1,8},{2,11},{3,10},{4,13},{5,12},{6,15},{7,14},{8,1},{9,0},... | collective-permute-start | bytes 98312 | tf_op jit(solution)/shard_map/ppermute | solution.py:168
  (52 shorter events, 15.3 us)
Async XLA Ops:
  0.0 17.8 %collective-permute-start.3 = (bf16[768,2048]{1,0:T(8,128)(2,1)}, bf16[768,2048]{1,0:T(8,128)(2,1)S(1)}, u32[]{:S(2)}, u32[]{:S(2)}) collective-permute-start(bf16[768,2048]{1,0:T(8,128)(2,1)} %bitcast.11), channel_id=1, source_target_pairs={{0,1},{1,0},{2,3},{3,2},{4,5},{5,4},{6,7},{7,6},{8,9},{9,8},{10,11... | collective-permute-start | bytes 9437192 | tf_op jit(solution)/shard_map/ppermute | solution.py:163
  0.5 17.4 %collective-permute-start.4 = (bf16[768,2048]{1,0:T(8,128)(2,1)}, bf16[768,2048]{1,0:T(8,128)(2,1)S(1)}, u32[]{:S(2)}, u32[]{:S(2)}) collective-permute-start(bf16[768,2048]{1,0:T(8,128)(2,1)} %bitcast.14), channel_id=1, source_target_pairs={{0,1},{1,0},{2,3},{3,2},{4,5},{5,4},{6,7},{7,6},{8,9},{9,8},{10,11... | collective-permute-start | bytes 9437192 | tf_op jit(solution)/shard_map/ppermute | solution.py:163
  0.5 56.0 %collective-permute-start.13 = (bf16[384,2048]{1,0:T(8,128)(2,1)}, bf16[384,2048]{1,0:T(8,128)(2,1)S(1)}, u32[]{:S(2)}, u32[]{:S(2)}) collective-permute-start(bf16[384,2048]{1,0:T(8,128)(2,1)} %bitcast.17), channel_id=1, source_target_pairs={{0,1},{1,0},{2,3},{3,2},{4,5},{5,4},{6,7},{7,6},{8,9},{9,8},{10,11... | collective-permute-start | bytes 4718600 | tf_op jit(solution)/shard_map/ppermute | solution.py:163
  1.0 55.5 %collective-permute-start.14 = (bf16[384,2048]{1,0:T(8,128)(2,1)}, bf16[384,2048]{1,0:T(8,128)(2,1)S(1)}, u32[]{:S(2)}, u32[]{:S(2)}) collective-permute-start(bf16[384,2048]{1,0:T(8,128)(2,1)} %bitcast.19), channel_id=1, source_target_pairs={{0,1},{1,0},{2,3},{3,2},{4,5},{5,4},{6,7},{7,6},{8,9},{9,8},{10,11... | collective-permute-start | bytes 4718600 | tf_op jit(solution)/shard_map/ppermute | solution.py:163
  1.8 16.0 %copy-start = (bf16[1,768,2048]{2,1,0:T(8,128)(2,1)S(1)}, bf16[1,768,2048]{2,1,0:T(8,128)(2,1)}, u32[]{:S(2)}) copy-start(bf16[1,768,2048]{2,1,0:T(8,128)(2,1)} %param.14) | copy-start | bytes 9437188
  1.8 16.0 %copy-start.1 = (bf16[1,768,2048]{2,1,0:T(8,128)(2,1)S(1)}, bf16[1,768,2048]{2,1,0:T(8,128)(2,1)}, u32[]{:S(2)}) copy-start(bf16[1,768,2048]{2,1,0:T(8,128)(2,1)} %param.15) | copy-start | bytes 9437188
  2.6 5.4 %collective-permute-start = (bf16[8,2176]{1,0:T(8,128)(2,1)S(1)}, bf16[8,2176]{1,0:T(8,128)(2,1)S(1)}, u32[]{:S(2)}, u32[]{:S(2)}) collective-permute-start(bf16[8,2176]{1,0:T(8,128)(2,1)S(1)} %shard_map.92.first), channel_id=1, source_target_pairs={{0,9},{1,8},{2,11},{3,10},{4,13},{5,12},{6,15},{7,14},{8,1},{9,0},... | collective-permute-start | bytes 104456 | tf_op jit(solution)/shard_map/ppermute | solution.py:168
  8.0 4.2 %collective-permute-start.1 = (bf16[16,2176]{1,0:T(8,128)(2,1)S(1)}, bf16[16,2176]{1,0:T(8,128)(2,1)S(1)}, u32[]{:S(2)}, u32[]{:S(2)}) collective-permute-start(bf16[16,2176]{1,0:T(8,128)(2,1)S(1)} %bitcast.27), channel_id=1, source_target_pairs={{0,5},{1,4},{2,7},{3,6},{4,1},{5,0},{6,3},{7,2},{8,13},{9,12},{10,... | collective-permute-start | bytes 208904 | tf_op jit(solution)/shard_map/ppermute | solution.py:168
  12.2 23.9 %copy-start.5 = (bf16[1,8,2048]{2,1,0:T(8,128)(2,1)S(1)}, bf16[1,8,2048]{2,1,0:T(8,128)(2,1)}, u32[]{:S(2)}) copy-start(bf16[1,8,2048]{2,1,0:T(8,128)(2,1)} %param.9) | copy-start | bytes 98308
  12.2 23.9 %copy-start.9 = (s32[1,4]{1,0:T(1,128)S(1)}, s32[1,4]{1,0:T(1,128)}, u32[]{:S(2)}) copy-start(s32[1,4]{1,0:T(1,128)} %changed.1) | copy-start | bytes 52
  12.2 5.6 %collective-permute-start.2 = (bf16[32,2176]{1,0:T(8,128)(2,1)S(1)}, bf16[32,2176]{1,0:T(8,128)(2,1)S(1)}, u32[]{:S(2)}, u32[]{:S(2)}) collective-permute-start(bf16[32,2176]{1,0:T(8,128)(2,1)S(1)} %bitcast.25), channel_id=1, source_target_pairs={{0,3},{1,2},{2,1},{3,0},{4,7},{5,6},{6,5},{7,4},{8,11},{9,10},{10,... | collective-permute-start | bytes 417800 | tf_op jit(solution)/shard_map/ppermute | solution.py:168
  21.3 5.6 %collective-permute-start.5 = (bf16[32,2048]{1,0:T(8,128)(2,1)S(1)}, bf16[32,2048]{1,0:T(8,128)(2,1)S(1)}, u32[]{:S(2)}, u32[]{:S(2)}) collective-permute-start(bf16[32,2048]{1,0:T(8,128)(2,1)S(1)} %get-tuple-element.24), channel_id=1, source_target_pairs={{0,3},{1,2},{2,1},{3,0},{4,7},{5,6},{6,5},{7,4},{8,11},{9,10},{10,... | collective-permute-start | bytes 393224 | tf_op jit(solution)/shard_map/ppermute | solution.py:168
  26.9 4.4 %collective-permute-start.6 = (bf16[16,2048]{1,0:T(8,128)(2,1)S(1)}, bf16[16,2048]{1,0:T(8,128)(2,1)S(1)}, u32[]{:S(2)}, u32[]{:S(2)}) collective-permute-start(bf16[16,2048]{1,0:T(8,128)(2,1)S(1)} %get-tuple-element.26), channel_id=1, source_target_pairs={{0,5},{1,4},{2,7},{3,6},{4,1},{5,0},{6,3},{7,2},{8,13},{9,12},{10,... | collective-permute-start | bytes 196616 | tf_op jit(solution)/shard_map/ppermute | solution.py:168
  31.3 4.8 %collective-permute-start.7 = (bf16[8,2048]{1,0:T(8,128)(2,1)S(1)}, bf16[8,2048]{1,0:T(8,128)(2,1)S(1)}, u32[]{:S(2)}, u32[]{:S(2)}) collective-permute-start(bf16[8,2048]{1,0:T(8,128)(2,1)S(1)} %get-tuple-element.28), channel_id=1, source_target_pairs={{0,9},{1,8},{2,11},{3,10},{4,13},{5,12},{6,15},{7,14},{8,1},{9,0},... | collective-permute-start | bytes 98312 | tf_op jit(solution)/shard_map/ppermute | solution.py:168
  36.3 4.3 %collective-permute-start.8 = (bf16[8,2176]{1,0:T(8,128)(2,1)S(1)}, bf16[8,2176]{1,0:T(8,128)(2,1)S(1)}, u32[]{:S(2)}, u32[]{:S(2)}) collective-permute-start(bf16[8,2176]{1,0:T(8,128)(2,1)S(1)} %get-tuple-element.30.first), channel_id=1, source_target_pairs={{0,9},{1,8},{2,11},{3,10},{4,13},{5,12},{6,15},{7,14},{8,1},{9,0},... | collective-permute-start | bytes 104456 | tf_op jit(solution)/shard_map/ppermute | solution.py:168
  40.6 4.7 %collective-permute-start.9 = (bf16[16,2176]{1,0:T(8,128)(2,1)S(1)}, bf16[16,2176]{1,0:T(8,128)(2,1)S(1)}, u32[]{:S(2)}, u32[]{:S(2)}) collective-permute-start(bf16[16,2176]{1,0:T(8,128)(2,1)S(1)} %bitcast.29), channel_id=1, source_target_pairs={{0,5},{1,4},{2,7},{3,6},{4,1},{5,0},{6,3},{7,2},{8,13},{9,12},{10,... | collective-permute-start | bytes 208904 | tf_op jit(solution)/shard_map/ppermute | solution.py:168
  45.4 5.7 %collective-permute-start.10 = (bf16[32,2176]{1,0:T(8,128)(2,1)S(1)}, bf16[32,2176]{1,0:T(8,128)(2,1)S(1)}, u32[]{:S(2)}, u32[]{:S(2)}) collective-permute-start(bf16[32,2176]{1,0:T(8,128)(2,1)S(1)} %bitcast.21), channel_id=1, source_target_pairs={{0,3},{1,2},{2,1},{3,0},{4,7},{5,6},{6,5},{7,4},{8,11},{9,10},{10,... | collective-permute-start | bytes 417800 | tf_op jit(solution)/shard_map/ppermute | solution.py:168
  46.7 9.9 %collective-permute-start.11 = (bf16[32,2176]{1,0:T(8,128)(2,1)S(1)}, bf16[32,2176]{1,0:T(8,128)(2,1)S(1)}, u32[]{:S(2)}, u32[]{:S(2)}) collective-permute-start(bf16[32,2176]{1,0:T(8,128)(2,1)S(1)} %bitcast.22), channel_id=1, source_target_pairs={{0,17},{1,16},{2,19},{3,18},{4,21},{5,20},{6,23},{7,22},{8,25},{9,... | collective-permute-start | bytes 417800 | tf_op jit(solution)/shard_map/ppermute | solution.py:174
  51.1 5.4 %collective-permute-start.12 = (bf16[32,2176]{1,0:T(8,128)(2,1)S(1)}, bf16[32,2176]{1,0:T(8,128)(2,1)S(1)}, u32[]{:S(2)}, u32[]{:S(2)}) collective-permute-start(bf16[32,2176]{1,0:T(8,128)(2,1)S(1)} %collective-permute-done.10.refs_1_), channel_id=1, source_target_pairs={{0,17},{1,16},{2,19},{3,18},{4,21},{5,20},{6,23},{7,22},{8,25},{9,... | collective-permute-start | bytes 417800 | tf_op jit(solution)/shard_map/ppermute | solution.py:174
  58.7 5.4 %collective-permute-start.16 = (bf16[32,2048]{1,0:T(8,128)(2,1)S(1)}, bf16[32,2048]{1,0:T(8,128)(2,1)S(1)}, u32[]{:S(2)}, u32[]{:S(2)}) collective-permute-start(bf16[32,2048]{1,0:T(8,128)(2,1)S(1)} %get-tuple-element.36), channel_id=1, source_target_pairs={{0,3},{1,2},{2,1},{3,0},{4,7},{5,6},{6,5},{7,4},{8,11},{9,10},{10,... | collective-permute-start | bytes 393224 | tf_op jit(solution)/shard_map/ppermute | solution.py:168
  60.2 6.7 %collective-permute-start.15 = (bf16[32,2048]{1,0:T(8,128)(2,1)S(1)}, bf16[32,2048]{1,0:T(8,128)(2,1)S(1)}, u32[]{:S(2)}, u32[]{:S(2)}) collective-permute-start(bf16[32,2048]{1,0:T(8,128)(2,1)S(1)} %get-tuple-element.34), channel_id=1, source_target_pairs={{0,3},{1,2},{2,1},{3,0},{4,7},{5,6},{6,5},{7,4},{8,11},{9,10},{10,... | collective-permute-start | bytes 393224 | tf_op jit(solution)/shard_map/ppermute | solution.py:168
  64.1 5.6 %collective-permute-start.17 = (bf16[32,2048]{1,0:T(8,128)(2,1)S(1)}, bf16[32,2048]{1,0:T(8,128)(2,1)S(1)}, u32[]{:S(2)}, u32[]{:S(2)}) collective-permute-start(bf16[32,2048]{1,0:T(8,128)(2,1)S(1)} %add_convert_fusion), channel_id=1, source_target_pairs={{0,17},{1,16},{2,19},{3,18},{4,21},{5,20},{6,23},{7,22},{8,25},{9,... | collective-permute-start | bytes 393224 | tf_op jit(solution)/shard_map/ppermute | solution.py:174
  69.8 3.8 %collective-permute-start.18 = (bf16[16,2048]{1,0:T(8,128)(2,1)S(1)}, bf16[16,2048]{1,0:T(8,128)(2,1)S(1)}, u32[]{:S(2)}, u32[]{:S(2)}) collective-permute-start(bf16[16,2048]{1,0:T(8,128)(2,1)S(1)} %get-tuple-element.38), channel_id=1, source_target_pairs={{0,5},{1,4},{2,7},{3,6},{4,1},{5,0},{6,3},{7,2},{8,13},{9,12},{10,... | collective-permute-start | bytes 196616 | tf_op jit(solution)/shard_map/ppermute | solution.py:168
  73.5 5.1 %collective-permute-start.19 = (bf16[8,2048]{1,0:T(8,128)(2,1)S(1)}, bf16[8,2048]{1,0:T(8,128)(2,1)S(1)}, u32[]{:S(2)}, u32[]{:S(2)}) collective-permute-start(bf16[8,2048]{1,0:T(8,128)(2,1)S(1)} %get-tuple-element.40), channel_id=1, source_target_pairs={{0,9},{1,8},{2,11},{3,10},{4,13},{5,12},{6,15},{7,14},{8,1},{9,0},... | collective-permute-start | bytes 98312 | tf_op jit(solution)/shard_map/ppermute | solution.py:168
  (6 other events, 25.3 us)

commit v11 on v8

--- a/solution.py
+++ b/solution.py
@@ -61,39 +61,55 @@
     out[...] = state * lax.rsqrt(jnp.mean(state * state, axis=-1, keepdims=True) + 1e-06)
 
 
-def pack_kernel(experts, scaled, gain, routes, scales, out):
-    width = scaled.shape[1]
+def pack_kernel(experts, scaled, gain, routes, scales, changed, out):
+    width, span = scaled.shape[1], table_width(experts)
     normed = (scaled[...] * gain[...]).astype(jnp.bfloat16)
-    table = weight_table(experts, routes[0, 0], scales[0, 0], [])
-    for j in range(out.shape[0]):
-        out[j, :, :width] = normed
-        out[j, :, width:] = table
-
-
-def next_kernel(experts, step, previous, returned, gain, routes, scales, changed, state_out, out):
-    width = previous.shape[1]
-    state = previous[...].astype(jnp.float32) + jnp.sum(returned[...].astype(jnp.float32), axis=0)
+    for chip in range(out.shape[0]):
+        out[chip, :, :width] = normed
+    for step in range(routes.shape[0]):
+        items = [changed[:, i : i + 1] for i in range(changed.shape[1])] if step > 0 else []
+        table = weight_table(experts, routes[step, 0], scales[step, 0], items)
+        for chip in range(out.shape[0]):
+            out[chip, :, width + step * span : width + (step + 1) * span] = table
+
+
+def sum_blocks(blocks):
+    total = blocks[0].astype(jnp.float32)
+    for chip in range(1, blocks.shape[0]):
+        total = total + blocks[chip].astype(jnp.float32)
+    return total
+
+
+def next_kernel(previous, returned, gain, state_out, out):
+    state = previous[...].astype(jnp.float32) + sum_blocks(returned)
     state_out[...] = state
     normed = normalize(state, gain[...])
-    items = [changed[0, i] for i in range(changed.shape[1])]
-    table = weight_table(experts, routes[step, 0], scales[step, 0], items)
-    for j in range(out.shape[0]):
-        out[j, :, :width] = normed
-        out[j, :, width:] = table
+    for chip in range(out.shape[0]):
+        out[chip] = normed
 
 
 def last_kernel(previous, returned, out):
-    state = previous[...] + jnp.sum(returned[...].astype(jnp.float32), axis=0)
-    out[...] = state.astype(jnp.bfloat16)
-
-
-def mlp_kernel(experts, fresh, row_sets, *refs):
-    sources, refs = refs[:row_sets], refs[row_sets:]
+    out[...] = (previous[...] + sum_blocks(returned)).astype(jnp.bfloat16)
+
+
+def fill(rows):
+    return jnp.concatenate([rows] * max(1, MATMUL_ROWS // rows.shape[0]), axis=0)
+
+
+def join_kernel(first, rows, tables, out):
+    width = rows.shape[1]
+    out[:, :width] = rows[...]
+    out[:, width:] = tables[:, first : first + out.shape[1] - width]
+
+
+def mlp_kernel(experts, fresh, set_count, *refs):
+    sources, refs = refs[:set_count], refs[set_count:]
     weights, outs = refs[:4], refs[4:]
     count, width = outs[0].shape
-    rows = jnp.concatenate([source[...] for source in sources], axis=0)
-    filled = jnp.concatenate([rows] * max(1, MATMUL_ROWS // rows.shape[0]), axis=0)
-    inputs, table = filled[:, :width], rows[:, width:]
+    span = table_width(experts)
+    rows = jnp.concatenate([source[:, :width] for source in sources], axis=0)
+    table = jnp.concatenate([source[:, width : width + span] for source in sources], axis=0)
+    inputs = jnp.concatenate([rows] * max(1, MATMUL_ROWS // rows.shape[0]), axis=0)
     own = lax.axis_index("expert")
     total = None
     for core in range(2):
@@ -110,101 +126,97 @@
         out[...] = total[i * count : (i + 1) * count].astype(out.dtype)
 
 
-def run_mlp(row_sets, weights, fresh, out_types):
-    experts = lax.axis_size("expert")
+def on_vmem(kernel, inputs, outputs, limit=4 * MIB, cost=None, after=()):
+    in_vmem = pl.BlockSpec(memory_space=pltpu.VMEM)
+    count = len(inputs)
+
+    def body(*refs):
+        kernel(*refs[:count], *refs[count + len(after) :])
+
+    return pl.pallas_call(
+        body,
+        out_shape=[jax.ShapeDtypeStruct(shape, kind) for shape, kind in outputs],
+        in_specs=[in_vmem] * count + [pl.BlockSpec(memory_space=pl.ANY)] * len(after),
+        out_specs=[in_vmem] * len(outputs),
+        compiler_params=pltpu.CompilerParams(vmem_limit_bytes=limit),
+        cost_estimate=cost,
+    )(*inputs, *after)
+
+
+def run_mlp(row_sets, weights, fresh, out_types, after=()):
     count, width = row_sets[0].shape[0], weights[0].shape[1]
-    hidden = sum(part.shape[0] for part in weights) // 2
-    in_vmem = pl.BlockSpec(memory_space=pltpu.VMEM)
-    return pl.pallas_call(
-        functools.partial(mlp_kernel, experts, fresh, len(row_sets)),
-        out_shape=[jax.ShapeDtypeStruct((count, width), out_type) for out_type in out_types],
-        in_specs=[in_vmem] * (len(row_sets) + len(weights)),
-        out_specs=[in_vmem] * len(out_types),
-        compiler_params=pltpu.CompilerParams(vmem_limit_bytes=16 * MIB),
-        cost_estimate=pl.CostEstimate(
-            flops=8 * count * hidden * width, bytes_accessed=4 * hidden * width, transcendentals=0
-        ),
-    )(*row_sets, *weights)
-
-
-def chip_groups(experts):
-    return [list(range(core, experts, 2)) for core in range(2)]
+    size = sum(part.size for part in weights)
+    cost = pl.CostEstimate(
+        flops=4 * MATMUL_ROWS * size, bytes_accessed=4 * size, transcendentals=0
+    )
+    kernel = functools.partial(mlp_kernel, lax.axis_size("expert"), fresh, len(row_sets))
+    outputs = [((count, width), out_type) for out_type in out_types]
+    return on_vmem(kernel, tuple(row_sets) + tuple(weights), outputs, 8 * MIB, cost, after)
+
+
+def swap_core(value):
+    size = lax.axis_size("expert")
+    return lax.ppermute(value, "expert", [(i, i ^ 1) for i in range(size)])
+
+
+def swap_group(value):
+    return lax.ppermute(value, "group", [(0, 1), (1, 0)])
 
 
 def spread(blocks):
-    return lax.all_to_all(
-        blocks, "expert", 0, 0, axis_index_groups=chip_groups(lax.axis_size("expert")), tiled=True
-    )
-
-
-def swap(value, axis):
-    size = lax.axis_size(axis)
-    return lax.ppermute(value, axis, [(i, i ^ 1) for i in range(size)])
+    size = lax.axis_size("expert")
+    groups = [list(range(core, size, 2)) for core in range(2)]
+    return lax.all_to_all(blocks, "expert", 0, 0, axis_index_groups=groups, tiled=True)
 
 
 def exchange_plan(tokens, norm_gain, routes, route_scale, changed, stale, learner):
     experts = lax.axis_size("expert")
     chips = experts // 2
     row_count, width = tokens.shape[1], tokens.shape[2]
-    packed = width + table_width(experts)
     half = chips * row_count
+    steps_total = routes.shape[0]
+    packed = width + steps_total * table_width(experts)
     gain = norm_gain[None]
-    blocks_shape = jax.ShapeDtypeStruct((chips, row_count, packed), jnp.bfloat16)
-    state_shape = jax.ShapeDtypeStruct((row_count, width), jnp.float32)
-    in_vmem = pl.BlockSpec(memory_space=pltpu.VMEM)
-    in_smem = pl.BlockSpec(memory_space=pltpu.SMEM)
-    small = pltpu.CompilerParams(vmem_limit_bytes=4 * MIB)
+    state_shape = ((row_count, width), jnp.float32)
     weight_bytes = 2 * sum(part.size for part in stale + learner)
     long = pl.CostEstimate(
         flops=1280 * weight_bytes, bytes_accessed=2 * weight_bytes, transcendentals=0
     )
-    stale = stale + tuple(swap(part, "expert") for part in stale)
-    learner = learner + tuple(swap(part, "expert") for part in learner)
-    state = tokens[0]
-    for step in range(routes.shape[0]):
+    stale = stale + tuple(swap_core(part) for part in stale)
+    learner = learner + tuple(swap_core(part) for part in learner)
+    (scaled,) = on_vmem(first_kernel, (tokens[0],), [state_shape], cost=long)
+    (blocks,) = on_vmem(
+        functools.partial(pack_kernel, experts),
+        (scaled, gain, routes, route_scale, changed),
+        [((chips, row_count, packed), jnp.bfloat16)],
+    )
+    tables = spread(blocks).reshape(half, packed)
+    rows, state = tables, tokens[0]
+    for step in range(steps_total):
         if step == 0:
-            scaled = pl.pallas_call(
-                first_kernel,
-                in_specs=[in_vmem],
-                out_specs=in_vmem,
-                out_shape=state_shape,
-                compiler_params=small,
-                cost_estimate=long,
-            )(state)
-            blocks = pl.pallas_call(
-                functools.partial(pack_kernel, experts),
-                in_specs=[in_vmem] * 4,
-                out_specs=in_vmem,
-                out_shape=blocks_shape,
-                compiler_params=small,
-            )(scaled, gain, routes, route_scale)
+            (share,) = run_mlp([rows], stale, False, [jnp.bfloat16], learner[2:])
         else:
-            state, blocks = pl.pallas_call(
-                functools.partial(next_kernel, experts, step),
-                in_specs=[in_vmem] * 5 + [in_smem],
-                out_specs=(in_vmem, in_vmem),
-                out_shape=(state_shape, blocks_shape),
-                compiler_params=small,
-                cost_estimate=long,
-            )(state, returned, gain, routes, route_scale, changed)
-        rows = spread(blocks).reshape(half, packed)
-        if step == 0:
-            (share,) = run_mlp([rows], stale, False, [jnp.bfloat16])
-        else:
-            other = swap(rows, "group")
+            state, blocks = on_vmem(
+                next_kernel,
+                (state, returned, gain),
+                [state_shape, ((chips, row_count, width), jnp.bfloat16)],
+            )
+            rows = spread(blocks).reshape(half, width)
+            span = table_width(experts)
+            (rows,) = on_vmem(
+                functools.partial(join_kernel, width + step * span),
+                (rows, tables),
+                [((half, width + span), jnp.bfloat16)],
+            )
+            other = swap_group(rows)
             (old,) = run_mlp([rows], stale, False, [jnp.float32])
             other, old = lax.optimization_barrier((other, old))
             new, away = run_mlp([rows, other], learner, True, [jnp.float32, jnp.bfloat16])
-            share = old + new + swap(away, "group").astype(jnp.float32)
+            share = old + new + swap_group(away).astype(jnp.float32)
             share = share.astype(jnp.bfloat16)
         returned = spread(share.reshape(chips, row_count, width))
-    return pl.pallas_call(
-        last_kernel,
-        in_specs=[in_vmem] * 2,
-        out_specs=in_vmem,
-        out_shape=jax.ShapeDtypeStruct((row_count, width), jnp.bfloat16),
-        compiler_params=small,
-    )(state, returned)[None]
+    (updated,) = on_vmem(last_kernel, (state, returned), [((row_count, width), jnp.bfloat16)])
+    return updated[None]
 
 
 def gather_plan(tokens, norm_gain, routes, route_scale, changed, stale, learner):
@@ -258,7 +270,7 @@
     experts = lax.axis_size("expert")
     groups = lax.axis_size("group")
     fewer = tokens.shape[1] * experts < learner_up.shape[1]
-    paired = experts % 2 == 0 and groups == 2 and routes.shape[0] == 2
+    paired = experts % 2 == 0 and groups == 2
     plan = exchange_plan if fewer and paired else gather_plan
     stale = (rollout_up[0], rollout_down[0])
     learner = (learner_up[0], learner_down[0])

time: 80 us -> 77.1 us (0.964)
  blocking collectives: 43.1 us -> 54.5 us
  waiting for transfers between devices: 14.2 us -> 6.49 us
  starting transfers between devices: 7.53 us -> 4.13 us
  Pallas kernels: 13.2 us -> 10.1 us
    all_to_all x3 -> x4, blocking collectives: 43.1 us -> 54.5 us  [spread(): lax.all_to_all(blocks, 'expert', 0, 0, axis_index_groups=groups, tiled=True)]
    all_to_all x1 -> x0, waiting for transfers between devices: 7.76 us -> none  [spread(): lax.all_to_all(blocks, 'expert', 0, 0, axis_index_groups=chip_groups(lax....]
    all_to_all x1 -> x0, starting transfers between devices: 3.41 us -> none  [spread(): lax.all_to_all(blocks, 'expert', 0, 0, axis_index_groups=chip_groups(lax....]
    pallas_call x7 -> x8, Pallas kernels: 13.2 us -> 10.1 us  [on_vmem(): pl.pallas_call(body, out_shape=[jax.ShapeDtypeStruct(shape, kind) for sha...]
  transfers between devices with their start and end apart: 7 -> 6, of which waited for: 3 -> 2; matrix products, arithmetic and copies ran while one was open for 0% -> 0% of each run, Pallas kernels for 5% -> 5%
where the time goes in v11:
time: 77.1 us; the launch traced here: 76.8 us
  blocking collectives  54.5 us (71%)
  Pallas kernels  10.1 us (13%)
  waiting for transfers between devices  6.49 us (8%)
  starting transfers between devices  4.13 us (5%)
  local copies, waits for them, and re-layouts  1.39 us (2%)
    all_to_all x4, blocking collectives, spread(): lax.all_to_all(blocks, 'expert', 0, 0, axis_index_groups=groups, tiled=True)  54.5 us
    pallas_call x8, Pallas kernels, on_vmem(): pl.pallas_call(body, out_shape=[jax.ShapeDtypeStruct(shape, kind) for sha...  10.1 us
    ppermute x2, waiting for transfers between devices, swap_group(): return lax.ppermute(value, 'group', [(0, 1), (1, 0)])  6.47 us
    ppermute x2, starting transfers between devices, swap_group(): return lax.ppermute(value, 'group', [(0, 1), (1, 0)])  3.11 us
  transfers between devices with their start and end apart: 6, of which 2 were waited for; matrix products, arithmetic and copies ran while one was open for 0% of the time, Pallas kernels for 5%

profile of v11, /device:TPU:0, one launch (start us, length us, event | category | flops | bytes accessed | tf_op | source)
XLA Modules:
  0.0 76.8 jit_solution(8688201831960564799)
XLA Ops:
  0.0 0.5 collective-permute-start
  0.5 0.1 collective-permute-start.1
  0.5 0.5 collective-permute-start.2
  1.0 0.1 collective-permute-start.3
  1.0 0.8 copy-done.4
  1.8 0.1 shard_map.91.refs_0_
  1.9 0.6 copy-done.6
  2.5 0.0 copy-done.7
  2.5 0.0 copy-done.8
  2.5 0.1 shard_map.92
  2.6 17.8 %all_to_all.20 = bf16[8,8,2304]{2,1,0:T(8,128)(2,1)S(1)} all-to-all(bf16[8,8,2304]{2,1,0:T(8,128)(2,1)S(1)} %shard_map.92), channel_id=1, replica_groups={{0,2,4,6,8,10,12,14},{1,3,5,7,9,11,13,15},{16,18,20,22,24,26,28,30},{17..., dimensions={0} | all-to-all | bytes 589824 | tf_op jit(solution)/shard_map/all_to_all | solution.py:169
  20.6 3.5 %shard_map.93 = bf16[64,2048]{1,0:T(8,128)(2,1)S(1)} custom-call(bf16[64,2304]{1,0:T(8,128)(2,1)S(1)} %bitcast.18, bf16[768,2048]{1,0:T(8,128)(2,1)S(1)} %bitcast.13, bf16[768,2048]{1,0:T(8,128)(2,1)S(1)} %bitcast.16, bf16[768,2048]{1,0:T(8,128)(2,1)S(1)} %collective-permute-done.refs_3_, bf16[768,2048]{1,0:T(8,128)(2,1)S(1)} %collective-permute-done.1.refs_4_, ...), custom_call_target="tpu_custom_call" | custom-call | flops 3221225472 | bytes 25165824 | tf_op jit(solution)/shard_map/pallas_call | solution.py:136
  24.0 11.5 %all_to_all.21.refs_1_ = bf16[8,8,2048]{2,1,0:T(8,128)(2,1)S(1)} all-to-all(bf16[8,8,2048]{2,1,0:T(8,128)(2,1)S(1)} %bitcast.24), channel_id=1, replica_groups={{0,2,4,6,8,10,12,14},{1,3,5,7,9,11,13,15},{16,18,20,22,24,26,28,30},{17..., dimensions={0} | all-to-all | bytes 524288 | tf_op jit(solution)/shard_map/all_to_all | solution.py:169
  35.5 0.2 shard_map.94
  35.6 12.0 %all_to_all.22 = bf16[8,8,2048]{2,1,0:T(8,128)(2,1)S(1)} all-to-all(bf16[8,8,2048]{2,1,0:T(8,128)(2,1)S(1)} %get-tuple-element.12), channel_id=1, replica_groups={{0,2,4,6,8,10,12,14},{1,3,5,7,9,11,13,15},{16,18,20,22,24,26,28,30},{17..., dimensions={0} | all-to-all | bytes 524288 | tf_op jit(solution)/shard_map/all_to_all | solution.py:169
  47.6 1.6 %collective-permute-start.4 = (bf16[64,2176]{1,0:T(8,128)(2,1)S(1)}, bf16[64,2176]{1,0:T(8,128)(2,1)S(1)}, u32[]{:S(2)}, u32[]{:S(2)}) collective-permute-start(bf16[64,2176]{1,0:T(8,128)(2,1)S(1)} %shard_map.95.refs_0_), channel_id=1, source_target_pairs={{0,16},{16,0},{1,17},{17,1},{2,18},{18,2},{3,19},{19,3},{4,20},{20... | collective-permute-start | bytes 835592 | tf_op jit(solution)/shard_map/ppermute | solution.py:163
  49.2 3.5 %shard_map.96 = f32[64,2048]{1,0:T(8,128)S(1)} custom-call(bf16[64,2176]{1,0:T(8,128)(2,1)S(1)} %shard_map.95.refs_0_, bf16[768,2048]{1,0:T(8,128)(2,1)S(1)} %bitcast.14, bf16[768,2048]{1,0:T(8,128)(2,1)S(1)} %bitcast.17, bf16[768,2048]{1,0:T(8,128)(2,1)S(1)} %collective-permute-done.refs_3_, bf16[768,2048]{1,0:T(8,128)(2,1)S(1)} %collective-permute-done.1.refs_4_), custom_call_target="tpu_custom_call" | custom-call | flops 3221225472 | bytes 25165824 | tf_op jit(solution)/shard_map/pallas_call | solution.py:136
  52.7 1.6 %collective-permute-done.4.refs_1_ = bf16[64,2176]{1,0:T(8,128)(2,1)S(1)} collective-permute-done((bf16[64,2176]{1,0:T(8,128)(2,1)S(1)}, bf16[64,2176]{1,0:T(8,128)(2,1)S(1)}, u32[]{:S(2)}, u32[]{:S(2)}) %collective-permute-start.4) | collective-permute-done | bytes 278560 | tf_op jit(solution)/shard_map/ppermute | solution.py:163
  54.3 2.1 %shard_map.97 = (f32[64,2048]{1,0:T(8,128)S(1)}, bf16[64,2048]{1,0:T(8,128)(2,1)S(1)}) custom-call(bf16[64,2176]{1,0:T(8,128)(2,1)S(1)} %shard_map.95.refs_0_, bf16[64,2176]{1,0:T(8,128)(2,1)S(1)} %collective-permute-done.4.refs_1_, bf16[384,2048]{1,0:T(8,128)(2,1)S(1)} %bitcast.21, bf16[384,2048]{1,0:T(8,128)(2,1)S(1)} %bitcast.23, ...), custom_call_target="tpu_custom_call" | custom-call | flops 1610612736 | bytes 12582912 | tf_op jit(solution)/shard_map/pallas_call | solution.py:136
  56.4 1.6 %collective-permute-start.5 = (bf16[64,2048]{1,0:T(8,128)(2,1)S(1)}, bf16[64,2048]{1,0:T(8,128)(2,1)S(1)}, u32[]{:S(2)}, u32[]{:S(2)}) collective-permute-start(bf16[64,2048]{1,0:T(8,128)(2,1)S(1)} %get-tuple-element.16), channel_id=1, source_target_pairs={{0,16},{16,0},{1,17},{17,1},{2,18},{18,2},{3,19},{19,3},{4,20},{20... | collective-permute-start | bytes 786440 | tf_op jit(solution)/shard_map/ppermute | solution.py:163
  57.9 4.9 %collective-permute-done.5 = bf16[64,2048]{1,0:T(8,128)(2,1)S(1)} collective-permute-done((bf16[64,2048]{1,0:T(8,128)(2,1)S(1)}, bf16[64,2048]{1,0:T(8,128)(2,1)S(1)}, u32[]{:S(2)}, u32[]{:S(2)}) %collective-permute-start.5) | collective-permute-done | bytes 262176 | tf_op jit(solution)/shard_map/ppermute | solution.py:163
  62.8 0.1 fusion
  62.9 13.2 %all_to_all.23.refs_1_ = bf16[8,8,2048]{2,1,0:T(8,128)(2,1)S(1)} all-to-all(bf16[8,8,2048]{2,1,0:T(8,128)(2,1)S(1)} %fusion), channel_id=1, replica_groups={{0,2,4,6,8,10,12,14},{1,3,5,7,9,11,13,15},{16,18,20,22,24,26,28,30},{17..., dimensions={0} | all-to-all | bytes 524288 | tf_op jit(solution)/shard_map/all_to_all | solution.py:169
  76.1 0.7 shard_map.98
  (21 shorter events, 0.1 us)
Async XLA Ops:
  0.0 20.5 %collective-permute-start = (bf16[768,2048]{1,0:T(8,128)(2,1)}, bf16[768,2048]{1,0:T(8,128)(2,1)S(1)}, u32[]{:S(2)}, u32[]{:S(2)}) collective-permute-start(bf16[768,2048]{1,0:T(8,128)(2,1)} %bitcast.12), channel_id=1, source_target_pairs={{0,1},{1,0},{2,3},{3,2},{4,5},{5,4},{6,7},{7,6},{8,9},{9,8},{10,11... | collective-permute-start | bytes 9437192 | tf_op jit(solution)/shard_map/ppermute | solution.py:159
  0.5 20.1 %collective-permute-start.1 = (bf16[768,2048]{1,0:T(8,128)(2,1)}, bf16[768,2048]{1,0:T(8,128)(2,1)S(1)}, u32[]{:S(2)}, u32[]{:S(2)}) collective-permute-start(bf16[768,2048]{1,0:T(8,128)(2,1)} %bitcast.15), channel_id=1, source_target_pairs={{0,1},{1,0},{2,3},{3,2},{4,5},{5,4},{6,7},{7,6},{8,9},{9,8},{10,11... | collective-permute-start | bytes 9437192 | tf_op jit(solution)/shard_map/ppermute | solution.py:159
  0.5 20.0 %collective-permute-start.2 = (bf16[384,2048]{1,0:T(8,128)(2,1)}, bf16[384,2048]{1,0:T(8,128)(2,1)S(1)}, u32[]{:S(2)}, u32[]{:S(2)}) collective-permute-start(bf16[384,2048]{1,0:T(8,128)(2,1)} %bitcast.20), channel_id=1, source_target_pairs={{0,1},{1,0},{2,3},{3,2},{4,5},{5,4},{6,7},{7,6},{8,9},{9,8},{10,11... | collective-permute-start | bytes 4718600 | tf_op jit(solution)/shard_map/ppermute | solution.py:159
  1.0 19.5 %collective-permute-start.3 = (bf16[384,2048]{1,0:T(8,128)(2,1)}, bf16[384,2048]{1,0:T(8,128)(2,1)S(1)}, u32[]{:S(2)}, u32[]{:S(2)}) collective-permute-start(bf16[384,2048]{1,0:T(8,128)(2,1)} %bitcast.22), channel_id=1, source_target_pairs={{0,1},{1,0},{2,3},{3,2},{4,5},{5,4},{6,7},{7,6},{8,9},{9,8},{10,11... | collective-permute-start | bytes 4718600 | tf_op jit(solution)/shard_map/ppermute | solution.py:159
  1.0 0.8 copy-start.4
  1.8 0.7 copy-start.6
  1.8 0.7 copy-start.7
  1.8 0.7 copy-start.8
  1.8 0.7 copy-start.9
  1.8 18.7 %copy-start = (bf16[1,768,2048]{2,1,0:T(8,128)(2,1)S(1)}, bf16[1,768,2048]{2,1,0:T(8,128)(2,1)}, u32[]{:S(2)}) copy-start(bf16[1,768,2048]{2,1,0:T(8,128)(2,1)} %param.14) | copy-start | bytes 9437188
  1.8 18.7 %copy-start.1 = (bf16[1,768,2048]{2,1,0:T(8,128)(2,1)S(1)}, bf16[1,768,2048]{2,1,0:T(8,128)(2,1)}, u32[]{:S(2)}) copy-start(bf16[1,768,2048]{2,1,0:T(8,128)(2,1)} %param.15) | copy-start | bytes 9437188
  20.5 14.9 %copy-start.5 = (bf16[1,8,2048]{2,1,0:T(8,128)(2,1)S(1)}, bf16[1,8,2048]{2,1,0:T(8,128)(2,1)}, u32[]{:S(2)}) copy-start(bf16[1,8,2048]{2,1,0:T(8,128)(2,1)} %param.9) | copy-start | bytes 98308
  47.6 6.6 %copy-start.2 = (bf16[1,384,2048]{2,1,0:T(8,128)(2,1)S(1)}, bf16[1,384,2048]{2,1,0:T(8,128)(2,1)}, u32[]{:S(2)}) copy-start(bf16[1,384,2048]{2,1,0:T(8,128)(2,1)} %param.16) | copy-start | bytes 4718596
  47.6 6.6 %copy-start.3 = (bf16[1,384,2048]{2,1,0:T(8,128)(2,1)S(1)}, bf16[1,384,2048]{2,1,0:T(8,128)(2,1)}, u32[]{:S(2)}) copy-start(bf16[1,384,2048]{2,1,0:T(8,128)(2,1)} %param.17) | copy-start | bytes 4718596
  47.6 6.6 %collective-permute-start.4 = (bf16[64,2176]{1,0:T(8,128)(2,1)S(1)}, bf16[64,2176]{1,0:T(8,128)(2,1)S(1)}, u32[]{:S(2)}, u32[]{:S(2)}) collective-permute-start(bf16[64,2176]{1,0:T(8,128)(2,1)S(1)} %shard_map.95.refs_0_), channel_id=1, source_target_pairs={{0,16},{16,0},{1,17},{17,1},{2,18},{18,2},{3,19},{19,3},{4,20},{20... | collective-permute-start | bytes 835592 | tf_op jit(solution)/shard_map/ppermute | solution.py:163
  56.4 6.4 %collective-permute-start.5 = (bf16[64,2048]{1,0:T(8,128)(2,1)S(1)}, bf16[64,2048]{1,0:T(8,128)(2,1)S(1)}, u32[]{:S(2)}, u32[]{:S(2)}) collective-permute-start(bf16[64,2048]{1,0:T(8,128)(2,1)S(1)} %get-tuple-element.16), channel_id=1, source_target_pairs={{0,16},{16,0},{1,17},{17,1},{2,18},{18,2},{3,19},{19,3},{4,20},{20... | collective-permute-start | bytes 786440 | tf_op jit(solution)/shard_map/ppermute | solution.py:163

commit v12 on v11

--- a/solution.py
+++ b/solution.py
@@ -24,35 +24,47 @@
     return jnp.dot(hidden, down_rows, preferred_element_type=jnp.float32)
 
 
-def table_width(experts):
-    return -(-6 * experts // LANES) * LANES
+def table_width(experts, steps_total):
+    sections = 2 + 4 * (steps_total - 1)
+    return -(-sections * experts // LANES) * LANES
+
+
+def first_section(step, fresh):
+    return 0 if step == 0 else 4 * step - 2 + 2 * fresh
 
 
 def weight_table(experts, chosen, weights, changed):
-    shape = (chosen.shape[0], table_width(experts))
+    steps_total, _, rows, top_count = chosen.shape
+    shape = (rows, table_width(experts, steps_total))
     lane = lax.broadcasted_iota(jnp.int32, shape, 1)
     section, expert = lane // experts, lane % experts
-    dense = jnp.zeros(shape, jnp.float32)
-    for k in range(chosen.shape[1]):
-        dense = jnp.where(chosen[:, k : k + 1] == expert, weights[:, k : k + 1], dense)
     fresh = section < 0
-    for item in changed:
-        fresh = fresh | (expert == item)
-    high = dense.astype(jnp.bfloat16).astype(jnp.float32)
-    rest = dense - high
-    middle = rest.astype(jnp.bfloat16).astype(jnp.float32)
-    low = rest - middle
-    part = section % 3
-    value = jnp.where(part == 0, high, jnp.where(part == 1, middle, low))
-    value = jnp.where(fresh, jnp.where(section < 3, 0.0, value), jnp.where(section < 3, value, 0.0))
-    return jnp.where(section < 6, value, 0.0).astype(jnp.bfloat16)
-
-
-def row_weights(experts, table, owner, fresh):
+    for i in range(changed.shape[1]):
+        fresh = fresh | (expert == changed[:, i : i + 1])
+    table = jnp.zeros(shape, jnp.float32)
+    for step in range(steps_total):
+        dense = jnp.zeros(shape, jnp.float32)
+        for k in range(top_count):
+            hit = chosen[step, 0, :, k : k + 1] == expert
+            dense = jnp.where(hit, weights[step, 0, :, k : k + 1], dense)
+        high = dense.astype(jnp.bfloat16).astype(jnp.float32)
+        value = jnp.where(section % 2 == 0, high, dense - high)
+        start = first_section(step, False)
+        if step == 0:
+            table = jnp.where(section < 2, value, table)
+        else:
+            old = jnp.where(fresh, 0.0, value)
+            new = jnp.where(fresh, value, 0.0)
+            table = jnp.where((section >= start) & (section < start + 2), old, table)
+            table = jnp.where((section >= start + 2) & (section < start + 4), new, table)
+    return table.astype(jnp.bfloat16)
+
+
+def row_weights(experts, table, owner, step, fresh):
     lane = lax.broadcasted_iota(jnp.int32, table.shape, 1)
     section = lane // experts
-    first = 3 if fresh else 0
-    mine = (lane % experts == owner) & (section >= first) & (section < first + 3)
+    first = first_section(step, fresh)
+    mine = (lane % experts == owner) & (section >= first) & (section < first + 2)
     return jnp.sum(jnp.where(mine, table.astype(jnp.float32), 0.0), axis=1, keepdims=True)
 
 
@@ -62,15 +74,12 @@
 
 
 def pack_kernel(experts, scaled, gain, routes, scales, changed, out):
-    width, span = scaled.shape[1], table_width(experts)
+    width = scaled.shape[1]
     normed = (scaled[...] * gain[...]).astype(jnp.bfloat16)
+    table = weight_table(experts, routes, scales, changed)
     for chip in range(out.shape[0]):
         out[chip, :, :width] = normed
-    for step in range(routes.shape[0]):
-        items = [changed[:, i : i + 1] for i in range(changed.shape[1])] if step > 0 else []
-        table = weight_table(experts, routes[step, 0], scales[step, 0], items)
-        for chip in range(out.shape[0]):
-            out[chip, :, width + step * span : width + (step + 1) * span] = table
+        out[chip, :, width:] = table
 
 
 def sum_blocks(blocks):
@@ -92,23 +101,18 @@
     out[...] = (previous[...] + sum_blocks(returned)).astype(jnp.bfloat16)
 
 
-def fill(rows):
-    return jnp.concatenate([rows] * max(1, MATMUL_ROWS // rows.shape[0]), axis=0)
-
-
-def join_kernel(first, rows, tables, out):
+def join_kernel(rows, tables, out):
     width = rows.shape[1]
     out[:, :width] = rows[...]
-    out[:, width:] = tables[:, first : first + out.shape[1] - width]
-
-
-def mlp_kernel(experts, fresh, set_count, *refs):
+    out[:, width:] = tables[:, width:]
+
+
+def mlp_kernel(experts, step, fresh, set_count, *refs):
     sources, refs = refs[:set_count], refs[set_count:]
     weights, outs = refs[:4], refs[4:]
     count, width = outs[0].shape
-    span = table_width(experts)
     rows = jnp.concatenate([source[:, :width] for source in sources], axis=0)
-    table = jnp.concatenate([source[:, width : width + span] for source in sources], axis=0)
+    table = jnp.concatenate([source[:, width:] for source in sources], axis=0)
     inputs = jnp.concatenate([rows] * max(1, MATMUL_ROWS // rows.shape[0]), axis=0)
     own = lax.axis_index("expert")
     total = None
@@ -120,7 +124,7 @@
         )
         hidden = (pre_act / (1.0 + jnp.exp(-pre_act))).astype(jnp.bfloat16)
         result = jnp.dot(hidden, down[...], preferred_element_type=jnp.float32)
-        result = result[: rows.shape[0]] * row_weights(experts, table, owner, fresh)
+        result = result[: rows.shape[0]] * row_weights(experts, table, owner, step, fresh)
         total = result if total is None else total + result
     for i, out in enumerate(outs):
         out[...] = total[i * count : (i + 1) * count].astype(out.dtype)
@@ -143,13 +147,13 @@
     )(*inputs, *after)
 
 
-def run_mlp(row_sets, weights, fresh, out_types, after=()):
+def run_mlp(row_sets, weights, step, fresh, out_types, after=()):
     count, width = row_sets[0].shape[0], weights[0].shape[1]
     size = sum(part.size for part in weights)
     cost = pl.CostEstimate(
         flops=4 * MATMUL_ROWS * size, bytes_accessed=4 * size, transcendentals=0
     )
-    kernel = functools.partial(mlp_kernel, lax.axis_size("expert"), fresh, len(row_sets))
+    kernel = functools.partial(mlp_kernel, lax.axis_size("expert"), step, fresh, len(row_sets))
     outputs = [((count, width), out_type) for out_type in out_types]
     return on_vmem(kernel, tuple(row_sets) + tuple(weights), outputs, 8 * MIB, cost, after)
 
@@ -165,7 +169,9 @@
 
 def spread(blocks):
     size = lax.axis_size("expert")
-    groups = [list(range(core, size, 2)) for core in range(2)]
+    groups = [
+        [start + core for y in range(2) for start in range(2 * y, size, 4)] for core in range(2)
+    ]
     return lax.all_to_all(blocks, "expert", 0, 0, axis_index_groups=groups, tiled=True)
 
 
@@ -175,7 +181,7 @@
     row_count, width = tokens.shape[1], tokens.shape[2]
     half = chips * row_count
     steps_total = routes.shape[0]
-    packed = width + steps_total * table_width(experts)
+    packed = width + table_width(experts, steps_total)
     gain = norm_gain[None]
     state_shape = ((row_count, width), jnp.float32)
     weight_bytes = 2 * sum(part.size for part in stale + learner)
@@ -194,7 +200,7 @@
     rows, state = tables, tokens[0]
     for step in range(steps_total):
         if step == 0:
-            (share,) = run_mlp([rows], stale, False, [jnp.bfloat16], learner[2:])
+            (share,) = run_mlp([rows], stale, step, False, [jnp.bfloat16], learner[2:])
         else:
             state, blocks = on_vmem(
                 next_kernel,
@@ -202,16 +208,11 @@
                 [state_shape, ((chips, row_count, width), jnp.bfloat16)],
             )
             rows = spread(blocks).reshape(half, width)
-            span = table_width(experts)
-            (rows,) = on_vmem(
-                functools.partial(join_kernel, width + step * span),
-                (rows, tables),
-                [((half, width + span), jnp.bfloat16)],
-            )
+            (rows,) = on_vmem(join_kernel, (rows, tables), [((half, packed), jnp.bfloat16)])
             other = swap_group(rows)
-            (old,) = run_mlp([rows], stale, False, [jnp.float32])
+            (old,) = run_mlp([rows], stale, step, False, [jnp.float32])
             other, old = lax.optimization_barrier((other, old))
-            new, away = run_mlp([rows, other], learner, True, [jnp.float32, jnp.bfloat16])
+            new, away = run_mlp([rows, other], learner, step, True, [jnp.float32, jnp.bfloat16])
             share = old + new + swap_group(away).astype(jnp.float32)
             share = share.astype(jnp.bfloat16)
         returned = spread(share.reshape(chips, row_count, width))
@@ -270,7 +271,7 @@
     experts = lax.axis_size("expert")
     groups = lax.axis_size("group")
     fewer = tokens.shape[1] * experts < learner_up.shape[1]
-    paired = experts % 2 == 0 and groups == 2
+    paired = experts % 4 == 0 and groups == 2
     plan = exchange_plan if fewer and paired else gather_plan
     stale = (rollout_up[0], rollout_down[0])
     learner = (learner_up[0], learner_down[0])

time: 77.1 us -> 76 us (0.986)
  blocking collectives: 54.5 us -> 53.4 us
    all_to_all x4, blocking collectives: 54.5 us -> 53.4 us  [spread(): lax.all_to_all(blocks, 'expert', 0, 0, axis_index_groups=groups, tiled=True)]
where the time goes in v12:
time: 76 us; the launch traced here: 75.7 us
  blocking collectives  53.4 us (70%)
  Pallas kernels  10.1 us (13%)
  waiting for transfers between devices  6.39 us (8%)
  starting transfers between devices  4.23 us (6%)
  local copies, waits for them, and re-layouts  1.39 us (2%)
    all_to_all x4, blocking collectives, spread(): lax.all_to_all(blocks, 'expert', 0, 0, axis_index_groups=groups, tiled=True)  53.4 us
    pallas_call x8, Pallas kernels, on_vmem(): pl.pallas_call(body, out_shape=[jax.ShapeDtypeStruct(shape, kind) for sha...  10.1 us
    ppermute x2, waiting for transfers between devices, swap_group(): return lax.ppermute(value, 'group', [(0, 1), (1, 0)])  6.38 us
    ppermute x2, starting transfers between devices, swap_group(): return lax.ppermute(value, 'group', [(0, 1), (1, 0)])  3.21 us
  transfers between devices with their start and end apart: 6, of which 2 were waited for; matrix products, arithmetic and copies ran while one was open for 0% of the time, Pallas kernels for 5%

profile of v12, /device:TPU:0, one launch (start us, length us, event | category | flops | bytes accessed | tf_op | source)
XLA Modules:
  0.0 75.7 jit_solution(1968330863455412067)
XLA Ops:
  0.0 0.5 collective-permute-start
  0.5 0.1 collective-permute-start.1
  0.5 0.5 collective-permute-start.2
  1.0 0.1 collective-permute-start.3
  1.0 0.8 copy-done.4
  1.8 0.1 shard_map.91.refs_0_
  1.9 0.6 copy-done.6
  2.5 0.0 copy-done.7
  2.5 0.0 copy-done.8
  2.5 0.1 shard_map.92
  2.6 17.6 %all_to_all.20 = bf16[8,8,2176]{2,1,0:T(8,128)(2,1)S(1)} all-to-all(bf16[8,8,2176]{2,1,0:T(8,128)(2,1)S(1)} %shard_map.92), channel_id=1, replica_groups={{0,4,8,12,2,6,10,14},{1,5,9,13,3,7,11,15},{16,20,24,28,18,22,26,30},{17..., dimensions={0} | all-to-all | bytes 557056 | tf_op jit(solution)/shard_map/all_to_all | solution.py:175
  20.3 3.5 %shard_map.93 = bf16[64,2048]{1,0:T(8,128)(2,1)S(1)} custom-call(bf16[64,2176]{1,0:T(8,128)(2,1)S(1)} %bitcast.18, bf16[768,2048]{1,0:T(8,128)(2,1)S(1)} %bitcast.13, bf16[768,2048]{1,0:T(8,128)(2,1)S(1)} %bitcast.16, bf16[768,2048]{1,0:T(8,128)(2,1)S(1)} %collective-permute-done.refs_3_, bf16[768,2048]{1,0:T(8,128)(2,1)S(1)} %collective-permute-done.1.refs_4_, ...), custom_call_target="tpu_custom_call" | custom-call | flops 3221225472 | bytes 25165824 | tf_op jit(solution)/shard_map/pallas_call | solution.py:140
  23.8 12.3 %all_to_all.21.refs_1_ = bf16[8,8,2048]{2,1,0:T(8,128)(2,1)S(1)} all-to-all(bf16[8,8,2048]{2,1,0:T(8,128)(2,1)S(1)} %bitcast.24), channel_id=1, replica_groups={{0,4,8,12,2,6,10,14},{1,5,9,13,3,7,11,15},{16,20,24,28,18,22,26,30},{17..., dimensions={0} | all-to-all | bytes 524288 | tf_op jit(solution)/shard_map/all_to_all | solution.py:175
  36.1 0.2 shard_map.94
  36.2 11.7 %all_to_all.22 = bf16[8,8,2048]{2,1,0:T(8,128)(2,1)S(1)} all-to-all(bf16[8,8,2048]{2,1,0:T(8,128)(2,1)S(1)} %get-tuple-element.12), channel_id=1, replica_groups={{0,4,8,12,2,6,10,14},{1,5,9,13,3,7,11,15},{16,20,24,28,18,22,26,30},{17..., dimensions={0} | all-to-all | bytes 524288 | tf_op jit(solution)/shard_map/all_to_all | solution.py:175
  48.0 1.6 %collective-permute-start.4 = (bf16[64,2176]{1,0:T(8,128)(2,1)S(1)}, bf16[64,2176]{1,0:T(8,128)(2,1)S(1)}, u32[]{:S(2)}, u32[]{:S(2)}) collective-permute-start(bf16[64,2176]{1,0:T(8,128)(2,1)S(1)} %shard_map.95.refs_0_), channel_id=1, source_target_pairs={{0,16},{16,0},{1,17},{17,1},{2,18},{18,2},{3,19},{19,3},{4,20},{20... | collective-permute-start | bytes 835592 | tf_op jit(solution)/shard_map/ppermute | solution.py:167
  49.6 3.5 %shard_map.96 = f32[64,2048]{1,0:T(8,128)S(1)} custom-call(bf16[64,2176]{1,0:T(8,128)(2,1)S(1)} %shard_map.95.refs_0_, bf16[768,2048]{1,0:T(8,128)(2,1)S(1)} %bitcast.14, bf16[768,2048]{1,0:T(8,128)(2,1)S(1)} %bitcast.17, bf16[768,2048]{1,0:T(8,128)(2,1)S(1)} %collective-permute-done.refs_3_, bf16[768,2048]{1,0:T(8,128)(2,1)S(1)} %collective-permute-done.1.refs_4_), custom_call_target="tpu_custom_call" | custom-call | flops 3221225472 | bytes 25165824 | tf_op jit(solution)/shard_map/pallas_call | solution.py:140
  53.1 1.5 %collective-permute-done.4.refs_1_ = bf16[64,2176]{1,0:T(8,128)(2,1)S(1)} collective-permute-done((bf16[64,2176]{1,0:T(8,128)(2,1)S(1)}, bf16[64,2176]{1,0:T(8,128)(2,1)S(1)}, u32[]{:S(2)}, u32[]{:S(2)}) %collective-permute-start.4) | collective-permute-done | bytes 278560 | tf_op jit(solution)/shard_map/ppermute | solution.py:167
  54.7 2.1 %shard_map.97 = (f32[64,2048]{1,0:T(8,128)S(1)}, bf16[64,2048]{1,0:T(8,128)(2,1)S(1)}) custom-call(bf16[64,2176]{1,0:T(8,128)(2,1)S(1)} %shard_map.95.refs_0_, bf16[64,2176]{1,0:T(8,128)(2,1)S(1)} %collective-permute-done.4.refs_1_, bf16[384,2048]{1,0:T(8,128)(2,1)S(1)} %bitcast.21, bf16[384,2048]{1,0:T(8,128)(2,1)S(1)} %bitcast.23, ...), custom_call_target="tpu_custom_call" | custom-call | flops 1610612736 | bytes 12582912 | tf_op jit(solution)/shard_map/pallas_call | solution.py:140
  56.8 1.6 %collective-permute-start.5 = (bf16[64,2048]{1,0:T(8,128)(2,1)S(1)}, bf16[64,2048]{1,0:T(8,128)(2,1)S(1)}, u32[]{:S(2)}, u32[]{:S(2)}) collective-permute-start(bf16[64,2048]{1,0:T(8,128)(2,1)S(1)} %get-tuple-element.16), channel_id=1, source_target_pairs={{0,16},{16,0},{1,17},{17,1},{2,18},{18,2},{3,19},{19,3},{4,20},{20... | collective-permute-start | bytes 786440 | tf_op jit(solution)/shard_map/ppermute | solution.py:167
  58.4 4.8 %collective-permute-done.5 = bf16[64,2048]{1,0:T(8,128)(2,1)S(1)} collective-permute-done((bf16[64,2048]{1,0:T(8,128)(2,1)S(1)}, bf16[64,2048]{1,0:T(8,128)(2,1)S(1)}, u32[]{:S(2)}, u32[]{:S(2)}) %collective-permute-start.5) | collective-permute-done | bytes 262176 | tf_op jit(solution)/shard_map/ppermute | solution.py:167
  63.2 0.1 fusion
  63.3 11.8 %all_to_all.23.refs_1_ = bf16[8,8,2048]{2,1,0:T(8,128)(2,1)S(1)} all-to-all(bf16[8,8,2048]{2,1,0:T(8,128)(2,1)S(1)} %fusion), channel_id=1, replica_groups={{0,4,8,12,2,6,10,14},{1,5,9,13,3,7,11,15},{16,20,24,28,18,22,26,30},{17..., dimensions={0} | all-to-all | bytes 524288 | tf_op jit(solution)/shard_map/all_to_all | solution.py:175
  75.0 0.7 shard_map.98
  (21 shorter events, 0.1 us)
Async XLA Ops:
  0.0 20.3 %collective-permute-start = (bf16[768,2048]{1,0:T(8,128)(2,1)}, bf16[768,2048]{1,0:T(8,128)(2,1)S(1)}, u32[]{:S(2)}, u32[]{:S(2)}) collective-permute-start(bf16[768,2048]{1,0:T(8,128)(2,1)} %bitcast.12), channel_id=1, source_target_pairs={{0,1},{1,0},{2,3},{3,2},{4,5},{5,4},{6,7},{7,6},{8,9},{9,8},{10,11... | collective-permute-start | bytes 9437192 | tf_op jit(solution)/shard_map/ppermute | solution.py:163
  0.5 19.8 %collective-permute-start.1 = (bf16[768,2048]{1,0:T(8,128)(2,1)}, bf16[768,2048]{1,0:T(8,128)(2,1)S(1)}, u32[]{:S(2)}, u32[]{:S(2)}) collective-permute-start(bf16[768,2048]{1,0:T(8,128)(2,1)} %bitcast.15), channel_id=1, source_target_pairs={{0,1},{1,0},{2,3},{3,2},{4,5},{5,4},{6,7},{7,6},{8,9},{9,8},{10,11... | collective-permute-start | bytes 9437192 | tf_op jit(solution)/shard_map/ppermute | solution.py:163
  0.5 19.8 %collective-permute-start.2 = (bf16[384,2048]{1,0:T(8,128)(2,1)}, bf16[384,2048]{1,0:T(8,128)(2,1)S(1)}, u32[]{:S(2)}, u32[]{:S(2)}) collective-permute-start(bf16[384,2048]{1,0:T(8,128)(2,1)} %bitcast.20), channel_id=1, source_target_pairs={{0,1},{1,0},{2,3},{3,2},{4,5},{5,4},{6,7},{7,6},{8,9},{9,8},{10,11... | collective-permute-start | bytes 4718600 | tf_op jit(solution)/shard_map/ppermute | solution.py:163
  1.0 19.3 %collective-permute-start.3 = (bf16[384,2048]{1,0:T(8,128)(2,1)}, bf16[384,2048]{1,0:T(8,128)(2,1)S(1)}, u32[]{:S(2)}, u32[]{:S(2)}) collective-permute-start(bf16[384,2048]{1,0:T(8,128)(2,1)} %bitcast.22), channel_id=1, source_target_pairs={{0,1},{1,0},{2,3},{3,2},{4,5},{5,4},{6,7},{7,6},{8,9},{9,8},{10,11... | collective-permute-start | bytes 4718600 | tf_op jit(solution)/shard_map/ppermute | solution.py:163
  1.0 0.8 %copy-start.4 = (bf16[1,8,2048]{2,1,0:T(8,128)(2,1)S(1)}, bf16[1,8,2048]{2,1,0:T(8,128)(2,1)}, u32[]{:S(2)}) copy-start(bf16[1,8,2048]{2,1,0:T(8,128)(2,1)} %param.9) | copy-start | bytes 98308
  1.8 0.7 copy-start.6
  1.8 0.7 copy-start.7
  1.8 0.7 copy-start.8
  1.8 0.7 copy-start.9
  1.8 18.5 %copy-start = (bf16[1,768,2048]{2,1,0:T(8,128)(2,1)S(1)}, bf16[1,768,2048]{2,1,0:T(8,128)(2,1)}, u32[]{:S(2)}) copy-start(bf16[1,768,2048]{2,1,0:T(8,128)(2,1)} %param.14) | copy-start | bytes 9437188
  1.8 18.5 %copy-start.1 = (bf16[1,768,2048]{2,1,0:T(8,128)(2,1)S(1)}, bf16[1,768,2048]{2,1,0:T(8,128)(2,1)}, u32[]{:S(2)}) copy-start(bf16[1,768,2048]{2,1,0:T(8,128)(2,1)} %param.15) | copy-start | bytes 9437188
  20.3 15.8 %copy-start.5 = (bf16[1,8,2048]{2,1,0:T(8,128)(2,1)S(1)}, bf16[1,8,2048]{2,1,0:T(8,128)(2,1)}, u32[]{:S(2)}) copy-start(bf16[1,8,2048]{2,1,0:T(8,128)(2,1)} %param.9) | copy-start | bytes 98308
  48.0 6.6 %copy-start.2 = (bf16[1,384,2048]{2,1,0:T(8,128)(2,1)S(1)}, bf16[1,384,2048]{2,1,0:T(8,128)(2,1)}, u32[]{:S(2)}) copy-start(bf16[1,384,2048]{2,1,0:T(8,128)(2,1)} %param.16) | copy-start | bytes 4718596
  48.0 6.6 %copy-start.3 = (bf16[1,384,2048]{2,1,0:T(8,128)(2,1)S(1)}, bf16[1,384,2048]{2,1,0:T(8,128)(2,1)}, u32[]{:S(2)}) copy-start(bf16[1,384,2048]{2,1,0:T(8,128)(2,1)} %param.17) | copy-start | bytes 4718596
  48.0 6.6 %collective-permute-start.4 = (bf16[64,2176]{1,0:T(8,128)(2,1)S(1)}, bf16[64,2176]{1,0:T(8,128)(2,1)S(1)}, u32[]{:S(2)}, u32[]{:S(2)}) collective-permute-start(bf16[64,2176]{1,0:T(8,128)(2,1)S(1)} %shard_map.95.refs_0_), channel_id=1, source_target_pairs={{0,16},{16,0},{1,17},{17,1},{2,18},{18,2},{3,19},{19,3},{4,20},{20... | collective-permute-start | bytes 835592 | tf_op jit(solution)/shard_map/ppermute | solution.py:167
  56.8 6.4 %collective-permute-start.5 = (bf16[64,2048]{1,0:T(8,128)(2,1)S(1)}, bf16[64,2048]{1,0:T(8,128)(2,1)S(1)}, u32[]{:S(2)}, u32[]{:S(2)}) collective-permute-start(bf16[64,2048]{1,0:T(8,128)(2,1)S(1)} %get-tuple-element.16), channel_id=1, source_target_pairs={{0,16},{16,0},{1,17},{17,1},{2,18},{18,2},{3,19},{19,3},{4,20},{20... | collective-permute-start | bytes 786440 | tf_op jit(solution)/shard_map/ppermute | solution.py:167

commit v13 on v12

--- a/solution.py
+++ b/solution.py
@@ -169,9 +169,8 @@
 
 def spread(blocks):
     size = lax.axis_size("expert")
-    groups = [
-        [start + core for y in range(2) for start in range(2 * y, size, 4)] for core in range(2)
-    ]
+    chips = [chip for y in range(2) for chip in range(y, size // 2, 2)]
+    groups = [[2 * chip + (core ^ (4 * chip >= size)) for chip in chips] for core in range(2)]
     return lax.all_to_all(blocks, "expert", 0, 0, axis_index_groups=groups, tiled=True)
 
 

time: 76 us -> 81.6 us (1.074)
  waiting for transfers between devices: 6.39 us -> 10.7 us
  blocking collectives: 53.4 us -> 54.4 us
    ppermute x2, waiting for transfers between devices: 6.38 us -> 10.7 us  [swap_group(): return lax.ppermute(value, 'group', [(0, 1), (1, 0)])]
    all_to_all x4, blocking collectives: 53.4 us -> 54.4 us  [spread(): lax.all_to_all(blocks, 'expert', 0, 0, axis_index_groups=groups, tiled=True)]
where the time goes in v13:
time: 81.6 us; the launch traced here: 81.3 us
  blocking collectives  54.4 us (67%)
  waiting for transfers between devices  10.7 us (13%)
  Pallas kernels  10.1 us (12%)
  starting transfers between devices  4.63 us (6%)
  local copies, waits for them, and re-layouts  1.39 us (2%)
    all_to_all x4, blocking collectives, spread(): lax.all_to_all(blocks, 'expert', 0, 0, axis_index_groups=groups, tiled=True)  54.4 us
    ppermute x2, waiting for transfers between devices, swap_group(): return lax.ppermute(value, 'group', [(0, 1), (1, 0)])  10.7 us
    pallas_call x8, Pallas kernels, on_vmem(): pl.pallas_call(body, out_shape=[jax.ShapeDtypeStruct(shape, kind) for sha...  10.1 us
    ppermute x2, starting transfers between devices, swap_group(): return lax.ppermute(value, 'group', [(0, 1), (1, 0)])  3.61 us
  transfers between devices with their start and end apart: 6, of which 2 were waited for; matrix products, arithmetic and copies ran while one was open for 0% of the time, Pallas kernels for 5%

profile of v13, /device:TPU:0, one launch (start us, length us, event | category | flops | bytes accessed | tf_op | source)
XLA Modules:
  0.0 81.3 jit_solution(15814566928218598324)
XLA Ops:
  0.0 0.5 collective-permute-start
  0.5 0.1 collective-permute-start.1
  0.5 0.5 collective-permute-start.2
  1.0 0.1 collective-permute-start.3
  1.0 0.8 copy-done.4
  1.8 0.1 shard_map.91.refs_0_
  1.9 0.6 copy-done.6
  2.5 0.0 copy-done.7
  2.5 0.0 copy-done.8
  2.5 0.1 shard_map.92
  2.6 16.7 %all_to_all.20 = bf16[8,8,2176]{2,1,0:T(8,128)(2,1)S(1)} all-to-all(bf16[8,8,2176]{2,1,0:T(8,128)(2,1)S(1)} %shard_map.92), channel_id=1, replica_groups={{0,4,9,13,2,6,11,15},{1,5,8,12,3,7,10,14},{16,20,25,29,18,22,27,31},{17..., dimensions={0} | all-to-all | bytes 557056 | tf_op jit(solution)/shard_map/all_to_all | solution.py:174
  19.4 3.5 %shard_map.93 = bf16[64,2048]{1,0:T(8,128)(2,1)S(1)} custom-call(bf16[64,2176]{1,0:T(8,128)(2,1)S(1)} %bitcast.18, bf16[768,2048]{1,0:T(8,128)(2,1)S(1)} %bitcast.13, bf16[768,2048]{1,0:T(8,128)(2,1)S(1)} %bitcast.16, bf16[768,2048]{1,0:T(8,128)(2,1)S(1)} %collective-permute-done.refs_3_, bf16[768,2048]{1,0:T(8,128)(2,1)S(1)} %collective-permute-done.1.refs_4_, ...), custom_call_target="tpu_custom_call" | custom-call | flops 3221225472 | bytes 25165824 | tf_op jit(solution)/shard_map/pallas_call | solution.py:140
  22.9 13.1 %all_to_all.21.refs_1_ = bf16[8,8,2048]{2,1,0:T(8,128)(2,1)S(1)} all-to-all(bf16[8,8,2048]{2,1,0:T(8,128)(2,1)S(1)} %bitcast.24), channel_id=1, replica_groups={{0,4,9,13,2,6,11,15},{1,5,8,12,3,7,10,14},{16,20,25,29,18,22,27,31},{17..., dimensions={0} | all-to-all | bytes 524288 | tf_op jit(solution)/shard_map/all_to_all | solution.py:174
  36.0 0.2 shard_map.94
  36.2 11.6 %all_to_all.22 = bf16[8,8,2048]{2,1,0:T(8,128)(2,1)S(1)} all-to-all(bf16[8,8,2048]{2,1,0:T(8,128)(2,1)S(1)} %get-tuple-element.12), channel_id=1, replica_groups={{0,4,9,13,2,6,11,15},{1,5,8,12,3,7,10,14},{16,20,25,29,18,22,27,31},{17..., dimensions={0} | all-to-all | bytes 524288 | tf_op jit(solution)/shard_map/all_to_all | solution.py:174
  47.8 1.8 %collective-permute-start.4 = (bf16[64,2176]{1,0:T(8,128)(2,1)S(1)}, bf16[64,2176]{1,0:T(8,128)(2,1)S(1)}, u32[]{:S(2)}, u32[]{:S(2)}) collective-permute-start(bf16[64,2176]{1,0:T(8,128)(2,1)S(1)} %shard_map.95.refs_0_), channel_id=1, source_target_pairs={{0,16},{16,0},{1,17},{17,1},{2,18},{18,2},{3,19},{19,3},{4,20},{20... | collective-permute-start | bytes 835592 | tf_op jit(solution)/shard_map/ppermute | solution.py:167
  49.5 3.5 %shard_map.96 = f32[64,2048]{1,0:T(8,128)S(1)} custom-call(bf16[64,2176]{1,0:T(8,128)(2,1)S(1)} %shard_map.95.refs_0_, bf16[768,2048]{1,0:T(8,128)(2,1)S(1)} %bitcast.14, bf16[768,2048]{1,0:T(8,128)(2,1)S(1)} %bitcast.17, bf16[768,2048]{1,0:T(8,128)(2,1)S(1)} %collective-permute-done.refs_3_, bf16[768,2048]{1,0:T(8,128)(2,1)S(1)} %collective-permute-done.1.refs_4_), custom_call_target="tpu_custom_call" | custom-call | flops 3221225472 | bytes 25165824 | tf_op jit(solution)/shard_map/pallas_call | solution.py:140
  53.0 4.1 %collective-permute-done.4.refs_1_ = bf16[64,2176]{1,0:T(8,128)(2,1)S(1)} collective-permute-done((bf16[64,2176]{1,0:T(8,128)(2,1)S(1)}, bf16[64,2176]{1,0:T(8,128)(2,1)S(1)}, u32[]{:S(2)}, u32[]{:S(2)}) %collective-permute-start.4) | collective-permute-done | bytes 278560 | tf_op jit(solution)/shard_map/ppermute | solution.py:167
  57.1 2.1 %shard_map.97 = (f32[64,2048]{1,0:T(8,128)S(1)}, bf16[64,2048]{1,0:T(8,128)(2,1)S(1)}) custom-call(bf16[64,2176]{1,0:T(8,128)(2,1)S(1)} %shard_map.95.refs_0_, bf16[64,2176]{1,0:T(8,128)(2,1)S(1)} %collective-permute-done.4.refs_1_, bf16[384,2048]{1,0:T(8,128)(2,1)S(1)} %bitcast.21, bf16[384,2048]{1,0:T(8,128)(2,1)S(1)} %bitcast.23, ...), custom_call_target="tpu_custom_call" | custom-call | flops 1610612736 | bytes 12582912 | tf_op jit(solution)/shard_map/pallas_call | solution.py:140
  59.2 1.9 %collective-permute-start.5 = (bf16[64,2048]{1,0:T(8,128)(2,1)S(1)}, bf16[64,2048]{1,0:T(8,128)(2,1)S(1)}, u32[]{:S(2)}, u32[]{:S(2)}) collective-permute-start(bf16[64,2048]{1,0:T(8,128)(2,1)S(1)} %get-tuple-element.16), channel_id=1, source_target_pairs={{0,16},{16,0},{1,17},{17,1},{2,18},{18,2},{3,19},{19,3},{4,20},{20... | collective-permute-start | bytes 786440 | tf_op jit(solution)/shard_map/ppermute | solution.py:167
  61.0 6.6 %collective-permute-done.5 = bf16[64,2048]{1,0:T(8,128)(2,1)S(1)} collective-permute-done((bf16[64,2048]{1,0:T(8,128)(2,1)S(1)}, bf16[64,2048]{1,0:T(8,128)(2,1)S(1)}, u32[]{:S(2)}, u32[]{:S(2)}) %collective-permute-start.5) | collective-permute-done | bytes 262176 | tf_op jit(solution)/shard_map/ppermute | solution.py:167
  67.6 0.1 fusion
  67.7 13.0 %all_to_all.23.refs_1_ = bf16[8,8,2048]{2,1,0:T(8,128)(2,1)S(1)} all-to-all(bf16[8,8,2048]{2,1,0:T(8,128)(2,1)S(1)} %fusion), channel_id=1, replica_groups={{0,4,9,13,2,6,11,15},{1,5,8,12,3,7,10,14},{16,20,25,29,18,22,27,31},{17..., dimensions={0} | all-to-all | bytes 524288 | tf_op jit(solution)/shard_map/all_to_all | solution.py:174
  80.7 0.7 shard_map.98
  (21 shorter events, 0.1 us)
Async XLA Ops:
  0.0 19.4 %collective-permute-start = (bf16[768,2048]{1,0:T(8,128)(2,1)}, bf16[768,2048]{1,0:T(8,128)(2,1)S(1)}, u32[]{:S(2)}, u32[]{:S(2)}) collective-permute-start(bf16[768,2048]{1,0:T(8,128)(2,1)} %bitcast.12), channel_id=1, source_target_pairs={{0,1},{1,0},{2,3},{3,2},{4,5},{5,4},{6,7},{7,6},{8,9},{9,8},{10,11... | collective-permute-start | bytes 9437192 | tf_op jit(solution)/shard_map/ppermute | solution.py:163
  0.5 18.9 %collective-permute-start.1 = (bf16[768,2048]{1,0:T(8,128)(2,1)}, bf16[768,2048]{1,0:T(8,128)(2,1)S(1)}, u32[]{:S(2)}, u32[]{:S(2)}) collective-permute-start(bf16[768,2048]{1,0:T(8,128)(2,1)} %bitcast.15), channel_id=1, source_target_pairs={{0,1},{1,0},{2,3},{3,2},{4,5},{5,4},{6,7},{7,6},{8,9},{9,8},{10,11... | collective-permute-start | bytes 9437192 | tf_op jit(solution)/shard_map/ppermute | solution.py:163
  0.5 18.9 %collective-permute-start.2 = (bf16[384,2048]{1,0:T(8,128)(2,1)}, bf16[384,2048]{1,0:T(8,128)(2,1)S(1)}, u32[]{:S(2)}, u32[]{:S(2)}) collective-permute-start(bf16[384,2048]{1,0:T(8,128)(2,1)} %bitcast.20), channel_id=1, source_target_pairs={{0,1},{1,0},{2,3},{3,2},{4,5},{5,4},{6,7},{7,6},{8,9},{9,8},{10,11... | collective-permute-start | bytes 4718600 | tf_op jit(solution)/shard_map/ppermute | solution.py:163
  1.0 18.4 %collective-permute-start.3 = (bf16[384,2048]{1,0:T(8,128)(2,1)}, bf16[384,2048]{1,0:T(8,128)(2,1)S(1)}, u32[]{:S(2)}, u32[]{:S(2)}) collective-permute-start(bf16[384,2048]{1,0:T(8,128)(2,1)} %bitcast.22), channel_id=1, source_target_pairs={{0,1},{1,0},{2,3},{3,2},{4,5},{5,4},{6,7},{7,6},{8,9},{9,8},{10,11... | collective-permute-start | bytes 4718600 | tf_op jit(solution)/shard_map/ppermute | solution.py:163
  1.0 0.8 copy-start.4
  1.8 0.7 copy-start.6
  1.8 0.7 copy-start.7
  1.8 0.7 copy-start.8
  1.8 0.7 copy-start.9
  1.8 17.6 %copy-start = (bf16[1,768,2048]{2,1,0:T(8,128)(2,1)S(1)}, bf16[1,768,2048]{2,1,0:T(8,128)(2,1)}, u32[]{:S(2)}) copy-start(bf16[1,768,2048]{2,1,0:T(8,128)(2,1)} %param.14) | copy-start | bytes 9437188
  1.8 17.6 %copy-start.1 = (bf16[1,768,2048]{2,1,0:T(8,128)(2,1)S(1)}, bf16[1,768,2048]{2,1,0:T(8,128)(2,1)}, u32[]{:S(2)}) copy-start(bf16[1,768,2048]{2,1,0:T(8,128)(2,1)} %param.15) | copy-start | bytes 9437188
  19.4 16.6 %copy-start.5 = (bf16[1,8,2048]{2,1,0:T(8,128)(2,1)S(1)}, bf16[1,8,2048]{2,1,0:T(8,128)(2,1)}, u32[]{:S(2)}) copy-start(bf16[1,8,2048]{2,1,0:T(8,128)(2,1)} %param.9) | copy-start | bytes 98308
  47.8 9.3 %copy-start.2 = (bf16[1,384,2048]{2,1,0:T(8,128)(2,1)S(1)}, bf16[1,384,2048]{2,1,0:T(8,128)(2,1)}, u32[]{:S(2)}) copy-start(bf16[1,384,2048]{2,1,0:T(8,128)(2,1)} %param.16) | copy-start | bytes 4718596
  47.8 9.3 %copy-start.3 = (bf16[1,384,2048]{2,1,0:T(8,128)(2,1)S(1)}, bf16[1,384,2048]{2,1,0:T(8,128)(2,1)}, u32[]{:S(2)}) copy-start(bf16[1,384,2048]{2,1,0:T(8,128)(2,1)} %param.17) | copy-start | bytes 4718596
  47.8 9.3 %collective-permute-start.4 = (bf16[64,2176]{1,0:T(8,128)(2,1)S(1)}, bf16[64,2176]{1,0:T(8,128)(2,1)S(1)}, u32[]{:S(2)}, u32[]{:S(2)}) collective-permute-start(bf16[64,2176]{1,0:T(8,128)(2,1)S(1)} %shard_map.95.refs_0_), channel_id=1, source_target_pairs={{0,16},{16,0},{1,17},{17,1},{2,18},{18,2},{3,19},{19,3},{4,20},{20... | collective-permute-start | bytes 835592 | tf_op jit(solution)/shard_map/ppermute | solution.py:167
  59.2 8.4 %collective-permute-start.5 = (bf16[64,2048]{1,0:T(8,128)(2,1)S(1)}, bf16[64,2048]{1,0:T(8,128)(2,1)S(1)}, u32[]{:S(2)}, u32[]{:S(2)}) collective-permute-start(bf16[64,2048]{1,0:T(8,128)(2,1)S(1)} %get-tuple-element.16), channel_id=1, source_target_pairs={{0,16},{16,0},{1,17},{17,1},{2,18},{18,2},{3,19},{19,3},{4,20},{20... | collective-permute-start | bytes 786440 | tf_op jit(solution)/shard_map/ppermute | solution.py:167

commit v14 on v12

--- a/solution.py
+++ b/solution.py
@@ -33,11 +33,15 @@
     return 0 if step == 0 else 4 * step - 2 + 2 * fresh
 
 
-def weight_table(experts, chosen, weights, changed):
-    steps_total, _, rows, top_count = chosen.shape
-    shape = (rows, table_width(experts, steps_total))
-    lane = lax.broadcasted_iota(jnp.int32, shape, 1)
-    section, expert = lane // experts, lane % experts
+def lane_kernel(experts, section_out, expert_out):
+    lane = lax.broadcasted_iota(jnp.int32, section_out.shape, 1)
+    section_out[...] = lane // experts
+    expert_out[...] = lane % experts
+
+
+def weight_table(section, expert, chosen, weights, changed):
+    steps_total, _, _, top_count = chosen.shape
+    shape = section.shape
     fresh = section < 0
     for i in range(changed.shape[1]):
         fresh = fresh | (expert == changed[:, i : i + 1])
@@ -68,15 +72,10 @@
     return jnp.sum(jnp.where(mine, table.astype(jnp.float32), 0.0), axis=1, keepdims=True)
 
 
-def first_kernel(tokens, out):
-    state = tokens[...].astype(jnp.float32)
-    out[...] = state * lax.rsqrt(jnp.mean(state * state, axis=-1, keepdims=True) + 1e-06)
-
-
-def pack_kernel(experts, scaled, gain, routes, scales, changed, out):
-    width = scaled.shape[1]
-    normed = (scaled[...] * gain[...]).astype(jnp.bfloat16)
-    table = weight_table(experts, routes, scales, changed)
+def pack_kernel(section, expert, tokens, gain, routes, scales, changed, out):
+    width = tokens.shape[1]
+    normed = normalize(tokens[...].astype(jnp.float32), gain[...])
+    table = weight_table(section[...], expert[...], routes, scales, changed)
     for chip in range(out.shape[0]):
         out[chip, :, :width] = normed
         out[chip, :, width:] = table
@@ -188,12 +187,15 @@
     long = pl.CostEstimate(
         flops=1280 * weight_bytes, bytes_accessed=2 * weight_bytes, transcendentals=0
     )
+    lanes = ((row_count, table_width(experts, steps_total)), jnp.int32)
+    section, expert = on_vmem(
+        functools.partial(lane_kernel, experts), (), [lanes, lanes], cost=long
+    )
     stale = stale + tuple(swap_core(part) for part in stale)
     learner = learner + tuple(swap_core(part) for part in learner)
-    (scaled,) = on_vmem(first_kernel, (tokens[0],), [state_shape], cost=long)
     (blocks,) = on_vmem(
-        functools.partial(pack_kernel, experts),
-        (scaled, gain, routes, route_scale, changed),
+        pack_kernel,
+        (section, expert, tokens[0], gain, routes, route_scale, changed),
         [((chips, row_count, packed), jnp.bfloat16)],
     )
     tables = spread(blocks).reshape(half, packed)

time: 76 us -> 75.5 us (level)
  local copies, waits for them, and re-layouts: 1.39 us -> 0.62 us
    unnamed x20 -> x18, local copies, waits for them, and re-layouts: 1.39 us -> 0.62 us
where the time goes in v14:
time: 75.5 us; the launch traced here: 75.2 us
  blocking collectives  53.7 us (71%)
  Pallas kernels  9.98 us (13%)
  waiting for transfers between devices  6.49 us (9%)
  starting transfers between devices  4.19 us (6%)
    all_to_all x4, blocking collectives, spread(): lax.all_to_all(blocks, 'expert', 0, 0, axis_index_groups=groups, tiled=True)  53.7 us
    pallas_call x8, Pallas kernels, on_vmem(): pl.pallas_call(body, out_shape=[jax.ShapeDtypeStruct(shape, kind) for sha...  9.98 us
    ppermute x2, waiting for transfers between devices, swap_group(): return lax.ppermute(value, 'group', [(0, 1), (1, 0)])  6.48 us
    ppermute x2, starting transfers between devices, swap_group(): return lax.ppermute(value, 'group', [(0, 1), (1, 0)])  3.11 us
  transfers between devices with their start and end apart: 6, of which 2 were waited for; matrix products, arithmetic and copies ran while one was open for 0% of the time, Pallas kernels for 5%

profile of v14, /device:TPU:0, one launch (start us, length us, event | category | flops | bytes accessed | tf_op | source)
XLA Modules:
  0.0 75.2 jit_solution(6821250709860027938)
XLA Ops:
  0.0 0.5 collective-permute-start
  0.5 0.1 collective-permute-start.1
  0.5 0.5 collective-permute-start.2
  1.0 0.1 collective-permute-start.3
  1.1 0.6 copy-done.4
  1.7 0.1 shard_map.92
  1.9 17.7 %all_to_all.20 = bf16[8,8,2176]{2,1,0:T(8,128)(2,1)S(1)} all-to-all(bf16[8,8,2176]{2,1,0:T(8,128)(2,1)S(1)} %shard_map.92), channel_id=1, replica_groups={{0,4,8,12,2,6,10,14},{1,5,9,13,3,7,11,15},{16,20,24,28,18,22,26,30},{17..., dimensions={0} | all-to-all | bytes 557056 | tf_op jit(solution)/shard_map/all_to_all | solution.py:174
  19.6 0.0 collective-permute-done.2.refs_5_.refs_4_
  19.6 0.0 collective-permute-done.3.refs_6_.refs_5_
  19.6 3.5 %shard_map.93 = bf16[64,2048]{1,0:T(8,128)(2,1)S(1)} custom-call(bf16[64,2176]{1,0:T(8,128)(2,1)S(1)} %bitcast.18, bf16[768,2048]{1,0:T(8,128)(2,1)S(1)} %bitcast.13, bf16[768,2048]{1,0:T(8,128)(2,1)S(1)} %bitcast.16, bf16[768,2048]{1,0:T(8,128)(2,1)S(1)} %collective-permute-done.refs_3_, bf16[768,2048]{1,0:T(8,128)(2,1)S(1)} %collective-permute-done.1.refs_4_, ...), custom_call_target="tpu_custom_call" | custom-call | flops 3221225472 | bytes 25165824 | tf_op jit(solution)/shard_map/pallas_call | solution.py:139
  23.1 12.4 %all_to_all.21.refs_1_ = bf16[8,8,2048]{2,1,0:T(8,128)(2,1)S(1)} all-to-all(bf16[8,8,2048]{2,1,0:T(8,128)(2,1)S(1)} %bitcast.24), channel_id=1, replica_groups={{0,4,8,12,2,6,10,14},{1,5,9,13,3,7,11,15},{16,20,24,28,18,22,26,30},{17..., dimensions={0} | all-to-all | bytes 524288 | tf_op jit(solution)/shard_map/all_to_all | solution.py:174
  35.5 0.2 shard_map.94
  35.7 11.8 %all_to_all.22 = bf16[8,8,2048]{2,1,0:T(8,128)(2,1)S(1)} all-to-all(bf16[8,8,2048]{2,1,0:T(8,128)(2,1)S(1)} %get-tuple-element.16), channel_id=1, replica_groups={{0,4,8,12,2,6,10,14},{1,5,9,13,3,7,11,15},{16,20,24,28,18,22,26,30},{17..., dimensions={0} | all-to-all | bytes 524288 | tf_op jit(solution)/shard_map/all_to_all | solution.py:174
  47.5 0.0 copy-start.2
  47.5 0.0 copy-start.3
  47.5 1.6 %collective-permute-start.4 = (bf16[64,2176]{1,0:T(8,128)(2,1)S(1)}, bf16[64,2176]{1,0:T(8,128)(2,1)S(1)}, u32[]{:S(2)}, u32[]{:S(2)}) collective-permute-start(bf16[64,2176]{1,0:T(8,128)(2,1)S(1)} %shard_map.95.refs_0_), channel_id=1, source_target_pairs={{0,16},{16,0},{1,17},{17,1},{2,18},{18,2},{3,19},{19,3},{4,20},{20... | collective-permute-start | bytes 835592 | tf_op jit(solution)/shard_map/ppermute | solution.py:166
  49.1 3.5 %shard_map.96 = f32[64,2048]{1,0:T(8,128)S(1)} custom-call(bf16[64,2176]{1,0:T(8,128)(2,1)S(1)} %shard_map.95.refs_0_, bf16[768,2048]{1,0:T(8,128)(2,1)S(1)} %bitcast.14, bf16[768,2048]{1,0:T(8,128)(2,1)S(1)} %bitcast.17, bf16[768,2048]{1,0:T(8,128)(2,1)S(1)} %collective-permute-done.refs_3_, bf16[768,2048]{1,0:T(8,128)(2,1)S(1)} %collective-permute-done.1.refs_4_), custom_call_target="tpu_custom_call" | custom-call | flops 3221225472 | bytes 25165824 | tf_op jit(solution)/shard_map/pallas_call | solution.py:139
  52.5 1.6 %collective-permute-done.4.refs_1_ = bf16[64,2176]{1,0:T(8,128)(2,1)S(1)} collective-permute-done((bf16[64,2176]{1,0:T(8,128)(2,1)S(1)}, bf16[64,2176]{1,0:T(8,128)(2,1)S(1)}, u32[]{:S(2)}, u32[]{:S(2)}) %collective-permute-start.4) | collective-permute-done | bytes 278560 | tf_op jit(solution)/shard_map/ppermute | solution.py:166
  54.1 2.1 %shard_map.97 = (f32[64,2048]{1,0:T(8,128)S(1)}, bf16[64,2048]{1,0:T(8,128)(2,1)S(1)}) custom-call(bf16[64,2176]{1,0:T(8,128)(2,1)S(1)} %shard_map.95.refs_0_, bf16[64,2176]{1,0:T(8,128)(2,1)S(1)} %collective-permute-done.4.refs_1_, bf16[384,2048]{1,0:T(8,128)(2,1)S(1)} %bitcast.21, bf16[384,2048]{1,0:T(8,128)(2,1)S(1)} %bitcast.23, ...), custom_call_target="tpu_custom_call" | custom-call | flops 1610612736 | bytes 12582912 | tf_op jit(solution)/shard_map/pallas_call | solution.py:139
  56.2 1.6 %collective-permute-start.5 = (bf16[64,2048]{1,0:T(8,128)(2,1)S(1)}, bf16[64,2048]{1,0:T(8,128)(2,1)S(1)}, u32[]{:S(2)}, u32[]{:S(2)}) collective-permute-start(bf16[64,2048]{1,0:T(8,128)(2,1)S(1)} %get-tuple-element.20), channel_id=1, source_target_pairs={{0,16},{16,0},{1,17},{17,1},{2,18},{18,2},{3,19},{19,3},{4,20},{20... | collective-permute-start | bytes 786440 | tf_op jit(solution)/shard_map/ppermute | solution.py:166
  57.8 4.9 %collective-permute-done.5 = bf16[64,2048]{1,0:T(8,128)(2,1)S(1)} collective-permute-done((bf16[64,2048]{1,0:T(8,128)(2,1)S(1)}, bf16[64,2048]{1,0:T(8,128)(2,1)S(1)}, u32[]{:S(2)}, u32[]{:S(2)}) %collective-permute-start.5) | collective-permute-done | bytes 262176 | tf_op jit(solution)/shard_map/ppermute | solution.py:166
  62.7 0.1 fusion
  62.7 11.8 %all_to_all.23.refs_1_ = bf16[8,8,2048]{2,1,0:T(8,128)(2,1)S(1)} all-to-all(bf16[8,8,2048]{2,1,0:T(8,128)(2,1)S(1)} %fusion), channel_id=1, replica_groups={{0,4,8,12,2,6,10,14},{1,5,9,13,3,7,11,15},{16,20,24,28,18,22,26,30},{17..., dimensions={0} | all-to-all | bytes 524288 | tf_op jit(solution)/shard_map/all_to_all | solution.py:174
  74.6 0.7 shard_map.98
  (19 shorter events, 0.1 us)
Async XLA Ops:
  0.0 19.6 %collective-permute-start = (bf16[768,2048]{1,0:T(8,128)(2,1)}, bf16[768,2048]{1,0:T(8,128)(2,1)S(1)}, u32[]{:S(2)}, u32[]{:S(2)}) collective-permute-start(bf16[768,2048]{1,0:T(8,128)(2,1)} %bitcast.12), channel_id=1, source_target_pairs={{0,1},{1,0},{2,3},{3,2},{4,5},{5,4},{6,7},{7,6},{8,9},{9,8},{10,11... | collective-permute-start | bytes 9437192 | tf_op jit(solution)/shard_map/ppermute | solution.py:162
  0.5 19.1 %collective-permute-start.1 = (bf16[768,2048]{1,0:T(8,128)(2,1)}, bf16[768,2048]{1,0:T(8,128)(2,1)S(1)}, u32[]{:S(2)}, u32[]{:S(2)}) collective-permute-start(bf16[768,2048]{1,0:T(8,128)(2,1)} %bitcast.15), channel_id=1, source_target_pairs={{0,1},{1,0},{2,3},{3,2},{4,5},{5,4},{6,7},{7,6},{8,9},{9,8},{10,11... | collective-permute-start | bytes 9437192 | tf_op jit(solution)/shard_map/ppermute | solution.py:162
  0.5 19.1 %collective-permute-start.2 = (bf16[384,2048]{1,0:T(8,128)(2,1)}, bf16[384,2048]{1,0:T(8,128)(2,1)S(1)}, u32[]{:S(2)}, u32[]{:S(2)}) collective-permute-start(bf16[384,2048]{1,0:T(8,128)(2,1)} %bitcast.20), channel_id=1, source_target_pairs={{0,1},{1,0},{2,3},{3,2},{4,5},{5,4},{6,7},{7,6},{8,9},{9,8},{10,11... | collective-permute-start | bytes 4718600 | tf_op jit(solution)/shard_map/ppermute | solution.py:162
  1.0 0.8 %copy-start.4 = (bf16[1,8,2048]{2,1,0:T(8,128)(2,1)S(1)}, bf16[1,8,2048]{2,1,0:T(8,128)(2,1)}, u32[]{:S(2)}) copy-start(bf16[1,8,2048]{2,1,0:T(8,128)(2,1)} %param.9) | copy-start | bytes 98308
  1.0 0.8 %copy-start.5 = (f32[2048]{0:T(1024)S(1)}, f32[2048]{0:T(1024)}, u32[]{:S(2)}) copy-start(f32[2048]{0:T(1024)} %param.10) | copy-start | bytes 24580
  1.0 0.8 %copy-start.6 = (s32[2,1,8,8]{3,2,1,0:T(8,128)S(1)}, s32[2,1,8,8]{3,2,1,0:T(8,128)}, u32[]{:S(2)}) copy-start(s32[2,1,8,8]{3,2,1,0:T(8,128)} %refs_4_.1) | copy-start | bytes 1540
  1.0 0.8 %copy-start.7 = (f32[2,1,8,8]{3,2,1,0:T(8,128)S(1)}, f32[2,1,8,8]{3,2,1,0:T(8,128)}, u32[]{:S(2)}) copy-start(f32[2,1,8,8]{3,2,1,0:T(8,128)} %refs_5_.1) | copy-start | bytes 1540
  1.0 0.8 %copy-start.8 = (s32[1,4]{1,0:T(1,128)S(1)}, s32[1,4]{1,0:T(1,128)}, u32[]{:S(2)}) copy-start(s32[1,4]{1,0:T(1,128)} %refs_6_.1) | copy-start | bytes 52
  1.0 18.6 %copy-start = (bf16[1,768,2048]{2,1,0:T(8,128)(2,1)S(1)}, bf16[1,768,2048]{2,1,0:T(8,128)(2,1)}, u32[]{:S(2)}) copy-start(bf16[1,768,2048]{2,1,0:T(8,128)(2,1)} %param.14) | copy-start | bytes 9437188
  1.0 18.6 %copy-start.1 = (bf16[1,768,2048]{2,1,0:T(8,128)(2,1)S(1)}, bf16[1,768,2048]{2,1,0:T(8,128)(2,1)}, u32[]{:S(2)}) copy-start(bf16[1,768,2048]{2,1,0:T(8,128)(2,1)} %param.15) | copy-start | bytes 9437188
  1.0 18.6 %collective-permute-start.3 = (bf16[384,2048]{1,0:T(8,128)(2,1)}, bf16[384,2048]{1,0:T(8,128)(2,1)S(1)}, u32[]{:S(2)}, u32[]{:S(2)}) collective-permute-start(bf16[384,2048]{1,0:T(8,128)(2,1)} %bitcast.22), channel_id=1, source_target_pairs={{0,1},{1,0},{2,3},{3,2},{4,5},{5,4},{6,7},{7,6},{8,9},{9,8},{10,11... | collective-permute-start | bytes 4718600 | tf_op jit(solution)/shard_map/ppermute | solution.py:162
  47.5 6.6 %copy-start.2 = (bf16[1,384,2048]{2,1,0:T(8,128)(2,1)S(1)}, bf16[1,384,2048]{2,1,0:T(8,128)(2,1)}, u32[]{:S(2)}) copy-start(bf16[1,384,2048]{2,1,0:T(8,128)(2,1)} %param.16) | copy-start | bytes 4718596
  47.5 6.6 %copy-start.3 = (bf16[1,384,2048]{2,1,0:T(8,128)(2,1)S(1)}, bf16[1,384,2048]{2,1,0:T(8,128)(2,1)}, u32[]{:S(2)}) copy-start(bf16[1,384,2048]{2,1,0:T(8,128)(2,1)} %param.17) | copy-start | bytes 4718596
  47.5 6.6 %collective-permute-start.4 = (bf16[64,2176]{1,0:T(8,128)(2,1)S(1)}, bf16[64,2176]{1,0:T(8,128)(2,1)S(1)}, u32[]{:S(2)}, u32[]{:S(2)}) collective-permute-start(bf16[64,2176]{1,0:T(8,128)(2,1)S(1)} %shard_map.95.refs_0_), channel_id=1, source_target_pairs={{0,16},{16,0},{1,17},{17,1},{2,18},{18,2},{3,19},{19,3},{4,20},{20... | collective-permute-start | bytes 835592 | tf_op jit(solution)/shard_map/ppermute | solution.py:166
  56.2 6.4 %collective-permute-start.5 = (bf16[64,2048]{1,0:T(8,128)(2,1)S(1)}, bf16[64,2048]{1,0:T(8,128)(2,1)S(1)}, u32[]{:S(2)}, u32[]{:S(2)}) collective-permute-start(bf16[64,2048]{1,0:T(8,128)(2,1)S(1)} %get-tuple-element.20), channel_id=1, source_target_pairs={{0,16},{16,0},{1,17},{17,1},{2,18},{18,2},{3,19},{19,3},{4,20},{20... | collective-permute-start | bytes 786440 | tf_op jit(solution)/shard_map/ppermute | solution.py:166

commit v15 on v14

--- a/solution.py
+++ b/solution.py
@@ -166,6 +166,12 @@
     return lax.ppermute(value, "group", [(0, 1), (1, 0)])
 
 
+def hop_group(value):
+    size = lax.axis_size("expert")
+    pairs = [(i, i ^ size) for i in range(1, 2 * size, 2)]
+    return lax.ppermute(value, ("group", "expert"), pairs)
+
+
 def spread(blocks):
     size = lax.axis_size("expert")
     groups = [
@@ -193,10 +199,12 @@
     )
     stale = stale + tuple(swap_core(part) for part in stale)
     learner = learner + tuple(swap_core(part) for part in learner)
+    turn = hop_group(section.astype(jnp.bfloat16))
     (blocks,) = on_vmem(
         pack_kernel,
         (section, expert, tokens[0], gain, routes, route_scale, changed),
         [((chips, row_count, packed), jnp.bfloat16)],
+        after=(turn,),
     )
     tables = spread(blocks).reshape(half, packed)
     rows, state = tables, tokens[0]

time: 75.5 us -> 79.3 us (1.050)
  blocking collectives: 53.7 us -> 56.8 us
    all_to_all x4, blocking collectives: 53.7 us -> 56.8 us  [spread(): lax.all_to_all(blocks, 'expert', 0, 0, axis_index_groups=groups, tiled=True)]
  transfers between devices with their start and end apart: 6 -> 7, of which waited for: 2 -> 2; matrix products, arithmetic and copies ran while one was open for 0% -> 0% of each run, Pallas kernels for 5% -> 5%
where the time goes in v15:
time: 79.3 us; the launch traced here: 79 us
  blocking collectives  56.8 us (72%)
  Pallas kernels  10.1 us (13%)
  waiting for transfers between devices  6.89 us (9%)
  starting transfers between devices  4.95 us (6%)
    all_to_all x4, blocking collectives, spread(): lax.all_to_all(blocks, 'expert', 0, 0, axis_index_groups=groups, tiled=True)  56.8 us
    pallas_call x8, Pallas kernels, on_vmem(): pl.pallas_call(body, out_shape=[jax.ShapeDtypeStruct(shape, kind) for sha...  10.1 us
    ppermute x2, waiting for transfers between devices, swap_group(): return lax.ppermute(value, 'group', [(0, 1), (1, 0)])  6.88 us
    ppermute x2, starting transfers between devices, swap_group(): return lax.ppermute(value, 'group', [(0, 1), (1, 0)])  3.07 us
  transfers between devices with their start and end apart: 7, of which 2 were waited for; matrix products, arithmetic and copies ran while one was open for 0% of the time, Pallas kernels for 5%

profile of v15, /device:TPU:0, one launch (start us, length us, event | category | flops | bytes accessed | tf_op | source)
XLA Modules:
  0.0 79.0 jit_solution(2177836722782146939)
XLA Ops:
  0.0 0.5 collective-permute-start.1
  0.5 0.1 collective-permute-start.2
  0.5 0.5 collective-permute-start.3
  1.0 0.1 collective-permute-start.4
  1.1 0.8 collective-permute-start
  1.9 0.0 collective-permute-done.refs_7_
  2.0 0.1 shard_map.92
  2.1 15.9 %all_to_all.20 = bf16[8,8,2176]{2,1,0:T(8,128)(2,1)S(1)} all-to-all(bf16[8,8,2176]{2,1,0:T(8,128)(2,1)S(1)} %shard_map.92), channel_id=1, replica_groups={{0,4,8,12,2,6,10,14},{1,5,9,13,3,7,11,15},{16,20,24,28,18,22,26,30},{17..., dimensions={0} | all-to-all | bytes 557056 | tf_op jit(solution)/shard_map/all_to_all | solution.py:180
  18.1 0.0 collective-permute-done.2.refs_4_
  18.1 3.5 %shard_map.93 = bf16[64,2048]{1,0:T(8,128)(2,1)S(1)} custom-call(bf16[64,2176]{1,0:T(8,128)(2,1)S(1)} %bitcast.18, bf16[768,2048]{1,0:T(8,128)(2,1)S(1)} %bitcast.13, bf16[768,2048]{1,0:T(8,128)(2,1)S(1)} %bitcast.16, bf16[768,2048]{1,0:T(8,128)(2,1)S(1)} %collective-permute-done.1.refs_3_, bf16[768,2048]{1,0:T(8,128)(2,1)S(1)} %collective-permute-done.2.refs_4_, ...), custom_call_target="tpu_custom_call" | custom-call | flops 3221225472 | bytes 25165824 | tf_op jit(solution)/shard_map/pallas_call | solution.py:139
  21.6 15.4 %all_to_all.21.refs_1_ = bf16[8,8,2048]{2,1,0:T(8,128)(2,1)S(1)} all-to-all(bf16[8,8,2048]{2,1,0:T(8,128)(2,1)S(1)} %bitcast.24), channel_id=1, replica_groups={{0,4,8,12,2,6,10,14},{1,5,9,13,3,7,11,15},{16,20,24,28,18,22,26,30},{17..., dimensions={0} | all-to-all | bytes 524288 | tf_op jit(solution)/shard_map/all_to_all | solution.py:180
  37.0 0.2 shard_map.94
  37.1 12.7 %all_to_all.22 = bf16[8,8,2048]{2,1,0:T(8,128)(2,1)S(1)} all-to-all(bf16[8,8,2048]{2,1,0:T(8,128)(2,1)S(1)} %get-tuple-element.16), channel_id=1, replica_groups={{0,4,8,12,2,6,10,14},{1,5,9,13,3,7,11,15},{16,20,24,28,18,22,26,30},{17..., dimensions={0} | all-to-all | bytes 524288 | tf_op jit(solution)/shard_map/all_to_all | solution.py:180
  49.8 0.0 copy-start.2
  49.8 0.0 copy-start.3
  49.8 1.5 %collective-permute-start.5 = (bf16[64,2176]{1,0:T(8,128)(2,1)S(1)}, bf16[64,2176]{1,0:T(8,128)(2,1)S(1)}, u32[]{:S(2)}, u32[]{:S(2)}) collective-permute-start(bf16[64,2176]{1,0:T(8,128)(2,1)S(1)} %shard_map.95.refs_0_), channel_id=1, source_target_pairs={{0,16},{16,0},{1,17},{17,1},{2,18},{18,2},{3,19},{19,3},{4,20},{20... | collective-permute-start | bytes 835592 | tf_op jit(solution)/shard_map/ppermute | solution.py:166
  51.4 3.5 %shard_map.96 = f32[64,2048]{1,0:T(8,128)S(1)} custom-call(bf16[64,2176]{1,0:T(8,128)(2,1)S(1)} %shard_map.95.refs_0_, bf16[768,2048]{1,0:T(8,128)(2,1)S(1)} %bitcast.14, bf16[768,2048]{1,0:T(8,128)(2,1)S(1)} %bitcast.17, bf16[768,2048]{1,0:T(8,128)(2,1)S(1)} %collective-permute-done.1.refs_3_, bf16[768,2048]{1,0:T(8,128)(2,1)S(1)} %collective-permute-done.2.refs_4_), custom_call_target="tpu_custom_call" | custom-call | flops 3221225472 | bytes 25165824 | tf_op jit(solution)/shard_map/pallas_call | solution.py:139
  54.9 2.0 %collective-permute-done.5.refs_1_ = bf16[64,2176]{1,0:T(8,128)(2,1)S(1)} collective-permute-done((bf16[64,2176]{1,0:T(8,128)(2,1)S(1)}, bf16[64,2176]{1,0:T(8,128)(2,1)S(1)}, u32[]{:S(2)}, u32[]{:S(2)}) %collective-permute-start.5) | collective-permute-done | bytes 278560 | tf_op jit(solution)/shard_map/ppermute | solution.py:166
  56.9 2.1 %shard_map.97 = (f32[64,2048]{1,0:T(8,128)S(1)}, bf16[64,2048]{1,0:T(8,128)(2,1)S(1)}) custom-call(bf16[64,2176]{1,0:T(8,128)(2,1)S(1)} %shard_map.95.refs_0_, bf16[64,2176]{1,0:T(8,128)(2,1)S(1)} %collective-permute-done.5.refs_1_, bf16[384,2048]{1,0:T(8,128)(2,1)S(1)} %bitcast.21, bf16[384,2048]{1,0:T(8,128)(2,1)S(1)} %bitcast.23, ...), custom_call_target="tpu_custom_call" | custom-call | flops 1610612736 | bytes 12582912 | tf_op jit(solution)/shard_map/pallas_call | solution.py:139
  59.0 1.5 %collective-permute-start.6 = (bf16[64,2048]{1,0:T(8,128)(2,1)S(1)}, bf16[64,2048]{1,0:T(8,128)(2,1)S(1)}, u32[]{:S(2)}, u32[]{:S(2)}) collective-permute-start(bf16[64,2048]{1,0:T(8,128)(2,1)S(1)} %get-tuple-element.20), channel_id=1, source_target_pairs={{0,16},{16,0},{1,17},{17,1},{2,18},{18,2},{3,19},{19,3},{4,20},{20... | collective-permute-start | bytes 786440 | tf_op jit(solution)/shard_map/ppermute | solution.py:166
  60.5 4.9 %collective-permute-done.6 = bf16[64,2048]{1,0:T(8,128)(2,1)S(1)} collective-permute-done((bf16[64,2048]{1,0:T(8,128)(2,1)S(1)}, bf16[64,2048]{1,0:T(8,128)(2,1)S(1)}, u32[]{:S(2)}, u32[]{:S(2)}) %collective-permute-start.6) | collective-permute-done | bytes 262176 | tf_op jit(solution)/shard_map/ppermute | solution.py:166
  65.4 0.1 fusion
  65.5 12.8 %all_to_all.23.refs_1_ = bf16[8,8,2048]{2,1,0:T(8,128)(2,1)S(1)} all-to-all(bf16[8,8,2048]{2,1,0:T(8,128)(2,1)S(1)} %fusion), channel_id=1, replica_groups={{0,4,8,12,2,6,10,14},{1,5,9,13,3,7,11,15},{16,20,24,28,18,22,26,30},{17..., dimensions={0} | all-to-all | bytes 524288 | tf_op jit(solution)/shard_map/all_to_all | solution.py:180
  78.4 0.7 shard_map.98
  (22 shorter events, 0.1 us)
Async XLA Ops:
  0.0 18.1 %collective-permute-start.1 = (bf16[768,2048]{1,0:T(8,128)(2,1)}, bf16[768,2048]{1,0:T(8,128)(2,1)S(1)}, u32[]{:S(2)}, u32[]{:S(2)}) collective-permute-start(bf16[768,2048]{1,0:T(8,128)(2,1)} %bitcast.12), channel_id=1, source_target_pairs={{0,1},{1,0},{2,3},{3,2},{4,5},{5,4},{6,7},{7,6},{8,9},{9,8},{10,11... | collective-permute-start | bytes 9437192 | tf_op jit(solution)/shard_map/ppermute | solution.py:162
  0.5 17.7 %collective-permute-start.2 = (bf16[768,2048]{1,0:T(8,128)(2,1)}, bf16[768,2048]{1,0:T(8,128)(2,1)S(1)}, u32[]{:S(2)}, u32[]{:S(2)}) collective-permute-start(bf16[768,2048]{1,0:T(8,128)(2,1)} %bitcast.15), channel_id=1, source_target_pairs={{0,1},{1,0},{2,3},{3,2},{4,5},{5,4},{6,7},{7,6},{8,9},{9,8},{10,11... | collective-permute-start | bytes 9437192 | tf_op jit(solution)/shard_map/ppermute | solution.py:162
  0.5 17.6 %collective-permute-start.3 = (bf16[384,2048]{1,0:T(8,128)(2,1)}, bf16[384,2048]{1,0:T(8,128)(2,1)S(1)}, u32[]{:S(2)}, u32[]{:S(2)}) collective-permute-start(bf16[384,2048]{1,0:T(8,128)(2,1)} %bitcast.20), channel_id=1, source_target_pairs={{0,1},{1,0},{2,3},{3,2},{4,5},{5,4},{6,7},{7,6},{8,9},{9,8},{10,11... | collective-permute-start | bytes 4718600 | tf_op jit(solution)/shard_map/ppermute | solution.py:162
  1.0 1.0 %copy-start.4 = (bf16[1,8,2048]{2,1,0:T(8,128)(2,1)S(1)}, bf16[1,8,2048]{2,1,0:T(8,128)(2,1)}, u32[]{:S(2)}) copy-start(bf16[1,8,2048]{2,1,0:T(8,128)(2,1)} %param.9) | copy-start | bytes 98308
  1.0 1.0 %copy-start.5 = (f32[2048]{0:T(1024)S(1)}, f32[2048]{0:T(1024)}, u32[]{:S(2)}) copy-start(f32[2048]{0:T(1024)} %param.10) | copy-start | bytes 24580
  1.0 1.0 %copy-start.6 = (s32[2,1,8,8]{3,2,1,0:T(8,128)S(1)}, s32[2,1,8,8]{3,2,1,0:T(8,128)}, u32[]{:S(2)}) copy-start(s32[2,1,8,8]{3,2,1,0:T(8,128)} %refs_4_.1) | copy-start | bytes 1540
  1.0 1.0 %copy-start.7 = (f32[2,1,8,8]{3,2,1,0:T(8,128)S(1)}, f32[2,1,8,8]{3,2,1,0:T(8,128)}, u32[]{:S(2)}) copy-start(f32[2,1,8,8]{3,2,1,0:T(8,128)} %refs_5_.1) | copy-start | bytes 1540
  1.0 1.0 %copy-start.8 = (s32[1,4]{1,0:T(1,128)S(1)}, s32[1,4]{1,0:T(1,128)}, u32[]{:S(2)}) copy-start(s32[1,4]{1,0:T(1,128)} %refs_6_.1) | copy-start | bytes 52
  1.0 17.1 %copy-start = (bf16[1,768,2048]{2,1,0:T(8,128)(2,1)S(1)}, bf16[1,768,2048]{2,1,0:T(8,128)(2,1)}, u32[]{:S(2)}) copy-start(bf16[1,768,2048]{2,1,0:T(8,128)(2,1)} %param.14) | copy-start | bytes 9437188
  1.0 17.1 %copy-start.1 = (bf16[1,768,2048]{2,1,0:T(8,128)(2,1)S(1)}, bf16[1,768,2048]{2,1,0:T(8,128)(2,1)}, u32[]{:S(2)}) copy-start(bf16[1,768,2048]{2,1,0:T(8,128)(2,1)} %param.15) | copy-start | bytes 9437188
  1.0 17.1 %collective-permute-start.4 = (bf16[384,2048]{1,0:T(8,128)(2,1)}, bf16[384,2048]{1,0:T(8,128)(2,1)S(1)}, u32[]{:S(2)}, u32[]{:S(2)}) collective-permute-start(bf16[384,2048]{1,0:T(8,128)(2,1)} %bitcast.22), channel_id=1, source_target_pairs={{0,1},{1,0},{2,3},{3,2},{4,5},{5,4},{6,7},{7,6},{8,9},{9,8},{10,11... | collective-permute-start | bytes 4718600 | tf_op jit(solution)/shard_map/ppermute | solution.py:162
  1.1 0.8 %collective-permute-start = (bf16[8,128]{1,0:T(8,128)(2,1)S(1)}, bf16[8,128]{1,0:T(8,128)(2,1)S(1)}, u32[]{:S(2)}, u32[]{:S(2)}) collective-permute-start(bf16[8,128]{1,0:T(8,128)(2,1)S(1)} %convert_element_type.9), channel_id=1, source_target_pairs={{1,17},{3,19},{5,21},{7,23},{9,25},{11,27},{13,29},{15,31},{17,1},... | collective-permute-start | bytes 6152 | tf_op jit(solution)/shard_map/ppermute | solution.py:172
  49.8 7.0 %copy-start.2 = (bf16[1,384,2048]{2,1,0:T(8,128)(2,1)S(1)}, bf16[1,384,2048]{2,1,0:T(8,128)(2,1)}, u32[]{:S(2)}) copy-start(bf16[1,384,2048]{2,1,0:T(8,128)(2,1)} %param.16) | copy-start | bytes 4718596
  49.8 7.0 %copy-start.3 = (bf16[1,384,2048]{2,1,0:T(8,128)(2,1)S(1)}, bf16[1,384,2048]{2,1,0:T(8,128)(2,1)}, u32[]{:S(2)}) copy-start(bf16[1,384,2048]{2,1,0:T(8,128)(2,1)} %param.17) | copy-start | bytes 4718596
  49.8 7.0 %collective-permute-start.5 = (bf16[64,2176]{1,0:T(8,128)(2,1)S(1)}, bf16[64,2176]{1,0:T(8,128)(2,1)S(1)}, u32[]{:S(2)}, u32[]{:S(2)}) collective-permute-start(bf16[64,2176]{1,0:T(8,128)(2,1)S(1)} %shard_map.95.refs_0_), channel_id=1, source_target_pairs={{0,16},{16,0},{1,17},{17,1},{2,18},{18,2},{3,19},{19,3},{4,20},{20... | collective-permute-start | bytes 835592 | tf_op jit(solution)/shard_map/ppermute | solution.py:166
  59.0 6.4 %collective-permute-start.6 = (bf16[64,2048]{1,0:T(8,128)(2,1)S(1)}, bf16[64,2048]{1,0:T(8,128)(2,1)S(1)}, u32[]{:S(2)}, u32[]{:S(2)}) collective-permute-start(bf16[64,2048]{1,0:T(8,128)(2,1)S(1)} %get-tuple-element.20), channel_id=1, source_target_pairs={{0,16},{16,0},{1,17},{17,1},{2,18},{18,2},{3,19},{19,3},{4,20},{20... | collective-permute-start | bytes 786440 | tf_op jit(solution)/shard_map/ppermute | solution.py:166

commit v16 on v14

--- a/solution.py
+++ b/solution.py
@@ -106,10 +106,7 @@
     out[:, width:] = tables[:, width:]
 
 
-def mlp_kernel(experts, step, fresh, set_count, *refs):
-    sources, refs = refs[:set_count], refs[set_count:]
-    weights, outs = refs[:4], refs[4:]
-    count, width = outs[0].shape
+def weighted_outputs(experts, step, fresh, sources, weights, width):
     rows = jnp.concatenate([source[:, :width] for source in sources], axis=0)
     table = jnp.concatenate([source[:, width:] for source in sources], axis=0)
     inputs = jnp.concatenate([rows] * max(1, MATMUL_ROWS // rows.shape[0]), axis=0)
@@ -125,8 +122,22 @@
         result = jnp.dot(hidden, down[...], preferred_element_type=jnp.float32)
         result = result[: rows.shape[0]] * row_weights(experts, table, owner, step, fresh)
         total = result if total is None else total + result
-    for i, out in enumerate(outs):
-        out[...] = total[i * count : (i + 1) * count].astype(out.dtype)
+    return total
+
+
+def stale_kernel(experts, step, rows, *refs):
+    weights, out = refs[:4], refs[4]
+    total = weighted_outputs(experts, step, False, [rows], weights, out.shape[1])
+    out[...] = total.astype(out.dtype)
+
+
+def fresh_kernel(experts, step, rows, other, *refs):
+    weights, old, out = refs[:4], refs[4], refs[5]
+    _, count, width = out.shape
+    total = weighted_outputs(experts, step, True, [rows, other], weights, width)
+    group = lax.axis_index("group")
+    out[group] = (old[...] + total[:count]).astype(out.dtype)
+    out[1 - group] = total[count:].astype(out.dtype)
 
 
 def on_vmem(kernel, inputs, outputs, limit=4 * MIB, cost=None, after=()):
@@ -146,15 +157,14 @@
     )(*inputs, *after)
 
 
-def run_mlp(row_sets, weights, step, fresh, out_types, after=()):
-    count, width = row_sets[0].shape[0], weights[0].shape[1]
+def run_mlp(kernel, step, row_sets, weights, output, before=(), after=()):
     size = sum(part.size for part in weights)
     cost = pl.CostEstimate(
         flops=4 * MATMUL_ROWS * size, bytes_accessed=4 * size, transcendentals=0
     )
-    kernel = functools.partial(mlp_kernel, lax.axis_size("expert"), step, fresh, len(row_sets))
-    outputs = [((count, width), out_type) for out_type in out_types]
-    return on_vmem(kernel, tuple(row_sets) + tuple(weights), outputs, 8 * MIB, cost, after)
+    kernel = functools.partial(kernel, lax.axis_size("expert"), step)
+    inputs = tuple(row_sets) + tuple(weights) + tuple(before)
+    return on_vmem(kernel, inputs, [output], 8 * MIB, cost, after)[0]
 
 
 def swap_core(value):
@@ -172,6 +182,21 @@
         [start + core for y in range(2) for start in range(2 * y, size, 4)] for core in range(2)
     ]
     return lax.all_to_all(blocks, "expert", 0, 0, axis_index_groups=groups, tiled=True)
+
+
+def spread_groups(blocks):
+    size = lax.axis_size("expert")
+    groups = [
+        [
+            group * size + start + core
+            for group in range(2)
+            for y in range(2)
+            for start in range(2 * y, size, 4)
+        ]
+        for core in range(2)
+    ]
+    axes = ("group", "expert")
+    return lax.all_to_all(blocks, axes, 0, 0, axis_index_groups=groups, tiled=True)
 
 
 def exchange_plan(tokens, norm_gain, routes, route_scale, changed, stale, learner):
@@ -202,7 +227,9 @@
     rows, state = tables, tokens[0]
     for step in range(steps_total):
         if step == 0:
-            (share,) = run_mlp([rows], stale, step, False, [jnp.bfloat16], learner[2:])
+            output = ((half, width), jnp.bfloat16)
+            share = run_mlp(stale_kernel, step, [rows], stale, output, after=learner[2:])
+            returned = spread(share.reshape(chips, row_count, width))
         else:
             state, blocks = on_vmem(
                 next_kernel,
@@ -212,12 +239,11 @@
             rows = spread(blocks).reshape(half, width)
             (rows,) = on_vmem(join_kernel, (rows, tables), [((half, packed), jnp.bfloat16)])
             other = swap_group(rows)
-            (old,) = run_mlp([rows], stale, step, False, [jnp.float32])
+            old = run_mlp(stale_kernel, step, [rows], stale, ((half, width), jnp.float32))
             other, old = lax.optimization_barrier((other, old))
-            new, away = run_mlp([rows, other], learner, step, True, [jnp.float32, jnp.bfloat16])
-            share = old + new + swap_group(away).astype(jnp.float32)
-            share = share.astype(jnp.bfloat16)
-        returned = spread(share.reshape(chips, row_count, width))
+            output = ((2, half, width), jnp.bfloat16)
+            share = run_mlp(fresh_kernel, step, [rows, other], learner, output, (old,))
+            returned = spread_groups(share.reshape(2 * chips, row_count, width))
     (updated,) = on_vmem(last_kernel, (state, returned), [((row_count, width), jnp.bfloat16)])
     return updated[None]
 

time: 75.5 us -> 76 us (level)
  blocking collectives: 53.7 us -> 60.7 us
  waiting for transfers between devices: 6.49 us -> 1.61 us
  starting transfers between devices: 4.19 us -> 2.64 us
    all_to_all x0 -> x1, blocking collectives: none -> 18.8 us  [spread_groups(): lax.all_to_all(blocks, axes, 0, 0, axis_index_groups=groups, tiled=True)]
    all_to_all x4 -> x3, blocking collectives: 53.7 us -> 41.9 us  [spread(): lax.all_to_all(blocks, 'expert', 0, 0, axis_index_groups=groups, tiled=True)]
    ppermute x2 -> x1, waiting for transfers between devices: 6.48 us -> 1.6 us  [swap_group(): return lax.ppermute(value, 'group', [(0, 1), (1, 0)])]
    ppermute x2 -> x1, starting transfers between devices: 3.11 us -> 1.55 us  [swap_group(): return lax.ppermute(value, 'group', [(0, 1), (1, 0)])]
  transfers between devices with their start and end apart: 6 -> 5, of which waited for: 2 -> 1; matrix products, arithmetic and copies ran while one was open for 0% -> 0% of each run, Pallas kernels for 5% -> 5%
where the time goes in v16:
time: 76 us; the launch traced here: 75.7 us
  blocking collectives  60.7 us (80%)
  Pallas kernels  10 us (13%)
  starting transfers between devices  2.64 us (3%)
  waiting for transfers between devices  1.61 us (2%)
    all_to_all x3, blocking collectives, spread(): lax.all_to_all(blocks, 'expert', 0, 0, axis_index_groups=groups, tiled=True)  41.9 us
    all_to_all x1, blocking collectives, spread_groups(): lax.all_to_all(blocks, axes, 0, 0, axis_index_groups=groups, tiled=True)  18.8 us
    pallas_call x8, Pallas kernels, on_vmem(): pl.pallas_call(body, out_shape=[jax.ShapeDtypeStruct(shape, kind) for sha...  10 us
    ppermute x1, waiting for transfers between devices, swap_group(): return lax.ppermute(value, 'group', [(0, 1), (1, 0)])  1.6 us
    ppermute x1, starting transfers between devices, swap_group(): return lax.ppermute(value, 'group', [(0, 1), (1, 0)])  1.55 us
  transfers between devices with their start and end apart: 5, of which 1 were waited for; matrix products, arithmetic and copies ran while one was open for 0% of the time, Pallas kernels for 5%

profile of v16, /device:TPU:0, one launch (start us, length us, event | category | flops | bytes accessed | tf_op | source)
XLA Modules:
  0.0 75.7 jit_solution(14343738302071156191)
XLA Ops:
  0.0 0.5 collective-permute-start
  0.5 0.1 collective-permute-start.1
  0.5 0.5 collective-permute-start.2
  1.0 0.1 collective-permute-start.3
  1.1 0.6 copy-done.4
  1.7 0.0 copy-done.7
  1.7 0.1 shard_map.92
  1.9 17.7 %all_to_all.20 = bf16[8,8,2176]{2,1,0:T(8,128)(2,1)S(1)} all-to-all(bf16[8,8,2176]{2,1,0:T(8,128)(2,1)S(1)} %shard_map.92), channel_id=1, replica_groups={{0,4,8,12,2,6,10,14},{1,5,9,13,3,7,11,15},{16,20,24,28,18,22,26,30},{17..., dimensions={0} | all-to-all | bytes 557056 | tf_op jit(solution)/shard_map/all_to_all | solution.py:184
  19.6 0.0 collective-permute-done.2.refs_5_.refs_4_
  19.6 0.0 collective-permute-done.3.refs_6_.refs_5_
  19.6 0.0 collective-permute-done.refs_3_
  19.6 0.0 collective-permute-done.1.refs_4_
  19.6 3.5 %shard_map.93 = bf16[64,2048]{1,0:T(8,128)(2,1)S(1)} custom-call(bf16[64,2176]{1,0:T(8,128)(2,1)S(1)} %bitcast.17, bf16[768,2048]{1,0:T(8,128)(2,1)S(1)} %bitcast.12, bf16[768,2048]{1,0:T(8,128)(2,1)S(1)} %bitcast.15, bf16[768,2048]{1,0:T(8,128)(2,1)S(1)} %collective-permute-done.refs_3_, bf16[768,2048]{1,0:T(8,128)(2,1)S(1)} %collective-permute-done.1.refs_4_, ...), custom_call_target="tpu_custom_call" | custom-call | flops 3221225472 | bytes 25165824 | tf_op jit(solution)/shard_map/pallas_call | solution.py:150
  23.1 12.4 %all_to_all.21.refs_1_ = bf16[8,8,2048]{2,1,0:T(8,128)(2,1)S(1)} all-to-all(bf16[8,8,2048]{2,1,0:T(8,128)(2,1)S(1)} %bitcast.24), channel_id=1, replica_groups={{0,4,8,12,2,6,10,14},{1,5,9,13,3,7,11,15},{16,20,24,28,18,22,26,30},{17..., dimensions={0} | all-to-all | bytes 524288 | tf_op jit(solution)/shard_map/all_to_all | solution.py:184
  35.5 0.2 shard_map.94
  35.7 11.8 %all_to_all.22 = bf16[8,8,2048]{2,1,0:T(8,128)(2,1)S(1)} all-to-all(bf16[8,8,2048]{2,1,0:T(8,128)(2,1)S(1)} %get-tuple-element.14), channel_id=1, replica_groups={{0,4,8,12,2,6,10,14},{1,5,9,13,3,7,11,15},{16,20,24,28,18,22,26,30},{17..., dimensions={0} | all-to-all | bytes 524288 | tf_op jit(solution)/shard_map/all_to_all | solution.py:184
  47.5 0.0 copy-start.2
  47.5 0.0 copy-start.3
  47.5 1.6 %collective-permute-start.4 = (bf16[64,2176]{1,0:T(8,128)(2,1)S(1)}, bf16[64,2176]{1,0:T(8,128)(2,1)S(1)}, u32[]{:S(2)}, u32[]{:S(2)}) collective-permute-start(bf16[64,2176]{1,0:T(8,128)(2,1)S(1)} %shard_map.95.refs_0_), channel_id=1, source_target_pairs={{0,16},{16,0},{1,17},{17,1},{2,18},{18,2},{3,19},{19,3},{4,20},{20... | collective-permute-start | bytes 835592 | tf_op jit(solution)/shard_map/ppermute | solution.py:176
  49.1 3.5 %shard_map.96.refs_6_ = f32[64,2048]{1,0:T(8,128)S(1)} custom-call(bf16[64,2176]{1,0:T(8,128)(2,1)S(1)} %shard_map.95.refs_0_, bf16[768,2048]{1,0:T(8,128)(2,1)S(1)} %bitcast.13, bf16[768,2048]{1,0:T(8,128)(2,1)S(1)} %bitcast.16, bf16[768,2048]{1,0:T(8,128)(2,1)S(1)} %collective-permute-done.refs_3_, bf16[768,2048]{1,0:T(8,128)(2,1)S(1)} %collective-permute-done.1.refs_4_), custom_call_target="tpu_custom_call" | custom-call | flops 3221225472 | bytes 25165824 | tf_op jit(solution)/shard_map/pallas_call | solution.py:150
  52.5 1.6 %collective-permute-done.4.refs_1_ = bf16[64,2176]{1,0:T(8,128)(2,1)S(1)} collective-permute-done((bf16[64,2176]{1,0:T(8,128)(2,1)S(1)}, bf16[64,2176]{1,0:T(8,128)(2,1)S(1)}, u32[]{:S(2)}, u32[]{:S(2)}) %collective-permute-start.4) | collective-permute-done | bytes 278560 | tf_op jit(solution)/shard_map/ppermute | solution.py:176
  54.1 2.1 %shard_map.97 = bf16[2,64,2048]{2,1,0:T(8,128)(2,1)S(1)} custom-call(bf16[64,2176]{1,0:T(8,128)(2,1)S(1)} %shard_map.95.refs_0_, bf16[64,2176]{1,0:T(8,128)(2,1)S(1)} %collective-permute-done.4.refs_1_, bf16[384,2048]{1,0:T(8,128)(2,1)S(1)} %bitcast.21, bf16[384,2048]{1,0:T(8,128)(2,1)S(1)} %bitcast.23, ...), custom_call_target="tpu_custom_call" | custom-call | flops 1610612736 | bytes 12582912 | tf_op jit(solution)/shard_map/pallas_call | solution.py:150
  56.2 18.8 %all_to_all.23.refs_1_ = bf16[16,8,2048]{2,1,0:T(8,128)(2,1)S(1)} all-to-all(bf16[16,8,2048]{2,1,0:T(8,128)(2,1)S(1)} %bitcast.19), channel_id=1, replica_groups={{0,4,8,12,2,6,10,14,16,20,24,28,18,22,26,30},{1,5,9,13,3,7,11,15,17,21,..., dimensions={0} | all-to-all | bytes 1048576 | tf_op jit(solution)/shard_map/all_to_all | solution.py:199
  75.0 0.7 shard_map.98
  (16 shorter events, 0.1 us)
Async XLA Ops:
  0.0 19.6 %collective-permute-start = (bf16[768,2048]{1,0:T(8,128)(2,1)}, bf16[768,2048]{1,0:T(8,128)(2,1)S(1)}, u32[]{:S(2)}, u32[]{:S(2)}) collective-permute-start(bf16[768,2048]{1,0:T(8,128)(2,1)} %bitcast.11), channel_id=1, source_target_pairs={{0,1},{1,0},{2,3},{3,2},{4,5},{5,4},{6,7},{7,6},{8,9},{9,8},{10,11... | collective-permute-start | bytes 9437192 | tf_op jit(solution)/shard_map/ppermute | solution.py:172
  0.5 19.1 %collective-permute-start.1 = (bf16[768,2048]{1,0:T(8,128)(2,1)}, bf16[768,2048]{1,0:T(8,128)(2,1)S(1)}, u32[]{:S(2)}, u32[]{:S(2)}) collective-permute-start(bf16[768,2048]{1,0:T(8,128)(2,1)} %bitcast.14), channel_id=1, source_target_pairs={{0,1},{1,0},{2,3},{3,2},{4,5},{5,4},{6,7},{7,6},{8,9},{9,8},{10,11... | collective-permute-start | bytes 9437192 | tf_op jit(solution)/shard_map/ppermute | solution.py:172
  0.5 19.1 %collective-permute-start.2 = (bf16[384,2048]{1,0:T(8,128)(2,1)}, bf16[384,2048]{1,0:T(8,128)(2,1)S(1)}, u32[]{:S(2)}, u32[]{:S(2)}) collective-permute-start(bf16[384,2048]{1,0:T(8,128)(2,1)} %bitcast.20), channel_id=1, source_target_pairs={{0,1},{1,0},{2,3},{3,2},{4,5},{5,4},{6,7},{7,6},{8,9},{9,8},{10,11... | collective-permute-start | bytes 4718600 | tf_op jit(solution)/shard_map/ppermute | solution.py:172
  1.0 0.8 %copy-start.4 = (bf16[1,8,2048]{2,1,0:T(8,128)(2,1)S(1)}, bf16[1,8,2048]{2,1,0:T(8,128)(2,1)}, u32[]{:S(2)}) copy-start(bf16[1,8,2048]{2,1,0:T(8,128)(2,1)} %param.9) | copy-start | bytes 98308
  1.0 0.8 %copy-start.5 = (f32[2048]{0:T(1024)S(1)}, f32[2048]{0:T(1024)}, u32[]{:S(2)}) copy-start(f32[2048]{0:T(1024)} %param.10) | copy-start | bytes 24580
  1.0 0.8 %copy-start.6 = (s32[2,1,8,8]{3,2,1,0:T(8,128)S(1)}, s32[2,1,8,8]{3,2,1,0:T(8,128)}, u32[]{:S(2)}) copy-start(s32[2,1,8,8]{3,2,1,0:T(8,128)} %refs_4_.1) | copy-start | bytes 1540
  1.0 0.8 %copy-start.7 = (f32[2,1,8,8]{3,2,1,0:T(8,128)S(1)}, f32[2,1,8,8]{3,2,1,0:T(8,128)}, u32[]{:S(2)}) copy-start(f32[2,1,8,8]{3,2,1,0:T(8,128)} %refs_5_.1) | copy-start | bytes 1540
  1.0 0.8 %copy-start.8 = (s32[1,4]{1,0:T(1,128)S(1)}, s32[1,4]{1,0:T(1,128)}, u32[]{:S(2)}) copy-start(s32[1,4]{1,0:T(1,128)} %refs_6_.1) | copy-start | bytes 52
  1.0 18.6 %copy-start = (bf16[1,768,2048]{2,1,0:T(8,128)(2,1)S(1)}, bf16[1,768,2048]{2,1,0:T(8,128)(2,1)}, u32[]{:S(2)}) copy-start(bf16[1,768,2048]{2,1,0:T(8,128)(2,1)} %param.14) | copy-start | bytes 9437188
  1.0 18.6 %copy-start.1 = (bf16[1,768,2048]{2,1,0:T(8,128)(2,1)S(1)}, bf16[1,768,2048]{2,1,0:T(8,128)(2,1)}, u32[]{:S(2)}) copy-start(bf16[1,768,2048]{2,1,0:T(8,128)(2,1)} %param.15) | copy-start | bytes 9437188
  1.0 18.6 %collective-permute-start.3 = (bf16[384,2048]{1,0:T(8,128)(2,1)}, bf16[384,2048]{1,0:T(8,128)(2,1)S(1)}, u32[]{:S(2)}, u32[]{:S(2)}) collective-permute-start(bf16[384,2048]{1,0:T(8,128)(2,1)} %bitcast.22), channel_id=1, source_target_pairs={{0,1},{1,0},{2,3},{3,2},{4,5},{5,4},{6,7},{7,6},{8,9},{9,8},{10,11... | collective-permute-start | bytes 4718600 | tf_op jit(solution)/shard_map/ppermute | solution.py:172
  47.5 6.6 %copy-start.2 = (bf16[1,384,2048]{2,1,0:T(8,128)(2,1)S(1)}, bf16[1,384,2048]{2,1,0:T(8,128)(2,1)}, u32[]{:S(2)}) copy-start(bf16[1,384,2048]{2,1,0:T(8,128)(2,1)} %param.16) | copy-start | bytes 4718596
  47.5 6.6 %copy-start.3 = (bf16[1,384,2048]{2,1,0:T(8,128)(2,1)S(1)}, bf16[1,384,2048]{2,1,0:T(8,128)(2,1)}, u32[]{:S(2)}) copy-start(bf16[1,384,2048]{2,1,0:T(8,128)(2,1)} %param.17) | copy-start | bytes 4718596
  47.5 6.6 %collective-permute-start.4 = (bf16[64,2176]{1,0:T(8,128)(2,1)S(1)}, bf16[64,2176]{1,0:T(8,128)(2,1)S(1)}, u32[]{:S(2)}, u32[]{:S(2)}) collective-permute-start(bf16[64,2176]{1,0:T(8,128)(2,1)S(1)} %shard_map.95.refs_0_), channel_id=1, source_target_pairs={{0,16},{16,0},{1,17},{17,1},{2,18},{18,2},{3,19},{19,3},{4,20},{20... | collective-permute-start | bytes 835592 | tf_op jit(solution)/shard_map/ppermute | solution.py:176

commit v17 on v14

--- a/solution.py
+++ b/solution.py
@@ -166,6 +166,11 @@
     return lax.ppermute(value, "group", [(0, 1), (1, 0)])
 
 
+def hop_core(value):
+    size = lax.axis_size("expert")
+    return lax.ppermute(value, "expert", [(i, i - 1) for i in range(1, size, 2)])
+
+
 def spread(blocks):
     size = lax.axis_size("expert")
     groups = [
@@ -193,10 +198,12 @@
     )
     stale = stale + tuple(swap_core(part) for part in stale)
     learner = learner + tuple(swap_core(part) for part in learner)
+    turn = hop_core(section.astype(jnp.bfloat16))
     (blocks,) = on_vmem(
         pack_kernel,
         (section, expert, tokens[0], gain, routes, route_scale, changed),
         [((chips, row_count, packed), jnp.bfloat16)],
+        after=(turn,),
     )
     tables = spread(blocks).reshape(half, packed)
     rows, state = tables, tokens[0]

time: 75.5 us -> 79.1 us (1.048)
  waiting for transfers between devices: 6.49 us -> 9.41 us
  starting transfers between devices: 4.19 us -> 5.75 us
    ppermute x0 -> x1, waiting for transfers between devices: none -> 2.96 us  [hop_core(): lax.ppermute(value, 'expert', [(i, i - 1) for i in range(1, size, 2)])]
    ppermute x0 -> x1, starting transfers between devices: none -> 1.55 us  [hop_core(): lax.ppermute(value, 'expert', [(i, i - 1) for i in range(1, size, 2)])]
  transfers between devices with their start and end apart: 6 -> 7, of which waited for: 2 -> 3; matrix products, arithmetic and copies ran while one was open for 0% -> 0% of each run, Pallas kernels for 5% -> 5%
where the time goes in v17:
time: 79.1 us; the launch traced here: 78.8 us
  blocking collectives  53.3 us (67%)
  Pallas kernels  10.1 us (13%)
  waiting for transfers between devices  9.41 us (12%)
  starting transfers between devices  5.75 us (7%)
    all_to_all x4, blocking collectives, spread(): lax.all_to_all(blocks, 'expert', 0, 0, axis_index_groups=groups, tiled=True)  53.3 us
    pallas_call x8, Pallas kernels, on_vmem(): pl.pallas_call(body, out_shape=[jax.ShapeDtypeStruct(shape, kind) for sha...  10.1 us
    ppermute x2, waiting for transfers between devices, swap_group(): return lax.ppermute(value, 'group', [(0, 1), (1, 0)])  6.44 us
    ppermute x2, starting transfers between devices, swap_group(): return lax.ppermute(value, 'group', [(0, 1), (1, 0)])  3.11 us
    ppermute x1, waiting for transfers between devices, hop_core(): lax.ppermute(value, 'expert', [(i, i - 1) for i in range(1, size, 2)])  2.96 us
  transfers between devices with their start and end apart: 7, of which 3 were waited for; matrix products, arithmetic and copies ran while one was open for 0% of the time, Pallas kernels for 5%

profile of v17, /device:TPU:0, one launch (start us, length us, event | category | flops | bytes accessed | tf_op | source)
XLA Modules:
  0.0 78.8 jit_solution(412575081318347807)
XLA Ops:
  0.0 0.5 collective-permute-start.1
  0.5 0.1 collective-permute-start.2
  0.5 0.5 collective-permute-start.3
  1.0 0.1 collective-permute-start.4
  1.1 1.6 %collective-permute-start = (bf16[8,128]{1,0:T(8,128)(2,1)S(1)}, bf16[8,128]{1,0:T(8,128)(2,1)S(1)}, u32[]{:S(2)}, u32[]{:S(2)}) collective-permute-start(bf16[8,128]{1,0:T(8,128)(2,1)S(1)} %convert_element_type.9), channel_id=1, source_target_pairs={{1,0},{3,2},{5,4},{7,6},{9,8},{11,10},{13,12},{15,14},{17,16},{19,... | collective-permute-start | bytes 6152 | tf_op jit(solution)/shard_map/ppermute | solution.py:171
  2.7 3.0 %collective-permute-done.refs_7_ = bf16[8,128]{1,0:T(8,128)(2,1)S(1)} collective-permute-done((bf16[8,128]{1,0:T(8,128)(2,1)S(1)}, bf16[8,128]{1,0:T(8,128)(2,1)S(1)}, u32[]{:S(2)}, u32[]{:S(2)}) %collective-permute-start) | collective-permute-done | bytes 2080 | tf_op jit(solution)/shard_map/ppermute | solution.py:171
  5.7 0.1 shard_map.92
  5.8 17.5 %all_to_all.20 = bf16[8,8,2176]{2,1,0:T(8,128)(2,1)S(1)} all-to-all(bf16[8,8,2176]{2,1,0:T(8,128)(2,1)S(1)} %shard_map.92), channel_id=1, replica_groups={{0,4,8,12,2,6,10,14},{1,5,9,13,3,7,11,15},{16,20,24,28,18,22,26,30},{17..., dimensions={0} | all-to-all | bytes 557056 | tf_op jit(solution)/shard_map/all_to_all | solution.py:179
  23.3 0.0 collective-permute-done.3.refs_5_.refs_4_
  23.4 3.5 %shard_map.93 = bf16[64,2048]{1,0:T(8,128)(2,1)S(1)} custom-call(bf16[64,2176]{1,0:T(8,128)(2,1)S(1)} %bitcast.18, bf16[768,2048]{1,0:T(8,128)(2,1)S(1)} %bitcast.13, bf16[768,2048]{1,0:T(8,128)(2,1)S(1)} %bitcast.16, bf16[768,2048]{1,0:T(8,128)(2,1)S(1)} %collective-permute-done.1.refs_3_, bf16[768,2048]{1,0:T(8,128)(2,1)S(1)} %collective-permute-done.2.refs_4_, ...), custom_call_target="tpu_custom_call" | custom-call | flops 3221225472 | bytes 25165824 | tf_op jit(solution)/shard_map/pallas_call | solution.py:139
  26.9 12.3 %all_to_all.21.refs_1_ = bf16[8,8,2048]{2,1,0:T(8,128)(2,1)S(1)} all-to-all(bf16[8,8,2048]{2,1,0:T(8,128)(2,1)S(1)} %bitcast.24), channel_id=1, replica_groups={{0,4,8,12,2,6,10,14},{1,5,9,13,3,7,11,15},{16,20,24,28,18,22,26,30},{17..., dimensions={0} | all-to-all | bytes 524288 | tf_op jit(solution)/shard_map/all_to_all | solution.py:179
  39.1 0.2 shard_map.94
  39.3 11.7 %all_to_all.22 = bf16[8,8,2048]{2,1,0:T(8,128)(2,1)S(1)} all-to-all(bf16[8,8,2048]{2,1,0:T(8,128)(2,1)S(1)} %get-tuple-element.16), channel_id=1, replica_groups={{0,4,8,12,2,6,10,14},{1,5,9,13,3,7,11,15},{16,20,24,28,18,22,26,30},{17..., dimensions={0} | all-to-all | bytes 524288 | tf_op jit(solution)/shard_map/all_to_all | solution.py:179
  51.1 0.0 copy-start.2
  51.1 0.0 copy-start.3
  51.1 1.6 %collective-permute-start.5 = (bf16[64,2176]{1,0:T(8,128)(2,1)S(1)}, bf16[64,2176]{1,0:T(8,128)(2,1)S(1)}, u32[]{:S(2)}, u32[]{:S(2)}) collective-permute-start(bf16[64,2176]{1,0:T(8,128)(2,1)S(1)} %shard_map.95.refs_0_), channel_id=1, source_target_pairs={{0,16},{16,0},{1,17},{17,1},{2,18},{18,2},{3,19},{19,3},{4,20},{20... | collective-permute-start | bytes 835592 | tf_op jit(solution)/shard_map/ppermute | solution.py:166
  52.7 3.5 %shard_map.96 = f32[64,2048]{1,0:T(8,128)S(1)} custom-call(bf16[64,2176]{1,0:T(8,128)(2,1)S(1)} %shard_map.95.refs_0_, bf16[768,2048]{1,0:T(8,128)(2,1)S(1)} %bitcast.14, bf16[768,2048]{1,0:T(8,128)(2,1)S(1)} %bitcast.17, bf16[768,2048]{1,0:T(8,128)(2,1)S(1)} %collective-permute-done.1.refs_3_, bf16[768,2048]{1,0:T(8,128)(2,1)S(1)} %collective-permute-done.2.refs_4_), custom_call_target="tpu_custom_call" | custom-call | flops 3221225472 | bytes 25165824 | tf_op jit(solution)/shard_map/pallas_call | solution.py:139
  56.2 1.6 %collective-permute-done.5.refs_1_ = bf16[64,2176]{1,0:T(8,128)(2,1)S(1)} collective-permute-done((bf16[64,2176]{1,0:T(8,128)(2,1)S(1)}, bf16[64,2176]{1,0:T(8,128)(2,1)S(1)}, u32[]{:S(2)}, u32[]{:S(2)}) %collective-permute-start.5) | collective-permute-done | bytes 278560 | tf_op jit(solution)/shard_map/ppermute | solution.py:166
  57.7 2.1 %shard_map.97 = (f32[64,2048]{1,0:T(8,128)S(1)}, bf16[64,2048]{1,0:T(8,128)(2,1)S(1)}) custom-call(bf16[64,2176]{1,0:T(8,128)(2,1)S(1)} %shard_map.95.refs_0_, bf16[64,2176]{1,0:T(8,128)(2,1)S(1)} %collective-permute-done.5.refs_1_, bf16[384,2048]{1,0:T(8,128)(2,1)S(1)} %bitcast.21, bf16[384,2048]{1,0:T(8,128)(2,1)S(1)} %bitcast.23, ...), custom_call_target="tpu_custom_call" | custom-call | flops 1610612736 | bytes 12582912 | tf_op jit(solution)/shard_map/pallas_call | solution.py:139
  59.8 1.6 %collective-permute-start.6 = (bf16[64,2048]{1,0:T(8,128)(2,1)S(1)}, bf16[64,2048]{1,0:T(8,128)(2,1)S(1)}, u32[]{:S(2)}, u32[]{:S(2)}) collective-permute-start(bf16[64,2048]{1,0:T(8,128)(2,1)S(1)} %get-tuple-element.20), channel_id=1, source_target_pairs={{0,16},{16,0},{1,17},{17,1},{2,18},{18,2},{3,19},{19,3},{4,20},{20... | collective-permute-start | bytes 786440 | tf_op jit(solution)/shard_map/ppermute | solution.py:166
  61.4 4.9 %collective-permute-done.6 = bf16[64,2048]{1,0:T(8,128)(2,1)S(1)} collective-permute-done((bf16[64,2048]{1,0:T(8,128)(2,1)S(1)}, bf16[64,2048]{1,0:T(8,128)(2,1)S(1)}, u32[]{:S(2)}, u32[]{:S(2)}) %collective-permute-start.6) | collective-permute-done | bytes 262176 | tf_op jit(solution)/shard_map/ppermute | solution.py:166
  66.3 0.1 fusion
  66.4 11.8 %all_to_all.23.refs_1_ = bf16[8,8,2048]{2,1,0:T(8,128)(2,1)S(1)} all-to-all(bf16[8,8,2048]{2,1,0:T(8,128)(2,1)S(1)} %fusion), channel_id=1, replica_groups={{0,4,8,12,2,6,10,14},{1,5,9,13,3,7,11,15},{16,20,24,28,18,22,26,30},{17..., dimensions={0} | all-to-all | bytes 524288 | tf_op jit(solution)/shard_map/all_to_all | solution.py:179
  78.1 0.7 shard_map.98
  (22 shorter events, 0.1 us)
Async XLA Ops:
  0.0 23.3 %collective-permute-start.1 = (bf16[768,2048]{1,0:T(8,128)(2,1)}, bf16[768,2048]{1,0:T(8,128)(2,1)S(1)}, u32[]{:S(2)}, u32[]{:S(2)}) collective-permute-start(bf16[768,2048]{1,0:T(8,128)(2,1)} %bitcast.12), channel_id=1, source_target_pairs={{0,1},{1,0},{2,3},{3,2},{4,5},{5,4},{6,7},{7,6},{8,9},{9,8},{10,11... | collective-permute-start | bytes 9437192 | tf_op jit(solution)/shard_map/ppermute | solution.py:162
  0.5 22.9 %collective-permute-start.2 = (bf16[768,2048]{1,0:T(8,128)(2,1)}, bf16[768,2048]{1,0:T(8,128)(2,1)S(1)}, u32[]{:S(2)}, u32[]{:S(2)}) collective-permute-start(bf16[768,2048]{1,0:T(8,128)(2,1)} %bitcast.15), channel_id=1, source_target_pairs={{0,1},{1,0},{2,3},{3,2},{4,5},{5,4},{6,7},{7,6},{8,9},{9,8},{10,11... | collective-permute-start | bytes 9437192 | tf_op jit(solution)/shard_map/ppermute | solution.py:162
  0.5 22.8 %collective-permute-start.3 = (bf16[384,2048]{1,0:T(8,128)(2,1)}, bf16[384,2048]{1,0:T(8,128)(2,1)S(1)}, u32[]{:S(2)}, u32[]{:S(2)}) collective-permute-start(bf16[384,2048]{1,0:T(8,128)(2,1)} %bitcast.20), channel_id=1, source_target_pairs={{0,1},{1,0},{2,3},{3,2},{4,5},{5,4},{6,7},{7,6},{8,9},{9,8},{10,11... | collective-permute-start | bytes 4718600 | tf_op jit(solution)/shard_map/ppermute | solution.py:162
  1.0 4.7 %copy-start.4 = (bf16[1,8,2048]{2,1,0:T(8,128)(2,1)S(1)}, bf16[1,8,2048]{2,1,0:T(8,128)(2,1)}, u32[]{:S(2)}) copy-start(bf16[1,8,2048]{2,1,0:T(8,128)(2,1)} %param.9) | copy-start | bytes 98308
  1.0 4.7 %copy-start.5 = (f32[2048]{0:T(1024)S(1)}, f32[2048]{0:T(1024)}, u32[]{:S(2)}) copy-start(f32[2048]{0:T(1024)} %param.10) | copy-start | bytes 24580
  1.0 4.7 %copy-start.6 = (s32[2,1,8,8]{3,2,1,0:T(8,128)S(1)}, s32[2,1,8,8]{3,2,1,0:T(8,128)}, u32[]{:S(2)}) copy-start(s32[2,1,8,8]{3,2,1,0:T(8,128)} %refs_4_.1) | copy-start | bytes 1540
  1.0 4.7 %copy-start.7 = (f32[2,1,8,8]{3,2,1,0:T(8,128)S(1)}, f32[2,1,8,8]{3,2,1,0:T(8,128)}, u32[]{:S(2)}) copy-start(f32[2,1,8,8]{3,2,1,0:T(8,128)} %refs_5_.1) | copy-start | bytes 1540
  1.0 4.7 %copy-start.8 = (s32[1,4]{1,0:T(1,128)S(1)}, s32[1,4]{1,0:T(1,128)}, u32[]{:S(2)}) copy-start(s32[1,4]{1,0:T(1,128)} %refs_6_.1) | copy-start | bytes 52
  1.0 22.4 %copy-start = (bf16[1,768,2048]{2,1,0:T(8,128)(2,1)S(1)}, bf16[1,768,2048]{2,1,0:T(8,128)(2,1)}, u32[]{:S(2)}) copy-start(bf16[1,768,2048]{2,1,0:T(8,128)(2,1)} %param.14) | copy-start | bytes 9437188
  1.0 22.4 %copy-start.1 = (bf16[1,768,2048]{2,1,0:T(8,128)(2,1)S(1)}, bf16[1,768,2048]{2,1,0:T(8,128)(2,1)}, u32[]{:S(2)}) copy-start(bf16[1,768,2048]{2,1,0:T(8,128)(2,1)} %param.15) | copy-start | bytes 9437188
  1.0 22.3 %collective-permute-start.4 = (bf16[384,2048]{1,0:T(8,128)(2,1)}, bf16[384,2048]{1,0:T(8,128)(2,1)S(1)}, u32[]{:S(2)}, u32[]{:S(2)}) collective-permute-start(bf16[384,2048]{1,0:T(8,128)(2,1)} %bitcast.22), channel_id=1, source_target_pairs={{0,1},{1,0},{2,3},{3,2},{4,5},{5,4},{6,7},{7,6},{8,9},{9,8},{10,11... | collective-permute-start | bytes 4718600 | tf_op jit(solution)/shard_map/ppermute | solution.py:162
  1.1 4.5 %collective-permute-start = (bf16[8,128]{1,0:T(8,128)(2,1)S(1)}, bf16[8,128]{1,0:T(8,128)(2,1)S(1)}, u32[]{:S(2)}, u32[]{:S(2)}) collective-permute-start(bf16[8,128]{1,0:T(8,128)(2,1)S(1)} %convert_element_type.9), channel_id=1, source_target_pairs={{1,0},{3,2},{5,4},{7,6},{9,8},{11,10},{13,12},{15,14},{17,16},{19,... | collective-permute-start | bytes 6152 | tf_op jit(solution)/shard_map/ppermute | solution.py:171
  51.1 6.6 %copy-start.2 = (bf16[1,384,2048]{2,1,0:T(8,128)(2,1)S(1)}, bf16[1,384,2048]{2,1,0:T(8,128)(2,1)}, u32[]{:S(2)}) copy-start(bf16[1,384,2048]{2,1,0:T(8,128)(2,1)} %param.16) | copy-start | bytes 4718596
  51.1 6.6 %copy-start.3 = (bf16[1,384,2048]{2,1,0:T(8,128)(2,1)S(1)}, bf16[1,384,2048]{2,1,0:T(8,128)(2,1)}, u32[]{:S(2)}) copy-start(bf16[1,384,2048]{2,1,0:T(8,128)(2,1)} %param.17) | copy-start | bytes 4718596
  51.1 6.6 %collective-permute-start.5 = (bf16[64,2176]{1,0:T(8,128)(2,1)S(1)}, bf16[64,2176]{1,0:T(8,128)(2,1)S(1)}, u32[]{:S(2)}, u32[]{:S(2)}) collective-permute-start(bf16[64,2176]{1,0:T(8,128)(2,1)S(1)} %shard_map.95.refs_0_), channel_id=1, source_target_pairs={{0,16},{16,0},{1,17},{17,1},{2,18},{18,2},{3,19},{19,3},{4,20},{20... | collective-permute-start | bytes 835592 | tf_op jit(solution)/shard_map/ppermute | solution.py:166
  59.8 6.4 %collective-permute-start.6 = (bf16[64,2048]{1,0:T(8,128)(2,1)S(1)}, bf16[64,2048]{1,0:T(8,128)(2,1)S(1)}, u32[]{:S(2)}, u32[]{:S(2)}) collective-permute-start(bf16[64,2048]{1,0:T(8,128)(2,1)S(1)} %get-tuple-element.20), channel_id=1, source_target_pairs={{0,16},{16,0},{1,17},{17,1},{2,18},{18,2},{3,19},{19,3},{4,20},{20... | collective-permute-start | bytes 786440 | tf_op jit(solution)/shard_map/ppermute | solution.py:166

commit v18 on v14

--- a/solution.py
+++ b/solution.py
@@ -75,10 +75,13 @@
 def pack_kernel(section, expert, tokens, gain, routes, scales, changed, out):
     width = tokens.shape[1]
     normed = normalize(tokens[...].astype(jnp.float32), gain[...])
-    table = weight_table(section[...], expert[...], routes, scales, changed)
-    for chip in range(out.shape[0]):
-        out[chip, :, :width] = normed
-        out[chip, :, width:] = table
+    out[:, :width] = normed
+    out[:, width:] = weight_table(section[...], expert[...], routes, scales, changed)
+
+
+def double_kernel(first, second, out):
+    out[0] = first[...]
+    out[1] = second[...]
 
 
 def sum_blocks(blocks):
@@ -103,13 +106,10 @@
 def join_kernel(rows, tables, out):
     width = rows.shape[1]
     out[:, :width] = rows[...]
-    out[:, width:] = tables[:, width:]
-
-
-def mlp_kernel(experts, step, fresh, set_count, *refs):
-    sources, refs = refs[:set_count], refs[set_count:]
-    weights, outs = refs[:4], refs[4:]
-    count, width = outs[0].shape
+    out[:, width:] = tables[...]
+
+
+def weighted_outputs(experts, step, fresh, sources, weights, width):
     rows = jnp.concatenate([source[:, :width] for source in sources], axis=0)
     table = jnp.concatenate([source[:, width:] for source in sources], axis=0)
     inputs = jnp.concatenate([rows] * max(1, MATMUL_ROWS // rows.shape[0]), axis=0)
@@ -125,6 +125,26 @@
         result = jnp.dot(hidden, down[...], preferred_element_type=jnp.float32)
         result = result[: rows.shape[0]] * row_weights(experts, table, owner, step, fresh)
         total = result if total is None else total + result
+    return table, total
+
+
+def first_kernel(experts, step, orders, rows, across, *refs):
+    weights, (out, tables_out) = refs[:4], refs[4:]
+    table, total = weighted_outputs(experts, step, False, [rows, across], weights, out.shape[2])
+    chips, count, _ = out.shape
+    own = lax.div(lax.axis_index("expert"), 2)
+    for block, distance in enumerate(orders):
+        chip = jnp.bitwise_xor(own, distance)
+        place = lax.rem(chip, 2) * (chips // 2) + lax.div(chip, 2)
+        span = slice(block * count, (block + 1) * count)
+        out[place] = total[span].astype(out.dtype)
+        tables_out[place] = table[span]
+
+
+def mlp_kernel(experts, step, fresh, set_count, *refs):
+    sources, weights, outs = refs[:set_count], refs[set_count:][:4], refs[set_count + 4 :]
+    count, width = outs[0].shape
+    _, total = weighted_outputs(experts, step, fresh, sources, weights, width)
     for i, out in enumerate(outs):
         out[...] = total[i * count : (i + 1) * count].astype(out.dtype)
 
@@ -146,14 +166,11 @@
     )(*inputs, *after)
 
 
-def run_mlp(row_sets, weights, step, fresh, out_types, after=()):
-    count, width = row_sets[0].shape[0], weights[0].shape[1]
+def run_mlp(kernel, row_sets, weights, outputs, after=()):
     size = sum(part.size for part in weights)
     cost = pl.CostEstimate(
         flops=4 * MATMUL_ROWS * size, bytes_accessed=4 * size, transcendentals=0
     )
-    kernel = functools.partial(mlp_kernel, lax.axis_size("expert"), step, fresh, len(row_sets))
-    outputs = [((count, width), out_type) for out_type in out_types]
     return on_vmem(kernel, tuple(row_sets) + tuple(weights), outputs, 8 * MIB, cost, after)
 
 
@@ -164,6 +181,23 @@
 
 def swap_group(value):
     return lax.ppermute(value, "group", [(0, 1), (1, 0)])
+
+
+def swap_chip(value, distance):
+    size = lax.axis_size("expert")
+    return lax.ppermute(value, "expert", [(i, i ^ 2 * distance) for i in range(size)])
+
+
+def gather(block, chips):
+    distance, orders = chips // 2, [0]
+    while distance > 1:
+        rows, width = block.shape
+        joined = ((2, rows, width), block.dtype)
+        (block,) = on_vmem(double_kernel, (block, swap_chip(block, distance)), [joined])
+        block = block.reshape(2 * rows, width)
+        orders = orders + [order ^ distance for order in orders]
+        distance = distance // 2
+    return block, swap_chip(block, 1), orders + [order ^ 1 for order in orders]
 
 
 def spread(blocks):
@@ -193,16 +227,26 @@
     )
     stale = stale + tuple(swap_core(part) for part in stale)
     learner = learner + tuple(swap_core(part) for part in learner)
-    (blocks,) = on_vmem(
+    (block,) = on_vmem(
         pack_kernel,
         (section, expert, tokens[0], gain, routes, route_scale, changed),
-        [((chips, row_count, packed), jnp.bfloat16)],
-    )
-    tables = spread(blocks).reshape(half, packed)
-    rows, state = tables, tokens[0]
+        [((row_count, packed), jnp.bfloat16)],
+    )
+    state = tokens[0]
     for step in range(steps_total):
         if step == 0:
-            (share,) = run_mlp([rows], stale, step, False, [jnp.bfloat16], learner[2:])
+            rows, across, orders = gather(block, chips)
+            share, tables = run_mlp(
+                functools.partial(first_kernel, experts, step, orders),
+                [rows, across],
+                stale,
+                [
+                    ((chips, row_count, width), jnp.bfloat16),
+                    ((chips, row_count, packed - width), jnp.bfloat16),
+                ],
+                learner[2:],
+            )
+            tables = tables.reshape(half, packed - width)
         else:
             state, blocks = on_vmem(
                 next_kernel,
@@ -212,12 +256,16 @@
             rows = spread(blocks).reshape(half, width)
             (rows,) = on_vmem(join_kernel, (rows, tables), [((half, packed), jnp.bfloat16)])
             other = swap_group(rows)
-            (old,) = run_mlp([rows], stale, step, False, [jnp.float32])
+            kept = ((half, width), jnp.float32)
+            kernel = functools.partial(mlp_kernel, experts, step, False, 1)
+            (old,) = run_mlp(kernel, [rows], stale, [kept])
             other, old = lax.optimization_barrier((other, old))
-            new, away = run_mlp([rows, other], learner, step, True, [jnp.float32, jnp.bfloat16])
+            kernel = functools.partial(mlp_kernel, experts, step, True, 2)
+            sent = ((half, width), jnp.bfloat16)
+            new, away = run_mlp(kernel, [rows, other], learner, [kept, sent])
             share = old + new + swap_group(away).astype(jnp.float32)
-            share = share.astype(jnp.bfloat16)
-        returned = spread(share.reshape(chips, row_count, width))
+            share = share.astype(jnp.bfloat16).reshape(chips, row_count, width)
+        returned = spread(share)
     (updated,) = on_vmem(last_kernel, (state, returned), [((row_count, width), jnp.bfloat16)])
     return updated[None]
 
@@ -273,7 +321,7 @@
     experts = lax.axis_size("expert")
     groups = lax.axis_size("group")
     fewer = tokens.shape[1] * experts < learner_up.shape[1]
-    paired = experts % 4 == 0 and groups == 2
+    paired = experts & (experts - 1) == 0 and experts >= 4 and groups == 2
     plan = exchange_plan if fewer and paired else gather_plan
     stale = (rollout_up[0], rollout_down[0])
     learner = (learner_up[0], learner_down[0])

time: 75.5 us -> 74 us (0.980)
  blocking collectives: 53.7 us -> 37.1 us
  waiting for transfers between devices: 6.49 us -> 14.6 us
  starting transfers between devices: 4.19 us -> 11.3 us
    all_to_all x4 -> x3, blocking collectives: 53.7 us -> 37.1 us  [spread(): lax.all_to_all(blocks, 'expert', 0, 0, axis_index_groups=groups, tiled=True)]
    ppermute x0 -> x3, waiting for transfers between devices: none -> 8.09 us  [swap_chip(): lax.ppermute(value, 'expert', [(i, i ^ 2 * distance) for i in range(size)])]
    ppermute x0 -> x3, starting transfers between devices: none -> 7.09 us  [swap_chip(): lax.ppermute(value, 'expert', [(i, i ^ 2 * distance) for i in range(size)])]
    pallas_call x8 -> x10, Pallas kernels: 9.98 us -> 10 us  [on_vmem(): pl.pallas_call(body, out_shape=[jax.ShapeDtypeStruct(shape, kind) for sha...]
  transfers between devices with their start and end apart: 6 -> 9, of which waited for: 2 -> 5; matrix products, arithmetic and copies ran while one was open for 0% -> 0% of each run, Pallas kernels for 5% -> 5%
where the time goes in v18:
time: 74 us; the launch traced here: 73.8 us
  blocking collectives  37.1 us (50%)
  waiting for transfers between devices  14.6 us (20%)
  starting transfers between devices  11.3 us (15%)
  Pallas kernels  10 us (14%)
    all_to_all x3, blocking collectives, spread(): lax.all_to_all(blocks, 'expert', 0, 0, axis_index_groups=groups, tiled=True)  37.1 us
    pallas_call x10, Pallas kernels, on_vmem(): pl.pallas_call(body, out_shape=[jax.ShapeDtypeStruct(shape, kind) for sha...  10 us
    ppermute x3, waiting for transfers between devices, swap_chip(): lax.ppermute(value, 'expert', [(i, i ^ 2 * distance) for i in range(size)])  8.09 us
    ppermute x3, starting transfers between devices, swap_chip(): lax.ppermute(value, 'expert', [(i, i ^ 2 * distance) for i in range(size)])  7.09 us
    ppermute x2, waiting for transfers between devices, swap_group(): return lax.ppermute(value, 'group', [(0, 1), (1, 0)])  6.48 us
    ppermute x2, starting transfers between devices, swap_group(): return lax.ppermute(value, 'group', [(0, 1), (1, 0)])  3.11 us
  transfers between devices with their start and end apart: 9, of which 5 were waited for; matrix products, arithmetic and copies ran while one was open for 0% of the time, Pallas kernels for 5%

profile of v18, /device:TPU:0, one launch (start us, length us, event | category | flops | bytes accessed | tf_op | source)
XLA Modules:
  0.0 73.8 jit_solution(15338370779733373466)
XLA Ops:
  0.0 0.5 collective-permute-start.3
  0.5 0.5 collective-permute-start.5
  1.0 0.1 collective-permute-start.6
  1.1 0.6 copy-done.4
  1.7 0.1 shard_map.92.refs_0_
  1.9 3.7 %collective-permute-start = (bf16[8,2176]{1,0:T(8,128)(2,1)S(1)}, bf16[8,2176]{1,0:T(8,128)(2,1)S(1)}, u32[]{:S(2)}, u32[]{:S(2)}) collective-permute-start(bf16[8,2176]{1,0:T(8,128)(2,1)S(1)} %shard_map.92.refs_0_), channel_id=1, source_target_pairs={{0,8},{1,9},{2,10},{3,11},{4,12},{5,13},{6,14},{7,15},{8,0},{9,1},... | collective-permute-start | bytes 104456 | tf_op jit(solution)/shard_map/ppermute | solution.py:188
  5.5 2.1 %collective-permute-done.refs_1_ = bf16[8,2176]{1,0:T(8,128)(2,1)S(1)} collective-permute-done((bf16[8,2176]{1,0:T(8,128)(2,1)S(1)}, bf16[8,2176]{1,0:T(8,128)(2,1)S(1)}, u32[]{:S(2)}, u32[]{:S(2)}) %collective-permute-start) | collective-permute-done | bytes 34848 | tf_op jit(solution)/shard_map/ppermute | solution.py:188
  7.6 1.7 %collective-permute-start.1 = (bf16[16,2176]{1,0:T(8,128)(2,1)S(1)}, bf16[16,2176]{1,0:T(8,128)(2,1)S(1)}, u32[]{:S(2)}, u32[]{:S(2)}) collective-permute-start(bf16[16,2176]{1,0:T(8,128)(2,1)S(1)} %bitcast.26), channel_id=1, source_target_pairs={{0,4},{1,5},{2,6},{3,7},{4,0},{5,1},{6,2},{7,3},{8,12},{9,13},{10,... | collective-permute-start | bytes 208904 | tf_op jit(solution)/shard_map/ppermute | solution.py:188
  9.4 2.6 %collective-permute-done.1.refs_1_ = bf16[16,2176]{1,0:T(8,128)(2,1)S(1)} collective-permute-done((bf16[16,2176]{1,0:T(8,128)(2,1)S(1)}, bf16[16,2176]{1,0:T(8,128)(2,1)S(1)}, u32[]{:S(2)}, u32[]{:S(2)}) %collective-permute-start.1) | collective-permute-done | bytes 69664 | tf_op jit(solution)/shard_map/ppermute | solution.py:188
  12.0 1.7 %collective-permute-start.2 = (bf16[32,2176]{1,0:T(8,128)(2,1)S(1)}, bf16[32,2176]{1,0:T(8,128)(2,1)S(1)}, u32[]{:S(2)}, u32[]{:S(2)}) collective-permute-start(bf16[32,2176]{1,0:T(8,128)(2,1)S(1)} %bitcast.24), channel_id=1, source_target_pairs={{0,2},{1,3},{2,0},{3,1},{4,6},{5,7},{6,4},{7,5},{8,10},{9,11},{10,... | collective-permute-start | bytes 417800 | tf_op jit(solution)/shard_map/ppermute | solution.py:188
  13.7 3.4 %collective-permute-done.2.refs_1_ = bf16[32,2176]{1,0:T(8,128)(2,1)S(1)} collective-permute-done((bf16[32,2176]{1,0:T(8,128)(2,1)S(1)}, bf16[32,2176]{1,0:T(8,128)(2,1)S(1)}, u32[]{:S(2)}, u32[]{:S(2)}) %collective-permute-start.2) | collective-permute-done | bytes 139296 | tf_op jit(solution)/shard_map/ppermute | solution.py:188
  17.1 3.5 %shard_map.95 = (bf16[8,8,2048]{2,1,0:T(8,128)(2,1)S(1)}, bf16[8,8,128]{2,1,0:T(8,128)(2,1)S(1)}) custom-call(bf16[32,2176]{1,0:T(8,128)(2,1)S(1)} %bitcast.25, bf16[32,2176]{1,0:T(8,128)(2,1)S(1)} %collective-permute-done.2.refs_1_, bf16[768,2048]{1,0:T(8,128)(2,1)S(1)} %bitcast.14, bf16[768,2048]{1,0:T(8,128)(2,1)S(1)} %bitcast.17, ...), custom_call_target="tpu_custom_call" | custom-call | flops 3221225472 | bytes 25165824 | tf_op jit(solution)/shard_map/pallas_call | solution.py:159
  20.6 15.1 %all_to_all.15.refs_1_ = bf16[8,8,2048]{2,1,0:T(8,128)(2,1)S(1)} all-to-all(bf16[8,8,2048]{2,1,0:T(8,128)(2,1)S(1)} %get-tuple-element.17), channel_id=1, replica_groups={{0,4,8,12,2,6,10,14},{1,5,9,13,3,7,11,15},{16,20,24,28,18,22,26,30},{17..., dimensions={0} | all-to-all | bytes 524288 | tf_op jit(solution)/shard_map/all_to_all | solution.py:208
  35.7 0.2 shard_map.96
  35.9 11.0 %all_to_all.16 = bf16[8,8,2048]{2,1,0:T(8,128)(2,1)S(1)} all-to-all(bf16[8,8,2048]{2,1,0:T(8,128)(2,1)S(1)} %get-tuple-element.19), channel_id=1, replica_groups={{0,4,8,12,2,6,10,14},{1,5,9,13,3,7,11,15},{16,20,24,28,18,22,26,30},{17..., dimensions={0} | all-to-all | bytes 524288 | tf_op jit(solution)/shard_map/all_to_all | solution.py:208
  46.9 1.6 %collective-permute-start.7 = (bf16[64,2176]{1,0:T(8,128)(2,1)S(1)}, bf16[64,2176]{1,0:T(8,128)(2,1)S(1)}, u32[]{:S(2)}, u32[]{:S(2)}) collective-permute-start(bf16[64,2176]{1,0:T(8,128)(2,1)S(1)} %shard_map.97.refs_0_), channel_id=1, source_target_pairs={{0,16},{16,0},{1,17},{17,1},{2,18},{18,2},{3,19},{19,3},{4,20},{20... | collective-permute-start | bytes 835592 | tf_op jit(solution)/shard_map/ppermute | solution.py:183
  48.5 3.5 %shard_map.98 = f32[64,2048]{1,0:T(8,128)S(1)} custom-call(bf16[64,2176]{1,0:T(8,128)(2,1)S(1)} %shard_map.97.refs_0_, bf16[768,2048]{1,0:T(8,128)(2,1)S(1)} %bitcast.15, bf16[768,2048]{1,0:T(8,128)(2,1)S(1)} %bitcast.18, bf16[768,2048]{1,0:T(8,128)(2,1)S(1)} %collective-permute-done.3.refs_4_.refs_3_, ...), custom_call_target="tpu_custom_call" | custom-call | flops 3221225472 | bytes 25165824 | tf_op jit(solution)/shard_map/pallas_call | solution.py:159
  51.9 1.6 %collective-permute-done.7.refs_1_ = bf16[64,2176]{1,0:T(8,128)(2,1)S(1)} collective-permute-done((bf16[64,2176]{1,0:T(8,128)(2,1)S(1)}, bf16[64,2176]{1,0:T(8,128)(2,1)S(1)}, u32[]{:S(2)}, u32[]{:S(2)}) %collective-permute-start.7) | collective-permute-done | bytes 278560 | tf_op jit(solution)/shard_map/ppermute | solution.py:183
  53.5 2.1 %shard_map.99 = (f32[64,2048]{1,0:T(8,128)S(1)}, bf16[64,2048]{1,0:T(8,128)(2,1)S(1)}) custom-call(bf16[64,2176]{1,0:T(8,128)(2,1)S(1)} %shard_map.97.refs_0_, bf16[64,2176]{1,0:T(8,128)(2,1)S(1)} %collective-permute-done.7.refs_1_, bf16[384,2048]{1,0:T(8,128)(2,1)S(1)} %bitcast.20, bf16[384,2048]{1,0:T(8,128)(2,1)S(1)} %bitcast.22, ...), custom_call_target="tpu_custom_call" | custom-call | flops 1610612736 | bytes 12582912 | tf_op jit(solution)/shard_map/pallas_call | solution.py:159
  55.6 1.6 %collective-permute-start.8 = (bf16[64,2048]{1,0:T(8,128)(2,1)S(1)}, bf16[64,2048]{1,0:T(8,128)(2,1)S(1)}, u32[]{:S(2)}, u32[]{:S(2)}) collective-permute-start(bf16[64,2048]{1,0:T(8,128)(2,1)S(1)} %get-tuple-element.24), channel_id=1, source_target_pairs={{0,16},{16,0},{1,17},{17,1},{2,18},{18,2},{3,19},{19,3},{4,20},{20... | collective-permute-start | bytes 786440 | tf_op jit(solution)/shard_map/ppermute | solution.py:183
  57.2 4.9 %collective-permute-done.8 = bf16[64,2048]{1,0:T(8,128)(2,1)S(1)} collective-permute-done((bf16[64,2048]{1,0:T(8,128)(2,1)S(1)}, bf16[64,2048]{1,0:T(8,128)(2,1)S(1)}, u32[]{:S(2)}, u32[]{:S(2)}) %collective-permute-start.8) | collective-permute-done | bytes 262176 | tf_op jit(solution)/shard_map/ppermute | solution.py:183
  62.1 0.1 fusion
  62.1 11.0 %all_to_all.17.refs_1_ = bf16[8,8,2048]{2,1,0:T(8,128)(2,1)S(1)} all-to-all(bf16[8,8,2048]{2,1,0:T(8,128)(2,1)S(1)} %fusion), channel_id=1, replica_groups={{0,4,8,12,2,6,10,14},{1,5,9,13,3,7,11,15},{16,20,24,28,18,22,26,30},{17..., dimensions={0} | all-to-all | bytes 524288 | tf_op jit(solution)/shard_map/all_to_all | solution.py:208
  73.1 0.7 shard_map.100
  (26 shorter events, 0.1 us)
Async XLA Ops:
  0.0 17.1 %collective-permute-start.3 = (bf16[768,2048]{1,0:T(8,128)(2,1)}, bf16[768,2048]{1,0:T(8,128)(2,1)S(1)}, u32[]{:S(2)}, u32[]{:S(2)}) collective-permute-start(bf16[768,2048]{1,0:T(8,128)(2,1)} %bitcast.13), channel_id=1, source_target_pairs={{0,1},{1,0},{2,3},{3,2},{4,5},{5,4},{6,7},{7,6},{8,9},{9,8},{10,11... | collective-permute-start | bytes 9437192 | tf_op jit(solution)/shard_map/ppermute | solution.py:179
  0.5 16.7 %collective-permute-start.4 = (bf16[768,2048]{1,0:T(8,128)(2,1)}, bf16[768,2048]{1,0:T(8,128)(2,1)S(1)}, u32[]{:S(2)}, u32[]{:S(2)}) collective-permute-start(bf16[768,2048]{1,0:T(8,128)(2,1)} %bitcast.16), channel_id=1, source_target_pairs={{0,1},{1,0},{2,3},{3,2},{4,5},{5,4},{6,7},{7,6},{8,9},{9,8},{10,11... | collective-permute-start | bytes 9437192 | tf_op jit(solution)/shard_map/ppermute | solution.py:179
  0.5 16.6 %collective-permute-start.5 = (bf16[384,2048]{1,0:T(8,128)(2,1)}, bf16[384,2048]{1,0:T(8,128)(2,1)S(1)}, u32[]{:S(2)}, u32[]{:S(2)}) collective-permute-start(bf16[384,2048]{1,0:T(8,128)(2,1)} %bitcast.19), channel_id=1, source_target_pairs={{0,1},{1,0},{2,3},{3,2},{4,5},{5,4},{6,7},{7,6},{8,9},{9,8},{10,11... | collective-permute-start | bytes 4718600 | tf_op jit(solution)/shard_map/ppermute | solution.py:179
  1.0 0.8 %copy-start.4 = (bf16[1,8,2048]{2,1,0:T(8,128)(2,1)S(1)}, bf16[1,8,2048]{2,1,0:T(8,128)(2,1)}, u32[]{:S(2)}) copy-start(bf16[1,8,2048]{2,1,0:T(8,128)(2,1)} %param.9) | copy-start | bytes 98308
  1.0 0.8 %copy-start.5 = (f32[2048]{0:T(1024)S(1)}, f32[2048]{0:T(1024)}, u32[]{:S(2)}) copy-start(f32[2048]{0:T(1024)} %param.10) | copy-start | bytes 24580
  1.0 0.8 %copy-start.6 = (s32[2,1,8,8]{3,2,1,0:T(8,128)S(1)}, s32[2,1,8,8]{3,2,1,0:T(8,128)}, u32[]{:S(2)}) copy-start(s32[2,1,8,8]{3,2,1,0:T(8,128)} %refs_4_.1) | copy-start | bytes 1540
  1.0 0.8 %copy-start.7 = (f32[2,1,8,8]{3,2,1,0:T(8,128)S(1)}, f32[2,1,8,8]{3,2,1,0:T(8,128)}, u32[]{:S(2)}) copy-start(f32[2,1,8,8]{3,2,1,0:T(8,128)} %refs_5_.1) | copy-start | bytes 1540
  1.0 0.8 %copy-start.8 = (s32[1,4]{1,0:T(1,128)S(1)}, s32[1,4]{1,0:T(1,128)}, u32[]{:S(2)}) copy-start(s32[1,4]{1,0:T(1,128)} %refs_6_.1) | copy-start | bytes 52
  1.0 16.1 %copy-start = (bf16[1,768,2048]{2,1,0:T(8,128)(2,1)S(1)}, bf16[1,768,2048]{2,1,0:T(8,128)(2,1)}, u32[]{:S(2)}) copy-start(bf16[1,768,2048]{2,1,0:T(8,128)(2,1)} %param.14) | copy-start | bytes 9437188
  1.0 16.1 %copy-start.1 = (bf16[1,768,2048]{2,1,0:T(8,128)(2,1)S(1)}, bf16[1,768,2048]{2,1,0:T(8,128)(2,1)}, u32[]{:S(2)}) copy-start(bf16[1,768,2048]{2,1,0:T(8,128)(2,1)} %param.15) | copy-start | bytes 9437188
  1.0 16.1 %collective-permute-start.6 = (bf16[384,2048]{1,0:T(8,128)(2,1)}, bf16[384,2048]{1,0:T(8,128)(2,1)S(1)}, u32[]{:S(2)}, u32[]{:S(2)}) collective-permute-start(bf16[384,2048]{1,0:T(8,128)(2,1)} %bitcast.21), channel_id=1, source_target_pairs={{0,1},{1,0},{2,3},{3,2},{4,5},{5,4},{6,7},{7,6},{8,9},{9,8},{10,11... | collective-permute-start | bytes 4718600 | tf_op jit(solution)/shard_map/ppermute | solution.py:179
  1.9 5.8 %collective-permute-start = (bf16[8,2176]{1,0:T(8,128)(2,1)S(1)}, bf16[8,2176]{1,0:T(8,128)(2,1)S(1)}, u32[]{:S(2)}, u32[]{:S(2)}) collective-permute-start(bf16[8,2176]{1,0:T(8,128)(2,1)S(1)} %shard_map.92.refs_0_), channel_id=1, source_target_pairs={{0,8},{1,9},{2,10},{3,11},{4,12},{5,13},{6,14},{7,15},{8,0},{9,1},... | collective-permute-start | bytes 104456 | tf_op jit(solution)/shard_map/ppermute | solution.py:188
  7.6 4.3 %collective-permute-start.1 = (bf16[16,2176]{1,0:T(8,128)(2,1)S(1)}, bf16[16,2176]{1,0:T(8,128)(2,1)S(1)}, u32[]{:S(2)}, u32[]{:S(2)}) collective-permute-start(bf16[16,2176]{1,0:T(8,128)(2,1)S(1)} %bitcast.26), channel_id=1, source_target_pairs={{0,4},{1,5},{2,6},{3,7},{4,0},{5,1},{6,2},{7,3},{8,12},{9,13},{10,... | collective-permute-start | bytes 208904 | tf_op jit(solution)/shard_map/ppermute | solution.py:188
  12.0 5.1 %collective-permute-start.2 = (bf16[32,2176]{1,0:T(8,128)(2,1)S(1)}, bf16[32,2176]{1,0:T(8,128)(2,1)S(1)}, u32[]{:S(2)}, u32[]{:S(2)}) collective-permute-start(bf16[32,2176]{1,0:T(8,128)(2,1)S(1)} %bitcast.24), channel_id=1, source_target_pairs={{0,2},{1,3},{2,0},{3,1},{4,6},{5,7},{6,4},{7,5},{8,10},{9,11},{10,... | collective-permute-start | bytes 417800 | tf_op jit(solution)/shard_map/ppermute | solution.py:188
  46.9 6.6 %copy-start.2 = (bf16[1,384,2048]{2,1,0:T(8,128)(2,1)S(1)}, bf16[1,384,2048]{2,1,0:T(8,128)(2,1)}, u32[]{:S(2)}) copy-start(bf16[1,384,2048]{2,1,0:T(8,128)(2,1)} %param.16) | copy-start | bytes 4718596
  46.9 6.6 %copy-start.3 = (bf16[1,384,2048]{2,1,0:T(8,128)(2,1)S(1)}, bf16[1,384,2048]{2,1,0:T(8,128)(2,1)}, u32[]{:S(2)}) copy-start(bf16[1,384,2048]{2,1,0:T(8,128)(2,1)} %param.17) | copy-start | bytes 4718596
  46.9 6.6 %collective-permute-start.7 = (bf16[64,2176]{1,0:T(8,128)(2,1)S(1)}, bf16[64,2176]{1,0:T(8,128)(2,1)S(1)}, u32[]{:S(2)}, u32[]{:S(2)}) collective-permute-start(bf16[64,2176]{1,0:T(8,128)(2,1)S(1)} %shard_map.97.refs_0_), channel_id=1, source_target_pairs={{0,16},{16,0},{1,17},{17,1},{2,18},{18,2},{3,19},{19,3},{4,20},{20... | collective-permute-start | bytes 835592 | tf_op jit(solution)/shard_map/ppermute | solution.py:183
  55.6 6.4 %collective-permute-start.8 = (bf16[64,2048]{1,0:T(8,128)(2,1)S(1)}, bf16[64,2048]{1,0:T(8,128)(2,1)S(1)}, u32[]{:S(2)}, u32[]{:S(2)}) collective-permute-start(bf16[64,2048]{1,0:T(8,128)(2,1)S(1)} %get-tuple-element.24), channel_id=1, source_target_pairs={{0,16},{16,0},{1,17},{17,1},{2,18},{18,2},{3,19},{19,3},{4,20},{20... | collective-permute-start | bytes 786440 | tf_op jit(solution)/shard_map/ppermute | solution.py:183

commit v19 on v18

--- a/solution.py
+++ b/solution.py
@@ -132,9 +132,11 @@
     weights, (out, tables_out) = refs[:4], refs[4:]
     table, total = weighted_outputs(experts, step, False, [rows, across], weights, out.shape[2])
     chips, count, _ = out.shape
-    own = lax.div(lax.axis_index("expert"), 2)
-    for block, distance in enumerate(orders):
-        chip = jnp.bitwise_xor(own, distance)
+    device = lax.axis_index("expert")
+    core = lax.rem(device, 2)
+    for block, distances in enumerate(zip(*orders)):
+        distance = distances[0] + core * (distances[1] - distances[0])
+        chip = jnp.bitwise_xor(lax.div(device, 2), distance)
         place = lax.rem(chip, 2) * (chips // 2) + lax.div(chip, 2)
         span = slice(block * count, (block + 1) * count)
         out[place] = total[span].astype(out.dtype)
@@ -183,21 +185,23 @@
     return lax.ppermute(value, "group", [(0, 1), (1, 0)])
 
 
-def swap_chip(value, distance):
-    size = lax.axis_size("expert")
-    return lax.ppermute(value, "expert", [(i, i ^ 2 * distance) for i in range(size)])
-
-
 def gather(block, chips):
-    distance, orders = chips // 2, [0]
-    while distance > 1:
+    size = 2 * chips
+    far = [1 << i for i in range(chips.bit_length() - 2, -1, -1)]
+    stages = list(zip(far[-1:] + far[:-1], far))
+    orders = [[0], [0]]
+    for distances in stages:
+        pairs = [(i, i ^ 2 * distances[i % 2]) for i in range(size)]
+        received = lax.ppermute(block, "expert", pairs)
+        orders = [
+            order + [held ^ distance for held in order]
+            for order, distance in zip(orders, distances)
+        ]
+        if distances is stages[-1]:
+            return block, received, orders
         rows, width = block.shape
         joined = ((2, rows, width), block.dtype)
-        (block,) = on_vmem(double_kernel, (block, swap_chip(block, distance)), [joined])
-        block = block.reshape(2 * rows, width)
-        orders = orders + [order ^ distance for order in orders]
-        distance = distance // 2
-    return block, swap_chip(block, 1), orders + [order ^ 1 for order in orders]
+        block = on_vmem(double_kernel, (block, received), [joined])[0].reshape(2 * rows, width)
 
 
 def spread(blocks):

time: 74 us -> 74 us (level)
  waiting for transfers between devices: 14.6 us -> 13.7 us
  starting transfers between devices: 11.3 us -> 12.1 us
    ppermute x3, waiting for transfers between devices: 8.09 us -> 7.24 us  [gather(): received = lax.ppermute(block, 'expert', pairs)]
    ppermute x3, starting transfers between devices: 7.09 us -> 7.89 us  [gather(): received = lax.ppermute(block, 'expert', pairs)]
where the time goes in v19:
time: 74 us; the launch traced here: 73.8 us
  blocking collectives  37.1 us (50%)
  waiting for transfers between devices  13.7 us (19%)
  starting transfers between devices  12.1 us (16%)
  Pallas kernels  10 us (14%)
    all_to_all x3, blocking collectives, spread(): lax.all_to_all(blocks, 'expert', 0, 0, axis_index_groups=groups, tiled=True)  37.1 us
    pallas_call x10, Pallas kernels, on_vmem(): pl.pallas_call(body, out_shape=[jax.ShapeDtypeStruct(shape, kind) for sha...  10 us
    ppermute x3, starting transfers between devices, gather(): received = lax.ppermute(block, 'expert', pairs)  7.89 us
    ppermute x3, waiting for transfers between devices, gather(): received = lax.ppermute(block, 'expert', pairs)  7.24 us
    ppermute x2, waiting for transfers between devices, swap_group(): return lax.ppermute(value, 'group', [(0, 1), (1, 0)])  6.48 us
    ppermute x2, starting transfers between devices, swap_group(): return lax.ppermute(value, 'group', [(0, 1), (1, 0)])  3.11 us
  transfers between devices with their start and end apart: 9, of which 5 were waited for; matrix products, arithmetic and copies ran while one was open for 0% of the time, Pallas kernels for 5%

profile of v19, /device:TPU:0, one launch (start us, length us, event | category | flops | bytes accessed | tf_op | source)
XLA Modules:
  0.0 73.8 jit_solution(18212622052165776887)
XLA Ops:
  0.0 0.5 collective-permute-start.3
  0.5 0.5 collective-permute-start.5
  1.0 0.1 collective-permute-start.6
  1.1 0.6 copy-done.4
  1.7 0.1 shard_map.92.refs_0_
  1.9 2.6 %collective-permute-start = (bf16[8,2176]{1,0:T(8,128)(2,1)S(1)}, bf16[8,2176]{1,0:T(8,128)(2,1)S(1)}, u32[]{:S(2)}, u32[]{:S(2)}) collective-permute-start(bf16[8,2176]{1,0:T(8,128)(2,1)S(1)} %shard_map.92.refs_0_), channel_id=1, source_target_pairs={{0,2},{1,9},{2,0},{3,11},{4,6},{5,13},{6,4},{7,15},{8,10},{9,1},{1... | collective-permute-start | bytes 104456 | tf_op jit(solution)/shard_map/ppermute | solution.py:195
  4.5 1.9 %collective-permute-done.refs_1_ = bf16[8,2176]{1,0:T(8,128)(2,1)S(1)} collective-permute-done((bf16[8,2176]{1,0:T(8,128)(2,1)S(1)}, bf16[8,2176]{1,0:T(8,128)(2,1)S(1)}, u32[]{:S(2)}, u32[]{:S(2)}) %collective-permute-start) | collective-permute-done | bytes 34848 | tf_op jit(solution)/shard_map/ppermute | solution.py:195
  6.4 3.1 %collective-permute-start.1 = (bf16[16,2176]{1,0:T(8,128)(2,1)S(1)}, bf16[16,2176]{1,0:T(8,128)(2,1)S(1)}, u32[]{:S(2)}, u32[]{:S(2)}) collective-permute-start(bf16[16,2176]{1,0:T(8,128)(2,1)S(1)} %bitcast.26), channel_id=1, source_target_pairs={{0,8},{1,5},{2,10},{3,7},{4,12},{5,1},{6,14},{7,3},{8,0},{9,13},{1... | collective-permute-start | bytes 208904 | tf_op jit(solution)/shard_map/ppermute | solution.py:195
  9.5 2.3 %collective-permute-done.1.refs_1_ = bf16[16,2176]{1,0:T(8,128)(2,1)S(1)} collective-permute-done((bf16[16,2176]{1,0:T(8,128)(2,1)S(1)}, bf16[16,2176]{1,0:T(8,128)(2,1)S(1)}, u32[]{:S(2)}, u32[]{:S(2)}) %collective-permute-start.1) | collective-permute-done | bytes 69664 | tf_op jit(solution)/shard_map/ppermute | solution.py:195
  11.8 2.2 %collective-permute-start.2 = (bf16[32,2176]{1,0:T(8,128)(2,1)S(1)}, bf16[32,2176]{1,0:T(8,128)(2,1)S(1)}, u32[]{:S(2)}, u32[]{:S(2)}) collective-permute-start(bf16[32,2176]{1,0:T(8,128)(2,1)S(1)} %bitcast.24), channel_id=1, source_target_pairs={{0,4},{1,3},{2,6},{3,1},{4,0},{5,7},{6,2},{7,5},{8,12},{9,11},{10,... | collective-permute-start | bytes 417800 | tf_op jit(solution)/shard_map/ppermute | solution.py:195
  14.0 3.0 %collective-permute-done.2.refs_1_ = bf16[32,2176]{1,0:T(8,128)(2,1)S(1)} collective-permute-done((bf16[32,2176]{1,0:T(8,128)(2,1)S(1)}, bf16[32,2176]{1,0:T(8,128)(2,1)S(1)}, u32[]{:S(2)}, u32[]{:S(2)}) %collective-permute-start.2) | collective-permute-done | bytes 139296 | tf_op jit(solution)/shard_map/ppermute | solution.py:195
  17.1 3.5 %shard_map.95 = (bf16[8,8,2048]{2,1,0:T(8,128)(2,1)S(1)}, bf16[8,8,128]{2,1,0:T(8,128)(2,1)S(1)}) custom-call(bf16[32,2176]{1,0:T(8,128)(2,1)S(1)} %bitcast.25, bf16[32,2176]{1,0:T(8,128)(2,1)S(1)} %collective-permute-done.2.refs_1_, bf16[768,2048]{1,0:T(8,128)(2,1)S(1)} %bitcast.14, bf16[768,2048]{1,0:T(8,128)(2,1)S(1)} %bitcast.17, ...), custom_call_target="tpu_custom_call" | custom-call | flops 3221225472 | bytes 25165824 | tf_op jit(solution)/shard_map/pallas_call | solution.py:161
  20.5 15.2 %all_to_all.15.refs_1_ = bf16[8,8,2048]{2,1,0:T(8,128)(2,1)S(1)} all-to-all(bf16[8,8,2048]{2,1,0:T(8,128)(2,1)S(1)} %get-tuple-element.17), channel_id=1, replica_groups={{0,4,8,12,2,6,10,14},{1,5,9,13,3,7,11,15},{16,20,24,28,18,22,26,30},{17..., dimensions={0} | all-to-all | bytes 524288 | tf_op jit(solution)/shard_map/all_to_all | solution.py:212
  35.7 0.2 shard_map.96
  35.9 11.0 %all_to_all.16 = bf16[8,8,2048]{2,1,0:T(8,128)(2,1)S(1)} all-to-all(bf16[8,8,2048]{2,1,0:T(8,128)(2,1)S(1)} %get-tuple-element.19), channel_id=1, replica_groups={{0,4,8,12,2,6,10,14},{1,5,9,13,3,7,11,15},{16,20,24,28,18,22,26,30},{17..., dimensions={0} | all-to-all | bytes 524288 | tf_op jit(solution)/shard_map/all_to_all | solution.py:212
  46.9 1.6 %collective-permute-start.7 = (bf16[64,2176]{1,0:T(8,128)(2,1)S(1)}, bf16[64,2176]{1,0:T(8,128)(2,1)S(1)}, u32[]{:S(2)}, u32[]{:S(2)}) collective-permute-start(bf16[64,2176]{1,0:T(8,128)(2,1)S(1)} %shard_map.97.refs_0_), channel_id=1, source_target_pairs={{0,16},{16,0},{1,17},{17,1},{2,18},{18,2},{3,19},{19,3},{4,20},{20... | collective-permute-start | bytes 835592 | tf_op jit(solution)/shard_map/ppermute | solution.py:185
  48.5 3.5 %shard_map.98 = f32[64,2048]{1,0:T(8,128)S(1)} custom-call(bf16[64,2176]{1,0:T(8,128)(2,1)S(1)} %shard_map.97.refs_0_, bf16[768,2048]{1,0:T(8,128)(2,1)S(1)} %bitcast.15, bf16[768,2048]{1,0:T(8,128)(2,1)S(1)} %bitcast.18, bf16[768,2048]{1,0:T(8,128)(2,1)S(1)} %collective-permute-done.3.refs_4_.refs_3_, ...), custom_call_target="tpu_custom_call" | custom-call | flops 3221225472 | bytes 25165824 | tf_op jit(solution)/shard_map/pallas_call | solution.py:161
  51.9 1.6 %collective-permute-done.7.refs_1_ = bf16[64,2176]{1,0:T(8,128)(2,1)S(1)} collective-permute-done((bf16[64,2176]{1,0:T(8,128)(2,1)S(1)}, bf16[64,2176]{1,0:T(8,128)(2,1)S(1)}, u32[]{:S(2)}, u32[]{:S(2)}) %collective-permute-start.7) | collective-permute-done | bytes 278560 | tf_op jit(solution)/shard_map/ppermute | solution.py:185
  53.5 2.1 %shard_map.99 = (f32[64,2048]{1,0:T(8,128)S(1)}, bf16[64,2048]{1,0:T(8,128)(2,1)S(1)}) custom-call(bf16[64,2176]{1,0:T(8,128)(2,1)S(1)} %shard_map.97.refs_0_, bf16[64,2176]{1,0:T(8,128)(2,1)S(1)} %collective-permute-done.7.refs_1_, bf16[384,2048]{1,0:T(8,128)(2,1)S(1)} %bitcast.20, bf16[384,2048]{1,0:T(8,128)(2,1)S(1)} %bitcast.22, ...), custom_call_target="tpu_custom_call" | custom-call | flops 1610612736 | bytes 12582912 | tf_op jit(solution)/shard_map/pallas_call | solution.py:161
  55.6 1.6 %collective-permute-start.8 = (bf16[64,2048]{1,0:T(8,128)(2,1)S(1)}, bf16[64,2048]{1,0:T(8,128)(2,1)S(1)}, u32[]{:S(2)}, u32[]{:S(2)}) collective-permute-start(bf16[64,2048]{1,0:T(8,128)(2,1)S(1)} %get-tuple-element.24), channel_id=1, source_target_pairs={{0,16},{16,0},{1,17},{17,1},{2,18},{18,2},{3,19},{19,3},{4,20},{20... | collective-permute-start | bytes 786440 | tf_op jit(solution)/shard_map/ppermute | solution.py:185
  57.2 4.9 %collective-permute-done.8 = bf16[64,2048]{1,0:T(8,128)(2,1)S(1)} collective-permute-done((bf16[64,2048]{1,0:T(8,128)(2,1)S(1)}, bf16[64,2048]{1,0:T(8,128)(2,1)S(1)}, u32[]{:S(2)}, u32[]{:S(2)}) %collective-permute-start.8) | collective-permute-done | bytes 262176 | tf_op jit(solution)/shard_map/ppermute | solution.py:185
  62.1 0.1 fusion
  62.1 11.0 %all_to_all.17.refs_1_ = bf16[8,8,2048]{2,1,0:T(8,128)(2,1)S(1)} all-to-all(bf16[8,8,2048]{2,1,0:T(8,128)(2,1)S(1)} %fusion), channel_id=1, replica_groups={{0,4,8,12,2,6,10,14},{1,5,9,13,3,7,11,15},{16,20,24,28,18,22,26,30},{17..., dimensions={0} | all-to-all | bytes 524288 | tf_op jit(solution)/shard_map/all_to_all | solution.py:212
  73.1 0.7 shard_map.100
  (26 shorter events, 0.1 us)
Async XLA Ops:
  0.0 17.0 %collective-permute-start.3 = (bf16[768,2048]{1,0:T(8,128)(2,1)}, bf16[768,2048]{1,0:T(8,128)(2,1)S(1)}, u32[]{:S(2)}, u32[]{:S(2)}) collective-permute-start(bf16[768,2048]{1,0:T(8,128)(2,1)} %bitcast.13), channel_id=1, source_target_pairs={{0,1},{1,0},{2,3},{3,2},{4,5},{5,4},{6,7},{7,6},{8,9},{9,8},{10,11... | collective-permute-start | bytes 9437192 | tf_op jit(solution)/shard_map/ppermute | solution.py:181
  0.5 16.6 %collective-permute-start.4 = (bf16[768,2048]{1,0:T(8,128)(2,1)}, bf16[768,2048]{1,0:T(8,128)(2,1)S(1)}, u32[]{:S(2)}, u32[]{:S(2)}) collective-permute-start(bf16[768,2048]{1,0:T(8,128)(2,1)} %bitcast.16), channel_id=1, source_target_pairs={{0,1},{1,0},{2,3},{3,2},{4,5},{5,4},{6,7},{7,6},{8,9},{9,8},{10,11... | collective-permute-start | bytes 9437192 | tf_op jit(solution)/shard_map/ppermute | solution.py:181
  0.5 16.5 %collective-permute-start.5 = (bf16[384,2048]{1,0:T(8,128)(2,1)}, bf16[384,2048]{1,0:T(8,128)(2,1)S(1)}, u32[]{:S(2)}, u32[]{:S(2)}) collective-permute-start(bf16[384,2048]{1,0:T(8,128)(2,1)} %bitcast.19), channel_id=1, source_target_pairs={{0,1},{1,0},{2,3},{3,2},{4,5},{5,4},{6,7},{7,6},{8,9},{9,8},{10,11... | collective-permute-start | bytes 4718600 | tf_op jit(solution)/shard_map/ppermute | solution.py:181
  1.0 0.8 %copy-start.4 = (bf16[1,8,2048]{2,1,0:T(8,128)(2,1)S(1)}, bf16[1,8,2048]{2,1,0:T(8,128)(2,1)}, u32[]{:S(2)}) copy-start(bf16[1,8,2048]{2,1,0:T(8,128)(2,1)} %param.9) | copy-start | bytes 98308
  1.0 0.8 %copy-start.5 = (f32[2048]{0:T(1024)S(1)}, f32[2048]{0:T(1024)}, u32[]{:S(2)}) copy-start(f32[2048]{0:T(1024)} %param.10) | copy-start | bytes 24580
  1.0 0.8 %copy-start.6 = (s32[2,1,8,8]{3,2,1,0:T(8,128)S(1)}, s32[2,1,8,8]{3,2,1,0:T(8,128)}, u32[]{:S(2)}) copy-start(s32[2,1,8,8]{3,2,1,0:T(8,128)} %refs_4_.1) | copy-start | bytes 1540
  1.0 0.8 %copy-start.7 = (f32[2,1,8,8]{3,2,1,0:T(8,128)S(1)}, f32[2,1,8,8]{3,2,1,0:T(8,128)}, u32[]{:S(2)}) copy-start(f32[2,1,8,8]{3,2,1,0:T(8,128)} %refs_5_.1) | copy-start | bytes 1540
  1.0 0.8 %copy-start.8 = (s32[1,4]{1,0:T(1,128)S(1)}, s32[1,4]{1,0:T(1,128)}, u32[]{:S(2)}) copy-start(s32[1,4]{1,0:T(1,128)} %refs_6_.1) | copy-start | bytes 52
  1.0 16.1 %copy-start = (bf16[1,768,2048]{2,1,0:T(8,128)(2,1)S(1)}, bf16[1,768,2048]{2,1,0:T(8,128)(2,1)}, u32[]{:S(2)}) copy-start(bf16[1,768,2048]{2,1,0:T(8,128)(2,1)} %param.14) | copy-start | bytes 9437188
  1.0 16.1 %copy-start.1 = (bf16[1,768,2048]{2,1,0:T(8,128)(2,1)S(1)}, bf16[1,768,2048]{2,1,0:T(8,128)(2,1)}, u32[]{:S(2)}) copy-start(bf16[1,768,2048]{2,1,0:T(8,128)(2,1)} %param.15) | copy-start | bytes 9437188
  1.0 16.0 %collective-permute-start.6 = (bf16[384,2048]{1,0:T(8,128)(2,1)}, bf16[384,2048]{1,0:T(8,128)(2,1)S(1)}, u32[]{:S(2)}, u32[]{:S(2)}) collective-permute-start(bf16[384,2048]{1,0:T(8,128)(2,1)} %bitcast.21), channel_id=1, source_target_pairs={{0,1},{1,0},{2,3},{3,2},{4,5},{5,4},{6,7},{7,6},{8,9},{9,8},{10,11... | collective-permute-start | bytes 4718600 | tf_op jit(solution)/shard_map/ppermute | solution.py:181
  1.9 4.5 %collective-permute-start = (bf16[8,2176]{1,0:T(8,128)(2,1)S(1)}, bf16[8,2176]{1,0:T(8,128)(2,1)S(1)}, u32[]{:S(2)}, u32[]{:S(2)}) collective-permute-start(bf16[8,2176]{1,0:T(8,128)(2,1)S(1)} %shard_map.92.refs_0_), channel_id=1, source_target_pairs={{0,2},{1,9},{2,0},{3,11},{4,6},{5,13},{6,4},{7,15},{8,10},{9,1},{1... | collective-permute-start | bytes 104456 | tf_op jit(solution)/shard_map/ppermute | solution.py:195
  6.4 5.4 %collective-permute-start.1 = (bf16[16,2176]{1,0:T(8,128)(2,1)S(1)}, bf16[16,2176]{1,0:T(8,128)(2,1)S(1)}, u32[]{:S(2)}, u32[]{:S(2)}) collective-permute-start(bf16[16,2176]{1,0:T(8,128)(2,1)S(1)} %bitcast.26), channel_id=1, source_target_pairs={{0,8},{1,5},{2,10},{3,7},{4,12},{5,1},{6,14},{7,3},{8,0},{9,13},{1... | collective-permute-start | bytes 208904 | tf_op jit(solution)/shard_map/ppermute | solution.py:195
  11.8 5.2 %collective-permute-start.2 = (bf16[32,2176]{1,0:T(8,128)(2,1)S(1)}, bf16[32,2176]{1,0:T(8,128)(2,1)S(1)}, u32[]{:S(2)}, u32[]{:S(2)}) collective-permute-start(bf16[32,2176]{1,0:T(8,128)(2,1)S(1)} %bitcast.24), channel_id=1, source_target_pairs={{0,4},{1,3},{2,6},{3,1},{4,0},{5,7},{6,2},{7,5},{8,12},{9,11},{10,... | collective-permute-start | bytes 417800 | tf_op jit(solution)/shard_map/ppermute | solution.py:195
  46.9 6.6 %copy-start.2 = (bf16[1,384,2048]{2,1,0:T(8,128)(2,1)S(1)}, bf16[1,384,2048]{2,1,0:T(8,128)(2,1)}, u32[]{:S(2)}) copy-start(bf16[1,384,2048]{2,1,0:T(8,128)(2,1)} %param.16) | copy-start | bytes 4718596
  46.9 6.6 %copy-start.3 = (bf16[1,384,2048]{2,1,0:T(8,128)(2,1)S(1)}, bf16[1,384,2048]{2,1,0:T(8,128)(2,1)}, u32[]{:S(2)}) copy-start(bf16[1,384,2048]{2,1,0:T(8,128)(2,1)} %param.17) | copy-start | bytes 4718596
  46.9 6.6 %collective-permute-start.7 = (bf16[64,2176]{1,0:T(8,128)(2,1)S(1)}, bf16[64,2176]{1,0:T(8,128)(2,1)S(1)}, u32[]{:S(2)}, u32[]{:S(2)}) collective-permute-start(bf16[64,2176]{1,0:T(8,128)(2,1)S(1)} %shard_map.97.refs_0_), channel_id=1, source_target_pairs={{0,16},{16,0},{1,17},{17,1},{2,18},{18,2},{3,19},{19,3},{4,20},{20... | collective-permute-start | bytes 835592 | tf_op jit(solution)/shard_map/ppermute | solution.py:185
  55.6 6.4 %collective-permute-start.8 = (bf16[64,2048]{1,0:T(8,128)(2,1)S(1)}, bf16[64,2048]{1,0:T(8,128)(2,1)S(1)}, u32[]{:S(2)}, u32[]{:S(2)}) collective-permute-start(bf16[64,2048]{1,0:T(8,128)(2,1)S(1)} %get-tuple-element.24), channel_id=1, source_target_pairs={{0,16},{16,0},{1,17},{17,1},{2,18},{18,2},{3,19},{19,3},{4,20},{20... | collective-permute-start | bytes 786440 | tf_op jit(solution)/shard_map/ppermute | solution.py:185

commit v20 on v18

--- a/solution.py
+++ b/solution.py
@@ -79,9 +79,9 @@
     out[:, width:] = weight_table(section[...], expert[...], routes, scales, changed)
 
 
-def double_kernel(first, second, out):
-    out[0] = first[...]
-    out[1] = second[...]
+def stack_kernel(*refs):
+    for i, part in enumerate(refs[:-1]):
+        refs[-1][i] = part[...]
 
 
 def sum_blocks(blocks):
@@ -188,16 +188,15 @@
     return lax.ppermute(value, "expert", [(i, i ^ 2 * distance) for i in range(size)])
 
 
-def gather(block, chips):
-    distance, orders = chips // 2, [0]
-    while distance > 1:
-        rows, width = block.shape
-        joined = ((2, rows, width), block.dtype)
-        (block,) = on_vmem(double_kernel, (block, swap_chip(block, distance)), [joined])
-        block = block.reshape(2 * rows, width)
-        orders = orders + [order ^ distance for order in orders]
-        distance = distance // 2
-    return block, swap_chip(block, 1), orders + [order ^ 1 for order in orders]
+def gather(block, chips, waiting):
+    orders = [0] + list(range(chips - 2, 0, -2))
+    received = [swap_chip(block, distance) for distance in orders[1:]]
+    received = lax.optimization_barrier(tuple(received) + tuple(waiting))
+    parts, waiting = (block,) + received[: len(orders) - 1], received[len(orders) - 1 :]
+    rows, width = block.shape
+    (block,) = on_vmem(stack_kernel, parts, [((len(parts), rows, width), block.dtype)])
+    block = block.reshape(len(parts) * rows, width)
+    return block, swap_chip(block, 1), orders + [order ^ 1 for order in orders], waiting
 
 
 def spread(blocks):
@@ -226,7 +225,6 @@
         functools.partial(lane_kernel, experts), (), [lanes, lanes], cost=long
     )
     stale = stale + tuple(swap_core(part) for part in stale)
-    learner = learner + tuple(swap_core(part) for part in learner)
     (block,) = on_vmem(
         pack_kernel,
         (section, expert, tokens[0], gain, routes, route_scale, changed),
@@ -235,7 +233,8 @@
     state = tokens[0]
     for step in range(steps_total):
         if step == 0:
-            rows, across, orders = gather(block, chips)
+            rows, across, orders, learner = gather(block, chips, learner)
+            learner = learner + tuple(swap_core(part) for part in learner)
             share, tables = run_mlp(
                 functools.partial(first_kernel, experts, step, orders),
                 [rows, across],
@@ -321,7 +320,7 @@
     experts = lax.axis_size("expert")
     groups = lax.axis_size("group")
     fewer = tokens.shape[1] * experts < learner_up.shape[1]
-    paired = experts & (experts - 1) == 0 and experts >= 4 and groups == 2
+    paired = experts & (experts - 1) == 0 and experts >= 8 and groups == 2
     plan = exchange_plan if fewer and paired else gather_plan
     stale = (rollout_up[0], rollout_down[0])
     learner = (learner_up[0], learner_down[0])

time: 74 us -> 75.2 us (1.016)
  waiting for transfers between devices: 14.6 us -> 16.3 us
    ppermute x3 -> x4, waiting for transfers between devices: 8.09 us -> 9.86 us  [swap_chip(): lax.ppermute(value, 'expert', [(i, i ^ 2 * distance) for i in range(size)])]
    ppermute x3 -> x4, starting transfers between devices: 7.09 us -> 6.82 us  [swap_chip(): lax.ppermute(value, 'expert', [(i, i ^ 2 * distance) for i in range(size)])]
    pallas_call x10 -> x9, Pallas kernels: 10 us -> 10 us  [on_vmem(): pl.pallas_call(body, out_shape=[jax.ShapeDtypeStruct(shape, kind) for sha...]
  transfers between devices with their start and end apart: 9 -> 10, of which waited for: 5 -> 5; matrix products, arithmetic and copies ran while one was open for 0% -> 0% of each run, Pallas kernels for 5% -> 5%
where the time goes in v20:
time: 75.2 us; the launch traced here: 75 us
  blocking collectives  36.8 us (49%)
  waiting for transfers between devices  16.3 us (22%)
  starting transfers between devices  11 us (15%)
  Pallas kernels  10 us (13%)
    all_to_all x3, blocking collectives, spread(): lax.all_to_all(blocks, 'expert', 0, 0, axis_index_groups=groups, tiled=True)  36.8 us
    pallas_call x9, Pallas kernels, on_vmem(): pl.pallas_call(body, out_shape=[jax.ShapeDtypeStruct(shape, kind) for sha...  10 us
    ppermute x4, waiting for transfers between devices, swap_chip(): lax.ppermute(value, 'expert', [(i, i ^ 2 * distance) for i in range(size)])  9.86 us
    ppermute x4, starting transfers between devices, swap_chip(): lax.ppermute(value, 'expert', [(i, i ^ 2 * distance) for i in range(size)])  6.82 us
    ppermute x2, waiting for transfers between devices, swap_group(): return lax.ppermute(value, 'group', [(0, 1), (1, 0)])  6.47 us
    ppermute x2, starting transfers between devices, swap_group(): return lax.ppermute(value, 'group', [(0, 1), (1, 0)])  3.11 us
  transfers between devices with their start and end apart: 10, of which 5 were waited for; matrix products, arithmetic and copies ran while one was open for 0% of the time, Pallas kernels for 5%

profile of v20, /device:TPU:0, one launch (start us, length us, event | category | flops | bytes accessed | tf_op | source)
XLA Modules:
  0.0 75.0 jit_solution(1978542726350236471)
XLA Ops:
  0.0 0.5 collective-permute-start.4
  0.5 0.1 collective-permute-start.5
  0.6 0.6 copy-done.4
  1.2 0.1 shard_map.92.refs_0_
  1.4 2.6 %collective-permute-start.2 = (bf16[8,2176]{1,0:T(8,128)(2,1)S(1)}, bf16[8,2176]{1,0:T(8,128)(2,1)S(1)}, u32[]{:S(2)}, u32[]{:S(2)}) collective-permute-start(bf16[8,2176]{1,0:T(8,128)(2,1)S(1)} %shard_map.92.refs_0_), channel_id=1, source_target_pairs={{0,4},{1,5},{2,6},{3,7},{4,0},{5,1},{6,2},{7,3},{8,12},{9,13},{10,... | collective-permute-start | bytes 104456 | tf_op jit(solution)/shard_map/ppermute | solution.py:188
  4.0 2.6 %collective-permute-start.1 = (bf16[8,2176]{1,0:T(8,128)(2,1)S(1)}, bf16[8,2176]{1,0:T(8,128)(2,1)S(1)}, u32[]{:S(2)}, u32[]{:S(2)}) collective-permute-start(bf16[8,2176]{1,0:T(8,128)(2,1)S(1)} %shard_map.92.refs_0_), channel_id=1, source_target_pairs={{0,8},{1,9},{2,10},{3,11},{4,12},{5,13},{6,14},{7,15},{8,0},{9,1},... | collective-permute-start | bytes 104456 | tf_op jit(solution)/shard_map/ppermute | solution.py:188
  6.6 3.0 %collective-permute-done.1.refs_2_ = bf16[8,2176]{1,0:T(8,128)(2,1)S(1)} collective-permute-done((bf16[8,2176]{1,0:T(8,128)(2,1)S(1)}, bf16[8,2176]{1,0:T(8,128)(2,1)S(1)}, u32[]{:S(2)}, u32[]{:S(2)}) %collective-permute-start.1) | collective-permute-done | bytes 34848 | tf_op jit(solution)/shard_map/ppermute | solution.py:188
  9.6 2.8 %collective-permute-done.refs_1_ = bf16[8,2176]{1,0:T(8,128)(2,1)S(1)} collective-permute-done((bf16[8,2176]{1,0:T(8,128)(2,1)S(1)}, bf16[8,2176]{1,0:T(8,128)(2,1)S(1)}, u32[]{:S(2)}, u32[]{:S(2)}) %collective-permute-start) | collective-permute-done | bytes 34848 | tf_op jit(solution)/shard_map/ppermute | solution.py:188
  12.3 0.5 collective-permute-start.7
  12.9 1.6 %collective-permute-start.3 = (bf16[32,2176]{1,0:T(8,128)(2,1)S(1)}, bf16[32,2176]{1,0:T(8,128)(2,1)S(1)}, u32[]{:S(2)}, u32[]{:S(2)}) collective-permute-start(bf16[32,2176]{1,0:T(8,128)(2,1)S(1)} %bitcast.23), channel_id=1, source_target_pairs={{0,2},{1,3},{2,0},{3,1},{4,6},{5,7},{6,4},{7,5},{8,10},{9,11},{10,... | collective-permute-start | bytes 417800 | tf_op jit(solution)/shard_map/ppermute | solution.py:188
  14.4 4.1 %collective-permute-done.3.refs_1_ = bf16[32,2176]{1,0:T(8,128)(2,1)S(1)} collective-permute-done((bf16[32,2176]{1,0:T(8,128)(2,1)S(1)}, bf16[32,2176]{1,0:T(8,128)(2,1)S(1)}, u32[]{:S(2)}, u32[]{:S(2)}) %collective-permute-start.3) | collective-permute-done | bytes 139296 | tf_op jit(solution)/shard_map/ppermute | solution.py:188
  18.6 3.5 %shard_map.94 = (bf16[8,8,2048]{2,1,0:T(8,128)(2,1)S(1)}, bf16[8,8,128]{2,1,0:T(8,128)(2,1)S(1)}) custom-call(bf16[32,2176]{1,0:T(8,128)(2,1)S(1)} %bitcast.24, bf16[32,2176]{1,0:T(8,128)(2,1)S(1)} %collective-permute-done.3.refs_1_, bf16[768,2048]{1,0:T(8,128)(2,1)S(1)} %bitcast.13, bf16[768,2048]{1,0:T(8,128)(2,1)S(1)} %bitcast.16, ...), custom_call_target="tpu_custom_call" | custom-call | flops 3221225472 | bytes 25165824 | tf_op jit(solution)/shard_map/pallas_call | solution.py:159
  22.1 13.2 %all_to_all.15.refs_1_ = bf16[8,8,2048]{2,1,0:T(8,128)(2,1)S(1)} all-to-all(bf16[8,8,2048]{2,1,0:T(8,128)(2,1)S(1)} %get-tuple-element.27), channel_id=1, replica_groups={{0,4,8,12,2,6,10,14},{1,5,9,13,3,7,11,15},{16,20,24,28,18,22,26,30},{17..., dimensions={0} | all-to-all | bytes 524288 | tf_op jit(solution)/shard_map/all_to_all | solution.py:207
  35.3 0.2 shard_map.95
  35.5 11.8 %all_to_all.16 = bf16[8,8,2048]{2,1,0:T(8,128)(2,1)S(1)} all-to-all(bf16[8,8,2048]{2,1,0:T(8,128)(2,1)S(1)} %get-tuple-element.29), channel_id=1, replica_groups={{0,4,8,12,2,6,10,14},{1,5,9,13,3,7,11,15},{16,20,24,28,18,22,26,30},{17..., dimensions={0} | all-to-all | bytes 524288 | tf_op jit(solution)/shard_map/all_to_all | solution.py:207
  47.3 1.6 %collective-permute-start.8 = (bf16[64,2176]{1,0:T(8,128)(2,1)S(1)}, bf16[64,2176]{1,0:T(8,128)(2,1)S(1)}, u32[]{:S(2)}, u32[]{:S(2)}) collective-permute-start(bf16[64,2176]{1,0:T(8,128)(2,1)S(1)} %shard_map.96.refs_0_), channel_id=1, source_target_pairs={{0,16},{16,0},{1,17},{17,1},{2,18},{18,2},{3,19},{19,3},{4,20},{20... | collective-permute-start | bytes 835592 | tf_op jit(solution)/shard_map/ppermute | solution.py:183
  48.8 3.5 %shard_map.97 = f32[64,2048]{1,0:T(8,128)S(1)} custom-call(bf16[64,2176]{1,0:T(8,128)(2,1)S(1)} %shard_map.96.refs_0_, bf16[768,2048]{1,0:T(8,128)(2,1)S(1)} %bitcast.14, bf16[768,2048]{1,0:T(8,128)(2,1)S(1)} %bitcast.17, bf16[768,2048]{1,0:T(8,128)(2,1)S(1)} %collective-permute-done.4.refs_4_.refs_3_, ...), custom_call_target="tpu_custom_call" | custom-call | flops 3221225472 | bytes 25165824 | tf_op jit(solution)/shard_map/pallas_call | solution.py:159
  52.3 1.6 %collective-permute-done.8.refs_1_ = bf16[64,2176]{1,0:T(8,128)(2,1)S(1)} collective-permute-done((bf16[64,2176]{1,0:T(8,128)(2,1)S(1)}, bf16[64,2176]{1,0:T(8,128)(2,1)S(1)}, u32[]{:S(2)}, u32[]{:S(2)}) %collective-permute-start.8) | collective-permute-done | bytes 278560 | tf_op jit(solution)/shard_map/ppermute | solution.py:183
  53.9 2.1 %shard_map.98 = (f32[64,2048]{1,0:T(8,128)S(1)}, bf16[64,2048]{1,0:T(8,128)(2,1)S(1)}) custom-call(bf16[64,2176]{1,0:T(8,128)(2,1)S(1)} %shard_map.96.refs_0_, bf16[64,2176]{1,0:T(8,128)(2,1)S(1)} %collective-permute-done.8.refs_1_, bf16[384,2048]{1,0:T(8,128)(2,1)S(1)} %bitcast.19, bf16[384,2048]{1,0:T(8,128)(2,1)S(1)} %bitcast.21, ...), custom_call_target="tpu_custom_call" | custom-call | flops 1610612736 | bytes 12582912 | tf_op jit(solution)/shard_map/pallas_call | solution.py:159
  56.0 1.6 %collective-permute-start.9 = (bf16[64,2048]{1,0:T(8,128)(2,1)S(1)}, bf16[64,2048]{1,0:T(8,128)(2,1)S(1)}, u32[]{:S(2)}, u32[]{:S(2)}) collective-permute-start(bf16[64,2048]{1,0:T(8,128)(2,1)S(1)} %get-tuple-element.34), channel_id=1, source_target_pairs={{0,16},{16,0},{1,17},{17,1},{2,18},{18,2},{3,19},{19,3},{4,20},{20... | collective-permute-start | bytes 786440 | tf_op jit(solution)/shard_map/ppermute | solution.py:183
  57.5 4.9 %collective-permute-done.9 = bf16[64,2048]{1,0:T(8,128)(2,1)S(1)} collective-permute-done((bf16[64,2048]{1,0:T(8,128)(2,1)S(1)}, bf16[64,2048]{1,0:T(8,128)(2,1)S(1)}, u32[]{:S(2)}, u32[]{:S(2)}) %collective-permute-start.9) | collective-permute-done | bytes 262176 | tf_op jit(solution)/shard_map/ppermute | solution.py:183
  62.4 0.1 fusion
  62.5 11.8 %all_to_all.17.refs_1_ = bf16[8,8,2048]{2,1,0:T(8,128)(2,1)S(1)} all-to-all(bf16[8,8,2048]{2,1,0:T(8,128)(2,1)S(1)} %fusion), channel_id=1, replica_groups={{0,4,8,12,2,6,10,14},{1,5,9,13,3,7,11,15},{16,20,24,28,18,22,26,30},{17..., dimensions={0} | all-to-all | bytes 524288 | tf_op jit(solution)/shard_map/all_to_all | solution.py:207
  74.3 0.7 shard_map.99
  (27 shorter events, 0.1 us)
Async XLA Ops:
  0.0 18.6 %collective-permute-start.4 = (bf16[768,2048]{1,0:T(8,128)(2,1)}, bf16[768,2048]{1,0:T(8,128)(2,1)S(1)}, u32[]{:S(2)}, u32[]{:S(2)}) collective-permute-start(bf16[768,2048]{1,0:T(8,128)(2,1)} %bitcast.12), channel_id=1, source_target_pairs={{0,1},{1,0},{2,3},{3,2},{4,5},{5,4},{6,7},{7,6},{8,9},{9,8},{10,11... | collective-permute-start | bytes 9437192 | tf_op jit(solution)/shard_map/ppermute | solution.py:179
  0.5 0.8 %copy-start.4 = (bf16[1,8,2048]{2,1,0:T(8,128)(2,1)S(1)}, bf16[1,8,2048]{2,1,0:T(8,128)(2,1)}, u32[]{:S(2)}) copy-start(bf16[1,8,2048]{2,1,0:T(8,128)(2,1)} %param.9) | copy-start | bytes 98308
  0.5 0.8 %copy-start.5 = (f32[2048]{0:T(1024)S(1)}, f32[2048]{0:T(1024)}, u32[]{:S(2)}) copy-start(f32[2048]{0:T(1024)} %param.10) | copy-start | bytes 24580
  0.5 0.8 %copy-start.6 = (s32[2,1,8,8]{3,2,1,0:T(8,128)S(1)}, s32[2,1,8,8]{3,2,1,0:T(8,128)}, u32[]{:S(2)}) copy-start(s32[2,1,8,8]{3,2,1,0:T(8,128)} %refs_4_.1) | copy-start | bytes 1540
  0.5 0.8 %copy-start.7 = (f32[2,1,8,8]{3,2,1,0:T(8,128)S(1)}, f32[2,1,8,8]{3,2,1,0:T(8,128)}, u32[]{:S(2)}) copy-start(f32[2,1,8,8]{3,2,1,0:T(8,128)} %refs_5_.1) | copy-start | bytes 1540
  0.5 0.8 %copy-start.8 = (s32[1,4]{1,0:T(1,128)S(1)}, s32[1,4]{1,0:T(1,128)}, u32[]{:S(2)}) copy-start(s32[1,4]{1,0:T(1,128)} %refs_6_.1) | copy-start | bytes 52
  0.5 11.9 %copy-start.2 = (bf16[1,384,2048]{2,1,0:T(8,128)(2,1)S(1)}, bf16[1,384,2048]{2,1,0:T(8,128)(2,1)}, u32[]{:S(2)}) copy-start(bf16[1,384,2048]{2,1,0:T(8,128)(2,1)} %param.16) | copy-start | bytes 4718596
  0.5 11.9 %copy-start.3 = (bf16[1,384,2048]{2,1,0:T(8,128)(2,1)S(1)}, bf16[1,384,2048]{2,1,0:T(8,128)(2,1)}, u32[]{:S(2)}) copy-start(bf16[1,384,2048]{2,1,0:T(8,128)(2,1)} %param.17) | copy-start | bytes 4718596
  0.5 18.1 %copy-start = (bf16[1,768,2048]{2,1,0:T(8,128)(2,1)S(1)}, bf16[1,768,2048]{2,1,0:T(8,128)(2,1)}, u32[]{:S(2)}) copy-start(bf16[1,768,2048]{2,1,0:T(8,128)(2,1)} %param.14) | copy-start | bytes 9437188
  0.5 18.1 %copy-start.1 = (bf16[1,768,2048]{2,1,0:T(8,128)(2,1)S(1)}, bf16[1,768,2048]{2,1,0:T(8,128)(2,1)}, u32[]{:S(2)}) copy-start(bf16[1,768,2048]{2,1,0:T(8,128)(2,1)} %param.15) | copy-start | bytes 9437188
  0.5 18.1 %collective-permute-start.5 = (bf16[768,2048]{1,0:T(8,128)(2,1)}, bf16[768,2048]{1,0:T(8,128)(2,1)S(1)}, u32[]{:S(2)}, u32[]{:S(2)}) collective-permute-start(bf16[768,2048]{1,0:T(8,128)(2,1)} %bitcast.15), channel_id=1, source_target_pairs={{0,1},{1,0},{2,3},{3,2},{4,5},{5,4},{6,7},{7,6},{8,9},{9,8},{10,11... | collective-permute-start | bytes 9437192 | tf_op jit(solution)/shard_map/ppermute | solution.py:179
  1.4 5.2 %collective-permute-start.2 = (bf16[8,2176]{1,0:T(8,128)(2,1)S(1)}, bf16[8,2176]{1,0:T(8,128)(2,1)S(1)}, u32[]{:S(2)}, u32[]{:S(2)}) collective-permute-start(bf16[8,2176]{1,0:T(8,128)(2,1)S(1)} %shard_map.92.refs_0_), channel_id=1, source_target_pairs={{0,4},{1,5},{2,6},{3,7},{4,0},{5,1},{6,2},{7,3},{8,12},{9,13},{10,... | collective-permute-start | bytes 104456 | tf_op jit(solution)/shard_map/ppermute | solution.py:188
  4.0 5.6 %collective-permute-start.1 = (bf16[8,2176]{1,0:T(8,128)(2,1)S(1)}, bf16[8,2176]{1,0:T(8,128)(2,1)S(1)}, u32[]{:S(2)}, u32[]{:S(2)}) collective-permute-start(bf16[8,2176]{1,0:T(8,128)(2,1)S(1)} %shard_map.92.refs_0_), channel_id=1, source_target_pairs={{0,8},{1,9},{2,10},{3,11},{4,12},{5,13},{6,14},{7,15},{8,0},{9,1},... | collective-permute-start | bytes 104456 | tf_op jit(solution)/shard_map/ppermute | solution.py:188
  6.6 5.7 %collective-permute-start = (bf16[8,2176]{1,0:T(8,128)(2,1)S(1)}, bf16[8,2176]{1,0:T(8,128)(2,1)S(1)}, u32[]{:S(2)}, u32[]{:S(2)}) collective-permute-start(bf16[8,2176]{1,0:T(8,128)(2,1)S(1)} %shard_map.92.refs_0_), channel_id=1, source_target_pairs={{0,12},{1,13},{2,14},{3,15},{4,8},{5,9},{6,10},{7,11},{8,4},{9,5},... | collective-permute-start | bytes 104456 | tf_op jit(solution)/shard_map/ppermute | solution.py:188
  12.3 6.2 %collective-permute-start.6 = (bf16[384,2048]{1,0:T(8,128)(2,1)S(1)}, bf16[384,2048]{1,0:T(8,128)(2,1)S(1)}, u32[]{:S(2)}, u32[]{:S(2)}) collective-permute-start(bf16[384,2048]{1,0:T(8,128)(2,1)S(1)} %bitcast.18), channel_id=1, source_target_pairs={{0,1},{1,0},{2,3},{3,2},{4,5},{5,4},{6,7},{7,6},{8,9},{9,8},{10,11... | collective-permute-start | bytes 4718600 | tf_op jit(solution)/shard_map/ppermute | solution.py:179
  12.3 6.2 %collective-permute-start.7 = (bf16[384,2048]{1,0:T(8,128)(2,1)S(1)}, bf16[384,2048]{1,0:T(8,128)(2,1)S(1)}, u32[]{:S(2)}, u32[]{:S(2)}) collective-permute-start(bf16[384,2048]{1,0:T(8,128)(2,1)S(1)} %bitcast.20), channel_id=1, source_target_pairs={{0,1},{1,0},{2,3},{3,2},{4,5},{5,4},{6,7},{7,6},{8,9},{9,8},{10,11... | collective-permute-start | bytes 4718600 | tf_op jit(solution)/shard_map/ppermute | solution.py:179
  12.9 5.7 %collective-permute-start.3 = (bf16[32,2176]{1,0:T(8,128)(2,1)S(1)}, bf16[32,2176]{1,0:T(8,128)(2,1)S(1)}, u32[]{:S(2)}, u32[]{:S(2)}) collective-permute-start(bf16[32,2176]{1,0:T(8,128)(2,1)S(1)} %bitcast.23), channel_id=1, source_target_pairs={{0,2},{1,3},{2,0},{3,1},{4,6},{5,7},{6,4},{7,5},{8,10},{9,11},{10,... | collective-permute-start | bytes 417800 | tf_op jit(solution)/shard_map/ppermute | solution.py:188
  47.3 6.6 %collective-permute-start.8 = (bf16[64,2176]{1,0:T(8,128)(2,1)S(1)}, bf16[64,2176]{1,0:T(8,128)(2,1)S(1)}, u32[]{:S(2)}, u32[]{:S(2)}) collective-permute-start(bf16[64,2176]{1,0:T(8,128)(2,1)S(1)} %shard_map.96.refs_0_), channel_id=1, source_target_pairs={{0,16},{16,0},{1,17},{17,1},{2,18},{18,2},{3,19},{19,3},{4,20},{20... | collective-permute-start | bytes 835592 | tf_op jit(solution)/shard_map/ppermute | solution.py:183
  56.0 6.4 %collective-permute-start.9 = (bf16[64,2048]{1,0:T(8,128)(2,1)S(1)}, bf16[64,2048]{1,0:T(8,128)(2,1)S(1)}, u32[]{:S(2)}, u32[]{:S(2)}) collective-permute-start(bf16[64,2048]{1,0:T(8,128)(2,1)S(1)} %get-tuple-element.34), channel_id=1, source_target_pairs={{0,16},{16,0},{1,17},{17,1},{2,18},{18,2},{3,19},{19,3},{4,20},{20... | collective-permute-start | bytes 786440 | tf_op jit(solution)/shard_map/ppermute | solution.py:183

commit v21 on v18

--- a/solution.py
+++ b/solution.py
@@ -75,13 +75,10 @@
 def pack_kernel(section, expert, tokens, gain, routes, scales, changed, out):
     width = tokens.shape[1]
     normed = normalize(tokens[...].astype(jnp.float32), gain[...])
-    out[:, :width] = normed
-    out[:, width:] = weight_table(section[...], expert[...], routes, scales, changed)
-
-
-def double_kernel(first, second, out):
-    out[0] = first[...]
-    out[1] = second[...]
+    table = weight_table(section[...], expert[...], routes, scales, changed)
+    for i in range(out.shape[0]):
+        out[i, :, :width] = normed
+        out[i, :, width:] = table
 
 
 def sum_blocks(blocks):
@@ -128,14 +125,14 @@
     return table, total
 
 
-def first_kernel(experts, step, orders, rows, across, *refs):
+def first_kernel(experts, step, rows, across, *refs):
     weights, (out, tables_out) = refs[:4], refs[4:]
     table, total = weighted_outputs(experts, step, False, [rows, across], weights, out.shape[2])
     chips, count, _ = out.shape
-    own = lax.div(lax.axis_index("expert"), 2)
-    for block, distance in enumerate(orders):
-        chip = jnp.bitwise_xor(own, distance)
-        place = lax.rem(chip, 2) * (chips // 2) + lax.div(chip, 2)
+    line = chips // 2
+    own = lax.rem(lax.div(lax.axis_index("expert"), 2), 2)
+    for block in range(chips):
+        place = (own if block < line else 1 - own) * line + block % line
         span = slice(block * count, (block + 1) * count)
         out[place] = total[span].astype(out.dtype)
         tables_out[place] = table[span]
@@ -183,21 +180,13 @@
     return lax.ppermute(value, "group", [(0, 1), (1, 0)])
 
 
-def swap_chip(value, distance):
+def gather(blocks):
     size = lax.axis_size("expert")
-    return lax.ppermute(value, "expert", [(i, i ^ 2 * distance) for i in range(size)])
-
-
-def gather(block, chips):
-    distance, orders = chips // 2, [0]
-    while distance > 1:
-        rows, width = block.shape
-        joined = ((2, rows, width), block.dtype)
-        (block,) = on_vmem(double_kernel, (block, swap_chip(block, distance)), [joined])
-        block = block.reshape(2 * rows, width)
-        orders = orders + [order ^ distance for order in orders]
-        distance = distance // 2
-    return block, swap_chip(block, 1), orders + [order ^ 1 for order in orders]
+    lines = [list(range(start, size, 4)) for start in range(4)]
+    rows = lax.all_to_all(blocks, "expert", 0, 0, axis_index_groups=lines, tiled=True)
+    rows = rows.reshape(-1, blocks.shape[-1])
+    across = lax.ppermute(rows, "expert", [(i, i ^ 2) for i in range(size)])
+    return rows, across
 
 
 def spread(blocks):
@@ -227,17 +216,17 @@
     )
     stale = stale + tuple(swap_core(part) for part in stale)
     learner = learner + tuple(swap_core(part) for part in learner)
-    (block,) = on_vmem(
+    (blocks,) = on_vmem(
         pack_kernel,
         (section, expert, tokens[0], gain, routes, route_scale, changed),
-        [((row_count, packed), jnp.bfloat16)],
+        [((chips // 2, row_count, packed), jnp.bfloat16)],
     )
     state = tokens[0]
     for step in range(steps_total):
         if step == 0:
-            rows, across, orders = gather(block, chips)
+            rows, across = gather(blocks)
             share, tables = run_mlp(
-                functools.partial(first_kernel, experts, step, orders),
+                functools.partial(first_kernel, experts, step),
                 [rows, across],
                 stale,
                 [
@@ -321,7 +310,7 @@
     experts = lax.axis_size("expert")
     groups = lax.axis_size("group")
     fewer = tokens.shape[1] * experts < learner_up.shape[1]
-    paired = experts & (experts - 1) == 0 and experts >= 4 and groups == 2
+    paired = experts % 4 == 0 and groups == 2
     plan = exchange_plan if fewer and paired else gather_plan
     stale = (rollout_up[0], rollout_down[0])
     learner = (learner_up[0], learner_down[0])

time: 74 us -> 74.4 us (level)
  blocking collectives: 37.1 us -> 47.6 us
  starting transfers between devices: 11.3 us -> 5.73 us
  waiting for transfers between devices: 14.6 us -> 10 us
    all_to_all x0 -> x1, blocking collectives: none -> 13 us  [gather(): lax.all_to_all(blocks, 'expert', 0, 0, axis_index_groups=lines, tiled=True)]
    ppermute x3 -> x1, starting transfers between devices: 7.09 us -> 1.52 us  [gather(): across = lax.ppermute(rows, 'expert', [(i, i ^ 2) for i in range(size)])]
    ppermute x3 -> x1, waiting for transfers between devices: 8.09 us -> 3.54 us  [gather(): across = lax.ppermute(rows, 'expert', [(i, i ^ 2) for i in range(size)])]
    all_to_all x3, blocking collectives: 37.1 us -> 34.7 us  [spread(): lax.all_to_all(blocks, 'expert', 0, 0, axis_index_groups=groups, tiled=True)]
    pallas_call x10 -> x8, Pallas kernels: 10 us -> 10 us  [on_vmem(): pl.pallas_call(body, out_shape=[jax.ShapeDtypeStruct(shape, kind) for sha...]
  transfers between devices with their start and end apart: 9 -> 7, of which waited for: 5 -> 3; matrix products, arithmetic and copies ran while one was open for 0% -> 0% of each run, Pallas kernels for 5% -> 5%
where the time goes in v21:
time: 74.4 us; the launch traced here: 74.2 us
  blocking collectives  47.6 us (64%)
  Pallas kernels  10 us (13%)
  waiting for transfers between devices  10 us (13%)
  starting transfers between devices  5.73 us (8%)
    all_to_all x3, blocking collectives, spread(): lax.all_to_all(blocks, 'expert', 0, 0, axis_index_groups=groups, tiled=True)  34.7 us
    all_to_all x1, blocking collectives, gather(): lax.all_to_all(blocks, 'expert', 0, 0, axis_index_groups=lines, tiled=True)  13 us
    pallas_call x8, Pallas kernels, on_vmem(): pl.pallas_call(body, out_shape=[jax.ShapeDtypeStruct(shape, kind) for sha...  10 us
    ppermute x2, waiting for transfers between devices, swap_group(): return lax.ppermute(value, 'group', [(0, 1), (1, 0)])  6.46 us
    ppermute x1, waiting for transfers between devices, gather(): across = lax.ppermute(rows, 'expert', [(i, i ^ 2) for i in range(size)])  3.54 us
    ppermute x2, starting transfers between devices, swap_group(): return lax.ppermute(value, 'group', [(0, 1), (1, 0)])  3.12 us
    ppermute x1, starting transfers between devices, gather(): across = lax.ppermute(rows, 'expert', [(i, i ^ 2) for i in range(size)])  1.52 us
  transfers between devices with their start and end apart: 7, of which 3 were waited for; matrix products, arithmetic and copies ran while one was open for 0% of the time, Pallas kernels for 5%

profile of v21, /device:TPU:0, one launch (start us, length us, event | category | flops | bytes accessed | tf_op | source)
XLA Modules:
  0.0 74.2 jit_solution(11466342696897405636)
XLA Ops:
  0.0 0.5 collective-permute-start.1
  0.5 0.1 collective-permute-start.2
  0.5 0.5 collective-permute-start.3
  1.0 0.1 collective-permute-start.4
  1.1 0.6 copy-done.4
  1.7 0.1 shard_map.92
  1.9 13.0 %all_to_all.20 = bf16[4,8,2176]{2,1,0:T(8,128)(2,1)S(1)} all-to-all(bf16[4,8,2176]{2,1,0:T(8,128)(2,1)S(1)} %shard_map.92), channel_id=1, replica_groups={{0,4,8,12},{1,5,9,13},{2,6,10,14},{3,7,11,15},{16,20,24,28},{17,21,25,2..., dimensions={0} | all-to-all | bytes 278528 | tf_op jit(solution)/shard_map/all_to_all | solution.py:186
  14.8 1.5 %collective-permute-start = (bf16[32,2176]{1,0:T(8,128)(2,1)S(1)}, bf16[32,2176]{1,0:T(8,128)(2,1)S(1)}, u32[]{:S(2)}, u32[]{:S(2)}) collective-permute-start(bf16[32,2176]{1,0:T(8,128)(2,1)S(1)} %bitcast.23), channel_id=1, source_target_pairs={{0,2},{1,3},{2,0},{3,1},{4,6},{5,7},{6,4},{7,5},{8,10},{9,11},{10,... | collective-permute-start | bytes 417800 | tf_op jit(solution)/shard_map/ppermute | solution.py:188
  16.4 3.5 %collective-permute-done.refs_1_ = bf16[32,2176]{1,0:T(8,128)(2,1)S(1)} collective-permute-done((bf16[32,2176]{1,0:T(8,128)(2,1)S(1)}, bf16[32,2176]{1,0:T(8,128)(2,1)S(1)}, u32[]{:S(2)}, u32[]{:S(2)}) %collective-permute-start) | collective-permute-done | bytes 139296 | tf_op jit(solution)/shard_map/ppermute | solution.py:188
  19.9 3.5 %shard_map.93 = (bf16[8,8,2048]{2,1,0:T(8,128)(2,1)S(1)}, bf16[8,8,128]{2,1,0:T(8,128)(2,1)S(1)}) custom-call(bf16[32,2176]{1,0:T(8,128)(2,1)S(1)} %bitcast.24, bf16[32,2176]{1,0:T(8,128)(2,1)S(1)} %collective-permute-done.refs_1_, bf16[768,2048]{1,0:T(8,128)(2,1)S(1)} %bitcast.13, bf16[768,2048]{1,0:T(8,128)(2,1)S(1)} %bitcast.16, ...), custom_call_target="tpu_custom_call" | custom-call | flops 3221225472 | bytes 25165824 | tf_op jit(solution)/shard_map/pallas_call | solution.py:156
  23.4 12.7 %all_to_all.21.refs_1_ = bf16[8,8,2048]{2,1,0:T(8,128)(2,1)S(1)} all-to-all(bf16[8,8,2048]{2,1,0:T(8,128)(2,1)S(1)} %get-tuple-element.17), channel_id=1, replica_groups={{0,4,8,12,2,6,10,14},{1,5,9,13,3,7,11,15},{16,20,24,28,18,22,26,30},{17..., dimensions={0} | all-to-all | bytes 524288 | tf_op jit(solution)/shard_map/all_to_all | solution.py:197
  36.1 0.2 shard_map.94
  36.3 11.0 %all_to_all.22 = bf16[8,8,2048]{2,1,0:T(8,128)(2,1)S(1)} all-to-all(bf16[8,8,2048]{2,1,0:T(8,128)(2,1)S(1)} %get-tuple-element.19), channel_id=1, replica_groups={{0,4,8,12,2,6,10,14},{1,5,9,13,3,7,11,15},{16,20,24,28,18,22,26,30},{17..., dimensions={0} | all-to-all | bytes 524288 | tf_op jit(solution)/shard_map/all_to_all | solution.py:197
  47.3 0.0 copy-start.2
  47.3 0.0 copy-start.3
  47.3 1.6 %collective-permute-start.5 = (bf16[64,2176]{1,0:T(8,128)(2,1)S(1)}, bf16[64,2176]{1,0:T(8,128)(2,1)S(1)}, u32[]{:S(2)}, u32[]{:S(2)}) collective-permute-start(bf16[64,2176]{1,0:T(8,128)(2,1)S(1)} %shard_map.95.refs_0_), channel_id=1, source_target_pairs={{0,16},{16,0},{1,17},{17,1},{2,18},{18,2},{3,19},{19,3},{4,20},{20... | collective-permute-start | bytes 835592 | tf_op jit(solution)/shard_map/ppermute | solution.py:180
  48.8 3.5 %shard_map.96 = f32[64,2048]{1,0:T(8,128)S(1)} custom-call(bf16[64,2176]{1,0:T(8,128)(2,1)S(1)} %shard_map.95.refs_0_, bf16[768,2048]{1,0:T(8,128)(2,1)S(1)} %bitcast.14, bf16[768,2048]{1,0:T(8,128)(2,1)S(1)} %bitcast.17, bf16[768,2048]{1,0:T(8,128)(2,1)S(1)} %collective-permute-done.1.refs_4_.refs_3_, ...), custom_call_target="tpu_custom_call" | custom-call | flops 3221225472 | bytes 25165824 | tf_op jit(solution)/shard_map/pallas_call | solution.py:156
  52.3 1.6 %collective-permute-done.5.refs_1_ = bf16[64,2176]{1,0:T(8,128)(2,1)S(1)} collective-permute-done((bf16[64,2176]{1,0:T(8,128)(2,1)S(1)}, bf16[64,2176]{1,0:T(8,128)(2,1)S(1)}, u32[]{:S(2)}, u32[]{:S(2)}) %collective-permute-start.5) | collective-permute-done | bytes 278560 | tf_op jit(solution)/shard_map/ppermute | solution.py:180
  53.9 2.1 %shard_map.97 = (f32[64,2048]{1,0:T(8,128)S(1)}, bf16[64,2048]{1,0:T(8,128)(2,1)S(1)}) custom-call(bf16[64,2176]{1,0:T(8,128)(2,1)S(1)} %shard_map.95.refs_0_, bf16[64,2176]{1,0:T(8,128)(2,1)S(1)} %collective-permute-done.5.refs_1_, bf16[384,2048]{1,0:T(8,128)(2,1)S(1)} %bitcast.19, bf16[384,2048]{1,0:T(8,128)(2,1)S(1)} %bitcast.21, ...), custom_call_target="tpu_custom_call" | custom-call | flops 1610612736 | bytes 12582912 | tf_op jit(solution)/shard_map/pallas_call | solution.py:156
  56.0 1.6 %collective-permute-start.6 = (bf16[64,2048]{1,0:T(8,128)(2,1)S(1)}, bf16[64,2048]{1,0:T(8,128)(2,1)S(1)}, u32[]{:S(2)}, u32[]{:S(2)}) collective-permute-start(bf16[64,2048]{1,0:T(8,128)(2,1)S(1)} %get-tuple-element.24), channel_id=1, source_target_pairs={{0,16},{16,0},{1,17},{17,1},{2,18},{18,2},{3,19},{19,3},{4,20},{20... | collective-permute-start | bytes 786440 | tf_op jit(solution)/shard_map/ppermute | solution.py:180
  57.6 4.9 %collective-permute-done.6 = bf16[64,2048]{1,0:T(8,128)(2,1)S(1)} collective-permute-done((bf16[64,2048]{1,0:T(8,128)(2,1)S(1)}, bf16[64,2048]{1,0:T(8,128)(2,1)S(1)}, u32[]{:S(2)}, u32[]{:S(2)}) %collective-permute-start.6) | collective-permute-done | bytes 262176 | tf_op jit(solution)/shard_map/ppermute | solution.py:180
  62.4 0.1 fusion
  62.5 11.0 %all_to_all.23.refs_1_ = bf16[8,8,2048]{2,1,0:T(8,128)(2,1)S(1)} all-to-all(bf16[8,8,2048]{2,1,0:T(8,128)(2,1)S(1)} %fusion), channel_id=1, replica_groups={{0,4,8,12,2,6,10,14},{1,5,9,13,3,7,11,15},{16,20,24,28,18,22,26,30},{17..., dimensions={0} | all-to-all | bytes 524288 | tf_op jit(solution)/shard_map/all_to_all | solution.py:197
  73.5 0.7 shard_map.98
  (21 shorter events, 0.1 us)
Async XLA Ops:
  0.0 19.9 %collective-permute-start.1 = (bf16[768,2048]{1,0:T(8,128)(2,1)}, bf16[768,2048]{1,0:T(8,128)(2,1)S(1)}, u32[]{:S(2)}, u32[]{:S(2)}) collective-permute-start(bf16[768,2048]{1,0:T(8,128)(2,1)} %bitcast.12), channel_id=1, source_target_pairs={{0,1},{1,0},{2,3},{3,2},{4,5},{5,4},{6,7},{7,6},{8,9},{9,8},{10,11... | collective-permute-start | bytes 9437192 | tf_op jit(solution)/shard_map/ppermute | solution.py:176
  0.5 19.5 %collective-permute-start.2 = (bf16[768,2048]{1,0:T(8,128)(2,1)}, bf16[768,2048]{1,0:T(8,128)(2,1)S(1)}, u32[]{:S(2)}, u32[]{:S(2)}) collective-permute-start(bf16[768,2048]{1,0:T(8,128)(2,1)} %bitcast.15), channel_id=1, source_target_pairs={{0,1},{1,0},{2,3},{3,2},{4,5},{5,4},{6,7},{7,6},{8,9},{9,8},{10,11... | collective-permute-start | bytes 9437192 | tf_op jit(solution)/shard_map/ppermute | solution.py:176
  0.5 19.4 %collective-permute-start.3 = (bf16[384,2048]{1,0:T(8,128)(2,1)}, bf16[384,2048]{1,0:T(8,128)(2,1)S(1)}, u32[]{:S(2)}, u32[]{:S(2)}) collective-permute-start(bf16[384,2048]{1,0:T(8,128)(2,1)} %bitcast.18), channel_id=1, source_target_pairs={{0,1},{1,0},{2,3},{3,2},{4,5},{5,4},{6,7},{7,6},{8,9},{9,8},{10,11... | collective-permute-start | bytes 4718600 | tf_op jit(solution)/shard_map/ppermute | solution.py:176
  1.0 0.8 %copy-start.4 = (bf16[1,8,2048]{2,1,0:T(8,128)(2,1)S(1)}, bf16[1,8,2048]{2,1,0:T(8,128)(2,1)}, u32[]{:S(2)}) copy-start(bf16[1,8,2048]{2,1,0:T(8,128)(2,1)} %param.9) | copy-start | bytes 98308
  1.0 0.8 %copy-start.5 = (f32[2048]{0:T(1024)S(1)}, f32[2048]{0:T(1024)}, u32[]{:S(2)}) copy-start(f32[2048]{0:T(1024)} %param.10) | copy-start | bytes 24580
  1.0 0.8 %copy-start.6 = (s32[2,1,8,8]{3,2,1,0:T(8,128)S(1)}, s32[2,1,8,8]{3,2,1,0:T(8,128)}, u32[]{:S(2)}) copy-start(s32[2,1,8,8]{3,2,1,0:T(8,128)} %refs_4_.1) | copy-start | bytes 1540
  1.0 0.8 %copy-start.7 = (f32[2,1,8,8]{3,2,1,0:T(8,128)S(1)}, f32[2,1,8,8]{3,2,1,0:T(8,128)}, u32[]{:S(2)}) copy-start(f32[2,1,8,8]{3,2,1,0:T(8,128)} %refs_5_.1) | copy-start | bytes 1540
  1.0 0.8 %copy-start.8 = (s32[1,4]{1,0:T(1,128)S(1)}, s32[1,4]{1,0:T(1,128)}, u32[]{:S(2)}) copy-start(s32[1,4]{1,0:T(1,128)} %refs_6_.1) | copy-start | bytes 52
  1.0 18.9 %copy-start = (bf16[1,768,2048]{2,1,0:T(8,128)(2,1)S(1)}, bf16[1,768,2048]{2,1,0:T(8,128)(2,1)}, u32[]{:S(2)}) copy-start(bf16[1,768,2048]{2,1,0:T(8,128)(2,1)} %param.14) | copy-start | bytes 9437188
  1.0 18.9 %copy-start.1 = (bf16[1,768,2048]{2,1,0:T(8,128)(2,1)S(1)}, bf16[1,768,2048]{2,1,0:T(8,128)(2,1)}, u32[]{:S(2)}) copy-start(bf16[1,768,2048]{2,1,0:T(8,128)(2,1)} %param.15) | copy-start | bytes 9437188
  1.0 18.9 %collective-permute-start.4 = (bf16[384,2048]{1,0:T(8,128)(2,1)}, bf16[384,2048]{1,0:T(8,128)(2,1)S(1)}, u32[]{:S(2)}, u32[]{:S(2)}) collective-permute-start(bf16[384,2048]{1,0:T(8,128)(2,1)} %bitcast.20), channel_id=1, source_target_pairs={{0,1},{1,0},{2,3},{3,2},{4,5},{5,4},{6,7},{7,6},{8,9},{9,8},{10,11... | collective-permute-start | bytes 4718600 | tf_op jit(solution)/shard_map/ppermute | solution.py:176
  14.8 5.1 %collective-permute-start = (bf16[32,2176]{1,0:T(8,128)(2,1)S(1)}, bf16[32,2176]{1,0:T(8,128)(2,1)S(1)}, u32[]{:S(2)}, u32[]{:S(2)}) collective-permute-start(bf16[32,2176]{1,0:T(8,128)(2,1)S(1)} %bitcast.23), channel_id=1, source_target_pairs={{0,2},{1,3},{2,0},{3,1},{4,6},{5,7},{6,4},{7,5},{8,10},{9,11},{10,... | collective-permute-start | bytes 417800 | tf_op jit(solution)/shard_map/ppermute | solution.py:188
  47.3 6.6 %copy-start.2 = (bf16[1,384,2048]{2,1,0:T(8,128)(2,1)S(1)}, bf16[1,384,2048]{2,1,0:T(8,128)(2,1)}, u32[]{:S(2)}) copy-start(bf16[1,384,2048]{2,1,0:T(8,128)(2,1)} %param.16) | copy-start | bytes 4718596
  47.3 6.6 %copy-start.3 = (bf16[1,384,2048]{2,1,0:T(8,128)(2,1)S(1)}, bf16[1,384,2048]{2,1,0:T(8,128)(2,1)}, u32[]{:S(2)}) copy-start(bf16[1,384,2048]{2,1,0:T(8,128)(2,1)} %param.17) | copy-start | bytes 4718596
  47.3 6.6 %collective-permute-start.5 = (bf16[64,2176]{1,0:T(8,128)(2,1)S(1)}, bf16[64,2176]{1,0:T(8,128)(2,1)S(1)}, u32[]{:S(2)}, u32[]{:S(2)}) collective-permute-start(bf16[64,2176]{1,0:T(8,128)(2,1)S(1)} %shard_map.95.refs_0_), channel_id=1, source_target_pairs={{0,16},{16,0},{1,17},{17,1},{2,18},{18,2},{3,19},{19,3},{4,20},{20... | collective-permute-start | bytes 835592 | tf_op jit(solution)/shard_map/ppermute | solution.py:180
  56.0 6.4 %collective-permute-start.6 = (bf16[64,2048]{1,0:T(8,128)(2,1)S(1)}, bf16[64,2048]{1,0:T(8,128)(2,1)S(1)}, u32[]{:S(2)}, u32[]{:S(2)}) collective-permute-start(bf16[64,2048]{1,0:T(8,128)(2,1)S(1)} %get-tuple-element.24), channel_id=1, source_target_pairs={{0,16},{16,0},{1,17},{17,1},{2,18},{18,2},{3,19},{19,3},{4,20},{20... | collective-permute-start | bytes 786440 | tf_op jit(solution)/shard_map/ppermute | solution.py:180

commit v22 on v20

--- a/solution.py
+++ b/solution.py
@@ -243,7 +243,6 @@
                     ((chips, row_count, width), jnp.bfloat16),
                     ((chips, row_count, packed - width), jnp.bfloat16),
                 ],
-                learner[2:],
             )
             tables = tables.reshape(half, packed - width)
         else:

time: 75.2 us -> 70.9 us (0.943)
  waiting for transfers between devices: 16.3 us -> 13.7 us
  blocking collectives: 36.8 us -> 35.1 us
    ppermute x4, waiting for transfers between devices: 9.86 us -> 7.21 us  [swap_chip(): lax.ppermute(value, 'expert', [(i, i ^ 2 * distance) for i in range(size)])]
    all_to_all x3, blocking collectives: 36.8 us -> 35.1 us  [spread(): lax.all_to_all(blocks, 'expert', 0, 0, axis_index_groups=groups, tiled=True)]
  transfers between devices with their start and end apart: 10 -> 10, of which waited for: 5 -> 5; matrix products, arithmetic and copies ran while one was open for 0% -> 0% of each run, Pallas kernels for 5% -> 10%
where the time goes in v22:
time: 70.9 us; the launch traced here: 70.7 us
  blocking collectives  35.1 us (50%)
  waiting for transfers between devices  13.7 us (19%)
  starting transfers between devices  11.1 us (16%)
  Pallas kernels  10 us (14%)
    all_to_all x3, blocking collectives, spread(): lax.all_to_all(blocks, 'expert', 0, 0, axis_index_groups=groups, tiled=True)  35.1 us
    pallas_call x9, Pallas kernels, on_vmem(): pl.pallas_call(body, out_shape=[jax.ShapeDtypeStruct(shape, kind) for sha...  10 us
    ppermute x4, waiting for transfers between devices, swap_chip(): lax.ppermute(value, 'expert', [(i, i ^ 2 * distance) for i in range(size)])  7.21 us
    ppermute x4, starting transfers between devices, swap_chip(): lax.ppermute(value, 'expert', [(i, i ^ 2 * distance) for i in range(size)])  6.89 us
    ppermute x2, waiting for transfers between devices, swap_group(): return lax.ppermute(value, 'group', [(0, 1), (1, 0)])  6.45 us
    ppermute x2, starting transfers between devices, swap_group(): return lax.ppermute(value, 'group', [(0, 1), (1, 0)])  3.13 us
  transfers between devices with their start and end apart: 10, of which 5 were waited for; matrix products, arithmetic and copies ran while one was open for 0% of the time, Pallas kernels for 10%

profile of v22, /device:TPU:0, one launch (start us, length us, event | category | flops | bytes accessed | tf_op | source)
XLA Modules:
  0.0 70.7 jit_solution(8374257190711725129)
XLA Ops:
  0.0 0.5 collective-permute-start.4
  0.5 0.1 collective-permute-start.5
  0.6 0.6 copy-done.4
  1.2 0.1 shard_map.92.refs_0_
  1.4 4.7 %collective-permute-start = (bf16[8,2176]{1,0:T(8,128)(2,1)S(1)}, bf16[8,2176]{1,0:T(8,128)(2,1)S(1)}, u32[]{:S(2)}, u32[]{:S(2)}) collective-permute-start(bf16[8,2176]{1,0:T(8,128)(2,1)S(1)} %shard_map.92.refs_0_), channel_id=1, source_target_pairs={{0,12},{1,13},{2,14},{3,15},{4,8},{5,9},{6,10},{7,11},{8,4},{9,5},... | collective-permute-start | bytes 104456 | tf_op jit(solution)/shard_map/ppermute | solution.py:188
  6.0 0.6 collective-permute-start.2
  6.7 1.5 %collective-permute-done.refs_1_ = bf16[8,2176]{1,0:T(8,128)(2,1)S(1)} collective-permute-done((bf16[8,2176]{1,0:T(8,128)(2,1)S(1)}, bf16[8,2176]{1,0:T(8,128)(2,1)S(1)}, u32[]{:S(2)}, u32[]{:S(2)}) %collective-permute-start) | collective-permute-done | bytes 34848 | tf_op jit(solution)/shard_map/ppermute | solution.py:188
  8.1 2.7 %collective-permute-done.1.refs_2_ = bf16[8,2176]{1,0:T(8,128)(2,1)S(1)} collective-permute-done((bf16[8,2176]{1,0:T(8,128)(2,1)S(1)}, bf16[8,2176]{1,0:T(8,128)(2,1)S(1)}, u32[]{:S(2)}, u32[]{:S(2)}) %collective-permute-start.1) | collective-permute-done | bytes 34848 | tf_op jit(solution)/shard_map/ppermute | solution.py:188
  10.9 1.6 %collective-permute-start.3 = (bf16[32,2176]{1,0:T(8,128)(2,1)S(1)}, bf16[32,2176]{1,0:T(8,128)(2,1)S(1)}, u32[]{:S(2)}, u32[]{:S(2)}) collective-permute-start(bf16[32,2176]{1,0:T(8,128)(2,1)S(1)} %bitcast.23), channel_id=1, source_target_pairs={{0,2},{1,3},{2,0},{3,1},{4,6},{5,7},{6,4},{7,5},{8,10},{9,11},{10,... | collective-permute-start | bytes 417800 | tf_op jit(solution)/shard_map/ppermute | solution.py:188
  12.5 0.5 collective-permute-start.8
  13.0 3.0 %collective-permute-done.3.refs_1_ = bf16[32,2176]{1,0:T(8,128)(2,1)S(1)} collective-permute-done((bf16[32,2176]{1,0:T(8,128)(2,1)S(1)}, bf16[32,2176]{1,0:T(8,128)(2,1)S(1)}, u32[]{:S(2)}, u32[]{:S(2)}) %collective-permute-start.3) | collective-permute-done | bytes 139296 | tf_op jit(solution)/shard_map/ppermute | solution.py:188
  16.0 3.5 %shard_map.94 = (bf16[8,8,2048]{2,1,0:T(8,128)(2,1)S(1)}, bf16[8,8,128]{2,1,0:T(8,128)(2,1)S(1)}) custom-call(bf16[32,2176]{1,0:T(8,128)(2,1)S(1)} %bitcast.24, bf16[32,2176]{1,0:T(8,128)(2,1)S(1)} %collective-permute-done.3.refs_1_, bf16[768,2048]{1,0:T(8,128)(2,1)S(1)} %bitcast.13, bf16[768,2048]{1,0:T(8,128)(2,1)S(1)} %bitcast.16, ...), custom_call_target="tpu_custom_call" | custom-call | flops 3221225472 | bytes 25165824 | tf_op jit(solution)/shard_map/pallas_call | solution.py:159
  19.5 13.1 %all_to_all.15.refs_1_ = bf16[8,8,2048]{2,1,0:T(8,128)(2,1)S(1)} all-to-all(bf16[8,8,2048]{2,1,0:T(8,128)(2,1)S(1)} %get-tuple-element.25), channel_id=1, replica_groups={{0,4,8,12,2,6,10,14},{1,5,9,13,3,7,11,15},{16,20,24,28,18,22,26,30},{17..., dimensions={0} | all-to-all | bytes 524288 | tf_op jit(solution)/shard_map/all_to_all | solution.py:207
  32.6 0.2 shard_map.95
  32.8 11.0 %all_to_all.16 = bf16[8,8,2048]{2,1,0:T(8,128)(2,1)S(1)} all-to-all(bf16[8,8,2048]{2,1,0:T(8,128)(2,1)S(1)} %get-tuple-element.27), channel_id=1, replica_groups={{0,4,8,12,2,6,10,14},{1,5,9,13,3,7,11,15},{16,20,24,28,18,22,26,30},{17..., dimensions={0} | all-to-all | bytes 524288 | tf_op jit(solution)/shard_map/all_to_all | solution.py:207
  43.8 1.6 %collective-permute-start.6 = (bf16[64,2176]{1,0:T(8,128)(2,1)S(1)}, bf16[64,2176]{1,0:T(8,128)(2,1)S(1)}, u32[]{:S(2)}, u32[]{:S(2)}) collective-permute-start(bf16[64,2176]{1,0:T(8,128)(2,1)S(1)} %shard_map.96.refs_0_), channel_id=1, source_target_pairs={{0,16},{16,0},{1,17},{17,1},{2,18},{18,2},{3,19},{19,3},{4,20},{20... | collective-permute-start | bytes 835592 | tf_op jit(solution)/shard_map/ppermute | solution.py:183
  45.4 3.5 %shard_map.97 = f32[64,2048]{1,0:T(8,128)S(1)} custom-call(bf16[64,2176]{1,0:T(8,128)(2,1)S(1)} %shard_map.96.refs_0_, bf16[768,2048]{1,0:T(8,128)(2,1)S(1)} %bitcast.14, bf16[768,2048]{1,0:T(8,128)(2,1)S(1)} %bitcast.17, bf16[768,2048]{1,0:T(8,128)(2,1)S(1)} %collective-permute-done.4.refs_4_.refs_3_, ...), custom_call_target="tpu_custom_call" | custom-call | flops 3221225472 | bytes 25165824 | tf_op jit(solution)/shard_map/pallas_call | solution.py:159
  48.8 1.6 %collective-permute-done.6.refs_1_ = bf16[64,2176]{1,0:T(8,128)(2,1)S(1)} collective-permute-done((bf16[64,2176]{1,0:T(8,128)(2,1)S(1)}, bf16[64,2176]{1,0:T(8,128)(2,1)S(1)}, u32[]{:S(2)}, u32[]{:S(2)}) %collective-permute-start.6) | collective-permute-done | bytes 278560 | tf_op jit(solution)/shard_map/ppermute | solution.py:183
  50.4 2.1 %shard_map.98 = (f32[64,2048]{1,0:T(8,128)S(1)}, bf16[64,2048]{1,0:T(8,128)(2,1)S(1)}) custom-call(bf16[64,2176]{1,0:T(8,128)(2,1)S(1)} %shard_map.96.refs_0_, bf16[64,2176]{1,0:T(8,128)(2,1)S(1)} %collective-permute-done.6.refs_1_, bf16[384,2048]{1,0:T(8,128)(2,1)S(1)} %bitcast.19, bf16[384,2048]{1,0:T(8,128)(2,1)S(1)} %bitcast.21, ...), custom_call_target="tpu_custom_call" | custom-call | flops 1610612736 | bytes 12582912 | tf_op jit(solution)/shard_map/pallas_call | solution.py:159
  52.5 1.6 %collective-permute-start.9 = (bf16[64,2048]{1,0:T(8,128)(2,1)S(1)}, bf16[64,2048]{1,0:T(8,128)(2,1)S(1)}, u32[]{:S(2)}, u32[]{:S(2)}) collective-permute-start(bf16[64,2048]{1,0:T(8,128)(2,1)S(1)} %get-tuple-element.34), channel_id=1, source_target_pairs={{0,16},{16,0},{1,17},{17,1},{2,18},{18,2},{3,19},{19,3},{4,20},{20... | collective-permute-start | bytes 786440 | tf_op jit(solution)/shard_map/ppermute | solution.py:183
  54.1 4.9 %collective-permute-done.9 = bf16[64,2048]{1,0:T(8,128)(2,1)S(1)} collective-permute-done((bf16[64,2048]{1,0:T(8,128)(2,1)S(1)}, bf16[64,2048]{1,0:T(8,128)(2,1)S(1)}, u32[]{:S(2)}, u32[]{:S(2)}) %collective-permute-start.9) | collective-permute-done | bytes 262176 | tf_op jit(solution)/shard_map/ppermute | solution.py:183
  59.0 0.1 fusion
  59.0 11.0 %all_to_all.17.refs_1_ = bf16[8,8,2048]{2,1,0:T(8,128)(2,1)S(1)} all-to-all(bf16[8,8,2048]{2,1,0:T(8,128)(2,1)S(1)} %fusion), channel_id=1, replica_groups={{0,4,8,12,2,6,10,14},{1,5,9,13,3,7,11,15},{16,20,24,28,18,22,26,30},{17..., dimensions={0} | all-to-all | bytes 524288 | tf_op jit(solution)/shard_map/all_to_all | solution.py:207
  70.0 0.7 shard_map.99
  (27 shorter events, 0.1 us)
Async XLA Ops:
  0.0 16.0 %collective-permute-start.4 = (bf16[768,2048]{1,0:T(8,128)(2,1)}, bf16[768,2048]{1,0:T(8,128)(2,1)S(1)}, u32[]{:S(2)}, u32[]{:S(2)}) collective-permute-start(bf16[768,2048]{1,0:T(8,128)(2,1)} %bitcast.12), channel_id=1, source_target_pairs={{0,1},{1,0},{2,3},{3,2},{4,5},{5,4},{6,7},{7,6},{8,9},{9,8},{10,11... | collective-permute-start | bytes 9437192 | tf_op jit(solution)/shard_map/ppermute | solution.py:179
  0.5 0.8 %copy-start.4 = (bf16[1,8,2048]{2,1,0:T(8,128)(2,1)S(1)}, bf16[1,8,2048]{2,1,0:T(8,128)(2,1)}, u32[]{:S(2)}) copy-start(bf16[1,8,2048]{2,1,0:T(8,128)(2,1)} %param.9) | copy-start | bytes 98308
  0.5 0.8 %copy-start.5 = (f32[2048]{0:T(1024)S(1)}, f32[2048]{0:T(1024)}, u32[]{:S(2)}) copy-start(f32[2048]{0:T(1024)} %param.10) | copy-start | bytes 24580
  0.5 0.8 %copy-start.6 = (s32[2,1,8,8]{3,2,1,0:T(8,128)S(1)}, s32[2,1,8,8]{3,2,1,0:T(8,128)}, u32[]{:S(2)}) copy-start(s32[2,1,8,8]{3,2,1,0:T(8,128)} %refs_4_.1) | copy-start | bytes 1540
  0.5 0.8 %copy-start.7 = (f32[2,1,8,8]{3,2,1,0:T(8,128)S(1)}, f32[2,1,8,8]{3,2,1,0:T(8,128)}, u32[]{:S(2)}) copy-start(f32[2,1,8,8]{3,2,1,0:T(8,128)} %refs_5_.1) | copy-start | bytes 1540
  0.5 0.8 %copy-start.8 = (s32[1,4]{1,0:T(1,128)S(1)}, s32[1,4]{1,0:T(1,128)}, u32[]{:S(2)}) copy-start(s32[1,4]{1,0:T(1,128)} %refs_6_.1) | copy-start | bytes 52
  0.5 12.0 %copy-start.2 = (bf16[1,384,2048]{2,1,0:T(8,128)(2,1)S(1)}, bf16[1,384,2048]{2,1,0:T(8,128)(2,1)}, u32[]{:S(2)}) copy-start(bf16[1,384,2048]{2,1,0:T(8,128)(2,1)} %param.16) | copy-start | bytes 4718596
  0.5 12.0 %copy-start.3 = (bf16[1,384,2048]{2,1,0:T(8,128)(2,1)S(1)}, bf16[1,384,2048]{2,1,0:T(8,128)(2,1)}, u32[]{:S(2)}) copy-start(bf16[1,384,2048]{2,1,0:T(8,128)(2,1)} %param.17) | copy-start | bytes 4718596
  0.5 15.5 %copy-start = (bf16[1,768,2048]{2,1,0:T(8,128)(2,1)S(1)}, bf16[1,768,2048]{2,1,0:T(8,128)(2,1)}, u32[]{:S(2)}) copy-start(bf16[1,768,2048]{2,1,0:T(8,128)(2,1)} %param.14) | copy-start | bytes 9437188
  0.5 15.5 %copy-start.1 = (bf16[1,768,2048]{2,1,0:T(8,128)(2,1)S(1)}, bf16[1,768,2048]{2,1,0:T(8,128)(2,1)}, u32[]{:S(2)}) copy-start(bf16[1,768,2048]{2,1,0:T(8,128)(2,1)} %param.15) | copy-start | bytes 9437188
  0.5 15.5 %collective-permute-start.5 = (bf16[768,2048]{1,0:T(8,128)(2,1)}, bf16[768,2048]{1,0:T(8,128)(2,1)S(1)}, u32[]{:S(2)}, u32[]{:S(2)}) collective-permute-start(bf16[768,2048]{1,0:T(8,128)(2,1)} %bitcast.15), channel_id=1, source_target_pairs={{0,1},{1,0},{2,3},{3,2},{4,5},{5,4},{6,7},{7,6},{8,9},{9,8},{10,11... | collective-permute-start | bytes 9437192 | tf_op jit(solution)/shard_map/ppermute | solution.py:179
  1.4 6.8 %collective-permute-start = (bf16[8,2176]{1,0:T(8,128)(2,1)S(1)}, bf16[8,2176]{1,0:T(8,128)(2,1)S(1)}, u32[]{:S(2)}, u32[]{:S(2)}) collective-permute-start(bf16[8,2176]{1,0:T(8,128)(2,1)S(1)} %shard_map.92.refs_0_), channel_id=1, source_target_pairs={{0,12},{1,13},{2,14},{3,15},{4,8},{5,9},{6,10},{7,11},{8,4},{9,5},... | collective-permute-start | bytes 104456 | tf_op jit(solution)/shard_map/ppermute | solution.py:188
  6.0 4.8 %collective-permute-start.1 = (bf16[8,2176]{1,0:T(8,128)(2,1)S(1)}, bf16[8,2176]{1,0:T(8,128)(2,1)S(1)}, u32[]{:S(2)}, u32[]{:S(2)}) collective-permute-start(bf16[8,2176]{1,0:T(8,128)(2,1)S(1)} %shard_map.92.refs_0_), channel_id=1, source_target_pairs={{0,8},{1,9},{2,10},{3,11},{4,12},{5,13},{6,14},{7,15},{8,0},{9,1},... | collective-permute-start | bytes 104456 | tf_op jit(solution)/shard_map/ppermute | solution.py:188
  6.0 4.8 %collective-permute-start.2 = (bf16[8,2176]{1,0:T(8,128)(2,1)S(1)}, bf16[8,2176]{1,0:T(8,128)(2,1)S(1)}, u32[]{:S(2)}, u32[]{:S(2)}) collective-permute-start(bf16[8,2176]{1,0:T(8,128)(2,1)S(1)} %shard_map.92.refs_0_), channel_id=1, source_target_pairs={{0,4},{1,5},{2,6},{3,7},{4,0},{5,1},{6,2},{7,3},{8,12},{9,13},{10,... | collective-permute-start | bytes 104456 | tf_op jit(solution)/shard_map/ppermute | solution.py:188
  10.9 5.1 %collective-permute-start.3 = (bf16[32,2176]{1,0:T(8,128)(2,1)S(1)}, bf16[32,2176]{1,0:T(8,128)(2,1)S(1)}, u32[]{:S(2)}, u32[]{:S(2)}) collective-permute-start(bf16[32,2176]{1,0:T(8,128)(2,1)S(1)} %bitcast.23), channel_id=1, source_target_pairs={{0,2},{1,3},{2,0},{3,1},{4,6},{5,7},{6,4},{7,5},{8,10},{9,11},{10,... | collective-permute-start | bytes 417800 | tf_op jit(solution)/shard_map/ppermute | solution.py:188
  12.5 37.9 %collective-permute-start.7 = (bf16[384,2048]{1,0:T(8,128)(2,1)S(1)}, bf16[384,2048]{1,0:T(8,128)(2,1)S(1)}, u32[]{:S(2)}, u32[]{:S(2)}) collective-permute-start(bf16[384,2048]{1,0:T(8,128)(2,1)S(1)} %bitcast.18), channel_id=1, source_target_pairs={{0,1},{1,0},{2,3},{3,2},{4,5},{5,4},{6,7},{7,6},{8,9},{9,8},{10,11... | collective-permute-start | bytes 4718600 | tf_op jit(solution)/shard_map/ppermute | solution.py:179
  12.5 37.9 %collective-permute-start.8 = (bf16[384,2048]{1,0:T(8,128)(2,1)S(1)}, bf16[384,2048]{1,0:T(8,128)(2,1)S(1)}, u32[]{:S(2)}, u32[]{:S(2)}) collective-permute-start(bf16[384,2048]{1,0:T(8,128)(2,1)S(1)} %bitcast.20), channel_id=1, source_target_pairs={{0,1},{1,0},{2,3},{3,2},{4,5},{5,4},{6,7},{7,6},{8,9},{9,8},{10,11... | collective-permute-start | bytes 4718600 | tf_op jit(solution)/shard_map/ppermute | solution.py:179
  43.8 6.6 %collective-permute-start.6 = (bf16[64,2176]{1,0:T(8,128)(2,1)S(1)}, bf16[64,2176]{1,0:T(8,128)(2,1)S(1)}, u32[]{:S(2)}, u32[]{:S(2)}) collective-permute-start(bf16[64,2176]{1,0:T(8,128)(2,1)S(1)} %shard_map.96.refs_0_), channel_id=1, source_target_pairs={{0,16},{16,0},{1,17},{17,1},{2,18},{18,2},{3,19},{19,3},{4,20},{20... | collective-permute-start | bytes 835592 | tf_op jit(solution)/shard_map/ppermute | solution.py:183
  52.5 6.4 %collective-permute-start.9 = (bf16[64,2048]{1,0:T(8,128)(2,1)S(1)}, bf16[64,2048]{1,0:T(8,128)(2,1)S(1)}, u32[]{:S(2)}, u32[]{:S(2)}) collective-permute-start(bf16[64,2048]{1,0:T(8,128)(2,1)S(1)} %get-tuple-element.34), channel_id=1, source_target_pairs={{0,16},{16,0},{1,17},{17,1},{2,18},{18,2},{3,19},{19,3},{4,20},{20... | collective-permute-start | bytes 786440 | tf_op jit(solution)/shard_map/ppermute | solution.py:183

commit v23 on v22

--- a/solution.py
+++ b/solution.py
@@ -91,22 +91,27 @@
     return total
 
 
-def next_kernel(previous, returned, gain, state_out, out):
+def next_kernel(previous, returned, gain, block, state_out, out):
+    width = previous.shape[1]
     state = previous[...].astype(jnp.float32) + sum_blocks(returned)
     state_out[...] = state
-    normed = normalize(state, gain[...])
-    for chip in range(out.shape[0]):
-        out[chip] = normed
-
-
-def last_kernel(previous, returned, out):
-    out[...] = (previous[...] + sum_blocks(returned)).astype(jnp.bfloat16)
-
-
-def join_kernel(rows, tables, out):
-    width = rows.shape[1]
-    out[:, :width] = rows[...]
-    out[:, width:] = tables[...]
+    out[:, :width] = normalize(state, gain[...])
+    out[:, width:] = block[:, width:]
+
+
+def part_kernel(kept, received, away, own_out, *sent_outs):
+    total = kept[...] + received[...].astype(jnp.float32) + away[...].astype(jnp.float32)
+    count = own_out.shape[0]
+    own_out[...] = total[:count]
+    for i, sent in enumerate(sent_outs):
+        sent[...] = total[(i + 1) * count : (i + 2) * count].astype(sent.dtype)
+
+
+def last_kernel(previous, own, *refs):
+    total = own[...]
+    for received in refs[:-1]:
+        total = total + received[...].astype(jnp.float32)
+    refs[-1][...] = (previous[...] + total).astype(jnp.bfloat16)
 
 
 def weighted_outputs(experts, step, fresh, sources, weights, width):
@@ -125,12 +130,12 @@
         result = jnp.dot(hidden, down[...], preferred_element_type=jnp.float32)
         result = result[: rows.shape[0]] * row_weights(experts, table, owner, step, fresh)
         total = result if total is None else total + result
-    return table, total
+    return total
 
 
 def first_kernel(experts, step, orders, rows, across, *refs):
-    weights, (out, tables_out) = refs[:4], refs[4:]
-    table, total = weighted_outputs(experts, step, False, [rows, across], weights, out.shape[2])
+    weights, out = refs[:4], refs[4]
+    total = weighted_outputs(experts, step, False, [rows, across], weights, out.shape[2])
     chips, count, _ = out.shape
     own = lax.div(lax.axis_index("expert"), 2)
     for block, distance in enumerate(orders):
@@ -138,15 +143,20 @@
         place = lax.rem(chip, 2) * (chips // 2) + lax.div(chip, 2)
         span = slice(block * count, (block + 1) * count)
         out[place] = total[span].astype(out.dtype)
-        tables_out[place] = table[span]
-
-
-def mlp_kernel(experts, step, fresh, set_count, *refs):
-    sources, weights, outs = refs[:set_count], refs[set_count:][:4], refs[set_count + 4 :]
-    count, width = outs[0].shape
-    _, total = weighted_outputs(experts, step, fresh, sources, weights, width)
-    for i, out in enumerate(outs):
-        out[...] = total[i * count : (i + 1) * count].astype(out.dtype)
+
+
+def mlp_kernel(experts, step, fresh, set_count, before, *refs):
+    sources, weights, refs = refs[:set_count], refs[set_count : set_count + 4], refs[set_count + 4 :]
+    earlier, outs = refs[:before], refs[before:]
+    total = weighted_outputs(experts, step, fresh, sources, weights, outs[0].shape[1])
+    start = 0
+    for out in outs:
+        end = start + out.shape[0]
+        part = total[start:end]
+        if before and end <= earlier[0].shape[0]:
+            part = part + earlier[0][start:end]
+        out[...] = part.astype(out.dtype)
+        start = end
 
 
 def on_vmem(kernel, inputs, outputs, limit=4 * MIB, cost=None, after=()):
@@ -235,36 +245,43 @@
         if step == 0:
             rows, across, orders, learner = gather(block, chips, learner)
             learner = learner + tuple(swap_core(part) for part in learner)
-            share, tables = run_mlp(
+        else:
+            state, block = on_vmem(
+                next_kernel,
+                (state, returned, gain, block),
+                [state_shape, ((row_count, packed), jnp.bfloat16)],
+            )
+            rows, across, orders, _ = gather(block, chips, ())
+        if step == 0:
+            (share,) = run_mlp(
                 functools.partial(first_kernel, experts, step, orders),
                 [rows, across],
                 stale,
-                [
-                    ((chips, row_count, width), jnp.bfloat16),
-                    ((chips, row_count, packed - width), jnp.bfloat16),
-                ],
+                [((chips, row_count, width), jnp.bfloat16)],
             )
-            tables = tables.reshape(half, packed - width)
-        else:
-            state, blocks = on_vmem(
-                next_kernel,
-                (state, returned, gain),
-                [state_shape, ((chips, row_count, width), jnp.bfloat16)],
-            )
-            rows = spread(blocks).reshape(half, width)
-            (rows,) = on_vmem(join_kernel, (rows, tables), [((half, packed), jnp.bfloat16)])
-            other = swap_group(rows)
-            kept = ((half, width), jnp.float32)
-            kernel = functools.partial(mlp_kernel, experts, step, False, 1)
-            (old,) = run_mlp(kernel, [rows], stale, [kept])
-            other, old = lax.optimization_barrier((other, old))
-            kernel = functools.partial(mlp_kernel, experts, step, True, 2)
-            sent = ((half, width), jnp.bfloat16)
-            new, away = run_mlp(kernel, [rows, other], learner, [kept, sent])
-            share = old + new + swap_group(away).astype(jnp.float32)
-            share = share.astype(jnp.bfloat16).reshape(chips, row_count, width)
-        returned = spread(share)
-    (updated,) = on_vmem(last_kernel, (state, returned), [((row_count, width), jnp.bfloat16)])
+            returned = spread(share)
+            continue
+        other, other_across = swap_group(rows), swap_group(across)
+        kernel = functools.partial(mlp_kernel, experts, step, False, 2, 0)
+        (old,) = run_mlp(kernel, [rows, across], stale, [((half, width), jnp.float32)])
+        other_across, old = lax.optimization_barrier((other_across, old))
+        kernel = functools.partial(mlp_kernel, experts, step, True, 4, 1)
+        line = [((half // 2, width), jnp.float32), ((half // 2, width), jnp.bfloat16)]
+        kept, sent, away_kept, away_sent = run_mlp(
+            kernel,
+            [rows, across, other, other_across],
+            tuple(learner) + (old,),
+            line + line,
+        )
+        away = away_kept + swap_chip(away_sent, 1).astype(jnp.float32)
+        away = swap_group(away.astype(jnp.bfloat16))
+        own = [((row_count, width), jnp.float32)]
+        others = [((row_count, width), jnp.bfloat16)] * (chips // 2 - 1)
+        own, *sent = on_vmem(part_kernel, (kept, swap_chip(sent, 1), away), own + others)
+        returned = [swap_chip(part, distance) for part, distance in zip(sent, orders[1:])]
+    (updated,) = on_vmem(
+        last_kernel, (state, own, *returned), [((row_count, width), jnp.bfloat16)]
+    )
     return updated[None]
 
 
@@ -319,7 +336,7 @@
     experts = lax.axis_size("expert")
     groups = lax.axis_size("group")
     fewer = tokens.shape[1] * experts < learner_up.shape[1]
-    paired = experts & (experts - 1) == 0 and experts >= 8 and groups == 2
+    paired = experts & (experts - 1) == 0 and experts >= 8 and groups == 2 and routes.shape[0] == 2
     plan = exchange_plan if fewer and paired else gather_plan
     stale = (rollout_up[0], rollout_down[0])
     learner = (learner_up[0], learner_down[0])

time: 70.9 us -> 71.4 us (level)
  blocking collectives: 35.1 us -> 13.4 us
  starting transfers between devices: 11.1 us -> 24.1 us
  waiting for transfers between devices: 13.7 us -> 22.9 us
    all_to_all x3 -> x1, blocking collectives: 35.1 us -> 13.4 us  [spread(): lax.all_to_all(blocks, 'expert', 0, 0, axis_index_groups=groups, tiled=True)]
    ppermute x4 -> x13, waiting for transfers between devices: 7.21 us -> 19.4 us  [swap_chip(): lax.ppermute(value, 'expert', [(i, i ^ 2 * distance) for i in range(size)])]
    ppermute x4 -> x13, starting transfers between devices: 6.89 us -> 18.5 us  [swap_chip(): lax.ppermute(value, 'expert', [(i, i ^ 2 * distance) for i in range(size)])]
    ppermute x2 -> x3, waiting for transfers between devices: 6.45 us -> 3.57 us  [swap_group(): return lax.ppermute(value, 'group', [(0, 1), (1, 0)])]
    ppermute x2 -> x3, starting transfers between devices: 3.13 us -> 4.53 us  [swap_group(): return lax.ppermute(value, 'group', [(0, 1), (1, 0)])]
    pallas_call x9 -> x10, Pallas kernels: 10 us -> 10 us  [on_vmem(): pl.pallas_call(body, out_shape=[jax.ShapeDtypeStruct(shape, kind) for sha...]
  transfers between devices with their start and end apart: 10 -> 20, of which waited for: 5 -> 12; matrix products, arithmetic and copies ran while one was open for 0% -> 0% of each run, Pallas kernels for 10% -> 10%
where the time goes in v23:
time: 71.4 us; the launch traced here: 71.3 us
  starting transfers between devices  24.1 us (34%)
  waiting for transfers between devices  22.9 us (32%)
  blocking collectives  13.4 us (19%)
  Pallas kernels  10 us (14%)
    ppermute x13, waiting for transfers between devices, swap_chip(): lax.ppermute(value, 'expert', [(i, i ^ 2 * distance) for i in range(size)])  19.4 us
    ppermute x13, starting transfers between devices, swap_chip(): lax.ppermute(value, 'expert', [(i, i ^ 2 * distance) for i in range(size)])  18.5 us
    all_to_all x1, blocking collectives, spread(): lax.all_to_all(blocks, 'expert', 0, 0, axis_index_groups=groups, tiled=True)  13.4 us
    pallas_call x10, Pallas kernels, on_vmem(): pl.pallas_call(body, out_shape=[jax.ShapeDtypeStruct(shape, kind) for sha...  10 us
    ppermute x3, starting transfers between devices, swap_group(): return lax.ppermute(value, 'group', [(0, 1), (1, 0)])  4.53 us
    ppermute x3, waiting for transfers between devices, swap_group(): return lax.ppermute(value, 'group', [(0, 1), (1, 0)])  3.57 us
  transfers between devices with their start and end apart: 20, of which 12 were waited for; matrix products, arithmetic and copies ran while one was open for 0% of the time, Pallas kernels for 10%

profile of v23, /device:TPU:0, one launch (start us, length us, event | category | flops | bytes accessed | tf_op | source)
XLA Modules:
  0.0 71.3 jit_solution(3743840810449911734)
XLA Ops:
  1.4 4.7 %collective-permute-start = (bf16[8,2176]{1,0:T(8,128)(2,1)S(1)}, bf16[8,2176]{1,0:T(8,128)(2,1)S(1)}, u32[]{:S(2)}, u32[]{:S(2)}) collective-permute-start(bf16[8,2176]{1,0:T(8,128)(2,1)S(1)} %shard_map.92.refs_0_.refs_3_), channel_id=1, source_target_pairs={{0,12},{1,13},{2,14},{3,15},{4,8},{5,9},{6,10},{7,11},{8,4},{9,5},... | collective-permute-start | bytes 104456 | tf_op jit(solution)/shard_map/ppermute | solution.py:198
  6.7 1.5 %collective-permute-done.refs_1_ = bf16[8,2176]{1,0:T(8,128)(2,1)S(1)} collective-permute-done((bf16[8,2176]{1,0:T(8,128)(2,1)S(1)}, bf16[8,2176]{1,0:T(8,128)(2,1)S(1)}, u32[]{:S(2)}, u32[]{:S(2)}) %collective-permute-start) | collective-permute-done | bytes 34848 | tf_op jit(solution)/shard_map/ppermute | solution.py:198
  8.1 2.7 %collective-permute-done.1.refs_2_ = bf16[8,2176]{1,0:T(8,128)(2,1)S(1)} collective-permute-done((bf16[8,2176]{1,0:T(8,128)(2,1)S(1)}, bf16[8,2176]{1,0:T(8,128)(2,1)S(1)}, u32[]{:S(2)}, u32[]{:S(2)}) %collective-permute-start.1) | collective-permute-done | bytes 34848 | tf_op jit(solution)/shard_map/ppermute | solution.py:198
  11.4 1.6 %collective-permute-start.3 = (bf16[32,2176]{1,0:T(8,128)(2,1)S(1)}, bf16[32,2176]{1,0:T(8,128)(2,1)S(1)}, u32[]{:S(2)}, u32[]{:S(2)}) collective-permute-start(bf16[32,2176]{1,0:T(8,128)(2,1)S(1)} %bitcast.23), channel_id=1, source_target_pairs={{0,2},{1,3},{2,0},{3,1},{4,6},{5,7},{6,4},{7,5},{8,10},{9,11},{10,... | collective-permute-start | bytes 417800 | tf_op jit(solution)/shard_map/ppermute | solution.py:198
  13.0 4.1 %collective-permute-done.3.refs_1_ = bf16[32,2176]{1,0:T(8,128)(2,1)S(1)} collective-permute-done((bf16[32,2176]{1,0:T(8,128)(2,1)S(1)}, bf16[32,2176]{1,0:T(8,128)(2,1)S(1)}, u32[]{:S(2)}, u32[]{:S(2)}) %collective-permute-start.3) | collective-permute-done | bytes 139296 | tf_op jit(solution)/shard_map/ppermute | solution.py:198
  17.2 3.5 %shard_map.94 = bf16[8,8,2048]{2,1,0:T(8,128)(2,1)S(1)} custom-call(bf16[32,2176]{1,0:T(8,128)(2,1)S(1)} %bitcast.24, bf16[32,2176]{1,0:T(8,128)(2,1)S(1)} %collective-permute-done.3.refs_1_, bf16[768,2048]{1,0:T(8,128)(2,1)S(1)} %bitcast.10, bf16[768,2048]{1,0:T(8,128)(2,1)S(1)} %bitcast.13, bf16[768,2048]{1,0:T(8,128)(2,1)S(1)} %collective-permute-done.4.refs_4_, ...), custom_call_target="tpu_custom_call" | custom-call | flops 3221225472 | bytes 25165824 | tf_op jit(solution)/shard_map/pallas_call | solution.py:169
  20.6 13.4 %all_to_all.5.refs_1_ = bf16[8,8,2048]{2,1,0:T(8,128)(2,1)S(1)} all-to-all(bf16[8,8,2048]{2,1,0:T(8,128)(2,1)S(1)} %shard_map.94), channel_id=1, replica_groups={{0,4,8,12,2,6,10,14},{1,5,9,13,3,7,11,15},{16,20,24,28,18,22,26,30},{17..., dimensions={0} | all-to-all | bytes 524288 | tf_op jit(solution)/shard_map/all_to_all | solution.py:217
  34.2 0.7 collective-permute-start.7
  34.9 3.7 %collective-permute-start.8 = (bf16[8,2176]{1,0:T(8,128)(2,1)S(1)}, bf16[8,2176]{1,0:T(8,128)(2,1)S(1)}, u32[]{:S(2)}, u32[]{:S(2)}) collective-permute-start(bf16[8,2176]{1,0:T(8,128)(2,1)S(1)} %get-tuple-element.33.refs_0_), channel_id=1, source_target_pairs={{0,4},{1,5},{2,6},{3,7},{4,0},{5,1},{6,2},{7,3},{8,12},{9,13},{10,... | collective-permute-start | bytes 104456 | tf_op jit(solution)/shard_map/ppermute | solution.py:198
  38.6 1.3 %collective-permute-done.6.refs_1_ = bf16[8,2176]{1,0:T(8,128)(2,1)S(1)} collective-permute-done((bf16[8,2176]{1,0:T(8,128)(2,1)S(1)}, bf16[8,2176]{1,0:T(8,128)(2,1)S(1)}, u32[]{:S(2)}, u32[]{:S(2)}) %collective-permute-start.6) | collective-permute-done | bytes 34848 | tf_op jit(solution)/shard_map/ppermute | solution.py:198
  41.2 1.5 %collective-permute-start.10 = (bf16[32,2176]{1,0:T(8,128)(2,1)S(1)}, bf16[32,2176]{1,0:T(8,128)(2,1)S(1)}, u32[]{:S(2)}, u32[]{:S(2)}) collective-permute-start(bf16[32,2176]{1,0:T(8,128)(2,1)S(1)} %bitcast.20), channel_id=1, source_target_pairs={{0,16},{16,0},{1,17},{17,1},{2,18},{18,2},{3,19},{19,3},{4,20},{20... | collective-permute-start | bytes 417800 | tf_op jit(solution)/shard_map/ppermute | solution.py:193
  42.7 3.0 %collective-permute-done.9.refs_1_ = bf16[32,2176]{1,0:T(8,128)(2,1)S(1)} collective-permute-done((bf16[32,2176]{1,0:T(8,128)(2,1)S(1)}, bf16[32,2176]{1,0:T(8,128)(2,1)S(1)}, u32[]{:S(2)}, u32[]{:S(2)}) %collective-permute-start.9) | collective-permute-done | bytes 139296 | tf_op jit(solution)/shard_map/ppermute | solution.py:198
  45.7 1.5 %collective-permute-start.11 = (bf16[32,2176]{1,0:T(8,128)(2,1)S(1)}, bf16[32,2176]{1,0:T(8,128)(2,1)S(1)}, u32[]{:S(2)}, u32[]{:S(2)}) collective-permute-start(bf16[32,2176]{1,0:T(8,128)(2,1)S(1)} %collective-permute-done.9.refs_1_), channel_id=1, source_target_pairs={{0,16},{16,0},{1,17},{17,1},{2,18},{18,2},{3,19},{19,3},{4,20},{20... | collective-permute-start | bytes 417800 | tf_op jit(solution)/shard_map/ppermute | solution.py:193
  47.2 3.5 %shard_map.97.refs_8_ = f32[64,2048]{1,0:T(8,128)S(1)} custom-call(bf16[32,2176]{1,0:T(8,128)(2,1)S(1)} %bitcast.21, bf16[32,2176]{1,0:T(8,128)(2,1)S(1)} %collective-permute-done.9.refs_1_, bf16[768,2048]{1,0:T(8,128)(2,1)S(1)} %bitcast.11, bf16[768,2048]{1,0:T(8,128)(2,1)S(1)} %bitcast.14, bf16[768,2048]{1,0:T(8,128)(2,1)S(1)} %collective-permute-done.4.refs_4_, ...), custom_call_target="tpu_custom_call" | custom-call | flops 3221225472 | bytes 25165824 | tf_op jit(solution)/shard_map/pallas_call | solution.py:169
  50.7 2.1 %shard_map.98 = (f32[32,2048]{1,0:T(8,128)S(1)}, bf16[32,2048]{1,0:T(8,128)(2,1)S(1)}, f32[32,2048]{1,0:T(8,128)S(1)}, bf16[32,2048]{1,0:T(8,128)(2,1)S(1)}) custom-call(bf16[32,2176]{1,0:T(8,128)(2,1)S(1)} %bitcast.22, bf16[32,2176]{1,0:T(8,128)(2,1)S(1)} %collective-permute-done.9.refs_1_, bf16[32,2176]{1,0:T(8,128)(2,1)S(1)} %collective-permute-done.10.refs_2_, ...), custom_call_target="tpu_custom_call" | custom-call | flops 1677721600 | bytes 13107200 | tf_op jit(solution)/shard_map/pallas_call | solution.py:169
  53.5 1.4 %collective-permute-start.14 = (bf16[32,2048]{1,0:T(8,128)(2,1)S(1)}, bf16[32,2048]{1,0:T(8,128)(2,1)S(1)}, u32[]{:S(2)}, u32[]{:S(2)}) collective-permute-start(bf16[32,2048]{1,0:T(8,128)(2,1)S(1)} %get-tuple-element.42), channel_id=1, source_target_pairs={{0,2},{1,3},{2,0},{3,1},{4,6},{5,7},{6,4},{7,5},{8,10},{9,11},{10,... | collective-permute-start | bytes 393224 | tf_op jit(solution)/shard_map/ppermute | solution.py:198
  54.9 2.9 %collective-permute-done.15 = bf16[32,2048]{1,0:T(8,128)(2,1)S(1)} collective-permute-done((bf16[32,2048]{1,0:T(8,128)(2,1)S(1)}, bf16[32,2048]{1,0:T(8,128)(2,1)S(1)}, u32[]{:S(2)}, u32[]{:S(2)}) %collective-permute-start.15) | collective-permute-done | bytes 131104 | tf_op jit(solution)/shard_map/ppermute | solution.py:198
  57.9 1.6 %collective-permute-start.16 = (bf16[32,2048]{1,0:T(8,128)(2,1)S(1)}, bf16[32,2048]{1,0:T(8,128)(2,1)S(1)}, u32[]{:S(2)}, u32[]{:S(2)}) collective-permute-start(bf16[32,2048]{1,0:T(8,128)(2,1)S(1)} %add_convert_fusion), channel_id=1, source_target_pairs={{0,16},{16,0},{1,17},{17,1},{2,18},{18,2},{3,19},{19,3},{4,20},{20... | collective-permute-start | bytes 393224 | tf_op jit(solution)/shard_map/ppermute | solution.py:193
  59.5 3.5 %collective-permute-done.16.refs_2_ = bf16[32,2048]{1,0:T(8,128)(2,1)S(1)} collective-permute-done((bf16[32,2048]{1,0:T(8,128)(2,1)S(1)}, bf16[32,2048]{1,0:T(8,128)(2,1)S(1)}, u32[]{:S(2)}, u32[]{:S(2)}) %collective-permute-start.16) | collective-permute-done | bytes 131104 | tf_op jit(solution)/shard_map/ppermute | solution.py:193
  63.0 2.5 %collective-permute-start.17 = (bf16[8,2048]{1,0:T(8,128)(2,1)S(1)}, bf16[8,2048]{1,0:T(8,128)(2,1)S(1)}, u32[]{:S(2)}, u32[]{:S(2)}) collective-permute-start(bf16[8,2048]{1,0:T(8,128)(2,1)S(1)} %get-tuple-element.46), channel_id=1, source_target_pairs={{0,12},{1,13},{2,14},{3,15},{4,8},{5,9},{6,10},{7,11},{8,4},{9,5},... | collective-permute-start | bytes 98312 | tf_op jit(solution)/shard_map/ppermute | solution.py:198
  65.5 1.1 %collective-permute-start.18 = (bf16[8,2048]{1,0:T(8,128)(2,1)S(1)}, bf16[8,2048]{1,0:T(8,128)(2,1)S(1)}, u32[]{:S(2)}, u32[]{:S(2)}) collective-permute-start(bf16[8,2048]{1,0:T(8,128)(2,1)S(1)} %get-tuple-element.47), channel_id=1, source_target_pairs={{0,8},{1,9},{2,10},{3,11},{4,12},{5,13},{6,14},{7,15},{8,0},{9,1},... | collective-permute-start | bytes 98312 | tf_op jit(solution)/shard_map/ppermute | solution.py:198
  66.5 0.9 %collective-permute-start.19 = (bf16[8,2048]{1,0:T(8,128)(2,1)S(1)}, bf16[8,2048]{1,0:T(8,128)(2,1)S(1)}, u32[]{:S(2)}, u32[]{:S(2)}) collective-permute-start(bf16[8,2048]{1,0:T(8,128)(2,1)S(1)} %get-tuple-element.48), channel_id=1, source_target_pairs={{0,4},{1,5},{2,6},{3,7},{4,0},{5,1},{6,2},{7,3},{8,12},{9,13},{10,... | collective-permute-start | bytes 98312 | tf_op jit(solution)/shard_map/ppermute | solution.py:198
  67.5 1.3 %collective-permute-done.17.refs_2_ = bf16[8,2048]{1,0:T(8,128)(2,1)S(1)} collective-permute-done((bf16[8,2048]{1,0:T(8,128)(2,1)S(1)}, bf16[8,2048]{1,0:T(8,128)(2,1)S(1)}, u32[]{:S(2)}, u32[]{:S(2)}) %collective-permute-start.17) | collective-permute-done | bytes 32800 | tf_op jit(solution)/shard_map/ppermute | solution.py:198
  68.8 1.5 %collective-permute-done.18.refs_3_ = bf16[8,2048]{1,0:T(8,128)(2,1)S(1)} collective-permute-done((bf16[8,2048]{1,0:T(8,128)(2,1)S(1)}, bf16[8,2048]{1,0:T(8,128)(2,1)S(1)}, u32[]{:S(2)}, u32[]{:S(2)}) %collective-permute-start.18) | collective-permute-done | bytes 32800 | tf_op jit(solution)/shard_map/ppermute | solution.py:198
  (46 shorter events, 5.7 us)
Async XLA Ops:
  0.0 17.1 %collective-permute-start.4 = (bf16[768,2048]{1,0:T(8,128)(2,1)}, bf16[768,2048]{1,0:T(8,128)(2,1)S(1)}, u32[]{:S(2)}, u32[]{:S(2)}) collective-permute-start(bf16[768,2048]{1,0:T(8,128)(2,1)} %bitcast.9), channel_id=1, source_target_pairs={{0,1},{1,0},{2,3},{3,2},{4,5},{5,4},{6,7},{7,6},{8,9},{9,8},{10,11... | collective-permute-start | bytes 9437192 | tf_op jit(solution)/shard_map/ppermute | solution.py:189
  0.5 10.4 %copy-start.2 = (bf16[1,384,2048]{2,1,0:T(8,128)(2,1)S(1)}, bf16[1,384,2048]{2,1,0:T(8,128)(2,1)}, u32[]{:S(2)}) copy-start(bf16[1,384,2048]{2,1,0:T(8,128)(2,1)} %param.16) | copy-start | bytes 4718596
  0.5 10.4 %copy-start.3 = (bf16[1,384,2048]{2,1,0:T(8,128)(2,1)S(1)}, bf16[1,384,2048]{2,1,0:T(8,128)(2,1)}, u32[]{:S(2)}) copy-start(bf16[1,384,2048]{2,1,0:T(8,128)(2,1)} %param.17) | copy-start | bytes 4718596
  0.5 16.6 %copy-start = (bf16[1,768,2048]{2,1,0:T(8,128)(2,1)S(1)}, bf16[1,768,2048]{2,1,0:T(8,128)(2,1)}, u32[]{:S(2)}) copy-start(bf16[1,768,2048]{2,1,0:T(8,128)(2,1)} %param.14) | copy-start | bytes 9437188
  0.5 16.6 %copy-start.1 = (bf16[1,768,2048]{2,1,0:T(8,128)(2,1)S(1)}, bf16[1,768,2048]{2,1,0:T(8,128)(2,1)}, u32[]{:S(2)}) copy-start(bf16[1,768,2048]{2,1,0:T(8,128)(2,1)} %param.15) | copy-start | bytes 9437188
  0.5 16.6 %collective-permute-start.5 = (bf16[768,2048]{1,0:T(8,128)(2,1)}, bf16[768,2048]{1,0:T(8,128)(2,1)S(1)}, u32[]{:S(2)}, u32[]{:S(2)}) collective-permute-start(bf16[768,2048]{1,0:T(8,128)(2,1)} %bitcast.12), channel_id=1, source_target_pairs={{0,1},{1,0},{2,3},{3,2},{4,5},{5,4},{6,7},{7,6},{8,9},{9,8},{10,11... | collective-permute-start | bytes 9437192 | tf_op jit(solution)/shard_map/ppermute | solution.py:189
  1.4 6.8 %collective-permute-start = (bf16[8,2176]{1,0:T(8,128)(2,1)S(1)}, bf16[8,2176]{1,0:T(8,128)(2,1)S(1)}, u32[]{:S(2)}, u32[]{:S(2)}) collective-permute-start(bf16[8,2176]{1,0:T(8,128)(2,1)S(1)} %shard_map.92.refs_0_.refs_3_), channel_id=1, source_target_pairs={{0,12},{1,13},{2,14},{3,15},{4,8},{5,9},{6,10},{7,11},{8,4},{9,5},... | collective-permute-start | bytes 104456 | tf_op jit(solution)/shard_map/ppermute | solution.py:198
  6.0 4.8 %collective-permute-start.1 = (bf16[8,2176]{1,0:T(8,128)(2,1)S(1)}, bf16[8,2176]{1,0:T(8,128)(2,1)S(1)}, u32[]{:S(2)}, u32[]{:S(2)}) collective-permute-start(bf16[8,2176]{1,0:T(8,128)(2,1)S(1)} %shard_map.92.refs_0_.refs_3_), channel_id=1, source_target_pairs={{0,8},{1,9},{2,10},{3,11},{4,12},{5,13},{6,14},{7,15},{8,0},{9,1},... | collective-permute-start | bytes 104456 | tf_op jit(solution)/shard_map/ppermute | solution.py:198
  6.0 4.8 %collective-permute-start.2 = (bf16[8,2176]{1,0:T(8,128)(2,1)S(1)}, bf16[8,2176]{1,0:T(8,128)(2,1)S(1)}, u32[]{:S(2)}, u32[]{:S(2)}) collective-permute-start(bf16[8,2176]{1,0:T(8,128)(2,1)S(1)} %shard_map.92.refs_0_.refs_3_), channel_id=1, source_target_pairs={{0,4},{1,5},{2,6},{3,7},{4,0},{5,1},{6,2},{7,3},{8,12},{9,13},{10,... | collective-permute-start | bytes 104456 | tf_op jit(solution)/shard_map/ppermute | solution.py:198
  10.9 39.8 %collective-permute-start.12 = (bf16[384,2048]{1,0:T(8,128)(2,1)S(1)}, bf16[384,2048]{1,0:T(8,128)(2,1)S(1)}, u32[]{:S(2)}, u32[]{:S(2)}) collective-permute-start(bf16[384,2048]{1,0:T(8,128)(2,1)S(1)} %bitcast.15), channel_id=1, source_target_pairs={{0,1},{1,0},{2,3},{3,2},{4,5},{5,4},{6,7},{7,6},{8,9},{9,8},{10,11... | collective-permute-start | bytes 4718600 | tf_op jit(solution)/shard_map/ppermute | solution.py:189
  10.9 39.8 %collective-permute-start.13 = (bf16[384,2048]{1,0:T(8,128)(2,1)S(1)}, bf16[384,2048]{1,0:T(8,128)(2,1)S(1)}, u32[]{:S(2)}, u32[]{:S(2)}) collective-permute-start(bf16[384,2048]{1,0:T(8,128)(2,1)S(1)} %bitcast.17), channel_id=1, source_target_pairs={{0,1},{1,0},{2,3},{3,2},{4,5},{5,4},{6,7},{7,6},{8,9},{9,8},{10,11... | collective-permute-start | bytes 4718600 | tf_op jit(solution)/shard_map/ppermute | solution.py:189
  11.4 5.7 %collective-permute-start.3 = (bf16[32,2176]{1,0:T(8,128)(2,1)S(1)}, bf16[32,2176]{1,0:T(8,128)(2,1)S(1)}, u32[]{:S(2)}, u32[]{:S(2)}) collective-permute-start(bf16[32,2176]{1,0:T(8,128)(2,1)S(1)} %bitcast.23), channel_id=1, source_target_pairs={{0,2},{1,3},{2,0},{3,1},{4,6},{5,7},{6,4},{7,5},{8,10},{9,11},{10,... | collective-permute-start | bytes 417800 | tf_op jit(solution)/shard_map/ppermute | solution.py:198
  34.2 5.8 %collective-permute-start.6 = (bf16[8,2176]{1,0:T(8,128)(2,1)S(1)}, bf16[8,2176]{1,0:T(8,128)(2,1)S(1)}, u32[]{:S(2)}, u32[]{:S(2)}) collective-permute-start(bf16[8,2176]{1,0:T(8,128)(2,1)S(1)} %get-tuple-element.33.refs_0_), channel_id=1, source_target_pairs={{0,12},{1,13},{2,14},{3,15},{4,8},{5,9},{6,10},{7,11},{8,4},{9,5},... | collective-permute-start | bytes 104456 | tf_op jit(solution)/shard_map/ppermute | solution.py:198
  34.2 5.7 %collective-permute-start.7 = (bf16[8,2176]{1,0:T(8,128)(2,1)S(1)}, bf16[8,2176]{1,0:T(8,128)(2,1)S(1)}, u32[]{:S(2)}, u32[]{:S(2)}) collective-permute-start(bf16[8,2176]{1,0:T(8,128)(2,1)S(1)} %get-tuple-element.33.refs_0_), channel_id=1, source_target_pairs={{0,8},{1,9},{2,10},{3,11},{4,12},{5,13},{6,14},{7,15},{8,0},{9,1},... | collective-permute-start | bytes 104456 | tf_op jit(solution)/shard_map/ppermute | solution.py:198
  34.9 5.6 %collective-permute-start.8 = (bf16[8,2176]{1,0:T(8,128)(2,1)S(1)}, bf16[8,2176]{1,0:T(8,128)(2,1)S(1)}, u32[]{:S(2)}, u32[]{:S(2)}) collective-permute-start(bf16[8,2176]{1,0:T(8,128)(2,1)S(1)} %get-tuple-element.33.refs_0_), channel_id=1, source_target_pairs={{0,4},{1,5},{2,6},{3,7},{4,0},{5,1},{6,2},{7,3},{8,12},{9,13},{10,... | collective-permute-start | bytes 104456 | tf_op jit(solution)/shard_map/ppermute | solution.py:198
  40.5 5.1 %collective-permute-start.9 = (bf16[32,2176]{1,0:T(8,128)(2,1)S(1)}, bf16[32,2176]{1,0:T(8,128)(2,1)S(1)}, u32[]{:S(2)}, u32[]{:S(2)}) collective-permute-start(bf16[32,2176]{1,0:T(8,128)(2,1)S(1)} %bitcast.19), channel_id=1, source_target_pairs={{0,2},{1,3},{2,0},{3,1},{4,6},{5,7},{6,4},{7,5},{8,10},{9,11},{10,... | collective-permute-start | bytes 417800 | tf_op jit(solution)/shard_map/ppermute | solution.py:198
  41.2 9.6 %collective-permute-start.10 = (bf16[32,2176]{1,0:T(8,128)(2,1)S(1)}, bf16[32,2176]{1,0:T(8,128)(2,1)S(1)}, u32[]{:S(2)}, u32[]{:S(2)}) collective-permute-start(bf16[32,2176]{1,0:T(8,128)(2,1)S(1)} %bitcast.20), channel_id=1, source_target_pairs={{0,16},{16,0},{1,17},{17,1},{2,18},{18,2},{3,19},{19,3},{4,20},{20... | collective-permute-start | bytes 417800 | tf_op jit(solution)/shard_map/ppermute | solution.py:193
  45.7 5.1 %collective-permute-start.11 = (bf16[32,2176]{1,0:T(8,128)(2,1)S(1)}, bf16[32,2176]{1,0:T(8,128)(2,1)S(1)}, u32[]{:S(2)}, u32[]{:S(2)}) collective-permute-start(bf16[32,2176]{1,0:T(8,128)(2,1)S(1)} %collective-permute-done.9.refs_1_), channel_id=1, source_target_pairs={{0,16},{16,0},{1,17},{17,1},{2,18},{18,2},{3,19},{19,3},{4,20},{20... | collective-permute-start | bytes 417800 | tf_op jit(solution)/shard_map/ppermute | solution.py:193
  52.8 5.0 %collective-permute-start.15 = (bf16[32,2048]{1,0:T(8,128)(2,1)S(1)}, bf16[32,2048]{1,0:T(8,128)(2,1)S(1)}, u32[]{:S(2)}, u32[]{:S(2)}) collective-permute-start(bf16[32,2048]{1,0:T(8,128)(2,1)S(1)} %get-tuple-element.44), channel_id=1, source_target_pairs={{0,2},{1,3},{2,0},{3,1},{4,6},{5,7},{6,4},{7,5},{8,10},{9,11},{10,... | collective-permute-start | bytes 393224 | tf_op jit(solution)/shard_map/ppermute | solution.py:198
  53.5 6.0 %collective-permute-start.14 = (bf16[32,2048]{1,0:T(8,128)(2,1)S(1)}, bf16[32,2048]{1,0:T(8,128)(2,1)S(1)}, u32[]{:S(2)}, u32[]{:S(2)}) collective-permute-start(bf16[32,2048]{1,0:T(8,128)(2,1)S(1)} %get-tuple-element.42), channel_id=1, source_target_pairs={{0,2},{1,3},{2,0},{3,1},{4,6},{5,7},{6,4},{7,5},{8,10},{9,11},{10,... | collective-permute-start | bytes 393224 | tf_op jit(solution)/shard_map/ppermute | solution.py:198
  57.9 5.0 %collective-permute-start.16 = (bf16[32,2048]{1,0:T(8,128)(2,1)S(1)}, bf16[32,2048]{1,0:T(8,128)(2,1)S(1)}, u32[]{:S(2)}, u32[]{:S(2)}) collective-permute-start(bf16[32,2048]{1,0:T(8,128)(2,1)S(1)} %add_convert_fusion), channel_id=1, source_target_pairs={{0,16},{16,0},{1,17},{17,1},{2,18},{18,2},{3,19},{19,3},{4,20},{20... | collective-permute-start | bytes 393224 | tf_op jit(solution)/shard_map/ppermute | solution.py:193
  63.0 5.8 %collective-permute-start.17 = (bf16[8,2048]{1,0:T(8,128)(2,1)S(1)}, bf16[8,2048]{1,0:T(8,128)(2,1)S(1)}, u32[]{:S(2)}, u32[]{:S(2)}) collective-permute-start(bf16[8,2048]{1,0:T(8,128)(2,1)S(1)} %get-tuple-element.46), channel_id=1, source_target_pairs={{0,12},{1,13},{2,14},{3,15},{4,8},{5,9},{6,10},{7,11},{8,4},{9,5},... | collective-permute-start | bytes 98312 | tf_op jit(solution)/shard_map/ppermute | solution.py:198
  65.5 4.8 %collective-permute-start.18 = (bf16[8,2048]{1,0:T(8,128)(2,1)S(1)}, bf16[8,2048]{1,0:T(8,128)(2,1)S(1)}, u32[]{:S(2)}, u32[]{:S(2)}) collective-permute-start(bf16[8,2048]{1,0:T(8,128)(2,1)S(1)} %get-tuple-element.47), channel_id=1, source_target_pairs={{0,8},{1,9},{2,10},{3,11},{4,12},{5,13},{6,14},{7,15},{8,0},{9,1},... | collective-permute-start | bytes 98312 | tf_op jit(solution)/shard_map/ppermute | solution.py:198
  66.5 4.1 %collective-permute-start.19 = (bf16[8,2048]{1,0:T(8,128)(2,1)S(1)}, bf16[8,2048]{1,0:T(8,128)(2,1)S(1)}, u32[]{:S(2)}, u32[]{:S(2)}) collective-permute-start(bf16[8,2048]{1,0:T(8,128)(2,1)S(1)} %get-tuple-element.48), channel_id=1, source_target_pairs={{0,4},{1,5},{2,6},{3,7},{4,0},{5,1},{6,2},{7,3},{8,12},{9,13},{10,... | collective-permute-start | bytes 98312 | tf_op jit(solution)/shard_map/ppermute | solution.py:198
  (5 other events, 3.8 us)

commit v24 on v22

--- a/solution.py
+++ b/solution.py
@@ -99,8 +99,33 @@
         out[chip] = normed
 
 
-def last_kernel(previous, returned, out):
-    out[...] = (previous[...] + sum_blocks(returned)).astype(jnp.bfloat16)
+def fresh_kernel(experts, step, rows, other, *refs):
+    weights, old, outs = refs[:4], refs[4], refs[5:]
+    line, count, width = outs[0].shape
+    half = line * count
+    _, total = weighted_outputs(experts, step, True, [rows, other], weights, width)
+    y = lax.rem(lax.div(lax.axis_index("expert"), 2), 2)
+    low = jnp.full((half, width), y, jnp.int32) == 0
+    for i, share in enumerate((total[: 2 * half] + old[...], total[2 * half :])):
+        first, second = share[:half], share[half:]
+        kept, sent = jnp.where(low, first, second), jnp.where(low, second, first)
+        outs[2 * i][...] = kept.reshape(line, count, width)
+        outs[2 * i + 1][...] = sent.reshape(line, count, width).astype(jnp.bfloat16)
+
+
+def part_kernel(distances, kept, received, away, own_out, *sent_outs):
+    z = lax.div(lax.axis_index("expert"), 4)
+    for distance, out in zip((0,) + distances, (own_out,) + sent_outs):
+        place = jnp.bitwise_xor(z, distance)
+        total = kept[place] + received[place].astype(jnp.float32)
+        out[...] = (total + away[place].astype(jnp.float32)).astype(out.dtype)
+
+
+def last_kernel(previous, own, *refs):
+    total = own[...]
+    for received in refs[:-1]:
+        total = total + received[...].astype(jnp.float32)
+    refs[-1][...] = (previous[...] + total).astype(jnp.bfloat16)
 
 
 def join_kernel(rows, tables, out):
@@ -258,13 +283,27 @@
             kernel = functools.partial(mlp_kernel, experts, step, False, 1)
             (old,) = run_mlp(kernel, [rows], stale, [kept])
             other, old = lax.optimization_barrier((other, old))
-            kernel = functools.partial(mlp_kernel, experts, step, True, 2)
-            sent = ((half, width), jnp.bfloat16)
-            new, away = run_mlp(kernel, [rows, other], learner, [kept, sent])
-            share = old + new + swap_group(away).astype(jnp.float32)
-            share = share.astype(jnp.bfloat16).reshape(chips, row_count, width)
+            line = (chips // 2, row_count, width)
+            kept, sent, away_kept, away_sent = run_mlp(
+                functools.partial(fresh_kernel, experts, step),
+                [rows, other],
+                tuple(learner) + (old,),
+                [(line, jnp.float32), (line, jnp.bfloat16)] * 2,
+            )
+            away = away_kept + swap_chip(away_sent, 1).astype(jnp.float32)
+            away = swap_group(away.astype(jnp.bfloat16))
+            distances = tuple(range(chips // 2 - 1, 0, -1))
+            own, *sent = on_vmem(
+                functools.partial(part_kernel, distances),
+                (kept, swap_chip(sent, 1), away),
+                [state_shape] + [((row_count, width), jnp.bfloat16)] * len(distances),
+            )
+            received = [swap_chip(part, 2 * d) for part, d in zip(sent, distances)]
+            break
         returned = spread(share)
-    (updated,) = on_vmem(last_kernel, (state, returned), [((row_count, width), jnp.bfloat16)])
+    (updated,) = on_vmem(
+        last_kernel, (state, own, *received), [((row_count, width), jnp.bfloat16)]
+    )
     return updated[None]
 
 
@@ -319,7 +358,7 @@
     experts = lax.axis_size("expert")
     groups = lax.axis_size("group")
     fewer = tokens.shape[1] * experts < learner_up.shape[1]
-    paired = experts & (experts - 1) == 0 and experts >= 8 and groups == 2
+    paired = experts & (experts - 1) == 0 and experts >= 8 and groups == 2 and routes.shape[0] == 2
     plan = exchange_plan if fewer and paired else gather_plan
     stale = (rollout_up[0], rollout_down[0])
     learner = (learner_up[0], learner_down[0])

time: 70.9 us -> 69.9 us (0.986)
  blocking collectives: 35.1 us -> 24.1 us
  starting transfers between devices: 11.1 us -> 17.7 us
  waiting for transfers between devices: 13.7 us -> 17.1 us
    all_to_all x3 -> x2, blocking collectives: 35.1 us -> 24.1 us  [spread(): lax.all_to_all(blocks, 'expert', 0, 0, axis_index_groups=groups, tiled=True)]
    ppermute x4 -> x9, starting transfers between devices: 6.89 us -> 13.4 us  [swap_chip(): lax.ppermute(value, 'expert', [(i, i ^ 2 * distance) for i in range(size)])]
    ppermute x4 -> x9, waiting for transfers between devices: 7.21 us -> 12 us  [swap_chip(): lax.ppermute(value, 'expert', [(i, i ^ 2 * distance) for i in range(size)])]
    ppermute x2, waiting for transfers between devices: 6.45 us -> 5.04 us  [swap_group(): return lax.ppermute(value, 'group', [(0, 1), (1, 0)])]
    pallas_call x9 -> x10, Pallas kernels: 10 us -> 10 us  [on_vmem(): pl.pallas_call(body, out_shape=[jax.ShapeDtypeStruct(shape, kind) for sha...]
  transfers between devices with their start and end apart: 10 -> 15, of which waited for: 5 -> 8; matrix products, arithmetic and copies ran while one was open for 0% -> 0% of each run, Pallas kernels for 10% -> 10%
where the time goes in v24:
time: 69.9 us; the launch traced here: 69.7 us
  blocking collectives  24.1 us (34%)
  starting transfers between devices  17.7 us (25%)
  waiting for transfers between devices  17.1 us (24%)
  Pallas kernels  10 us (14%)
    all_to_all x2, blocking collectives, spread(): lax.all_to_all(blocks, 'expert', 0, 0, axis_index_groups=groups, tiled=True)  24.1 us
    ppermute x9, starting transfers between devices, swap_chip(): lax.ppermute(value, 'expert', [(i, i ^ 2 * distance) for i in range(size)])  13.4 us
    ppermute x9, waiting for transfers between devices, swap_chip(): lax.ppermute(value, 'expert', [(i, i ^ 2 * distance) for i in range(size)])  12 us
    pallas_call x10, Pallas kernels, on_vmem(): pl.pallas_call(body, out_shape=[jax.ShapeDtypeStruct(shape, kind) for sha...  10 us
    ppermute x2, waiting for transfers between devices, swap_group(): return lax.ppermute(value, 'group', [(0, 1), (1, 0)])  5.04 us
    ppermute x2, starting transfers between devices, swap_group(): return lax.ppermute(value, 'group', [(0, 1), (1, 0)])  3.13 us
  transfers between devices with their start and end apart: 15, of which 8 were waited for; matrix products, arithmetic and copies ran while one was open for 0% of the time, Pallas kernels for 10%

profile of v24, /device:TPU:0, one launch (start us, length us, event | category | flops | bytes accessed | tf_op | source)
XLA Modules:
  0.0 69.7 jit_solution(3845155822720424554)
XLA Ops:
  0.6 0.6 copy-done.4
  1.4 4.7 %collective-permute-start = (bf16[8,2176]{1,0:T(8,128)(2,1)S(1)}, bf16[8,2176]{1,0:T(8,128)(2,1)S(1)}, u32[]{:S(2)}, u32[]{:S(2)}) collective-permute-start(bf16[8,2176]{1,0:T(8,128)(2,1)S(1)} %shard_map.92.refs_0_), channel_id=1, source_target_pairs={{0,12},{1,13},{2,14},{3,15},{4,8},{5,9},{6,10},{7,11},{8,4},{9,5},... | collective-permute-start | bytes 104456 | tf_op jit(solution)/shard_map/ppermute | solution.py:213
  6.0 0.6 collective-permute-start.2
  6.7 1.5 %collective-permute-done.refs_1_ = bf16[8,2176]{1,0:T(8,128)(2,1)S(1)} collective-permute-done((bf16[8,2176]{1,0:T(8,128)(2,1)S(1)}, bf16[8,2176]{1,0:T(8,128)(2,1)S(1)}, u32[]{:S(2)}, u32[]{:S(2)}) %collective-permute-start) | collective-permute-done | bytes 34848 | tf_op jit(solution)/shard_map/ppermute | solution.py:213
  8.1 2.7 %collective-permute-done.1.refs_2_ = bf16[8,2176]{1,0:T(8,128)(2,1)S(1)} collective-permute-done((bf16[8,2176]{1,0:T(8,128)(2,1)S(1)}, bf16[8,2176]{1,0:T(8,128)(2,1)S(1)}, u32[]{:S(2)}, u32[]{:S(2)}) %collective-permute-start.1) | collective-permute-done | bytes 34848 | tf_op jit(solution)/shard_map/ppermute | solution.py:213
  10.9 1.6 %collective-permute-start.3 = (bf16[32,2176]{1,0:T(8,128)(2,1)S(1)}, bf16[32,2176]{1,0:T(8,128)(2,1)S(1)}, u32[]{:S(2)}, u32[]{:S(2)}) collective-permute-start(bf16[32,2176]{1,0:T(8,128)(2,1)S(1)} %bitcast.21), channel_id=1, source_target_pairs={{0,2},{1,3},{2,0},{3,1},{4,6},{5,7},{6,4},{7,5},{8,10},{9,11},{10,... | collective-permute-start | bytes 417800 | tf_op jit(solution)/shard_map/ppermute | solution.py:213
  13.0 3.0 %collective-permute-done.3.refs_1_ = bf16[32,2176]{1,0:T(8,128)(2,1)S(1)} collective-permute-done((bf16[32,2176]{1,0:T(8,128)(2,1)S(1)}, bf16[32,2176]{1,0:T(8,128)(2,1)S(1)}, u32[]{:S(2)}, u32[]{:S(2)}) %collective-permute-start.3) | collective-permute-done | bytes 139296 | tf_op jit(solution)/shard_map/ppermute | solution.py:213
  16.0 3.5 %shard_map.94 = (bf16[8,8,2048]{2,1,0:T(8,128)(2,1)S(1)}, bf16[8,8,128]{2,1,0:T(8,128)(2,1)S(1)}) custom-call(bf16[32,2176]{1,0:T(8,128)(2,1)S(1)} %bitcast.22, bf16[32,2176]{1,0:T(8,128)(2,1)S(1)} %collective-permute-done.3.refs_1_, bf16[768,2048]{1,0:T(8,128)(2,1)S(1)} %bitcast.11, bf16[768,2048]{1,0:T(8,128)(2,1)S(1)} %bitcast.14, ...), custom_call_target="tpu_custom_call" | custom-call | flops 3221225472 | bytes 25165824 | tf_op jit(solution)/shard_map/pallas_call | solution.py:184
  19.5 13.1 %all_to_all.10.refs_1_ = bf16[8,8,2048]{2,1,0:T(8,128)(2,1)S(1)} all-to-all(bf16[8,8,2048]{2,1,0:T(8,128)(2,1)S(1)} %get-tuple-element.31), channel_id=1, replica_groups={{0,4,8,12,2,6,10,14},{1,5,9,13,3,7,11,15},{16,20,24,28,18,22,26,30},{17..., dimensions={0} | all-to-all | bytes 524288 | tf_op jit(solution)/shard_map/all_to_all | solution.py:232
  32.8 11.0 %all_to_all.11 = bf16[8,8,2048]{2,1,0:T(8,128)(2,1)S(1)} all-to-all(bf16[8,8,2048]{2,1,0:T(8,128)(2,1)S(1)} %get-tuple-element.33), channel_id=1, replica_groups={{0,4,8,12,2,6,10,14},{1,5,9,13,3,7,11,15},{16,20,24,28,18,22,26,30},{17..., dimensions={0} | all-to-all | bytes 524288 | tf_op jit(solution)/shard_map/all_to_all | solution.py:232
  43.8 1.6 %collective-permute-start.6 = (bf16[64,2176]{1,0:T(8,128)(2,1)S(1)}, bf16[64,2176]{1,0:T(8,128)(2,1)S(1)}, u32[]{:S(2)}, u32[]{:S(2)}) collective-permute-start(bf16[64,2176]{1,0:T(8,128)(2,1)S(1)} %shard_map.96.refs_0_), channel_id=1, source_target_pairs={{0,16},{16,0},{1,17},{17,1},{2,18},{18,2},{3,19},{19,3},{4,20},{20... | collective-permute-start | bytes 835592 | tf_op jit(solution)/shard_map/ppermute | solution.py:208
  45.4 3.5 %shard_map.97.refs_6_ = f32[64,2048]{1,0:T(8,128)S(1)} custom-call(bf16[64,2176]{1,0:T(8,128)(2,1)S(1)} %shard_map.96.refs_0_, bf16[768,2048]{1,0:T(8,128)(2,1)S(1)} %bitcast.12, bf16[768,2048]{1,0:T(8,128)(2,1)S(1)} %bitcast.15, bf16[768,2048]{1,0:T(8,128)(2,1)S(1)} %collective-permute-done.4.refs_4_.refs_3_, ...), custom_call_target="tpu_custom_call" | custom-call | flops 3221225472 | bytes 25165824 | tf_op jit(solution)/shard_map/pallas_call | solution.py:184
  48.8 1.6 %collective-permute-done.6.refs_1_ = bf16[64,2176]{1,0:T(8,128)(2,1)S(1)} collective-permute-done((bf16[64,2176]{1,0:T(8,128)(2,1)S(1)}, bf16[64,2176]{1,0:T(8,128)(2,1)S(1)}, u32[]{:S(2)}, u32[]{:S(2)}) %collective-permute-start.6) | collective-permute-done | bytes 278560 | tf_op jit(solution)/shard_map/ppermute | solution.py:208
  50.4 2.1 %shard_map.98 = (f32[4,8,2048]{2,1,0:T(8,128)S(1)}, bf16[4,8,2048]{2,1,0:T(8,128)(2,1)S(1)}, f32[4,8,2048]{2,1,0:T(8,128)S(1)}, bf16[4,8,2048]{2,1,0:T(8,128)(2,1)S(1)}) custom-call(bf16[64,2176]{1,0:T(8,128)(2,1)S(1)} %shard_map.96.refs_0_, bf16[64,2176]{1,0:T(8,128)(2,1)S(1)} %collective-permute-done.6.refs_1_, bf16[384,2048]{1,0:T(8,128)(2,1)S(1)} %bitcast.17, ...), custom_call_target="tpu_custom_call" | custom-call | flops 1677721600 | bytes 13107200 | tf_op jit(solution)/shard_map/pallas_call | solution.py:184
  52.5 0.6 collective-permute-start.10
  53.2 1.5 %collective-permute-start.9 = (bf16[4,8,2048]{2,1,0:T(8,128)(2,1)S(1)}, bf16[4,8,2048]{2,1,0:T(8,128)(2,1)S(1)}, u32[]{:S(2)}, u32[]{:S(2)}) collective-permute-start(bf16[4,8,2048]{2,1,0:T(8,128)(2,1)S(1)} %get-tuple-element.40), channel_id=1, source_target_pairs={{0,2},{1,3},{2,0},{3,1},{4,6},{5,7},{6,4},{7,5},{8,10},{9,11},{10,... | collective-permute-start | bytes 393224 | tf_op jit(solution)/shard_map/ppermute | solution.py:213
  54.6 2.9 %collective-permute-done.10 = bf16[4,8,2048]{2,1,0:T(8,128)(2,1)S(1)} collective-permute-done((bf16[4,8,2048]{2,1,0:T(8,128)(2,1)S(1)}, bf16[4,8,2048]{2,1,0:T(8,128)(2,1)S(1)}, u32[]{:S(2)}, u32[]{:S(2)}) %collective-permute-start.10) | collective-permute-done | bytes 131104 | tf_op jit(solution)/shard_map/ppermute | solution.py:213
  57.6 1.6 %collective-permute-start.11 = (bf16[4,8,2048]{2,1,0:T(8,128)(2,1)S(1)}, bf16[4,8,2048]{2,1,0:T(8,128)(2,1)S(1)}, u32[]{:S(2)}, u32[]{:S(2)}) collective-permute-start(bf16[4,8,2048]{2,1,0:T(8,128)(2,1)S(1)} %add_convert_fusion), channel_id=1, source_target_pairs={{0,16},{16,0},{1,17},{17,1},{2,18},{18,2},{3,19},{19,3},{4,20},{20... | collective-permute-start | bytes 393224 | tf_op jit(solution)/shard_map/ppermute | solution.py:208
  59.2 3.5 %collective-permute-done.11.refs_2_ = bf16[4,8,2048]{2,1,0:T(8,128)(2,1)S(1)} collective-permute-done((bf16[4,8,2048]{2,1,0:T(8,128)(2,1)S(1)}, bf16[4,8,2048]{2,1,0:T(8,128)(2,1)S(1)}, u32[]{:S(2)}, u32[]{:S(2)}) %collective-permute-start.11) | collective-permute-done | bytes 131104 | tf_op jit(solution)/shard_map/ppermute | solution.py:208
  63.0 1.1 %collective-permute-start.13 = (bf16[8,2048]{1,0:T(8,128)(2,1)S(1)}, bf16[8,2048]{1,0:T(8,128)(2,1)S(1)}, u32[]{:S(2)}, u32[]{:S(2)}) collective-permute-start(bf16[8,2048]{1,0:T(8,128)(2,1)S(1)} %get-tuple-element.45), channel_id=1, source_target_pairs={{0,8},{1,9},{2,10},{3,11},{4,12},{5,13},{6,14},{7,15},{8,0},{9,1},... | collective-permute-start | bytes 98312 | tf_op jit(solution)/shard_map/ppermute | solution.py:213
  64.1 3.1 %collective-permute-start.14 = (bf16[8,2048]{1,0:T(8,128)(2,1)S(1)}, bf16[8,2048]{1,0:T(8,128)(2,1)S(1)}, u32[]{:S(2)}, u32[]{:S(2)}) collective-permute-start(bf16[8,2048]{1,0:T(8,128)(2,1)S(1)} %get-tuple-element.46), channel_id=1, source_target_pairs={{0,4},{1,5},{2,6},{3,7},{4,0},{5,1},{6,2},{7,3},{8,12},{9,13},{10,... | collective-permute-start | bytes 98312 | tf_op jit(solution)/shard_map/ppermute | solution.py:213
  67.1 1.3 %collective-permute-done.12.refs_2_ = bf16[8,2048]{1,0:T(8,128)(2,1)S(1)} collective-permute-done((bf16[8,2048]{1,0:T(8,128)(2,1)S(1)}, bf16[8,2048]{1,0:T(8,128)(2,1)S(1)}, u32[]{:S(2)}, u32[]{:S(2)}) %collective-permute-start.12) | collective-permute-done | bytes 32800 | tf_op jit(solution)/shard_map/ppermute | solution.py:213
  68.5 0.6 collective-permute-done.14.refs_4_
  69.0 0.6 shard_map.100
  (37 shorter events, 1.8 us)
Async XLA Ops:
  0.0 16.0 %collective-permute-start.4 = (bf16[768,2048]{1,0:T(8,128)(2,1)}, bf16[768,2048]{1,0:T(8,128)(2,1)S(1)}, u32[]{:S(2)}, u32[]{:S(2)}) collective-permute-start(bf16[768,2048]{1,0:T(8,128)(2,1)} %bitcast.10), channel_id=1, source_target_pairs={{0,1},{1,0},{2,3},{3,2},{4,5},{5,4},{6,7},{7,6},{8,9},{9,8},{10,11... | collective-permute-start | bytes 9437192 | tf_op jit(solution)/shard_map/ppermute | solution.py:204
  0.5 0.8 %copy-start.4 = (bf16[1,8,2048]{2,1,0:T(8,128)(2,1)S(1)}, bf16[1,8,2048]{2,1,0:T(8,128)(2,1)}, u32[]{:S(2)}) copy-start(bf16[1,8,2048]{2,1,0:T(8,128)(2,1)} %param.9) | copy-start | bytes 98308
  0.5 0.8 %copy-start.5 = (f32[2048]{0:T(1024)S(1)}, f32[2048]{0:T(1024)}, u32[]{:S(2)}) copy-start(f32[2048]{0:T(1024)} %param.10) | copy-start | bytes 24580
  0.5 0.8 %copy-start.6 = (s32[2,1,8,8]{3,2,1,0:T(8,128)S(1)}, s32[2,1,8,8]{3,2,1,0:T(8,128)}, u32[]{:S(2)}) copy-start(s32[2,1,8,8]{3,2,1,0:T(8,128)} %refs_4_.1) | copy-start | bytes 1540
  0.5 0.8 %copy-start.7 = (f32[2,1,8,8]{3,2,1,0:T(8,128)S(1)}, f32[2,1,8,8]{3,2,1,0:T(8,128)}, u32[]{:S(2)}) copy-start(f32[2,1,8,8]{3,2,1,0:T(8,128)} %refs_5_.1) | copy-start | bytes 1540
  0.5 0.8 %copy-start.8 = (s32[1,4]{1,0:T(1,128)S(1)}, s32[1,4]{1,0:T(1,128)}, u32[]{:S(2)}) copy-start(s32[1,4]{1,0:T(1,128)} %refs_6_.1) | copy-start | bytes 52
  0.5 12.0 %copy-start.2 = (bf16[1,384,2048]{2,1,0:T(8,128)(2,1)S(1)}, bf16[1,384,2048]{2,1,0:T(8,128)(2,1)}, u32[]{:S(2)}) copy-start(bf16[1,384,2048]{2,1,0:T(8,128)(2,1)} %param.16) | copy-start | bytes 4718596
  0.5 12.0 %copy-start.3 = (bf16[1,384,2048]{2,1,0:T(8,128)(2,1)S(1)}, bf16[1,384,2048]{2,1,0:T(8,128)(2,1)}, u32[]{:S(2)}) copy-start(bf16[1,384,2048]{2,1,0:T(8,128)(2,1)} %param.17) | copy-start | bytes 4718596
  0.5 15.5 %copy-start = (bf16[1,768,2048]{2,1,0:T(8,128)(2,1)S(1)}, bf16[1,768,2048]{2,1,0:T(8,128)(2,1)}, u32[]{:S(2)}) copy-start(bf16[1,768,2048]{2,1,0:T(8,128)(2,1)} %param.14) | copy-start | bytes 9437188
  0.5 15.5 %copy-start.1 = (bf16[1,768,2048]{2,1,0:T(8,128)(2,1)S(1)}, bf16[1,768,2048]{2,1,0:T(8,128)(2,1)}, u32[]{:S(2)}) copy-start(bf16[1,768,2048]{2,1,0:T(8,128)(2,1)} %param.15) | copy-start | bytes 9437188
  0.5 15.5 %collective-permute-start.5 = (bf16[768,2048]{1,0:T(8,128)(2,1)}, bf16[768,2048]{1,0:T(8,128)(2,1)S(1)}, u32[]{:S(2)}, u32[]{:S(2)}) collective-permute-start(bf16[768,2048]{1,0:T(8,128)(2,1)} %bitcast.13), channel_id=1, source_target_pairs={{0,1},{1,0},{2,3},{3,2},{4,5},{5,4},{6,7},{7,6},{8,9},{9,8},{10,11... | collective-permute-start | bytes 9437192 | tf_op jit(solution)/shard_map/ppermute | solution.py:204
  1.4 6.8 %collective-permute-start = (bf16[8,2176]{1,0:T(8,128)(2,1)S(1)}, bf16[8,2176]{1,0:T(8,128)(2,1)S(1)}, u32[]{:S(2)}, u32[]{:S(2)}) collective-permute-start(bf16[8,2176]{1,0:T(8,128)(2,1)S(1)} %shard_map.92.refs_0_), channel_id=1, source_target_pairs={{0,12},{1,13},{2,14},{3,15},{4,8},{5,9},{6,10},{7,11},{8,4},{9,5},... | collective-permute-start | bytes 104456 | tf_op jit(solution)/shard_map/ppermute | solution.py:213
  6.0 4.8 %collective-permute-start.1 = (bf16[8,2176]{1,0:T(8,128)(2,1)S(1)}, bf16[8,2176]{1,0:T(8,128)(2,1)S(1)}, u32[]{:S(2)}, u32[]{:S(2)}) collective-permute-start(bf16[8,2176]{1,0:T(8,128)(2,1)S(1)} %shard_map.92.refs_0_), channel_id=1, source_target_pairs={{0,8},{1,9},{2,10},{3,11},{4,12},{5,13},{6,14},{7,15},{8,0},{9,1},... | collective-permute-start | bytes 104456 | tf_op jit(solution)/shard_map/ppermute | solution.py:213
  6.0 4.8 %collective-permute-start.2 = (bf16[8,2176]{1,0:T(8,128)(2,1)S(1)}, bf16[8,2176]{1,0:T(8,128)(2,1)S(1)}, u32[]{:S(2)}, u32[]{:S(2)}) collective-permute-start(bf16[8,2176]{1,0:T(8,128)(2,1)S(1)} %shard_map.92.refs_0_), channel_id=1, source_target_pairs={{0,4},{1,5},{2,6},{3,7},{4,0},{5,1},{6,2},{7,3},{8,12},{9,13},{10,... | collective-permute-start | bytes 104456 | tf_op jit(solution)/shard_map/ppermute | solution.py:213
  10.9 5.1 %collective-permute-start.3 = (bf16[32,2176]{1,0:T(8,128)(2,1)S(1)}, bf16[32,2176]{1,0:T(8,128)(2,1)S(1)}, u32[]{:S(2)}, u32[]{:S(2)}) collective-permute-start(bf16[32,2176]{1,0:T(8,128)(2,1)S(1)} %bitcast.21), channel_id=1, source_target_pairs={{0,2},{1,3},{2,0},{3,1},{4,6},{5,7},{6,4},{7,5},{8,10},{9,11},{10,... | collective-permute-start | bytes 417800 | tf_op jit(solution)/shard_map/ppermute | solution.py:213
  12.5 37.9 %collective-permute-start.7 = (bf16[384,2048]{1,0:T(8,128)(2,1)S(1)}, bf16[384,2048]{1,0:T(8,128)(2,1)S(1)}, u32[]{:S(2)}, u32[]{:S(2)}) collective-permute-start(bf16[384,2048]{1,0:T(8,128)(2,1)S(1)} %bitcast.16), channel_id=1, source_target_pairs={{0,1},{1,0},{2,3},{3,2},{4,5},{5,4},{6,7},{7,6},{8,9},{9,8},{10,11... | collective-permute-start | bytes 4718600 | tf_op jit(solution)/shard_map/ppermute | solution.py:204
  12.5 37.9 %collective-permute-start.8 = (bf16[384,2048]{1,0:T(8,128)(2,1)S(1)}, bf16[384,2048]{1,0:T(8,128)(2,1)S(1)}, u32[]{:S(2)}, u32[]{:S(2)}) collective-permute-start(bf16[384,2048]{1,0:T(8,128)(2,1)S(1)} %bitcast.18), channel_id=1, source_target_pairs={{0,1},{1,0},{2,3},{3,2},{4,5},{5,4},{6,7},{7,6},{8,9},{9,8},{10,11... | collective-permute-start | bytes 4718600 | tf_op jit(solution)/shard_map/ppermute | solution.py:204
  43.8 6.6 %collective-permute-start.6 = (bf16[64,2176]{1,0:T(8,128)(2,1)S(1)}, bf16[64,2176]{1,0:T(8,128)(2,1)S(1)}, u32[]{:S(2)}, u32[]{:S(2)}) collective-permute-start(bf16[64,2176]{1,0:T(8,128)(2,1)S(1)} %shard_map.96.refs_0_), channel_id=1, source_target_pairs={{0,16},{16,0},{1,17},{17,1},{2,18},{18,2},{3,19},{19,3},{4,20},{20... | collective-permute-start | bytes 835592 | tf_op jit(solution)/shard_map/ppermute | solution.py:208
  52.5 5.0 %collective-permute-start.10 = (bf16[4,8,2048]{2,1,0:T(8,128)(2,1)S(1)}, bf16[4,8,2048]{2,1,0:T(8,128)(2,1)S(1)}, u32[]{:S(2)}, u32[]{:S(2)}) collective-permute-start(bf16[4,8,2048]{2,1,0:T(8,128)(2,1)S(1)} %get-tuple-element.42), channel_id=1, source_target_pairs={{0,2},{1,3},{2,0},{3,1},{4,6},{5,7},{6,4},{7,5},{8,10},{9,11},{10,... | collective-permute-start | bytes 393224 | tf_op jit(solution)/shard_map/ppermute | solution.py:213
  53.2 6.0 %collective-permute-start.9 = (bf16[4,8,2048]{2,1,0:T(8,128)(2,1)S(1)}, bf16[4,8,2048]{2,1,0:T(8,128)(2,1)S(1)}, u32[]{:S(2)}, u32[]{:S(2)}) collective-permute-start(bf16[4,8,2048]{2,1,0:T(8,128)(2,1)S(1)} %get-tuple-element.40), channel_id=1, source_target_pairs={{0,2},{1,3},{2,0},{3,1},{4,6},{5,7},{6,4},{7,5},{8,10},{9,11},{10,... | collective-permute-start | bytes 393224 | tf_op jit(solution)/shard_map/ppermute | solution.py:213
  57.6 5.0 %collective-permute-start.11 = (bf16[4,8,2048]{2,1,0:T(8,128)(2,1)S(1)}, bf16[4,8,2048]{2,1,0:T(8,128)(2,1)S(1)}, u32[]{:S(2)}, u32[]{:S(2)}) collective-permute-start(bf16[4,8,2048]{2,1,0:T(8,128)(2,1)S(1)} %add_convert_fusion), channel_id=1, source_target_pairs={{0,16},{16,0},{1,17},{17,1},{2,18},{18,2},{3,19},{19,3},{4,20},{20... | collective-permute-start | bytes 393224 | tf_op jit(solution)/shard_map/ppermute | solution.py:208
  62.7 5.8 %collective-permute-start.12 = (bf16[8,2048]{1,0:T(8,128)(2,1)S(1)}, bf16[8,2048]{1,0:T(8,128)(2,1)S(1)}, u32[]{:S(2)}, u32[]{:S(2)}) collective-permute-start(bf16[8,2048]{1,0:T(8,128)(2,1)S(1)} %get-tuple-element.44), channel_id=1, source_target_pairs={{0,12},{1,13},{2,14},{3,15},{4,8},{5,9},{6,10},{7,11},{8,4},{9,5},... | collective-permute-start | bytes 98312 | tf_op jit(solution)/shard_map/ppermute | solution.py:213
  63.0 5.5 %collective-permute-start.13 = (bf16[8,2048]{1,0:T(8,128)(2,1)S(1)}, bf16[8,2048]{1,0:T(8,128)(2,1)S(1)}, u32[]{:S(2)}, u32[]{:S(2)}) collective-permute-start(bf16[8,2048]{1,0:T(8,128)(2,1)S(1)} %get-tuple-element.45), channel_id=1, source_target_pairs={{0,8},{1,9},{2,10},{3,11},{4,12},{5,13},{6,14},{7,15},{8,0},{9,1},... | collective-permute-start | bytes 98312 | tf_op jit(solution)/shard_map/ppermute | solution.py:213
  64.1 5.0 %collective-permute-start.14 = (bf16[8,2048]{1,0:T(8,128)(2,1)S(1)}, bf16[8,2048]{1,0:T(8,128)(2,1)S(1)}, u32[]{:S(2)}, u32[]{:S(2)}) collective-permute-start(bf16[8,2048]{1,0:T(8,128)(2,1)S(1)} %get-tuple-element.46), channel_id=1, source_target_pairs={{0,4},{1,5},{2,6},{3,7},{4,0},{5,1},{6,2},{7,3},{8,12},{9,13},{10,... | collective-permute-start | bytes 98312 | tf_op jit(solution)/shard_map/ppermute | solution.py:213

commit v25 on v24

--- a/solution.py
+++ b/solution.py
@@ -163,7 +163,7 @@
         place = lax.rem(chip, 2) * (chips // 2) + lax.div(chip, 2)
         span = slice(block * count, (block + 1) * count)
         out[place] = total[span].astype(out.dtype)
-        tables_out[place] = table[span]
+        tables_out[place] = table.astype(jnp.float32)[span].astype(tables_out.dtype)
 
 
 def mlp_kernel(experts, step, fresh, set_count, *refs):
@@ -174,29 +174,24 @@
         out[...] = total[i * count : (i + 1) * count].astype(out.dtype)
 
 
-def on_vmem(kernel, inputs, outputs, limit=4 * MIB, cost=None, after=()):
+def on_vmem(kernel, inputs, outputs, limit=4 * MIB, cost=None):
     in_vmem = pl.BlockSpec(memory_space=pltpu.VMEM)
-    count = len(inputs)
-
-    def body(*refs):
-        kernel(*refs[:count], *refs[count + len(after) :])
-
     return pl.pallas_call(
-        body,
+        kernel,
         out_shape=[jax.ShapeDtypeStruct(shape, kind) for shape, kind in outputs],
-        in_specs=[in_vmem] * count + [pl.BlockSpec(memory_space=pl.ANY)] * len(after),
+        in_specs=[in_vmem] * len(inputs),
         out_specs=[in_vmem] * len(outputs),
         compiler_params=pltpu.CompilerParams(vmem_limit_bytes=limit),
         cost_estimate=cost,
-    )(*inputs, *after)
-
-
-def run_mlp(kernel, row_sets, weights, outputs, after=()):
+    )(*inputs)
+
+
+def run_mlp(kernel, row_sets, weights, outputs):
     size = sum(part.size for part in weights)
     cost = pl.CostEstimate(
         flops=4 * MATMUL_ROWS * size, bytes_accessed=4 * size, transcendentals=0
     )
-    return on_vmem(kernel, tuple(row_sets) + tuple(weights), outputs, 8 * MIB, cost, after)
+    return on_vmem(kernel, tuple(row_sets) + tuple(weights), outputs, 8 * MIB, cost)
 
 
 def swap_core(value):
@@ -292,7 +287,7 @@
             )
             away = away_kept + swap_chip(away_sent, 1).astype(jnp.float32)
             away = swap_group(away.astype(jnp.bfloat16))
-            distances = tuple(range(chips // 2 - 1, 0, -1))
+            distances = tuple(range(1, chips // 2))
             own, *sent = on_vmem(
                 functools.partial(part_kernel, distances),
                 (kept, swap_chip(sent, 1), away),

time: 69.9 us -> 70.2 us (level)
  no operation moved by 1% of the time
where the time goes in v25:
time: 70.2 us; the launch traced here: 70 us
  blocking collectives  24.1 us (34%)
  starting transfers between devices  17.6 us (25%)
  waiting for transfers between devices  17.5 us (25%)
  Pallas kernels  10 us (14%)
    all_to_all x2, blocking collectives, spread(): lax.all_to_all(blocks, 'expert', 0, 0, axis_index_groups=groups, tiled=True)  24.1 us
    ppermute x9, starting transfers between devices, swap_chip(): lax.ppermute(value, 'expert', [(i, i ^ 2 * distance) for i in range(size)])  13.4 us
    ppermute x9, waiting for transfers between devices, swap_chip(): lax.ppermute(value, 'expert', [(i, i ^ 2 * distance) for i in range(size)])  12.4 us
    pallas_call x10, Pallas kernels, on_vmem(): pl.pallas_call(kernel, out_shape=[jax.ShapeDtypeStruct(shape, kind) for s...  10 us
    ppermute x2, waiting for transfers between devices, swap_group(): return lax.ppermute(value, 'group', [(0, 1), (1, 0)])  5.04 us
    ppermute x2, starting transfers between devices, swap_group(): return lax.ppermute(value, 'group', [(0, 1), (1, 0)])  3.13 us
  transfers between devices with their start and end apart: 15, of which 8 were waited for; matrix products, arithmetic and copies ran while one was open for 0% of the time, Pallas kernels for 10%

profile of v25, /device:TPU:0, one launch (start us, length us, event | category | flops | bytes accessed | tf_op | source)
XLA Modules:
  0.0 70.0 jit_solution(17168317721906575362)
XLA Ops:
  0.6 0.6 copy-done.4
  1.4 4.7 %collective-permute-start = (bf16[8,2176]{1,0:T(8,128)(2,1)S(1)}, bf16[8,2176]{1,0:T(8,128)(2,1)S(1)}, u32[]{:S(2)}, u32[]{:S(2)}) collective-permute-start(bf16[8,2176]{1,0:T(8,128)(2,1)S(1)} %shard_map.92.refs_0_), channel_id=1, source_target_pairs={{0,12},{1,13},{2,14},{3,15},{4,8},{5,9},{6,10},{7,11},{8,4},{9,5},... | collective-permute-start | bytes 104456 | tf_op jit(solution)/shard_map/ppermute | solution.py:208
  6.0 0.6 collective-permute-start.2
  6.7 1.5 %collective-permute-done.refs_1_ = bf16[8,2176]{1,0:T(8,128)(2,1)S(1)} collective-permute-done((bf16[8,2176]{1,0:T(8,128)(2,1)S(1)}, bf16[8,2176]{1,0:T(8,128)(2,1)S(1)}, u32[]{:S(2)}, u32[]{:S(2)}) %collective-permute-start) | collective-permute-done | bytes 34848 | tf_op jit(solution)/shard_map/ppermute | solution.py:208
  8.1 2.7 %collective-permute-done.1.refs_2_ = bf16[8,2176]{1,0:T(8,128)(2,1)S(1)} collective-permute-done((bf16[8,2176]{1,0:T(8,128)(2,1)S(1)}, bf16[8,2176]{1,0:T(8,128)(2,1)S(1)}, u32[]{:S(2)}, u32[]{:S(2)}) %collective-permute-start.1) | collective-permute-done | bytes 34848 | tf_op jit(solution)/shard_map/ppermute | solution.py:208
  10.9 1.6 %collective-permute-start.3 = (bf16[32,2176]{1,0:T(8,128)(2,1)S(1)}, bf16[32,2176]{1,0:T(8,128)(2,1)S(1)}, u32[]{:S(2)}, u32[]{:S(2)}) collective-permute-start(bf16[32,2176]{1,0:T(8,128)(2,1)S(1)} %bitcast.21), channel_id=1, source_target_pairs={{0,2},{1,3},{2,0},{3,1},{4,6},{5,7},{6,4},{7,5},{8,10},{9,11},{10,... | collective-permute-start | bytes 417800 | tf_op jit(solution)/shard_map/ppermute | solution.py:208
  12.5 0.5 collective-permute-start.8
  13.0 3.0 %collective-permute-done.3.across = bf16[32,2176]{1,0:T(8,128)(2,1)S(1)} collective-permute-done((bf16[32,2176]{1,0:T(8,128)(2,1)S(1)}, bf16[32,2176]{1,0:T(8,128)(2,1)S(1)}, u32[]{:S(2)}, u32[]{:S(2)}) %collective-permute-start.3) | collective-permute-done | bytes 139296 | tf_op jit(solution)/shard_map/ppermute | solution.py:208
  16.0 3.5 %shard_map.94 = (bf16[8,8,2048]{2,1,0:T(8,128)(2,1)S(1)}, bf16[8,8,128]{2,1,0:T(8,128)(2,1)S(1)}) custom-call(bf16[32,2176]{1,0:T(8,128)(2,1)S(1)} %bitcast.22, bf16[32,2176]{1,0:T(8,128)(2,1)S(1)} %collective-permute-done.3.across, bf16[768,2048]{1,0:T(8,128)(2,1)S(1)} %bitcast.11, bf16[768,2048]{1,0:T(8,128)(2,1)S(1)} %bitcast.14, ...), custom_call_target="tpu_custom_call" | custom-call | flops 3221225472 | bytes 25165824 | tf_op jit(solution)/shard_map/pallas_call | solution.py:179
  19.5 13.1 %all_to_all.10.returned = bf16[8,8,2048]{2,1,0:T(8,128)(2,1)S(1)} all-to-all(bf16[8,8,2048]{2,1,0:T(8,128)(2,1)S(1)} %get-tuple-element.31), channel_id=1, replica_groups={{0,4,8,12,2,6,10,14},{1,5,9,13,3,7,11,15},{16,20,24,28,18,22,26,30},{17..., dimensions={0} | all-to-all | bytes 524288 | tf_op jit(solution)/shard_map/all_to_all | solution.py:227
  32.8 11.0 %all_to_all.11 = bf16[8,8,2048]{2,1,0:T(8,128)(2,1)S(1)} all-to-all(bf16[8,8,2048]{2,1,0:T(8,128)(2,1)S(1)} %get-tuple-element.33), channel_id=1, replica_groups={{0,4,8,12,2,6,10,14},{1,5,9,13,3,7,11,15},{16,20,24,28,18,22,26,30},{17..., dimensions={0} | all-to-all | bytes 524288 | tf_op jit(solution)/shard_map/all_to_all | solution.py:227
  43.8 1.6 %collective-permute-start.6 = (bf16[64,2176]{1,0:T(8,128)(2,1)S(1)}, bf16[64,2176]{1,0:T(8,128)(2,1)S(1)}, u32[]{:S(2)}, u32[]{:S(2)}) collective-permute-start(bf16[64,2176]{1,0:T(8,128)(2,1)S(1)} %shard_map.96.refs_0_.rows), channel_id=1, source_target_pairs={{0,16},{16,0},{1,17},{17,1},{2,18},{18,2},{3,19},{19,3},{4,20},{20... | collective-permute-start | bytes 835592 | tf_op jit(solution)/shard_map/ppermute | solution.py:203
  45.4 3.5 %shard_map.97.refs_4_ = f32[64,2048]{1,0:T(8,128)S(1)} custom-call(bf16[64,2176]{1,0:T(8,128)(2,1)S(1)} %shard_map.96.refs_0_.rows, bf16[768,2048]{1,0:T(8,128)(2,1)S(1)} %bitcast.12, bf16[768,2048]{1,0:T(8,128)(2,1)S(1)} %bitcast.15, bf16[768,2048]{1,0:T(8,128)(2,1)S(1)} %collective-permute-done.4.refs_2_.refs_3_, ...), custom_call_target="tpu_custom_call" | custom-call | flops 3221225472 | bytes 25165824 | tf_op jit(solution)/shard_map/pallas_call | solution.py:179
  48.8 1.6 %collective-permute-done.6.other = bf16[64,2176]{1,0:T(8,128)(2,1)S(1)} collective-permute-done((bf16[64,2176]{1,0:T(8,128)(2,1)S(1)}, bf16[64,2176]{1,0:T(8,128)(2,1)S(1)}, u32[]{:S(2)}, u32[]{:S(2)}) %collective-permute-start.6) | collective-permute-done | bytes 278560 | tf_op jit(solution)/shard_map/ppermute | solution.py:203
  50.4 2.1 %shard_map.98 = (f32[4,8,2048]{2,1,0:T(8,128)S(1)}, bf16[4,8,2048]{2,1,0:T(8,128)(2,1)S(1)}, f32[4,8,2048]{2,1,0:T(8,128)S(1)}, bf16[4,8,2048]{2,1,0:T(8,128)(2,1)S(1)}) custom-call(bf16[64,2176]{1,0:T(8,128)(2,1)S(1)} %shard_map.96.refs_0_.rows, bf16[64,2176]{1,0:T(8,128)(2,1)S(1)} %collective-permute-done.6.other, bf16[384,2048]{1,0:T(8,128)(2,1)S(1)} %bitcast.17, ...), custom_call_target="tpu_custom_call" | custom-call | flops 1677721600 | bytes 13107200 | tf_op jit(solution)/shard_map/pallas_call | solution.py:179
  52.5 0.6 collective-permute-start.10
  53.2 1.5 %collective-permute-start.9 = (bf16[4,8,2048]{2,1,0:T(8,128)(2,1)S(1)}, bf16[4,8,2048]{2,1,0:T(8,128)(2,1)S(1)}, u32[]{:S(2)}, u32[]{:S(2)}) collective-permute-start(bf16[4,8,2048]{2,1,0:T(8,128)(2,1)S(1)} %get-tuple-element.40), channel_id=1, source_target_pairs={{0,2},{1,3},{2,0},{3,1},{4,6},{5,7},{6,4},{7,5},{8,10},{9,11},{10,... | collective-permute-start | bytes 393224 | tf_op jit(solution)/shard_map/ppermute | solution.py:208
  54.6 2.9 %collective-permute-done.10 = bf16[4,8,2048]{2,1,0:T(8,128)(2,1)S(1)} collective-permute-done((bf16[4,8,2048]{2,1,0:T(8,128)(2,1)S(1)}, bf16[4,8,2048]{2,1,0:T(8,128)(2,1)S(1)}, u32[]{:S(2)}, u32[]{:S(2)}) %collective-permute-start.10) | collective-permute-done | bytes 131104 | tf_op jit(solution)/shard_map/ppermute | solution.py:208
  57.6 1.6 %collective-permute-start.11 = (bf16[4,8,2048]{2,1,0:T(8,128)(2,1)S(1)}, bf16[4,8,2048]{2,1,0:T(8,128)(2,1)S(1)}, u32[]{:S(2)}, u32[]{:S(2)}) collective-permute-start(bf16[4,8,2048]{2,1,0:T(8,128)(2,1)S(1)} %add_convert_fusion), channel_id=1, source_target_pairs={{0,16},{16,0},{1,17},{17,1},{2,18},{18,2},{3,19},{19,3},{4,20},{20... | collective-permute-start | bytes 393224 | tf_op jit(solution)/shard_map/ppermute | solution.py:203
  59.2 3.5 %collective-permute-done.11.away = bf16[4,8,2048]{2,1,0:T(8,128)(2,1)S(1)} collective-permute-done((bf16[4,8,2048]{2,1,0:T(8,128)(2,1)S(1)}, bf16[4,8,2048]{2,1,0:T(8,128)(2,1)S(1)}, u32[]{:S(2)}, u32[]{:S(2)}) %collective-permute-start.11) | collective-permute-done | bytes 131104 | tf_op jit(solution)/shard_map/ppermute | solution.py:203
  62.8 0.8 %collective-permute-start.13 = (bf16[8,2048]{1,0:T(8,128)(2,1)S(1)}, bf16[8,2048]{1,0:T(8,128)(2,1)S(1)}, u32[]{:S(2)}, u32[]{:S(2)}) collective-permute-start(bf16[8,2048]{1,0:T(8,128)(2,1)S(1)} %get-tuple-element.45), channel_id=1, source_target_pairs={{0,8},{1,9},{2,10},{3,11},{4,12},{5,13},{6,14},{7,15},{8,0},{9,1},... | collective-permute-start | bytes 98312 | tf_op jit(solution)/shard_map/ppermute | solution.py:208
  63.5 3.6 %collective-permute-start.14 = (bf16[8,2048]{1,0:T(8,128)(2,1)S(1)}, bf16[8,2048]{1,0:T(8,128)(2,1)S(1)}, u32[]{:S(2)}, u32[]{:S(2)}) collective-permute-start(bf16[8,2048]{1,0:T(8,128)(2,1)S(1)} %get-tuple-element.46), channel_id=1, source_target_pairs={{0,12},{1,13},{2,14},{3,15},{4,8},{5,9},{6,10},{7,11},{8,4},{9,5},... | collective-permute-start | bytes 98312 | tf_op jit(solution)/shard_map/ppermute | solution.py:208
  67.7 1.7 %collective-permute-done.14.refs_2_ = bf16[8,2048]{1,0:T(8,128)(2,1)S(1)} collective-permute-done((bf16[8,2048]{1,0:T(8,128)(2,1)S(1)}, bf16[8,2048]{1,0:T(8,128)(2,1)S(1)}, u32[]{:S(2)}, u32[]{:S(2)}) %collective-permute-start.14) | collective-permute-done | bytes 32800 | tf_op jit(solution)/shard_map/ppermute | solution.py:208
  69.4 0.6 shard_map.100
  (37 shorter events, 1.6 us)
Async XLA Ops:
  0.0 16.0 %collective-permute-start.4 = (bf16[768,2048]{1,0:T(8,128)(2,1)}, bf16[768,2048]{1,0:T(8,128)(2,1)S(1)}, u32[]{:S(2)}, u32[]{:S(2)}) collective-permute-start(bf16[768,2048]{1,0:T(8,128)(2,1)} %bitcast.10), channel_id=1, source_target_pairs={{0,1},{1,0},{2,3},{3,2},{4,5},{5,4},{6,7},{7,6},{8,9},{9,8},{10,11... | collective-permute-start | bytes 9437192 | tf_op jit(solution)/shard_map/ppermute | solution.py:199
  0.5 0.8 %copy-start.4 = (bf16[1,8,2048]{2,1,0:T(8,128)(2,1)S(1)}, bf16[1,8,2048]{2,1,0:T(8,128)(2,1)}, u32[]{:S(2)}) copy-start(bf16[1,8,2048]{2,1,0:T(8,128)(2,1)} %param.9) | copy-start | bytes 98308
  0.5 0.8 %copy-start.5 = (f32[2048]{0:T(1024)S(1)}, f32[2048]{0:T(1024)}, u32[]{:S(2)}) copy-start(f32[2048]{0:T(1024)} %param.10) | copy-start | bytes 24580
  0.5 0.8 %copy-start.6 = (s32[2,1,8,8]{3,2,1,0:T(8,128)S(1)}, s32[2,1,8,8]{3,2,1,0:T(8,128)}, u32[]{:S(2)}) copy-start(s32[2,1,8,8]{3,2,1,0:T(8,128)} %routes.1) | copy-start | bytes 1540
  0.5 0.8 %copy-start.7 = (f32[2,1,8,8]{3,2,1,0:T(8,128)S(1)}, f32[2,1,8,8]{3,2,1,0:T(8,128)}, u32[]{:S(2)}) copy-start(f32[2,1,8,8]{3,2,1,0:T(8,128)} %scales.1) | copy-start | bytes 1540
  0.5 0.8 %copy-start.8 = (s32[1,4]{1,0:T(1,128)S(1)}, s32[1,4]{1,0:T(1,128)}, u32[]{:S(2)}) copy-start(s32[1,4]{1,0:T(1,128)} %changed.1) | copy-start | bytes 52
  0.5 12.0 %copy-start.2 = (bf16[1,384,2048]{2,1,0:T(8,128)(2,1)S(1)}, bf16[1,384,2048]{2,1,0:T(8,128)(2,1)}, u32[]{:S(2)}) copy-start(bf16[1,384,2048]{2,1,0:T(8,128)(2,1)} %param.16) | copy-start | bytes 4718596
  0.5 12.0 %copy-start.3 = (bf16[1,384,2048]{2,1,0:T(8,128)(2,1)S(1)}, bf16[1,384,2048]{2,1,0:T(8,128)(2,1)}, u32[]{:S(2)}) copy-start(bf16[1,384,2048]{2,1,0:T(8,128)(2,1)} %param.17) | copy-start | bytes 4718596
  0.5 15.5 %copy-start = (bf16[1,768,2048]{2,1,0:T(8,128)(2,1)S(1)}, bf16[1,768,2048]{2,1,0:T(8,128)(2,1)}, u32[]{:S(2)}) copy-start(bf16[1,768,2048]{2,1,0:T(8,128)(2,1)} %param.14) | copy-start | bytes 9437188
  0.5 15.5 %copy-start.1 = (bf16[1,768,2048]{2,1,0:T(8,128)(2,1)S(1)}, bf16[1,768,2048]{2,1,0:T(8,128)(2,1)}, u32[]{:S(2)}) copy-start(bf16[1,768,2048]{2,1,0:T(8,128)(2,1)} %param.15) | copy-start | bytes 9437188
  0.5 15.5 %collective-permute-start.5 = (bf16[768,2048]{1,0:T(8,128)(2,1)}, bf16[768,2048]{1,0:T(8,128)(2,1)S(1)}, u32[]{:S(2)}, u32[]{:S(2)}) collective-permute-start(bf16[768,2048]{1,0:T(8,128)(2,1)} %bitcast.13), channel_id=1, source_target_pairs={{0,1},{1,0},{2,3},{3,2},{4,5},{5,4},{6,7},{7,6},{8,9},{9,8},{10,11... | collective-permute-start | bytes 9437192 | tf_op jit(solution)/shard_map/ppermute | solution.py:199
  1.4 6.8 %collective-permute-start = (bf16[8,2176]{1,0:T(8,128)(2,1)S(1)}, bf16[8,2176]{1,0:T(8,128)(2,1)S(1)}, u32[]{:S(2)}, u32[]{:S(2)}) collective-permute-start(bf16[8,2176]{1,0:T(8,128)(2,1)S(1)} %shard_map.92.refs_0_), channel_id=1, source_target_pairs={{0,12},{1,13},{2,14},{3,15},{4,8},{5,9},{6,10},{7,11},{8,4},{9,5},... | collective-permute-start | bytes 104456 | tf_op jit(solution)/shard_map/ppermute | solution.py:208
  6.0 4.8 %collective-permute-start.1 = (bf16[8,2176]{1,0:T(8,128)(2,1)S(1)}, bf16[8,2176]{1,0:T(8,128)(2,1)S(1)}, u32[]{:S(2)}, u32[]{:S(2)}) collective-permute-start(bf16[8,2176]{1,0:T(8,128)(2,1)S(1)} %shard_map.92.refs_0_), channel_id=1, source_target_pairs={{0,8},{1,9},{2,10},{3,11},{4,12},{5,13},{6,14},{7,15},{8,0},{9,1},... | collective-permute-start | bytes 104456 | tf_op jit(solution)/shard_map/ppermute | solution.py:208
  6.0 4.8 %collective-permute-start.2 = (bf16[8,2176]{1,0:T(8,128)(2,1)S(1)}, bf16[8,2176]{1,0:T(8,128)(2,1)S(1)}, u32[]{:S(2)}, u32[]{:S(2)}) collective-permute-start(bf16[8,2176]{1,0:T(8,128)(2,1)S(1)} %shard_map.92.refs_0_), channel_id=1, source_target_pairs={{0,4},{1,5},{2,6},{3,7},{4,0},{5,1},{6,2},{7,3},{8,12},{9,13},{10,... | collective-permute-start | bytes 104456 | tf_op jit(solution)/shard_map/ppermute | solution.py:208
  10.9 5.1 %collective-permute-start.3 = (bf16[32,2176]{1,0:T(8,128)(2,1)S(1)}, bf16[32,2176]{1,0:T(8,128)(2,1)S(1)}, u32[]{:S(2)}, u32[]{:S(2)}) collective-permute-start(bf16[32,2176]{1,0:T(8,128)(2,1)S(1)} %bitcast.21), channel_id=1, source_target_pairs={{0,2},{1,3},{2,0},{3,1},{4,6},{5,7},{6,4},{7,5},{8,10},{9,11},{10,... | collective-permute-start | bytes 417800 | tf_op jit(solution)/shard_map/ppermute | solution.py:208
  12.5 37.9 %collective-permute-start.7 = (bf16[384,2048]{1,0:T(8,128)(2,1)S(1)}, bf16[384,2048]{1,0:T(8,128)(2,1)S(1)}, u32[]{:S(2)}, u32[]{:S(2)}) collective-permute-start(bf16[384,2048]{1,0:T(8,128)(2,1)S(1)} %bitcast.16), channel_id=1, source_target_pairs={{0,1},{1,0},{2,3},{3,2},{4,5},{5,4},{6,7},{7,6},{8,9},{9,8},{10,11... | collective-permute-start | bytes 4718600 | tf_op jit(solution)/shard_map/ppermute | solution.py:199
  12.5 37.9 %collective-permute-start.8 = (bf16[384,2048]{1,0:T(8,128)(2,1)S(1)}, bf16[384,2048]{1,0:T(8,128)(2,1)S(1)}, u32[]{:S(2)}, u32[]{:S(2)}) collective-permute-start(bf16[384,2048]{1,0:T(8,128)(2,1)S(1)} %bitcast.18), channel_id=1, source_target_pairs={{0,1},{1,0},{2,3},{3,2},{4,5},{5,4},{6,7},{7,6},{8,9},{9,8},{10,11... | collective-permute-start | bytes 4718600 | tf_op jit(solution)/shard_map/ppermute | solution.py:199
  43.8 6.6 %collective-permute-start.6 = (bf16[64,2176]{1,0:T(8,128)(2,1)S(1)}, bf16[64,2176]{1,0:T(8,128)(2,1)S(1)}, u32[]{:S(2)}, u32[]{:S(2)}) collective-permute-start(bf16[64,2176]{1,0:T(8,128)(2,1)S(1)} %shard_map.96.refs_0_.rows), channel_id=1, source_target_pairs={{0,16},{16,0},{1,17},{17,1},{2,18},{18,2},{3,19},{19,3},{4,20},{20... | collective-permute-start | bytes 835592 | tf_op jit(solution)/shard_map/ppermute | solution.py:203
  52.5 5.0 %collective-permute-start.10 = (bf16[4,8,2048]{2,1,0:T(8,128)(2,1)S(1)}, bf16[4,8,2048]{2,1,0:T(8,128)(2,1)S(1)}, u32[]{:S(2)}, u32[]{:S(2)}) collective-permute-start(bf16[4,8,2048]{2,1,0:T(8,128)(2,1)S(1)} %get-tuple-element.42), channel_id=1, source_target_pairs={{0,2},{1,3},{2,0},{3,1},{4,6},{5,7},{6,4},{7,5},{8,10},{9,11},{10,... | collective-permute-start | bytes 393224 | tf_op jit(solution)/shard_map/ppermute | solution.py:208
  53.2 6.0 %collective-permute-start.9 = (bf16[4,8,2048]{2,1,0:T(8,128)(2,1)S(1)}, bf16[4,8,2048]{2,1,0:T(8,128)(2,1)S(1)}, u32[]{:S(2)}, u32[]{:S(2)}) collective-permute-start(bf16[4,8,2048]{2,1,0:T(8,128)(2,1)S(1)} %get-tuple-element.40), channel_id=1, source_target_pairs={{0,2},{1,3},{2,0},{3,1},{4,6},{5,7},{6,4},{7,5},{8,10},{9,11},{10,... | collective-permute-start | bytes 393224 | tf_op jit(solution)/shard_map/ppermute | solution.py:208
  57.6 5.0 %collective-permute-start.11 = (bf16[4,8,2048]{2,1,0:T(8,128)(2,1)S(1)}, bf16[4,8,2048]{2,1,0:T(8,128)(2,1)S(1)}, u32[]{:S(2)}, u32[]{:S(2)}) collective-permute-start(bf16[4,8,2048]{2,1,0:T(8,128)(2,1)S(1)} %add_convert_fusion), channel_id=1, source_target_pairs={{0,16},{16,0},{1,17},{17,1},{2,18},{18,2},{3,19},{19,3},{4,20},{20... | collective-permute-start | bytes 393224 | tf_op jit(solution)/shard_map/ppermute | solution.py:203
  62.7 4.5 %collective-permute-start.12 = (bf16[8,2048]{1,0:T(8,128)(2,1)S(1)}, bf16[8,2048]{1,0:T(8,128)(2,1)S(1)}, u32[]{:S(2)}, u32[]{:S(2)}) collective-permute-start(bf16[8,2048]{1,0:T(8,128)(2,1)S(1)} %get-tuple-element.44), channel_id=1, source_target_pairs={{0,4},{1,5},{2,6},{3,7},{4,0},{5,1},{6,2},{7,3},{8,12},{9,13},{10,... | collective-permute-start | bytes 98312 | tf_op jit(solution)/shard_map/ppermute | solution.py:208
  62.8 4.9 %collective-permute-start.13 = (bf16[8,2048]{1,0:T(8,128)(2,1)S(1)}, bf16[8,2048]{1,0:T(8,128)(2,1)S(1)}, u32[]{:S(2)}, u32[]{:S(2)}) collective-permute-start(bf16[8,2048]{1,0:T(8,128)(2,1)S(1)} %get-tuple-element.45), channel_id=1, source_target_pairs={{0,8},{1,9},{2,10},{3,11},{4,12},{5,13},{6,14},{7,15},{8,0},{9,1},... | collective-permute-start | bytes 98312 | tf_op jit(solution)/shard_map/ppermute | solution.py:208
  63.5 5.9 %collective-permute-start.14 = (bf16[8,2048]{1,0:T(8,128)(2,1)S(1)}, bf16[8,2048]{1,0:T(8,128)(2,1)S(1)}, u32[]{:S(2)}, u32[]{:S(2)}) collective-permute-start(bf16[8,2048]{1,0:T(8,128)(2,1)S(1)} %get-tuple-element.46), channel_id=1, source_target_pairs={{0,12},{1,13},{2,14},{3,15},{4,8},{5,9},{6,10},{7,11},{8,4},{9,5},... | collective-permute-start | bytes 98312 | tf_op jit(solution)/shard_map/ppermute | solution.py:208

commit v26 on v25

--- a/solution.py
+++ b/solution.py
@@ -287,7 +287,7 @@
             )
             away = away_kept + swap_chip(away_sent, 1).astype(jnp.float32)
             away = swap_group(away.astype(jnp.bfloat16))
-            distances = tuple(range(1, chips // 2))
+            distances = tuple(range(chips // 2 - 1, 0, -1))
             own, *sent = on_vmem(
                 functools.partial(part_kernel, distances),
                 (kept, swap_chip(sent, 1), away),

time: 70.2 us -> 69.9 us (level)
  no operation moved by 1% of the time
where the time goes in v26:
time: 69.9 us; the launch traced here: 69.7 us
  blocking collectives  24.1 us (34%)
  starting transfers between devices  17.7 us (25%)
  waiting for transfers between devices  17.1 us (24%)
  Pallas kernels  10 us (14%)
    all_to_all x2, blocking collectives, spread(): lax.all_to_all(blocks, 'expert', 0, 0, axis_index_groups=groups, tiled=True)  24.1 us
    ppermute x9, starting transfers between devices, swap_chip(): lax.ppermute(value, 'expert', [(i, i ^ 2 * distance) for i in range(size)])  13.4 us
    ppermute x9, waiting for transfers between devices, swap_chip(): lax.ppermute(value, 'expert', [(i, i ^ 2 * distance) for i in range(size)])  12 us
    pallas_call x10, Pallas kernels, on_vmem(): pl.pallas_call(kernel, out_shape=[jax.ShapeDtypeStruct(shape, kind) for s...  10 us
    ppermute x2, waiting for transfers between devices, swap_group(): return lax.ppermute(value, 'group', [(0, 1), (1, 0)])  5.04 us
    ppermute x2, starting transfers between devices, swap_group(): return lax.ppermute(value, 'group', [(0, 1), (1, 0)])  3.13 us
  transfers between devices with their start and end apart: 15, of which 8 were waited for; matrix products, arithmetic and copies ran while one was open for 0% of the time, Pallas kernels for 10%

profile of v26, /device:TPU:0, one launch (start us, length us, event | category | flops | bytes accessed | tf_op | source)
XLA Modules:
  0.0 69.7 jit_solution(7618180700189370098)
XLA Ops:
  0.6 0.6 copy-done.4
  1.4 4.7 %collective-permute-start = (bf16[8,2176]{1,0:T(8,128)(2,1)S(1)}, bf16[8,2176]{1,0:T(8,128)(2,1)S(1)}, u32[]{:S(2)}, u32[]{:S(2)}) collective-permute-start(bf16[8,2176]{1,0:T(8,128)(2,1)S(1)} %shard_map.92.refs_0_), channel_id=1, source_target_pairs={{0,12},{1,13},{2,14},{3,15},{4,8},{5,9},{6,10},{7,11},{8,4},{9,5},... | collective-permute-start | bytes 104456 | tf_op jit(solution)/shard_map/ppermute | solution.py:208
  6.0 0.6 collective-permute-start.2
  6.7 1.5 %collective-permute-done.refs_1_ = bf16[8,2176]{1,0:T(8,128)(2,1)S(1)} collective-permute-done((bf16[8,2176]{1,0:T(8,128)(2,1)S(1)}, bf16[8,2176]{1,0:T(8,128)(2,1)S(1)}, u32[]{:S(2)}, u32[]{:S(2)}) %collective-permute-start) | collective-permute-done | bytes 34848 | tf_op jit(solution)/shard_map/ppermute | solution.py:208
  8.1 2.7 %collective-permute-done.1.refs_2_ = bf16[8,2176]{1,0:T(8,128)(2,1)S(1)} collective-permute-done((bf16[8,2176]{1,0:T(8,128)(2,1)S(1)}, bf16[8,2176]{1,0:T(8,128)(2,1)S(1)}, u32[]{:S(2)}, u32[]{:S(2)}) %collective-permute-start.1) | collective-permute-done | bytes 34848 | tf_op jit(solution)/shard_map/ppermute | solution.py:208
  10.9 1.6 %collective-permute-start.3 = (bf16[32,2176]{1,0:T(8,128)(2,1)S(1)}, bf16[32,2176]{1,0:T(8,128)(2,1)S(1)}, u32[]{:S(2)}, u32[]{:S(2)}) collective-permute-start(bf16[32,2176]{1,0:T(8,128)(2,1)S(1)} %bitcast.21), channel_id=1, source_target_pairs={{0,2},{1,3},{2,0},{3,1},{4,6},{5,7},{6,4},{7,5},{8,10},{9,11},{10,... | collective-permute-start | bytes 417800 | tf_op jit(solution)/shard_map/ppermute | solution.py:208
  13.0 3.0 %collective-permute-done.3.across = bf16[32,2176]{1,0:T(8,128)(2,1)S(1)} collective-permute-done((bf16[32,2176]{1,0:T(8,128)(2,1)S(1)}, bf16[32,2176]{1,0:T(8,128)(2,1)S(1)}, u32[]{:S(2)}, u32[]{:S(2)}) %collective-permute-start.3) | collective-permute-done | bytes 139296 | tf_op jit(solution)/shard_map/ppermute | solution.py:208
  16.0 3.5 %shard_map.94 = (bf16[8,8,2048]{2,1,0:T(8,128)(2,1)S(1)}, bf16[8,8,128]{2,1,0:T(8,128)(2,1)S(1)}) custom-call(bf16[32,2176]{1,0:T(8,128)(2,1)S(1)} %bitcast.22, bf16[32,2176]{1,0:T(8,128)(2,1)S(1)} %collective-permute-done.3.across, bf16[768,2048]{1,0:T(8,128)(2,1)S(1)} %bitcast.11, bf16[768,2048]{1,0:T(8,128)(2,1)S(1)} %bitcast.14, ...), custom_call_target="tpu_custom_call" | custom-call | flops 3221225472 | bytes 25165824 | tf_op jit(solution)/shard_map/pallas_call | solution.py:179
  19.5 13.1 %all_to_all.10.returned = bf16[8,8,2048]{2,1,0:T(8,128)(2,1)S(1)} all-to-all(bf16[8,8,2048]{2,1,0:T(8,128)(2,1)S(1)} %get-tuple-element.31), channel_id=1, replica_groups={{0,4,8,12,2,6,10,14},{1,5,9,13,3,7,11,15},{16,20,24,28,18,22,26,30},{17..., dimensions={0} | all-to-all | bytes 524288 | tf_op jit(solution)/shard_map/all_to_all | solution.py:227
  32.8 11.0 %all_to_all.11 = bf16[8,8,2048]{2,1,0:T(8,128)(2,1)S(1)} all-to-all(bf16[8,8,2048]{2,1,0:T(8,128)(2,1)S(1)} %get-tuple-element.33), channel_id=1, replica_groups={{0,4,8,12,2,6,10,14},{1,5,9,13,3,7,11,15},{16,20,24,28,18,22,26,30},{17..., dimensions={0} | all-to-all | bytes 524288 | tf_op jit(solution)/shard_map/all_to_all | solution.py:227
  43.8 1.6 %collective-permute-start.6 = (bf16[64,2176]{1,0:T(8,128)(2,1)S(1)}, bf16[64,2176]{1,0:T(8,128)(2,1)S(1)}, u32[]{:S(2)}, u32[]{:S(2)}) collective-permute-start(bf16[64,2176]{1,0:T(8,128)(2,1)S(1)} %shard_map.96.refs_0_.rows), channel_id=1, source_target_pairs={{0,16},{16,0},{1,17},{17,1},{2,18},{18,2},{3,19},{19,3},{4,20},{20... | collective-permute-start | bytes 835592 | tf_op jit(solution)/shard_map/ppermute | solution.py:203
  45.4 3.5 %shard_map.97.refs_4_ = f32[64,2048]{1,0:T(8,128)S(1)} custom-call(bf16[64,2176]{1,0:T(8,128)(2,1)S(1)} %shard_map.96.refs_0_.rows, bf16[768,2048]{1,0:T(8,128)(2,1)S(1)} %bitcast.12, bf16[768,2048]{1,0:T(8,128)(2,1)S(1)} %bitcast.15, bf16[768,2048]{1,0:T(8,128)(2,1)S(1)} %collective-permute-done.4.refs_2_.refs_3_, ...), custom_call_target="tpu_custom_call" | custom-call | flops 3221225472 | bytes 25165824 | tf_op jit(solution)/shard_map/pallas_call | solution.py:179
  48.8 1.6 %collective-permute-done.6.other = bf16[64,2176]{1,0:T(8,128)(2,1)S(1)} collective-permute-done((bf16[64,2176]{1,0:T(8,128)(2,1)S(1)}, bf16[64,2176]{1,0:T(8,128)(2,1)S(1)}, u32[]{:S(2)}, u32[]{:S(2)}) %collective-permute-start.6) | collective-permute-done | bytes 278560 | tf_op jit(solution)/shard_map/ppermute | solution.py:203
  50.4 2.1 %shard_map.98 = (f32[4,8,2048]{2,1,0:T(8,128)S(1)}, bf16[4,8,2048]{2,1,0:T(8,128)(2,1)S(1)}, f32[4,8,2048]{2,1,0:T(8,128)S(1)}, bf16[4,8,2048]{2,1,0:T(8,128)(2,1)S(1)}) custom-call(bf16[64,2176]{1,0:T(8,128)(2,1)S(1)} %shard_map.96.refs_0_.rows, bf16[64,2176]{1,0:T(8,128)(2,1)S(1)} %collective-permute-done.6.other, bf16[384,2048]{1,0:T(8,128)(2,1)S(1)} %bitcast.17, ...), custom_call_target="tpu_custom_call" | custom-call | flops 1677721600 | bytes 13107200 | tf_op jit(solution)/shard_map/pallas_call | solution.py:179
  52.5 0.6 collective-permute-start.10
  53.2 1.5 %collective-permute-start.9 = (bf16[4,8,2048]{2,1,0:T(8,128)(2,1)S(1)}, bf16[4,8,2048]{2,1,0:T(8,128)(2,1)S(1)}, u32[]{:S(2)}, u32[]{:S(2)}) collective-permute-start(bf16[4,8,2048]{2,1,0:T(8,128)(2,1)S(1)} %get-tuple-element.40), channel_id=1, source_target_pairs={{0,2},{1,3},{2,0},{3,1},{4,6},{5,7},{6,4},{7,5},{8,10},{9,11},{10,... | collective-permute-start | bytes 393224 | tf_op jit(solution)/shard_map/ppermute | solution.py:208
  54.6 2.9 %collective-permute-done.10 = bf16[4,8,2048]{2,1,0:T(8,128)(2,1)S(1)} collective-permute-done((bf16[4,8,2048]{2,1,0:T(8,128)(2,1)S(1)}, bf16[4,8,2048]{2,1,0:T(8,128)(2,1)S(1)}, u32[]{:S(2)}, u32[]{:S(2)}) %collective-permute-start.10) | collective-permute-done | bytes 131104 | tf_op jit(solution)/shard_map/ppermute | solution.py:208
  57.6 1.6 %collective-permute-start.11 = (bf16[4,8,2048]{2,1,0:T(8,128)(2,1)S(1)}, bf16[4,8,2048]{2,1,0:T(8,128)(2,1)S(1)}, u32[]{:S(2)}, u32[]{:S(2)}) collective-permute-start(bf16[4,8,2048]{2,1,0:T(8,128)(2,1)S(1)} %add_convert_fusion), channel_id=1, source_target_pairs={{0,16},{16,0},{1,17},{17,1},{2,18},{18,2},{3,19},{19,3},{4,20},{20... | collective-permute-start | bytes 393224 | tf_op jit(solution)/shard_map/ppermute | solution.py:203
  59.2 3.5 %collective-permute-done.11.away = bf16[4,8,2048]{2,1,0:T(8,128)(2,1)S(1)} collective-permute-done((bf16[4,8,2048]{2,1,0:T(8,128)(2,1)S(1)}, bf16[4,8,2048]{2,1,0:T(8,128)(2,1)S(1)}, u32[]{:S(2)}, u32[]{:S(2)}) %collective-permute-start.11) | collective-permute-done | bytes 131104 | tf_op jit(solution)/shard_map/ppermute | solution.py:203
  63.0 1.1 %collective-permute-start.13 = (bf16[8,2048]{1,0:T(8,128)(2,1)S(1)}, bf16[8,2048]{1,0:T(8,128)(2,1)S(1)}, u32[]{:S(2)}, u32[]{:S(2)}) collective-permute-start(bf16[8,2048]{1,0:T(8,128)(2,1)S(1)} %get-tuple-element.45), channel_id=1, source_target_pairs={{0,8},{1,9},{2,10},{3,11},{4,12},{5,13},{6,14},{7,15},{8,0},{9,1},... | collective-permute-start | bytes 98312 | tf_op jit(solution)/shard_map/ppermute | solution.py:208
  64.1 3.1 %collective-permute-start.14 = (bf16[8,2048]{1,0:T(8,128)(2,1)S(1)}, bf16[8,2048]{1,0:T(8,128)(2,1)S(1)}, u32[]{:S(2)}, u32[]{:S(2)}) collective-permute-start(bf16[8,2048]{1,0:T(8,128)(2,1)S(1)} %get-tuple-element.46), channel_id=1, source_target_pairs={{0,4},{1,5},{2,6},{3,7},{4,0},{5,1},{6,2},{7,3},{8,12},{9,13},{10,... | collective-permute-start | bytes 98312 | tf_op jit(solution)/shard_map/ppermute | solution.py:208
  67.1 1.3 %collective-permute-done.12.refs_0_ = bf16[8,2048]{1,0:T(8,128)(2,1)S(1)} collective-permute-done((bf16[8,2048]{1,0:T(8,128)(2,1)S(1)}, bf16[8,2048]{1,0:T(8,128)(2,1)S(1)}, u32[]{:S(2)}, u32[]{:S(2)}) %collective-permute-start.12) | collective-permute-done | bytes 32800 | tf_op jit(solution)/shard_map/ppermute | solution.py:208
  68.5 0.6 collective-permute-done.14.refs_2_
  69.0 0.6 shard_map.100
  (37 shorter events, 1.8 us)
Async XLA Ops:
  0.0 16.0 %collective-permute-start.4 = (bf16[768,2048]{1,0:T(8,128)(2,1)}, bf16[768,2048]{1,0:T(8,128)(2,1)S(1)}, u32[]{:S(2)}, u32[]{:S(2)}) collective-permute-start(bf16[768,2048]{1,0:T(8,128)(2,1)} %bitcast.10), channel_id=1, source_target_pairs={{0,1},{1,0},{2,3},{3,2},{4,5},{5,4},{6,7},{7,6},{8,9},{9,8},{10,11... | collective-permute-start | bytes 9437192 | tf_op jit(solution)/shard_map/ppermute | solution.py:199
  0.5 0.8 %copy-start.4 = (bf16[1,8,2048]{2,1,0:T(8,128)(2,1)S(1)}, bf16[1,8,2048]{2,1,0:T(8,128)(2,1)}, u32[]{:S(2)}) copy-start(bf16[1,8,2048]{2,1,0:T(8,128)(2,1)} %param.9) | copy-start | bytes 98308
  0.5 0.8 %copy-start.5 = (f32[2048]{0:T(1024)S(1)}, f32[2048]{0:T(1024)}, u32[]{:S(2)}) copy-start(f32[2048]{0:T(1024)} %param.10) | copy-start | bytes 24580
  0.5 0.8 %copy-start.6 = (s32[2,1,8,8]{3,2,1,0:T(8,128)S(1)}, s32[2,1,8,8]{3,2,1,0:T(8,128)}, u32[]{:S(2)}) copy-start(s32[2,1,8,8]{3,2,1,0:T(8,128)} %routes.1) | copy-start | bytes 1540
  0.5 0.8 %copy-start.7 = (f32[2,1,8,8]{3,2,1,0:T(8,128)S(1)}, f32[2,1,8,8]{3,2,1,0:T(8,128)}, u32[]{:S(2)}) copy-start(f32[2,1,8,8]{3,2,1,0:T(8,128)} %scales.1) | copy-start | bytes 1540
  0.5 0.8 %copy-start.8 = (s32[1,4]{1,0:T(1,128)S(1)}, s32[1,4]{1,0:T(1,128)}, u32[]{:S(2)}) copy-start(s32[1,4]{1,0:T(1,128)} %changed.1) | copy-start | bytes 52
  0.5 12.0 %copy-start.2 = (bf16[1,384,2048]{2,1,0:T(8,128)(2,1)S(1)}, bf16[1,384,2048]{2,1,0:T(8,128)(2,1)}, u32[]{:S(2)}) copy-start(bf16[1,384,2048]{2,1,0:T(8,128)(2,1)} %param.16) | copy-start | bytes 4718596
  0.5 12.0 %copy-start.3 = (bf16[1,384,2048]{2,1,0:T(8,128)(2,1)S(1)}, bf16[1,384,2048]{2,1,0:T(8,128)(2,1)}, u32[]{:S(2)}) copy-start(bf16[1,384,2048]{2,1,0:T(8,128)(2,1)} %param.17) | copy-start | bytes 4718596
  0.5 15.5 %copy-start = (bf16[1,768,2048]{2,1,0:T(8,128)(2,1)S(1)}, bf16[1,768,2048]{2,1,0:T(8,128)(2,1)}, u32[]{:S(2)}) copy-start(bf16[1,768,2048]{2,1,0:T(8,128)(2,1)} %param.14) | copy-start | bytes 9437188
  0.5 15.5 %copy-start.1 = (bf16[1,768,2048]{2,1,0:T(8,128)(2,1)S(1)}, bf16[1,768,2048]{2,1,0:T(8,128)(2,1)}, u32[]{:S(2)}) copy-start(bf16[1,768,2048]{2,1,0:T(8,128)(2,1)} %param.15) | copy-start | bytes 9437188
  0.5 15.5 %collective-permute-start.5 = (bf16[768,2048]{1,0:T(8,128)(2,1)}, bf16[768,2048]{1,0:T(8,128)(2,1)S(1)}, u32[]{:S(2)}, u32[]{:S(2)}) collective-permute-start(bf16[768,2048]{1,0:T(8,128)(2,1)} %bitcast.13), channel_id=1, source_target_pairs={{0,1},{1,0},{2,3},{3,2},{4,5},{5,4},{6,7},{7,6},{8,9},{9,8},{10,11... | collective-permute-start | bytes 9437192 | tf_op jit(solution)/shard_map/ppermute | solution.py:199
  1.4 6.8 %collective-permute-start = (bf16[8,2176]{1,0:T(8,128)(2,1)S(1)}, bf16[8,2176]{1,0:T(8,128)(2,1)S(1)}, u32[]{:S(2)}, u32[]{:S(2)}) collective-permute-start(bf16[8,2176]{1,0:T(8,128)(2,1)S(1)} %shard_map.92.refs_0_), channel_id=1, source_target_pairs={{0,12},{1,13},{2,14},{3,15},{4,8},{5,9},{6,10},{7,11},{8,4},{9,5},... | collective-permute-start | bytes 104456 | tf_op jit(solution)/shard_map/ppermute | solution.py:208
  6.0 4.8 %collective-permute-start.1 = (bf16[8,2176]{1,0:T(8,128)(2,1)S(1)}, bf16[8,2176]{1,0:T(8,128)(2,1)S(1)}, u32[]{:S(2)}, u32[]{:S(2)}) collective-permute-start(bf16[8,2176]{1,0:T(8,128)(2,1)S(1)} %shard_map.92.refs_0_), channel_id=1, source_target_pairs={{0,8},{1,9},{2,10},{3,11},{4,12},{5,13},{6,14},{7,15},{8,0},{9,1},... | collective-permute-start | bytes 104456 | tf_op jit(solution)/shard_map/ppermute | solution.py:208
  6.0 4.8 %collective-permute-start.2 = (bf16[8,2176]{1,0:T(8,128)(2,1)S(1)}, bf16[8,2176]{1,0:T(8,128)(2,1)S(1)}, u32[]{:S(2)}, u32[]{:S(2)}) collective-permute-start(bf16[8,2176]{1,0:T(8,128)(2,1)S(1)} %shard_map.92.refs_0_), channel_id=1, source_target_pairs={{0,4},{1,5},{2,6},{3,7},{4,0},{5,1},{6,2},{7,3},{8,12},{9,13},{10,... | collective-permute-start | bytes 104456 | tf_op jit(solution)/shard_map/ppermute | solution.py:208
  10.9 5.1 %collective-permute-start.3 = (bf16[32,2176]{1,0:T(8,128)(2,1)S(1)}, bf16[32,2176]{1,0:T(8,128)(2,1)S(1)}, u32[]{:S(2)}, u32[]{:S(2)}) collective-permute-start(bf16[32,2176]{1,0:T(8,128)(2,1)S(1)} %bitcast.21), channel_id=1, source_target_pairs={{0,2},{1,3},{2,0},{3,1},{4,6},{5,7},{6,4},{7,5},{8,10},{9,11},{10,... | collective-permute-start | bytes 417800 | tf_op jit(solution)/shard_map/ppermute | solution.py:208
  12.5 37.9 %collective-permute-start.7 = (bf16[384,2048]{1,0:T(8,128)(2,1)S(1)}, bf16[384,2048]{1,0:T(8,128)(2,1)S(1)}, u32[]{:S(2)}, u32[]{:S(2)}) collective-permute-start(bf16[384,2048]{1,0:T(8,128)(2,1)S(1)} %bitcast.16), channel_id=1, source_target_pairs={{0,1},{1,0},{2,3},{3,2},{4,5},{5,4},{6,7},{7,6},{8,9},{9,8},{10,11... | collective-permute-start | bytes 4718600 | tf_op jit(solution)/shard_map/ppermute | solution.py:199
  12.5 37.9 %collective-permute-start.8 = (bf16[384,2048]{1,0:T(8,128)(2,1)S(1)}, bf16[384,2048]{1,0:T(8,128)(2,1)S(1)}, u32[]{:S(2)}, u32[]{:S(2)}) collective-permute-start(bf16[384,2048]{1,0:T(8,128)(2,1)S(1)} %bitcast.18), channel_id=1, source_target_pairs={{0,1},{1,0},{2,3},{3,2},{4,5},{5,4},{6,7},{7,6},{8,9},{9,8},{10,11... | collective-permute-start | bytes 4718600 | tf_op jit(solution)/shard_map/ppermute | solution.py:199
  43.8 6.6 %collective-permute-start.6 = (bf16[64,2176]{1,0:T(8,128)(2,1)S(1)}, bf16[64,2176]{1,0:T(8,128)(2,1)S(1)}, u32[]{:S(2)}, u32[]{:S(2)}) collective-permute-start(bf16[64,2176]{1,0:T(8,128)(2,1)S(1)} %shard_map.96.refs_0_.rows), channel_id=1, source_target_pairs={{0,16},{16,0},{1,17},{17,1},{2,18},{18,2},{3,19},{19,3},{4,20},{20... | collective-permute-start | bytes 835592 | tf_op jit(solution)/shard_map/ppermute | solution.py:203
  52.5 5.0 %collective-permute-start.10 = (bf16[4,8,2048]{2,1,0:T(8,128)(2,1)S(1)}, bf16[4,8,2048]{2,1,0:T(8,128)(2,1)S(1)}, u32[]{:S(2)}, u32[]{:S(2)}) collective-permute-start(bf16[4,8,2048]{2,1,0:T(8,128)(2,1)S(1)} %get-tuple-element.42), channel_id=1, source_target_pairs={{0,2},{1,3},{2,0},{3,1},{4,6},{5,7},{6,4},{7,5},{8,10},{9,11},{10,... | collective-permute-start | bytes 393224 | tf_op jit(solution)/shard_map/ppermute | solution.py:208
  53.2 6.0 %collective-permute-start.9 = (bf16[4,8,2048]{2,1,0:T(8,128)(2,1)S(1)}, bf16[4,8,2048]{2,1,0:T(8,128)(2,1)S(1)}, u32[]{:S(2)}, u32[]{:S(2)}) collective-permute-start(bf16[4,8,2048]{2,1,0:T(8,128)(2,1)S(1)} %get-tuple-element.40), channel_id=1, source_target_pairs={{0,2},{1,3},{2,0},{3,1},{4,6},{5,7},{6,4},{7,5},{8,10},{9,11},{10,... | collective-permute-start | bytes 393224 | tf_op jit(solution)/shard_map/ppermute | solution.py:208
  57.6 5.0 %collective-permute-start.11 = (bf16[4,8,2048]{2,1,0:T(8,128)(2,1)S(1)}, bf16[4,8,2048]{2,1,0:T(8,128)(2,1)S(1)}, u32[]{:S(2)}, u32[]{:S(2)}) collective-permute-start(bf16[4,8,2048]{2,1,0:T(8,128)(2,1)S(1)} %add_convert_fusion), channel_id=1, source_target_pairs={{0,16},{16,0},{1,17},{17,1},{2,18},{18,2},{3,19},{19,3},{4,20},{20... | collective-permute-start | bytes 393224 | tf_op jit(solution)/shard_map/ppermute | solution.py:203
  62.7 5.8 %collective-permute-start.12 = (bf16[8,2048]{1,0:T(8,128)(2,1)S(1)}, bf16[8,2048]{1,0:T(8,128)(2,1)S(1)}, u32[]{:S(2)}, u32[]{:S(2)}) collective-permute-start(bf16[8,2048]{1,0:T(8,128)(2,1)S(1)} %get-tuple-element.44), channel_id=1, source_target_pairs={{0,12},{1,13},{2,14},{3,15},{4,8},{5,9},{6,10},{7,11},{8,4},{9,5},... | collective-permute-start | bytes 98312 | tf_op jit(solution)/shard_map/ppermute | solution.py:208
  63.0 5.5 %collective-permute-start.13 = (bf16[8,2048]{1,0:T(8,128)(2,1)S(1)}, bf16[8,2048]{1,0:T(8,128)(2,1)S(1)}, u32[]{:S(2)}, u32[]{:S(2)}) collective-permute-start(bf16[8,2048]{1,0:T(8,128)(2,1)S(1)} %get-tuple-element.45), channel_id=1, source_target_pairs={{0,8},{1,9},{2,10},{3,11},{4,12},{5,13},{6,14},{7,15},{8,0},{9,1},... | collective-permute-start | bytes 98312 | tf_op jit(solution)/shard_map/ppermute | solution.py:208
  64.1 5.0 %collective-permute-start.14 = (bf16[8,2048]{1,0:T(8,128)(2,1)S(1)}, bf16[8,2048]{1,0:T(8,128)(2,1)S(1)}, u32[]{:S(2)}, u32[]{:S(2)}) collective-permute-start(bf16[8,2048]{1,0:T(8,128)(2,1)S(1)} %get-tuple-element.46), channel_id=1, source_target_pairs={{0,4},{1,5},{2,6},{3,7},{4,0},{5,1},{6,2},{7,3},{8,12},{9,13},{10,... | collective-permute-start | bytes 98312 | tf_op jit(solution)/shard_map/ppermute | solution.py:208

commit v27 on v26

--- a/solution.py
+++ b/solution.py
@@ -208,8 +208,13 @@
     return lax.ppermute(value, "expert", [(i, i ^ 2 * distance) for i in range(size)])
 
 
+def line_distances(chips):
+    middle = chips // 4
+    return (middle,) + tuple(d for d in range(chips // 2 - 1, 0, -1) if d != middle)
+
+
 def gather(block, chips, waiting):
-    orders = [0] + list(range(chips - 2, 0, -2))
+    orders = [0] + [2 * distance for distance in line_distances(chips)]
     received = [swap_chip(block, distance) for distance in orders[1:]]
     received = lax.optimization_barrier(tuple(received) + tuple(waiting))
     parts, waiting = (block,) + received[: len(orders) - 1], received[len(orders) - 1 :]
@@ -287,7 +292,7 @@
             )
             away = away_kept + swap_chip(away_sent, 1).astype(jnp.float32)
             away = swap_group(away.astype(jnp.bfloat16))
-            distances = tuple(range(chips // 2 - 1, 0, -1))
+            distances = line_distances(chips)
             own, *sent = on_vmem(
                 functools.partial(part_kernel, distances),
                 (kept, swap_chip(sent, 1), away),

time: 69.9 us -> 70.2 us (level)
  starting transfers between devices: 17.7 us -> 16.7 us
  waiting for transfers between devices: 17.1 us -> 17.9 us
    ppermute x9, starting transfers between devices: 13.4 us -> 12.5 us  [swap_chip(): lax.ppermute(value, 'expert', [(i, i ^ 2 * distance) for i in range(size)])]
    ppermute x9, waiting for transfers between devices: 12 us -> 12.9 us  [swap_chip(): lax.ppermute(value, 'expert', [(i, i ^ 2 * distance) for i in range(size)])]
  transfers between devices with their start and end apart: 15 -> 15, of which waited for: 8 -> 9; matrix products, arithmetic and copies ran while one was open for 0% -> 0% of each run, Pallas kernels for 10% -> 10%
where the time goes in v27:
time: 70.2 us; the launch traced here: 70 us
  blocking collectives  24.6 us (35%)
  waiting for transfers between devices  17.9 us (25%)
  starting transfers between devices  16.7 us (24%)
  Pallas kernels  10 us (14%)
    all_to_all x2, blocking collectives, spread(): lax.all_to_all(blocks, 'expert', 0, 0, axis_index_groups=groups, tiled=True)  24.6 us
    ppermute x9, waiting for transfers between devices, swap_chip(): lax.ppermute(value, 'expert', [(i, i ^ 2 * distance) for i in range(size)])  12.9 us
    ppermute x9, starting transfers between devices, swap_chip(): lax.ppermute(value, 'expert', [(i, i ^ 2 * distance) for i in range(size)])  12.5 us
    pallas_call x10, Pallas kernels, on_vmem(): pl.pallas_call(kernel, out_shape=[jax.ShapeDtypeStruct(shape, kind) for s...  10 us
    ppermute x2, waiting for transfers between devices, swap_group(): return lax.ppermute(value, 'group', [(0, 1), (1, 0)])  5.06 us
    ppermute x2, starting transfers between devices, swap_group(): return lax.ppermute(value, 'group', [(0, 1), (1, 0)])  3.13 us
  transfers between devices with their start and end apart: 15, of which 9 were waited for; matrix products, arithmetic and copies ran while one was open for 0% of the time, Pallas kernels for 10%

profile of v27, /device:TPU:0, one launch (start us, length us, event | category | flops | bytes accessed | tf_op | source)
XLA Modules:
  0.0 70.0 jit_solution(10770472600240145334)
XLA Ops:
  0.6 0.6 copy-done.4
  1.4 3.7 %collective-permute-start = (bf16[8,2176]{1,0:T(8,128)(2,1)S(1)}, bf16[8,2176]{1,0:T(8,128)(2,1)S(1)}, u32[]{:S(2)}, u32[]{:S(2)}) collective-permute-start(bf16[8,2176]{1,0:T(8,128)(2,1)S(1)} %shard_map.92.refs_0_), channel_id=1, source_target_pairs={{0,8},{1,9},{2,10},{3,11},{4,12},{5,13},{6,14},{7,15},{8,0},{9,1},... | collective-permute-start | bytes 104456 | tf_op jit(solution)/shard_map/ppermute | solution.py:208
  5.0 1.3 %collective-permute-start.1 = (bf16[8,2176]{1,0:T(8,128)(2,1)S(1)}, bf16[8,2176]{1,0:T(8,128)(2,1)S(1)}, u32[]{:S(2)}, u32[]{:S(2)}) collective-permute-start(bf16[8,2176]{1,0:T(8,128)(2,1)S(1)} %shard_map.92.refs_0_), channel_id=1, source_target_pairs={{0,12},{1,13},{2,14},{3,15},{4,8},{5,9},{6,10},{7,11},{8,4},{9,5},... | collective-permute-start | bytes 104456 | tf_op jit(solution)/shard_map/ppermute | solution.py:208
  6.6 0.5 collective-permute-done.refs_1_
  7.1 3.7 %collective-permute-done.1.refs_2_ = bf16[8,2176]{1,0:T(8,128)(2,1)S(1)} collective-permute-done((bf16[8,2176]{1,0:T(8,128)(2,1)S(1)}, bf16[8,2176]{1,0:T(8,128)(2,1)S(1)}, u32[]{:S(2)}, u32[]{:S(2)}) %collective-permute-start.1) | collective-permute-done | bytes 34848 | tf_op jit(solution)/shard_map/ppermute | solution.py:208
  10.9 1.6 %collective-permute-start.3 = (bf16[32,2176]{1,0:T(8,128)(2,1)S(1)}, bf16[32,2176]{1,0:T(8,128)(2,1)S(1)}, u32[]{:S(2)}, u32[]{:S(2)}) collective-permute-start(bf16[32,2176]{1,0:T(8,128)(2,1)S(1)} %bitcast.21), channel_id=1, source_target_pairs={{0,2},{1,3},{2,0},{3,1},{4,6},{5,7},{6,4},{7,5},{8,10},{9,11},{10,... | collective-permute-start | bytes 417800 | tf_op jit(solution)/shard_map/ppermute | solution.py:208
  13.0 3.0 %collective-permute-done.3.across = bf16[32,2176]{1,0:T(8,128)(2,1)S(1)} collective-permute-done((bf16[32,2176]{1,0:T(8,128)(2,1)S(1)}, bf16[32,2176]{1,0:T(8,128)(2,1)S(1)}, u32[]{:S(2)}, u32[]{:S(2)}) %collective-permute-start.3) | collective-permute-done | bytes 139296 | tf_op jit(solution)/shard_map/ppermute | solution.py:208
  16.0 3.5 %shard_map.94 = (bf16[8,8,2048]{2,1,0:T(8,128)(2,1)S(1)}, bf16[8,8,128]{2,1,0:T(8,128)(2,1)S(1)}) custom-call(bf16[32,2176]{1,0:T(8,128)(2,1)S(1)} %bitcast.22, bf16[32,2176]{1,0:T(8,128)(2,1)S(1)} %collective-permute-done.3.across, bf16[768,2048]{1,0:T(8,128)(2,1)S(1)} %bitcast.11, bf16[768,2048]{1,0:T(8,128)(2,1)S(1)} %bitcast.14, ...), custom_call_target="tpu_custom_call" | custom-call | flops 3221225472 | bytes 25165824 | tf_op jit(solution)/shard_map/pallas_call | solution.py:179
  19.5 13.6 %all_to_all.10.returned = bf16[8,8,2048]{2,1,0:T(8,128)(2,1)S(1)} all-to-all(bf16[8,8,2048]{2,1,0:T(8,128)(2,1)S(1)} %get-tuple-element.31), channel_id=1, replica_groups={{0,4,8,12,2,6,10,14},{1,5,9,13,3,7,11,15},{16,20,24,28,18,22,26,30},{17..., dimensions={0} | all-to-all | bytes 524288 | tf_op jit(solution)/shard_map/all_to_all | solution.py:232
  33.2 11.0 %all_to_all.11 = bf16[8,8,2048]{2,1,0:T(8,128)(2,1)S(1)} all-to-all(bf16[8,8,2048]{2,1,0:T(8,128)(2,1)S(1)} %get-tuple-element.33), channel_id=1, replica_groups={{0,4,8,12,2,6,10,14},{1,5,9,13,3,7,11,15},{16,20,24,28,18,22,26,30},{17..., dimensions={0} | all-to-all | bytes 524288 | tf_op jit(solution)/shard_map/all_to_all | solution.py:232
  44.2 1.6 %collective-permute-start.6 = (bf16[64,2176]{1,0:T(8,128)(2,1)S(1)}, bf16[64,2176]{1,0:T(8,128)(2,1)S(1)}, u32[]{:S(2)}, u32[]{:S(2)}) collective-permute-start(bf16[64,2176]{1,0:T(8,128)(2,1)S(1)} %shard_map.96.refs_0_.rows), channel_id=1, source_target_pairs={{0,16},{16,0},{1,17},{17,1},{2,18},{18,2},{3,19},{19,3},{4,20},{20... | collective-permute-start | bytes 835592 | tf_op jit(solution)/shard_map/ppermute | solution.py:203
  45.8 3.5 %shard_map.97.refs_4_ = f32[64,2048]{1,0:T(8,128)S(1)} custom-call(bf16[64,2176]{1,0:T(8,128)(2,1)S(1)} %shard_map.96.refs_0_.rows, bf16[768,2048]{1,0:T(8,128)(2,1)S(1)} %bitcast.12, bf16[768,2048]{1,0:T(8,128)(2,1)S(1)} %bitcast.15, bf16[768,2048]{1,0:T(8,128)(2,1)S(1)} %collective-permute-done.4.refs_2_.refs_3_, ...), custom_call_target="tpu_custom_call" | custom-call | flops 3221225472 | bytes 25165824 | tf_op jit(solution)/shard_map/pallas_call | solution.py:179
  49.3 1.6 %collective-permute-done.6.other = bf16[64,2176]{1,0:T(8,128)(2,1)S(1)} collective-permute-done((bf16[64,2176]{1,0:T(8,128)(2,1)S(1)}, bf16[64,2176]{1,0:T(8,128)(2,1)S(1)}, u32[]{:S(2)}, u32[]{:S(2)}) %collective-permute-start.6) | collective-permute-done | bytes 278560 | tf_op jit(solution)/shard_map/ppermute | solution.py:203
  50.9 2.1 %shard_map.98 = (f32[4,8,2048]{2,1,0:T(8,128)S(1)}, bf16[4,8,2048]{2,1,0:T(8,128)(2,1)S(1)}, f32[4,8,2048]{2,1,0:T(8,128)S(1)}, bf16[4,8,2048]{2,1,0:T(8,128)(2,1)S(1)}) custom-call(bf16[64,2176]{1,0:T(8,128)(2,1)S(1)} %shard_map.96.refs_0_.rows, bf16[64,2176]{1,0:T(8,128)(2,1)S(1)} %collective-permute-done.6.other, bf16[384,2048]{1,0:T(8,128)(2,1)S(1)} %bitcast.17, ...), custom_call_target="tpu_custom_call" | custom-call | flops 1677721600 | bytes 13107200 | tf_op jit(solution)/shard_map/pallas_call | solution.py:179
  53.0 0.6 collective-permute-start.10
  53.6 1.5 %collective-permute-start.9 = (bf16[4,8,2048]{2,1,0:T(8,128)(2,1)S(1)}, bf16[4,8,2048]{2,1,0:T(8,128)(2,1)S(1)}, u32[]{:S(2)}, u32[]{:S(2)}) collective-permute-start(bf16[4,8,2048]{2,1,0:T(8,128)(2,1)S(1)} %get-tuple-element.40), channel_id=1, source_target_pairs={{0,2},{1,3},{2,0},{3,1},{4,6},{5,7},{6,4},{7,5},{8,10},{9,11},{10,... | collective-permute-start | bytes 393224 | tf_op jit(solution)/shard_map/ppermute | solution.py:208
  55.1 2.9 %collective-permute-done.10 = bf16[4,8,2048]{2,1,0:T(8,128)(2,1)S(1)} collective-permute-done((bf16[4,8,2048]{2,1,0:T(8,128)(2,1)S(1)}, bf16[4,8,2048]{2,1,0:T(8,128)(2,1)S(1)}, u32[]{:S(2)}, u32[]{:S(2)}) %collective-permute-start.10) | collective-permute-done | bytes 131104 | tf_op jit(solution)/shard_map/ppermute | solution.py:208
  58.0 1.6 %collective-permute-start.11 = (bf16[4,8,2048]{2,1,0:T(8,128)(2,1)S(1)}, bf16[4,8,2048]{2,1,0:T(8,128)(2,1)S(1)}, u32[]{:S(2)}, u32[]{:S(2)}) collective-permute-start(bf16[4,8,2048]{2,1,0:T(8,128)(2,1)S(1)} %add_convert_fusion), channel_id=1, source_target_pairs={{0,16},{16,0},{1,17},{17,1},{2,18},{18,2},{3,19},{19,3},{4,20},{20... | collective-permute-start | bytes 393224 | tf_op jit(solution)/shard_map/ppermute | solution.py:203
  59.6 3.5 %collective-permute-done.11.away = bf16[4,8,2048]{2,1,0:T(8,128)(2,1)S(1)} collective-permute-done((bf16[4,8,2048]{2,1,0:T(8,128)(2,1)S(1)}, bf16[4,8,2048]{2,1,0:T(8,128)(2,1)S(1)}, u32[]{:S(2)}, u32[]{:S(2)}) %collective-permute-start.11) | collective-permute-done | bytes 131104 | tf_op jit(solution)/shard_map/ppermute | solution.py:203
  63.2 2.2 %collective-permute-start.13 = (bf16[8,2048]{1,0:T(8,128)(2,1)S(1)}, bf16[8,2048]{1,0:T(8,128)(2,1)S(1)}, u32[]{:S(2)}, u32[]{:S(2)}) collective-permute-start(bf16[8,2048]{1,0:T(8,128)(2,1)S(1)} %get-tuple-element.45), channel_id=1, source_target_pairs={{0,12},{1,13},{2,14},{3,15},{4,8},{5,9},{6,10},{7,11},{8,4},{9,5},... | collective-permute-start | bytes 98312 | tf_op jit(solution)/shard_map/ppermute | solution.py:208
  65.4 1.3 %collective-permute-start.14 = (bf16[8,2048]{1,0:T(8,128)(2,1)S(1)}, bf16[8,2048]{1,0:T(8,128)(2,1)S(1)}, u32[]{:S(2)}, u32[]{:S(2)}) collective-permute-start(bf16[8,2048]{1,0:T(8,128)(2,1)S(1)} %get-tuple-element.46), channel_id=1, source_target_pairs={{0,4},{1,5},{2,6},{3,7},{4,0},{5,1},{6,2},{7,3},{8,12},{9,13},{10,... | collective-permute-start | bytes 98312 | tf_op jit(solution)/shard_map/ppermute | solution.py:208
  66.7 1.3 %collective-permute-done.12.refs_0_ = bf16[8,2048]{1,0:T(8,128)(2,1)S(1)} collective-permute-done((bf16[8,2048]{1,0:T(8,128)(2,1)S(1)}, bf16[8,2048]{1,0:T(8,128)(2,1)S(1)}, u32[]{:S(2)}, u32[]{:S(2)}) %collective-permute-start.12) | collective-permute-done | bytes 32800 | tf_op jit(solution)/shard_map/ppermute | solution.py:208
  68.0 1.0 %collective-permute-done.13.refs_1_ = bf16[8,2048]{1,0:T(8,128)(2,1)S(1)} collective-permute-done((bf16[8,2048]{1,0:T(8,128)(2,1)S(1)}, bf16[8,2048]{1,0:T(8,128)(2,1)S(1)}, u32[]{:S(2)}, u32[]{:S(2)}) %collective-permute-start.13) | collective-permute-done | bytes 32800 | tf_op jit(solution)/shard_map/ppermute | solution.py:208
  69.3 0.6 shard_map.100
  (37 shorter events, 2.2 us)
Async XLA Ops:
  0.0 16.0 %collective-permute-start.4 = (bf16[768,2048]{1,0:T(8,128)(2,1)}, bf16[768,2048]{1,0:T(8,128)(2,1)S(1)}, u32[]{:S(2)}, u32[]{:S(2)}) collective-permute-start(bf16[768,2048]{1,0:T(8,128)(2,1)} %bitcast.10), channel_id=1, source_target_pairs={{0,1},{1,0},{2,3},{3,2},{4,5},{5,4},{6,7},{7,6},{8,9},{9,8},{10,11... | collective-permute-start | bytes 9437192 | tf_op jit(solution)/shard_map/ppermute | solution.py:199
  0.5 0.8 %copy-start.4 = (bf16[1,8,2048]{2,1,0:T(8,128)(2,1)S(1)}, bf16[1,8,2048]{2,1,0:T(8,128)(2,1)}, u32[]{:S(2)}) copy-start(bf16[1,8,2048]{2,1,0:T(8,128)(2,1)} %param.9) | copy-start | bytes 98308
  0.5 0.8 %copy-start.5 = (f32[2048]{0:T(1024)S(1)}, f32[2048]{0:T(1024)}, u32[]{:S(2)}) copy-start(f32[2048]{0:T(1024)} %param.10) | copy-start | bytes 24580
  0.5 0.8 %copy-start.6 = (s32[2,1,8,8]{3,2,1,0:T(8,128)S(1)}, s32[2,1,8,8]{3,2,1,0:T(8,128)}, u32[]{:S(2)}) copy-start(s32[2,1,8,8]{3,2,1,0:T(8,128)} %routes.1) | copy-start | bytes 1540
  0.5 0.8 %copy-start.7 = (f32[2,1,8,8]{3,2,1,0:T(8,128)S(1)}, f32[2,1,8,8]{3,2,1,0:T(8,128)}, u32[]{:S(2)}) copy-start(f32[2,1,8,8]{3,2,1,0:T(8,128)} %scales.1) | copy-start | bytes 1540
  0.5 0.8 %copy-start.8 = (s32[1,4]{1,0:T(1,128)S(1)}, s32[1,4]{1,0:T(1,128)}, u32[]{:S(2)}) copy-start(s32[1,4]{1,0:T(1,128)} %changed.1) | copy-start | bytes 52
  0.5 12.0 %copy-start.2 = (bf16[1,384,2048]{2,1,0:T(8,128)(2,1)S(1)}, bf16[1,384,2048]{2,1,0:T(8,128)(2,1)}, u32[]{:S(2)}) copy-start(bf16[1,384,2048]{2,1,0:T(8,128)(2,1)} %param.16) | copy-start | bytes 4718596
  0.5 12.0 %copy-start.3 = (bf16[1,384,2048]{2,1,0:T(8,128)(2,1)S(1)}, bf16[1,384,2048]{2,1,0:T(8,128)(2,1)}, u32[]{:S(2)}) copy-start(bf16[1,384,2048]{2,1,0:T(8,128)(2,1)} %param.17) | copy-start | bytes 4718596
  0.5 15.5 %copy-start = (bf16[1,768,2048]{2,1,0:T(8,128)(2,1)S(1)}, bf16[1,768,2048]{2,1,0:T(8,128)(2,1)}, u32[]{:S(2)}) copy-start(bf16[1,768,2048]{2,1,0:T(8,128)(2,1)} %param.14) | copy-start | bytes 9437188
  0.5 15.5 %copy-start.1 = (bf16[1,768,2048]{2,1,0:T(8,128)(2,1)S(1)}, bf16[1,768,2048]{2,1,0:T(8,128)(2,1)}, u32[]{:S(2)}) copy-start(bf16[1,768,2048]{2,1,0:T(8,128)(2,1)} %param.15) | copy-start | bytes 9437188
  0.5 15.5 %collective-permute-start.5 = (bf16[768,2048]{1,0:T(8,128)(2,1)}, bf16[768,2048]{1,0:T(8,128)(2,1)S(1)}, u32[]{:S(2)}, u32[]{:S(2)}) collective-permute-start(bf16[768,2048]{1,0:T(8,128)(2,1)} %bitcast.13), channel_id=1, source_target_pairs={{0,1},{1,0},{2,3},{3,2},{4,5},{5,4},{6,7},{7,6},{8,9},{9,8},{10,11... | collective-permute-start | bytes 9437192 | tf_op jit(solution)/shard_map/ppermute | solution.py:199
  1.4 5.8 %collective-permute-start = (bf16[8,2176]{1,0:T(8,128)(2,1)S(1)}, bf16[8,2176]{1,0:T(8,128)(2,1)S(1)}, u32[]{:S(2)}, u32[]{:S(2)}) collective-permute-start(bf16[8,2176]{1,0:T(8,128)(2,1)S(1)} %shard_map.92.refs_0_), channel_id=1, source_target_pairs={{0,8},{1,9},{2,10},{3,11},{4,12},{5,13},{6,14},{7,15},{8,0},{9,1},... | collective-permute-start | bytes 104456 | tf_op jit(solution)/shard_map/ppermute | solution.py:208
  5.0 5.8 %collective-permute-start.1 = (bf16[8,2176]{1,0:T(8,128)(2,1)S(1)}, bf16[8,2176]{1,0:T(8,128)(2,1)S(1)}, u32[]{:S(2)}, u32[]{:S(2)}) collective-permute-start(bf16[8,2176]{1,0:T(8,128)(2,1)S(1)} %shard_map.92.refs_0_), channel_id=1, source_target_pairs={{0,12},{1,13},{2,14},{3,15},{4,8},{5,9},{6,10},{7,11},{8,4},{9,5},... | collective-permute-start | bytes 104456 | tf_op jit(solution)/shard_map/ppermute | solution.py:208
  6.4 4.5 %collective-permute-start.2 = (bf16[8,2176]{1,0:T(8,128)(2,1)S(1)}, bf16[8,2176]{1,0:T(8,128)(2,1)S(1)}, u32[]{:S(2)}, u32[]{:S(2)}) collective-permute-start(bf16[8,2176]{1,0:T(8,128)(2,1)S(1)} %shard_map.92.refs_0_), channel_id=1, source_target_pairs={{0,4},{1,5},{2,6},{3,7},{4,0},{5,1},{6,2},{7,3},{8,12},{9,13},{10,... | collective-permute-start | bytes 104456 | tf_op jit(solution)/shard_map/ppermute | solution.py:208
  10.9 5.1 %collective-permute-start.3 = (bf16[32,2176]{1,0:T(8,128)(2,1)S(1)}, bf16[32,2176]{1,0:T(8,128)(2,1)S(1)}, u32[]{:S(2)}, u32[]{:S(2)}) collective-permute-start(bf16[32,2176]{1,0:T(8,128)(2,1)S(1)} %bitcast.21), channel_id=1, source_target_pairs={{0,2},{1,3},{2,0},{3,1},{4,6},{5,7},{6,4},{7,5},{8,10},{9,11},{10,... | collective-permute-start | bytes 417800 | tf_op jit(solution)/shard_map/ppermute | solution.py:208
  12.5 38.4 %collective-permute-start.7 = (bf16[384,2048]{1,0:T(8,128)(2,1)S(1)}, bf16[384,2048]{1,0:T(8,128)(2,1)S(1)}, u32[]{:S(2)}, u32[]{:S(2)}) collective-permute-start(bf16[384,2048]{1,0:T(8,128)(2,1)S(1)} %bitcast.16), channel_id=1, source_target_pairs={{0,1},{1,0},{2,3},{3,2},{4,5},{5,4},{6,7},{7,6},{8,9},{9,8},{10,11... | collective-permute-start | bytes 4718600 | tf_op jit(solution)/shard_map/ppermute | solution.py:199
  12.5 38.4 %collective-permute-start.8 = (bf16[384,2048]{1,0:T(8,128)(2,1)S(1)}, bf16[384,2048]{1,0:T(8,128)(2,1)S(1)}, u32[]{:S(2)}, u32[]{:S(2)}) collective-permute-start(bf16[384,2048]{1,0:T(8,128)(2,1)S(1)} %bitcast.18), channel_id=1, source_target_pairs={{0,1},{1,0},{2,3},{3,2},{4,5},{5,4},{6,7},{7,6},{8,9},{9,8},{10,11... | collective-permute-start | bytes 4718600 | tf_op jit(solution)/shard_map/ppermute | solution.py:199
  44.2 6.6 %collective-permute-start.6 = (bf16[64,2176]{1,0:T(8,128)(2,1)S(1)}, bf16[64,2176]{1,0:T(8,128)(2,1)S(1)}, u32[]{:S(2)}, u32[]{:S(2)}) collective-permute-start(bf16[64,2176]{1,0:T(8,128)(2,1)S(1)} %shard_map.96.refs_0_.rows), channel_id=1, source_target_pairs={{0,16},{16,0},{1,17},{17,1},{2,18},{18,2},{3,19},{19,3},{4,20},{20... | collective-permute-start | bytes 835592 | tf_op jit(solution)/shard_map/ppermute | solution.py:203
  53.0 5.0 %collective-permute-start.10 = (bf16[4,8,2048]{2,1,0:T(8,128)(2,1)S(1)}, bf16[4,8,2048]{2,1,0:T(8,128)(2,1)S(1)}, u32[]{:S(2)}, u32[]{:S(2)}) collective-permute-start(bf16[4,8,2048]{2,1,0:T(8,128)(2,1)S(1)} %get-tuple-element.42), channel_id=1, source_target_pairs={{0,2},{1,3},{2,0},{3,1},{4,6},{5,7},{6,4},{7,5},{8,10},{9,11},{10,... | collective-permute-start | bytes 393224 | tf_op jit(solution)/shard_map/ppermute | solution.py:208
  53.6 6.0 %collective-permute-start.9 = (bf16[4,8,2048]{2,1,0:T(8,128)(2,1)S(1)}, bf16[4,8,2048]{2,1,0:T(8,128)(2,1)S(1)}, u32[]{:S(2)}, u32[]{:S(2)}) collective-permute-start(bf16[4,8,2048]{2,1,0:T(8,128)(2,1)S(1)} %get-tuple-element.40), channel_id=1, source_target_pairs={{0,2},{1,3},{2,0},{3,1},{4,6},{5,7},{6,4},{7,5},{8,10},{9,11},{10,... | collective-permute-start | bytes 393224 | tf_op jit(solution)/shard_map/ppermute | solution.py:208
  58.0 5.0 %collective-permute-start.11 = (bf16[4,8,2048]{2,1,0:T(8,128)(2,1)S(1)}, bf16[4,8,2048]{2,1,0:T(8,128)(2,1)S(1)}, u32[]{:S(2)}, u32[]{:S(2)}) collective-permute-start(bf16[4,8,2048]{2,1,0:T(8,128)(2,1)S(1)} %add_convert_fusion), channel_id=1, source_target_pairs={{0,16},{16,0},{1,17},{17,1},{2,18},{18,2},{3,19},{19,3},{4,20},{20... | collective-permute-start | bytes 393224 | tf_op jit(solution)/shard_map/ppermute | solution.py:203
  63.1 4.9 %collective-permute-start.12 = (bf16[8,2048]{1,0:T(8,128)(2,1)S(1)}, bf16[8,2048]{1,0:T(8,128)(2,1)S(1)}, u32[]{:S(2)}, u32[]{:S(2)}) collective-permute-start(bf16[8,2048]{1,0:T(8,128)(2,1)S(1)} %get-tuple-element.44), channel_id=1, source_target_pairs={{0,8},{1,9},{2,10},{3,11},{4,12},{5,13},{6,14},{7,15},{8,0},{9,1},... | collective-permute-start | bytes 98312 | tf_op jit(solution)/shard_map/ppermute | solution.py:208
  63.2 5.8 %collective-permute-start.13 = (bf16[8,2048]{1,0:T(8,128)(2,1)S(1)}, bf16[8,2048]{1,0:T(8,128)(2,1)S(1)}, u32[]{:S(2)}, u32[]{:S(2)}) collective-permute-start(bf16[8,2048]{1,0:T(8,128)(2,1)S(1)} %get-tuple-element.45), channel_id=1, source_target_pairs={{0,12},{1,13},{2,14},{3,15},{4,8},{5,9},{6,10},{7,11},{8,4},{9,5},... | collective-permute-start | bytes 98312 | tf_op jit(solution)/shard_map/ppermute | solution.py:208
  65.4 3.9 %collective-permute-start.14 = (bf16[8,2048]{1,0:T(8,128)(2,1)S(1)}, bf16[8,2048]{1,0:T(8,128)(2,1)S(1)}, u32[]{:S(2)}, u32[]{:S(2)}) collective-permute-start(bf16[8,2048]{1,0:T(8,128)(2,1)S(1)} %get-tuple-element.46), channel_id=1, source_target_pairs={{0,4},{1,5},{2,6},{3,7},{4,0},{5,1},{6,2},{7,3},{8,12},{9,13},{10,... | collective-permute-start | bytes 98312 | tf_op jit(solution)/shard_map/ppermute | solution.py:208

commit v28 on v26

--- a/solution.py
+++ b/solution.py
@@ -287,7 +287,8 @@
             )
             away = away_kept + swap_chip(away_sent, 1).astype(jnp.float32)
             away = swap_group(away.astype(jnp.bfloat16))
-            distances = tuple(range(chips // 2 - 1, 0, -1))
+            middle = chips // 4
+            distances = (middle,) + tuple(d for d in range(chips // 2 - 1, 0, -1) if d != middle)
             own, *sent = on_vmem(
                 functools.partial(part_kernel, distances),
                 (kept, swap_chip(sent, 1), away),

time: 69.9 us -> 69.7 us (level)
  starting transfers between devices: 17.7 us -> 16.7 us
  waiting for transfers between devices: 17.1 us -> 17.9 us
    ppermute x9, starting transfers between devices: 13.4 us -> 12.5 us  [swap_chip(): lax.ppermute(value, 'expert', [(i, i ^ 2 * distance) for i in range(size)])]
    ppermute x9, waiting for transfers between devices: 12 us -> 12.8 us  [swap_chip(): lax.ppermute(value, 'expert', [(i, i ^ 2 * distance) for i in range(size)])]
  transfers between devices with their start and end apart: 15 -> 15, of which waited for: 8 -> 9; matrix products, arithmetic and copies ran while one was open for 0% -> 0% of each run, Pallas kernels for 10% -> 10%
where the time goes in v28:
time: 69.7 us; the launch traced here: 69.5 us
  blocking collectives  24.1 us (35%)
  waiting for transfers between devices  17.9 us (26%)
  starting transfers between devices  16.7 us (24%)
  Pallas kernels  10 us (14%)
    all_to_all x2, blocking collectives, spread(): lax.all_to_all(blocks, 'expert', 0, 0, axis_index_groups=groups, tiled=True)  24.1 us
    ppermute x9, waiting for transfers between devices, swap_chip(): lax.ppermute(value, 'expert', [(i, i ^ 2 * distance) for i in range(size)])  12.8 us
    ppermute x9, starting transfers between devices, swap_chip(): lax.ppermute(value, 'expert', [(i, i ^ 2 * distance) for i in range(size)])  12.5 us
    pallas_call x10, Pallas kernels, on_vmem(): pl.pallas_call(kernel, out_shape=[jax.ShapeDtypeStruct(shape, kind) for s...  10 us
    ppermute x2, waiting for transfers between devices, swap_group(): return lax.ppermute(value, 'group', [(0, 1), (1, 0)])  5.04 us
    ppermute x2, starting transfers between devices, swap_group(): return lax.ppermute(value, 'group', [(0, 1), (1, 0)])  3.13 us
  transfers between devices with their start and end apart: 15, of which 9 were waited for; matrix products, arithmetic and copies ran while one was open for 0% of the time, Pallas kernels for 10%

profile of v28, /device:TPU:0, one launch (start us, length us, event | category | flops | bytes accessed | tf_op | source)
XLA Modules:
  0.0 69.5 jit_solution(4036206024471004405)
XLA Ops:
  0.6 0.6 copy-done.4
  1.4 4.7 %collective-permute-start = (bf16[8,2176]{1,0:T(8,128)(2,1)S(1)}, bf16[8,2176]{1,0:T(8,128)(2,1)S(1)}, u32[]{:S(2)}, u32[]{:S(2)}) collective-permute-start(bf16[8,2176]{1,0:T(8,128)(2,1)S(1)} %shard_map.92.refs_0_), channel_id=1, source_target_pairs={{0,12},{1,13},{2,14},{3,15},{4,8},{5,9},{6,10},{7,11},{8,4},{9,5},... | collective-permute-start | bytes 104456 | tf_op jit(solution)/shard_map/ppermute | solution.py:208
  6.0 0.6 collective-permute-start.2
  6.7 1.5 %collective-permute-done.refs_1_ = bf16[8,2176]{1,0:T(8,128)(2,1)S(1)} collective-permute-done((bf16[8,2176]{1,0:T(8,128)(2,1)S(1)}, bf16[8,2176]{1,0:T(8,128)(2,1)S(1)}, u32[]{:S(2)}, u32[]{:S(2)}) %collective-permute-start) | collective-permute-done | bytes 34848 | tf_op jit(solution)/shard_map/ppermute | solution.py:208
  8.1 2.7 %collective-permute-done.1.refs_2_ = bf16[8,2176]{1,0:T(8,128)(2,1)S(1)} collective-permute-done((bf16[8,2176]{1,0:T(8,128)(2,1)S(1)}, bf16[8,2176]{1,0:T(8,128)(2,1)S(1)}, u32[]{:S(2)}, u32[]{:S(2)}) %collective-permute-start.1) | collective-permute-done | bytes 34848 | tf_op jit(solution)/shard_map/ppermute | solution.py:208
  10.9 1.6 %collective-permute-start.3 = (bf16[32,2176]{1,0:T(8,128)(2,1)S(1)}, bf16[32,2176]{1,0:T(8,128)(2,1)S(1)}, u32[]{:S(2)}, u32[]{:S(2)}) collective-permute-start(bf16[32,2176]{1,0:T(8,128)(2,1)S(1)} %bitcast.21), channel_id=1, source_target_pairs={{0,2},{1,3},{2,0},{3,1},{4,6},{5,7},{6,4},{7,5},{8,10},{9,11},{10,... | collective-permute-start | bytes 417800 | tf_op jit(solution)/shard_map/ppermute | solution.py:208
  13.0 3.0 %collective-permute-done.3.across = bf16[32,2176]{1,0:T(8,128)(2,1)S(1)} collective-permute-done((bf16[32,2176]{1,0:T(8,128)(2,1)S(1)}, bf16[32,2176]{1,0:T(8,128)(2,1)S(1)}, u32[]{:S(2)}, u32[]{:S(2)}) %collective-permute-start.3) | collective-permute-done | bytes 139296 | tf_op jit(solution)/shard_map/ppermute | solution.py:208
  16.0 3.5 %shard_map.94 = (bf16[8,8,2048]{2,1,0:T(8,128)(2,1)S(1)}, bf16[8,8,128]{2,1,0:T(8,128)(2,1)S(1)}) custom-call(bf16[32,2176]{1,0:T(8,128)(2,1)S(1)} %bitcast.22, bf16[32,2176]{1,0:T(8,128)(2,1)S(1)} %collective-permute-done.3.across, bf16[768,2048]{1,0:T(8,128)(2,1)S(1)} %bitcast.11, bf16[768,2048]{1,0:T(8,128)(2,1)S(1)} %bitcast.14, ...), custom_call_target="tpu_custom_call" | custom-call | flops 3221225472 | bytes 25165824 | tf_op jit(solution)/shard_map/pallas_call | solution.py:179
  19.5 13.1 %all_to_all.10.returned = bf16[8,8,2048]{2,1,0:T(8,128)(2,1)S(1)} all-to-all(bf16[8,8,2048]{2,1,0:T(8,128)(2,1)S(1)} %get-tuple-element.31), channel_id=1, replica_groups={{0,4,8,12,2,6,10,14},{1,5,9,13,3,7,11,15},{16,20,24,28,18,22,26,30},{17..., dimensions={0} | all-to-all | bytes 524288 | tf_op jit(solution)/shard_map/all_to_all | solution.py:227
  32.8 11.0 %all_to_all.11 = bf16[8,8,2048]{2,1,0:T(8,128)(2,1)S(1)} all-to-all(bf16[8,8,2048]{2,1,0:T(8,128)(2,1)S(1)} %get-tuple-element.33), channel_id=1, replica_groups={{0,4,8,12,2,6,10,14},{1,5,9,13,3,7,11,15},{16,20,24,28,18,22,26,30},{17..., dimensions={0} | all-to-all | bytes 524288 | tf_op jit(solution)/shard_map/all_to_all | solution.py:227
  43.8 1.6 %collective-permute-start.6 = (bf16[64,2176]{1,0:T(8,128)(2,1)S(1)}, bf16[64,2176]{1,0:T(8,128)(2,1)S(1)}, u32[]{:S(2)}, u32[]{:S(2)}) collective-permute-start(bf16[64,2176]{1,0:T(8,128)(2,1)S(1)} %shard_map.96.refs_0_.rows), channel_id=1, source_target_pairs={{0,16},{16,0},{1,17},{17,1},{2,18},{18,2},{3,19},{19,3},{4,20},{20... | collective-permute-start | bytes 835592 | tf_op jit(solution)/shard_map/ppermute | solution.py:203
  45.4 3.5 %shard_map.97.refs_4_ = f32[64,2048]{1,0:T(8,128)S(1)} custom-call(bf16[64,2176]{1,0:T(8,128)(2,1)S(1)} %shard_map.96.refs_0_.rows, bf16[768,2048]{1,0:T(8,128)(2,1)S(1)} %bitcast.12, bf16[768,2048]{1,0:T(8,128)(2,1)S(1)} %bitcast.15, bf16[768,2048]{1,0:T(8,128)(2,1)S(1)} %collective-permute-done.4.refs_2_.refs_3_, ...), custom_call_target="tpu_custom_call" | custom-call | flops 3221225472 | bytes 25165824 | tf_op jit(solution)/shard_map/pallas_call | solution.py:179
  48.8 1.6 %collective-permute-done.6.other = bf16[64,2176]{1,0:T(8,128)(2,1)S(1)} collective-permute-done((bf16[64,2176]{1,0:T(8,128)(2,1)S(1)}, bf16[64,2176]{1,0:T(8,128)(2,1)S(1)}, u32[]{:S(2)}, u32[]{:S(2)}) %collective-permute-start.6) | collective-permute-done | bytes 278560 | tf_op jit(solution)/shard_map/ppermute | solution.py:203
  50.4 2.1 %shard_map.98 = (f32[4,8,2048]{2,1,0:T(8,128)S(1)}, bf16[4,8,2048]{2,1,0:T(8,128)(2,1)S(1)}, f32[4,8,2048]{2,1,0:T(8,128)S(1)}, bf16[4,8,2048]{2,1,0:T(8,128)(2,1)S(1)}) custom-call(bf16[64,2176]{1,0:T(8,128)(2,1)S(1)} %shard_map.96.refs_0_.rows, bf16[64,2176]{1,0:T(8,128)(2,1)S(1)} %collective-permute-done.6.other, bf16[384,2048]{1,0:T(8,128)(2,1)S(1)} %bitcast.17, ...), custom_call_target="tpu_custom_call" | custom-call | flops 1677721600 | bytes 13107200 | tf_op jit(solution)/shard_map/pallas_call | solution.py:179
  52.5 0.6 collective-permute-start.10
  53.2 1.5 %collective-permute-start.9 = (bf16[4,8,2048]{2,1,0:T(8,128)(2,1)S(1)}, bf16[4,8,2048]{2,1,0:T(8,128)(2,1)S(1)}, u32[]{:S(2)}, u32[]{:S(2)}) collective-permute-start(bf16[4,8,2048]{2,1,0:T(8,128)(2,1)S(1)} %get-tuple-element.40), channel_id=1, source_target_pairs={{0,2},{1,3},{2,0},{3,1},{4,6},{5,7},{6,4},{7,5},{8,10},{9,11},{10,... | collective-permute-start | bytes 393224 | tf_op jit(solution)/shard_map/ppermute | solution.py:208
  54.6 2.9 %collective-permute-done.10 = bf16[4,8,2048]{2,1,0:T(8,128)(2,1)S(1)} collective-permute-done((bf16[4,8,2048]{2,1,0:T(8,128)(2,1)S(1)}, bf16[4,8,2048]{2,1,0:T(8,128)(2,1)S(1)}, u32[]{:S(2)}, u32[]{:S(2)}) %collective-permute-start.10) | collective-permute-done | bytes 131104 | tf_op jit(solution)/shard_map/ppermute | solution.py:208
  57.6 1.6 %collective-permute-start.11 = (bf16[4,8,2048]{2,1,0:T(8,128)(2,1)S(1)}, bf16[4,8,2048]{2,1,0:T(8,128)(2,1)S(1)}, u32[]{:S(2)}, u32[]{:S(2)}) collective-permute-start(bf16[4,8,2048]{2,1,0:T(8,128)(2,1)S(1)} %add_convert_fusion), channel_id=1, source_target_pairs={{0,16},{16,0},{1,17},{17,1},{2,18},{18,2},{3,19},{19,3},{4,20},{20... | collective-permute-start | bytes 393224 | tf_op jit(solution)/shard_map/ppermute | solution.py:203
  59.2 3.5 %collective-permute-done.11.away = bf16[4,8,2048]{2,1,0:T(8,128)(2,1)S(1)} collective-permute-done((bf16[4,8,2048]{2,1,0:T(8,128)(2,1)S(1)}, bf16[4,8,2048]{2,1,0:T(8,128)(2,1)S(1)}, u32[]{:S(2)}, u32[]{:S(2)}) %collective-permute-start.11) | collective-permute-done | bytes 131104 | tf_op jit(solution)/shard_map/ppermute | solution.py:203
  62.8 2.2 %collective-permute-start.13 = (bf16[8,2048]{1,0:T(8,128)(2,1)S(1)}, bf16[8,2048]{1,0:T(8,128)(2,1)S(1)}, u32[]{:S(2)}, u32[]{:S(2)}) collective-permute-start(bf16[8,2048]{1,0:T(8,128)(2,1)S(1)} %get-tuple-element.45), channel_id=1, source_target_pairs={{0,12},{1,13},{2,14},{3,15},{4,8},{5,9},{6,10},{7,11},{8,4},{9,5},... | collective-permute-start | bytes 98312 | tf_op jit(solution)/shard_map/ppermute | solution.py:208
  65.0 1.3 %collective-permute-start.14 = (bf16[8,2048]{1,0:T(8,128)(2,1)S(1)}, bf16[8,2048]{1,0:T(8,128)(2,1)S(1)}, u32[]{:S(2)}, u32[]{:S(2)}) collective-permute-start(bf16[8,2048]{1,0:T(8,128)(2,1)S(1)} %get-tuple-element.46), channel_id=1, source_target_pairs={{0,4},{1,5},{2,6},{3,7},{4,0},{5,1},{6,2},{7,3},{8,12},{9,13},{10,... | collective-permute-start | bytes 98312 | tf_op jit(solution)/shard_map/ppermute | solution.py:208
  66.2 1.3 %collective-permute-done.12.refs_0_ = bf16[8,2048]{1,0:T(8,128)(2,1)S(1)} collective-permute-done((bf16[8,2048]{1,0:T(8,128)(2,1)S(1)}, bf16[8,2048]{1,0:T(8,128)(2,1)S(1)}, u32[]{:S(2)}, u32[]{:S(2)}) %collective-permute-start.12) | collective-permute-done | bytes 32800 | tf_op jit(solution)/shard_map/ppermute | solution.py:208
  67.6 1.0 %collective-permute-done.13.refs_1_ = bf16[8,2048]{1,0:T(8,128)(2,1)S(1)} collective-permute-done((bf16[8,2048]{1,0:T(8,128)(2,1)S(1)}, bf16[8,2048]{1,0:T(8,128)(2,1)S(1)}, u32[]{:S(2)}, u32[]{:S(2)}) %collective-permute-start.13) | collective-permute-done | bytes 32800 | tf_op jit(solution)/shard_map/ppermute | solution.py:208
  68.9 0.6 shard_map.100
  (37 shorter events, 2.0 us)
Async XLA Ops:
  0.0 16.0 %collective-permute-start.4 = (bf16[768,2048]{1,0:T(8,128)(2,1)}, bf16[768,2048]{1,0:T(8,128)(2,1)S(1)}, u32[]{:S(2)}, u32[]{:S(2)}) collective-permute-start(bf16[768,2048]{1,0:T(8,128)(2,1)} %bitcast.10), channel_id=1, source_target_pairs={{0,1},{1,0},{2,3},{3,2},{4,5},{5,4},{6,7},{7,6},{8,9},{9,8},{10,11... | collective-permute-start | bytes 9437192 | tf_op jit(solution)/shard_map/ppermute | solution.py:199
  0.5 0.8 %copy-start.4 = (bf16[1,8,2048]{2,1,0:T(8,128)(2,1)S(1)}, bf16[1,8,2048]{2,1,0:T(8,128)(2,1)}, u32[]{:S(2)}) copy-start(bf16[1,8,2048]{2,1,0:T(8,128)(2,1)} %param.9) | copy-start | bytes 98308
  0.5 0.8 %copy-start.5 = (f32[2048]{0:T(1024)S(1)}, f32[2048]{0:T(1024)}, u32[]{:S(2)}) copy-start(f32[2048]{0:T(1024)} %param.10) | copy-start | bytes 24580
  0.5 0.8 %copy-start.6 = (s32[2,1,8,8]{3,2,1,0:T(8,128)S(1)}, s32[2,1,8,8]{3,2,1,0:T(8,128)}, u32[]{:S(2)}) copy-start(s32[2,1,8,8]{3,2,1,0:T(8,128)} %routes.1) | copy-start | bytes 1540
  0.5 0.8 %copy-start.7 = (f32[2,1,8,8]{3,2,1,0:T(8,128)S(1)}, f32[2,1,8,8]{3,2,1,0:T(8,128)}, u32[]{:S(2)}) copy-start(f32[2,1,8,8]{3,2,1,0:T(8,128)} %scales.1) | copy-start | bytes 1540
  0.5 0.8 %copy-start.8 = (s32[1,4]{1,0:T(1,128)S(1)}, s32[1,4]{1,0:T(1,128)}, u32[]{:S(2)}) copy-start(s32[1,4]{1,0:T(1,128)} %changed.1) | copy-start | bytes 52
  0.5 12.0 %copy-start.2 = (bf16[1,384,2048]{2,1,0:T(8,128)(2,1)S(1)}, bf16[1,384,2048]{2,1,0:T(8,128)(2,1)}, u32[]{:S(2)}) copy-start(bf16[1,384,2048]{2,1,0:T(8,128)(2,1)} %param.16) | copy-start | bytes 4718596
  0.5 12.0 %copy-start.3 = (bf16[1,384,2048]{2,1,0:T(8,128)(2,1)S(1)}, bf16[1,384,2048]{2,1,0:T(8,128)(2,1)}, u32[]{:S(2)}) copy-start(bf16[1,384,2048]{2,1,0:T(8,128)(2,1)} %param.17) | copy-start | bytes 4718596
  0.5 15.5 %copy-start = (bf16[1,768,2048]{2,1,0:T(8,128)(2,1)S(1)}, bf16[1,768,2048]{2,1,0:T(8,128)(2,1)}, u32[]{:S(2)}) copy-start(bf16[1,768,2048]{2,1,0:T(8,128)(2,1)} %param.14) | copy-start | bytes 9437188
  0.5 15.5 %copy-start.1 = (bf16[1,768,2048]{2,1,0:T(8,128)(2,1)S(1)}, bf16[1,768,2048]{2,1,0:T(8,128)(2,1)}, u32[]{:S(2)}) copy-start(bf16[1,768,2048]{2,1,0:T(8,128)(2,1)} %param.15) | copy-start | bytes 9437188
  0.5 15.5 %collective-permute-start.5 = (bf16[768,2048]{1,0:T(8,128)(2,1)}, bf16[768,2048]{1,0:T(8,128)(2,1)S(1)}, u32[]{:S(2)}, u32[]{:S(2)}) collective-permute-start(bf16[768,2048]{1,0:T(8,128)(2,1)} %bitcast.13), channel_id=1, source_target_pairs={{0,1},{1,0},{2,3},{3,2},{4,5},{5,4},{6,7},{7,6},{8,9},{9,8},{10,11... | collective-permute-start | bytes 9437192 | tf_op jit(solution)/shard_map/ppermute | solution.py:199
  1.4 6.8 %collective-permute-start = (bf16[8,2176]{1,0:T(8,128)(2,1)S(1)}, bf16[8,2176]{1,0:T(8,128)(2,1)S(1)}, u32[]{:S(2)}, u32[]{:S(2)}) collective-permute-start(bf16[8,2176]{1,0:T(8,128)(2,1)S(1)} %shard_map.92.refs_0_), channel_id=1, source_target_pairs={{0,12},{1,13},{2,14},{3,15},{4,8},{5,9},{6,10},{7,11},{8,4},{9,5},... | collective-permute-start | bytes 104456 | tf_op jit(solution)/shard_map/ppermute | solution.py:208
  6.0 4.8 %collective-permute-start.1 = (bf16[8,2176]{1,0:T(8,128)(2,1)S(1)}, bf16[8,2176]{1,0:T(8,128)(2,1)S(1)}, u32[]{:S(2)}, u32[]{:S(2)}) collective-permute-start(bf16[8,2176]{1,0:T(8,128)(2,1)S(1)} %shard_map.92.refs_0_), channel_id=1, source_target_pairs={{0,8},{1,9},{2,10},{3,11},{4,12},{5,13},{6,14},{7,15},{8,0},{9,1},... | collective-permute-start | bytes 104456 | tf_op jit(solution)/shard_map/ppermute | solution.py:208
  6.0 4.8 %collective-permute-start.2 = (bf16[8,2176]{1,0:T(8,128)(2,1)S(1)}, bf16[8,2176]{1,0:T(8,128)(2,1)S(1)}, u32[]{:S(2)}, u32[]{:S(2)}) collective-permute-start(bf16[8,2176]{1,0:T(8,128)(2,1)S(1)} %shard_map.92.refs_0_), channel_id=1, source_target_pairs={{0,4},{1,5},{2,6},{3,7},{4,0},{5,1},{6,2},{7,3},{8,12},{9,13},{10,... | collective-permute-start | bytes 104456 | tf_op jit(solution)/shard_map/ppermute | solution.py:208
  10.9 5.1 %collective-permute-start.3 = (bf16[32,2176]{1,0:T(8,128)(2,1)S(1)}, bf16[32,2176]{1,0:T(8,128)(2,1)S(1)}, u32[]{:S(2)}, u32[]{:S(2)}) collective-permute-start(bf16[32,2176]{1,0:T(8,128)(2,1)S(1)} %bitcast.21), channel_id=1, source_target_pairs={{0,2},{1,3},{2,0},{3,1},{4,6},{5,7},{6,4},{7,5},{8,10},{9,11},{10,... | collective-permute-start | bytes 417800 | tf_op jit(solution)/shard_map/ppermute | solution.py:208
  12.5 37.9 %collective-permute-start.7 = (bf16[384,2048]{1,0:T(8,128)(2,1)S(1)}, bf16[384,2048]{1,0:T(8,128)(2,1)S(1)}, u32[]{:S(2)}, u32[]{:S(2)}) collective-permute-start(bf16[384,2048]{1,0:T(8,128)(2,1)S(1)} %bitcast.16), channel_id=1, source_target_pairs={{0,1},{1,0},{2,3},{3,2},{4,5},{5,4},{6,7},{7,6},{8,9},{9,8},{10,11... | collective-permute-start | bytes 4718600 | tf_op jit(solution)/shard_map/ppermute | solution.py:199
  12.5 37.9 %collective-permute-start.8 = (bf16[384,2048]{1,0:T(8,128)(2,1)S(1)}, bf16[384,2048]{1,0:T(8,128)(2,1)S(1)}, u32[]{:S(2)}, u32[]{:S(2)}) collective-permute-start(bf16[384,2048]{1,0:T(8,128)(2,1)S(1)} %bitcast.18), channel_id=1, source_target_pairs={{0,1},{1,0},{2,3},{3,2},{4,5},{5,4},{6,7},{7,6},{8,9},{9,8},{10,11... | collective-permute-start | bytes 4718600 | tf_op jit(solution)/shard_map/ppermute | solution.py:199
  43.8 6.6 %collective-permute-start.6 = (bf16[64,2176]{1,0:T(8,128)(2,1)S(1)}, bf16[64,2176]{1,0:T(8,128)(2,1)S(1)}, u32[]{:S(2)}, u32[]{:S(2)}) collective-permute-start(bf16[64,2176]{1,0:T(8,128)(2,1)S(1)} %shard_map.96.refs_0_.rows), channel_id=1, source_target_pairs={{0,16},{16,0},{1,17},{17,1},{2,18},{18,2},{3,19},{19,3},{4,20},{20... | collective-permute-start | bytes 835592 | tf_op jit(solution)/shard_map/ppermute | solution.py:203
  52.5 5.0 %collective-permute-start.10 = (bf16[4,8,2048]{2,1,0:T(8,128)(2,1)S(1)}, bf16[4,8,2048]{2,1,0:T(8,128)(2,1)S(1)}, u32[]{:S(2)}, u32[]{:S(2)}) collective-permute-start(bf16[4,8,2048]{2,1,0:T(8,128)(2,1)S(1)} %get-tuple-element.42), channel_id=1, source_target_pairs={{0,2},{1,3},{2,0},{3,1},{4,6},{5,7},{6,4},{7,5},{8,10},{9,11},{10,... | collective-permute-start | bytes 393224 | tf_op jit(solution)/shard_map/ppermute | solution.py:208
  53.2 6.0 %collective-permute-start.9 = (bf16[4,8,2048]{2,1,0:T(8,128)(2,1)S(1)}, bf16[4,8,2048]{2,1,0:T(8,128)(2,1)S(1)}, u32[]{:S(2)}, u32[]{:S(2)}) collective-permute-start(bf16[4,8,2048]{2,1,0:T(8,128)(2,1)S(1)} %get-tuple-element.40), channel_id=1, source_target_pairs={{0,2},{1,3},{2,0},{3,1},{4,6},{5,7},{6,4},{7,5},{8,10},{9,11},{10,... | collective-permute-start | bytes 393224 | tf_op jit(solution)/shard_map/ppermute | solution.py:208
  57.6 5.0 %collective-permute-start.11 = (bf16[4,8,2048]{2,1,0:T(8,128)(2,1)S(1)}, bf16[4,8,2048]{2,1,0:T(8,128)(2,1)S(1)}, u32[]{:S(2)}, u32[]{:S(2)}) collective-permute-start(bf16[4,8,2048]{2,1,0:T(8,128)(2,1)S(1)} %add_convert_fusion), channel_id=1, source_target_pairs={{0,16},{16,0},{1,17},{17,1},{2,18},{18,2},{3,19},{19,3},{4,20},{20... | collective-permute-start | bytes 393224 | tf_op jit(solution)/shard_map/ppermute | solution.py:203
  62.7 4.9 %collective-permute-start.12 = (bf16[8,2048]{1,0:T(8,128)(2,1)S(1)}, bf16[8,2048]{1,0:T(8,128)(2,1)S(1)}, u32[]{:S(2)}, u32[]{:S(2)}) collective-permute-start(bf16[8,2048]{1,0:T(8,128)(2,1)S(1)} %get-tuple-element.44), channel_id=1, source_target_pairs={{0,8},{1,9},{2,10},{3,11},{4,12},{5,13},{6,14},{7,15},{8,0},{9,1},... | collective-permute-start | bytes 98312 | tf_op jit(solution)/shard_map/ppermute | solution.py:208
  62.8 5.8 %collective-permute-start.13 = (bf16[8,2048]{1,0:T(8,128)(2,1)S(1)}, bf16[8,2048]{1,0:T(8,128)(2,1)S(1)}, u32[]{:S(2)}, u32[]{:S(2)}) collective-permute-start(bf16[8,2048]{1,0:T(8,128)(2,1)S(1)} %get-tuple-element.45), channel_id=1, source_target_pairs={{0,12},{1,13},{2,14},{3,15},{4,8},{5,9},{6,10},{7,11},{8,4},{9,5},... | collective-permute-start | bytes 98312 | tf_op jit(solution)/shard_map/ppermute | solution.py:208
  65.0 3.9 %collective-permute-start.14 = (bf16[8,2048]{1,0:T(8,128)(2,1)S(1)}, bf16[8,2048]{1,0:T(8,128)(2,1)S(1)}, u32[]{:S(2)}, u32[]{:S(2)}) collective-permute-start(bf16[8,2048]{1,0:T(8,128)(2,1)S(1)} %get-tuple-element.46), channel_id=1, source_target_pairs={{0,4},{1,5},{2,6},{3,7},{4,0},{5,1},{6,2},{7,3},{8,12},{9,13},{10,... | collective-permute-start | bytes 98312 | tf_op jit(solution)/shard_map/ppermute | solution.py:208
